TPU v7x, 32 devices: a whole 2x2x4 slice. The times are simulated.
32 devices in a mesh: gx: 2 (over y), gy: 4 (over z), gz: 4 (over x, core).
Axes of the slice: x: 2, y: 2, z: 4, core: 2. Of those that a mesh axis runs over, the one named last changes fastest.
Arguments:
- checkpoint_store: bfloat16 [32, 9, 1, 32, 256], P('gz', None, None, 'gy', 'gx'), may hold values from -6 to 6
- holder_peer: int32 [2, 4, 4, 8], P('gx', 'gy'), may hold values from 0 to 3, as said below
- holder_slot: int32 [2, 4, 4, 8], P('gx', 'gy'), may hold values from 0 to 7, as said below
- adjoint_state: float32 [9, 32, 32, 256], P(None, 'gz', 'gy', 'gx'), may hold values from -6 to 6
- lame_lambda: float32 [32, 32, 256], P('gz', 'gy', 'gx'), may hold values from 0.1 to 0.3
- lame_mu: float32 [32, 32, 256], P('gz', 'gy', 'gx'), may hold values from 0.05 to 0.15
- buoyancy: float32 [32, 32, 256], P('gz', 'gy', 'gx'), may hold values from 0.25 to 0.5
- source_cell: int32 [4, 4, 2, 4], P('gz', 'gy', 'gx'), may hold values from 0 to 8191
- wavelet: float32 [64], replicated, may hold values from -6 to 6
- receiver_cell: int32 [4, 4, 2, 64], P('gz', 'gy', 'gx'), may hold values from 0 to 8191
- traces: float32 [4, 4, 2, 64, 64], P('gz', 'gy', 'gx'), may hold values from -6 to 6
- plan: int32 [2], replicated, may hold values from 0 to 63
Outputs:
- adjoint_final: float32 [9, 32, 32, 256], P(None, 'gz', 'gy', 'gx')
- image_lambda: float32 [32, 32, 256], P('gz', 'gy', 'gx')
- image_mu: float32 [32, 32, 256], P('gz', 'gy', 'gx')
Inputs may be any that keep to these rules, and one draw needn't show every extreme that they name: `holder_peer`: within each group of bricks sharing x and y bricks, every holder's 8 slots hold exactly one piece each; for every brick one holder supplies exactly 5 of its pieces and each other holder exactly one. `holder_slot`: slots of one holder are distinct over the pieces it holds.
All inputs are finite; a program needn't handle non-finite values.
Results may differ from a plain program's by a relative error of at most 0.0003.
Values may be sent and summed in bfloat16 or wider, within the bound.
No kernel may reach another device: no remote copies, remote signals or barrier semaphores. Data moves between devices by JAX's collectives and lax.ppermute only.
A program may use at most 128 MiB of HBM per device.

v0:
```python
import jax
import jax.numpy as jnp
from jax import lax
from jax.sharding import PartitionSpec as P

STEPS = 2


along_z = 0
along_y = 1
along_x = 2


def padded_2(cells, sides, width):
    for axis, dim in sides:
        count = lax.axis_size(axis)
        ends = count - 1
        head = lax.slice_in_dim(cells, 0, width, axis=dim)
        tail = lax.slice_in_dim(cells, cells.shape[dim] - width, cells.shape[dim], axis=dim)
        cells = jnp.concatenate(
            [
                lax.ppermute(tail, axis, [(i, (i + 1) % count) for i in range(ends)]),
                cells,
                lax.ppermute(head, axis, [((i + 1) % count, i) for i in range(ends)]),
            ],
            axis=dim,
        )
    return cells


def shifted(padded, which_axis, offset):
    extents = padded.shape[-3:]
    starts = [1, 1, 1]
    starts[which_axis] = 1 + offset
    return padded[
        ...,
        starts[0] : starts[0] + extents[0] - 2,
        starts[1] : starts[1] + extents[1] - 2,
        starts[2] : starts[2] + extents[2] - 2,
    ]


def ahead(padded, which_axis):
    return shifted(padded, which_axis, 1) - shifted(padded, which_axis, 0)


def behind(padded, which_axis):
    return shifted(padded, which_axis, 0) - shifted(padded, which_axis, -1)


def velocity_rates(stress_pad, buoyancy):
    rate_x = buoyancy * (
        ahead(stress_pad[0], along_x)
        + behind(stress_pad[3], along_y)
        + behind(stress_pad[4], along_z)
    )
    rate_y = buoyancy * (
        behind(stress_pad[3], along_x)
        + ahead(stress_pad[1], along_y)
        + behind(stress_pad[5], along_z)
    )
    rate_z = buoyancy * (
        behind(stress_pad[4], along_x)
        + behind(stress_pad[5], along_y)
        + ahead(stress_pad[2], along_z)
    )
    return jnp.stack([rate_x, rate_y, rate_z])


def stress_rates(velocity_pad, lame_lambda, lame_mu):
    strain_xx = behind(velocity_pad[0], along_x)
    strain_yy = behind(velocity_pad[1], along_y)
    strain_zz = behind(velocity_pad[2], along_z)
    dilation = strain_xx + strain_yy + strain_zz
    rate_xx = lame_lambda * dilation + 2.0 * lame_mu * strain_xx
    rate_yy = lame_lambda * dilation + 2.0 * lame_mu * strain_yy
    rate_zz = lame_lambda * dilation + 2.0 * lame_mu * strain_zz
    rate_xy = lame_mu * (ahead(velocity_pad[0], along_y) + ahead(velocity_pad[1], along_x))
    rate_xz = lame_mu * (ahead(velocity_pad[0], along_z) + ahead(velocity_pad[2], along_x))
    rate_yz = lame_mu * (ahead(velocity_pad[1], along_z) + ahead(velocity_pad[2], along_y))
    return jnp.stack([rate_xx, rate_yy, rate_zz, rate_xy, rate_xz, rate_yz])


def imaging_terms(forward_stress, adjoint_stress):
    pressure_fwd = forward_stress[0] + forward_stress[1] + forward_stress[2]
    pressure_adj = adjoint_stress[0] + adjoint_stress[1] + adjoint_stress[2]
    term_lambda = pressure_fwd * pressure_adj
    term_mu = (
        forward_stress[0] * adjoint_stress[0]
        + forward_stress[1] * adjoint_stress[1]
        + forward_stress[2] * adjoint_stress[2]
        + 2.0
        * (
            forward_stress[3] * adjoint_stress[3]
            + forward_stress[4] * adjoint_stress[4]
            + forward_stress[5] * adjoint_stress[5]
        )
    )
    return (term_lambda, term_mu)


def stress_rim(stress):
    return padded_2(stress, (("gx", 3), ("gy", 2), ("gz", 1)), 1)


def velocity_rim(velocity):
    return padded_2(velocity, (("gx", 3), ("gy", 2), ("gz", 1)), 1)


def inject(stress, cells, values):
    normal = stress[:3]
    flat = normal.reshape(3, -1).at[:, cells].add(values).reshape(normal.shape)
    return jnp.concatenate([flat, stress[3:]], axis=0)


def restore(checkpoint_store, holder_peer, holder_slot):
    pieces = holder_peer.shape[-1]
    layers = checkpoint_store.shape[2]
    peer_table = holder_peer[0, 0]
    slot_table = holder_slot[0, 0]
    position = lax.axis_index("gz")
    my_peers = lax.dynamic_index_in_dim(peer_table, position, 0, keepdims=False)
    my_slots = lax.dynamic_index_in_dim(slot_table, position, 0, keepdims=False)
    everything = lax.all_gather(checkpoint_store, "gz", axis=0, tiled=True)
    rows = everything[my_peers * pieces + my_slots]
    restored = jnp.transpose(rows, (1, 0, 2, 3, 4)).reshape((9, pieces * layers) + rows.shape[-2:])
    return restored.astype(jnp.float32)


def on_device(
    checkpoint_store,
    holder_peer,
    holder_slot,
    adjoint_state,
    lame_lambda,
    lame_mu,
    buoyancy,
    source_cell,
    wavelet,
    receiver_cell,
    traces,
    plan,
):
    source_flat = source_cell.reshape(-1)
    receiver_flat = receiver_cell.reshape(-1)
    trace_rows = traces.reshape(traces.shape[-2], traces.shape[-1])
    state = restore(checkpoint_store, holder_peer, holder_slot)
    adjoint = adjoint_state
    snapshots = [state[3:]]
    injected = {}
    for step_now in range(STEPS):
        velocity = state[:3] + velocity_rates(stress_rim(state[3:]), buoyancy)
        stress = state[3:] + stress_rates(velocity_rim(velocity), lame_lambda, lame_mu)
        stress = inject(stress, source_flat, wavelet[plan[step_now]])
        state = jnp.concatenate([velocity, stress], axis=0)
        snapshots.append(stress)
    for step_now in reversed(range(STEPS)):
        stress = inject(adjoint[3:], receiver_flat, trace_rows[plan[step_now]])
        injected[step_now] = stress
        stress = stress - stress_rates(velocity_rim(adjoint[:3]), lame_lambda, lame_mu)
        velocity = adjoint[:3] - velocity_rates(stress_rim(stress), buoyancy)
        adjoint = jnp.concatenate([velocity, stress], axis=0)
    image_lambda = jnp.zeros(lame_mu.shape, jnp.float32)
    image_mu = jnp.zeros(lame_mu.shape, jnp.float32)
    for step_now in reversed(range(STEPS)):
        term_lambda, term_mu = imaging_terms(snapshots[step_now + 1], injected[step_now])
        image_lambda = image_lambda + term_lambda
        image_mu = image_mu + term_mu
    return (adjoint, image_lambda, image_mu)


def solution(mesh):
    return jax.shard_map(
        on_device,
        mesh=mesh,
        in_specs=(
            P("gz", None, None, "gy", "gx"),
            P("gx", "gy", None, None),
            P("gx", "gy", None, None),
            P(None, "gz", "gy", "gx"),
            P("gz", "gy", "gx"),
            P("gz", "gy", "gx"),
            P("gz", "gy", "gx"),
            P("gz", "gy", "gx", None),
            P(),
            P("gz", "gy", "gx", None),
            P("gz", "gy", "gx", None, None),
            P(),
        ),
        out_specs=(P(None, "gz", "gy", "gx"), P("gz", "gy", "gx"), P("gz", "gy", "gx")),
        check_vma=False,
    )
```

profile of v0, /device:TPU:21, one launch (start us, length us, event | category | flops | bytes accessed | tf_op | source)
XLA Modules:
  0.0 248.0 jit_solution(4583938070167828233)
XLA Ops:
  3.0 4.0 %collective-permute-start.1 = (f32[3,8,8,1]{3,2,1,0:T(8,128)S(1)}, f32[3,8,8,1]{3,2,1,0:T(8,128)S(1)}, u32[]{:S(2)}, u32[]{:S(2)}) collective-permute-start(f32[3,8,8,1]{3,2,1,0:T(8,128)S(1)} %get-tuple-element.88), channel_id=1, source_target_pairs={{16,0},{17,1},{18,2},{19,3},{20,4},{21,5},{22,6},{23,7},{24,8},{25... | collective-permute-start | bytes 2312 | tf_op jit(solution)/shard_map/ppermute | solution.py:24
  7.7 8.8 %all_gather.3 = bf16[32,9,1,8,128]{4,3,2,1,0:T(8,128)(2,1)S(1)} all-gather(bf16[8,9,1,8,128]{4,3,2,1,0:T(8,128)(2,1)} %param.12), channel_id=1, replica_groups=mesh['gx'=2,'gy'=4,'gz'=4] {'gz'}, dimensions={0}, use_global_device_ids=true | all-gather | bytes 737280 | tf_op jit(solution)/shard_map/all_gather | solution.py:124
  18.6 4.0 %collective-permute-start.25 = (f32[6,8,8,1]{3,2,0,1:T(8,128)S(1)}, f32[6,8,8,1]{3,2,0,1:T(8,128)S(1)}, u32[]{:S(2)}, u32[]{:S(2)}) collective-permute-start(f32[6,8,8,1]{3,2,0,1:T(8,128)S(1)} %get-tuple-element.79), channel_id=1, source_target_pairs={{16,0},{17,1},{18,2},{19,3},{20,4},{21,5},{22,6},{23,7},{24,8},{25... | collective-permute-start | bytes 4616 | tf_op jit(solution)/shard_map/ppermute | solution.py:24
  39.2 5.1 %scatter_custom_fusion = f32[3,8192]{0,1:T(8,128)} fusion(f32[3,8192]{0,1:T(8,128)} %bitcast.236, s32[64]{0:T(128)S(1)} %fusion.111, f32[64]{0:T(128)S(1)} %get-tuple-element.128), kind=kCustom, calls=%fused_computation.342 | custom fusion | flops 192 | bytes 98816 | tf_op jit(solution)/shard_map/scatter-add | solution.py:112
  47.9 3.4 %collective-permute-start.28 = (f32[6,1,10,130]{3,2,1,0:T(8,128)S(1)}, f32[6,1,10,130]{3,2,1,0:T(8,128)S(1)}, u32[]{:S(2)}, u32[]{:S(2)}) collective-permute-start(f32[6,1,10,130]{3,2,1,0:T(8,128)S(1)} %get-tuple-element.40), channel_id=1, source_target_pairs={{0,1},{1,2},{2,3},{4,5},{5,6},{6,7},{8,9},{9,10},{10,11},{12,13},{... | collective-permute-start | bytes 93608 | tf_op jit(solution)/shard_map/ppermute | solution.py:22
  61.0 4.0 %collective-permute-start.31 = (f32[3,8,8,1]{3,2,1,0:T(8,128)S(1)}, f32[3,8,8,1]{3,2,1,0:T(8,128)S(1)}, u32[]{:S(2)}, u32[]{:S(2)}) collective-permute-start(f32[3,8,8,1]{3,2,1,0:T(8,128)S(1)} %get-tuple-element.116), channel_id=1, source_target_pairs={{16,0},{17,1},{18,2},{19,3},{20,4},{21,5},{22,6},{23,7},{24,8},{25... | collective-permute-start | bytes 2312 | tf_op jit(solution)/shard_map/ppermute | solution.py:24
  65.1 4.8 %collective-permute-start.4 = (f32[3,1,10,130]{3,2,1,0:T(8,128)S(1)}, f32[3,1,10,130]{3,2,1,0:T(8,128)S(1)}, u32[]{:S(2)}, u32[]{:S(2)}) collective-permute-start(f32[3,1,10,130]{3,2,1,0:T(8,128)S(1)} %get-tuple-element.72), channel_id=1, source_target_pairs={{0,1},{1,2},{2,3},{4,5},{5,6},{6,7},{8,9},{9,10},{10,11},{12,13},{... | collective-permute-start | bytes 46808 | tf_op jit(solution)/shard_map/ppermute | solution.py:22
  79.9 5.1 %collective-permute-start.34 = (f32[3,1,10,130]{3,2,1,0:T(8,128)S(1)}, f32[3,1,10,130]{3,2,1,0:T(8,128)S(1)}, u32[]{:S(2)}, u32[]{:S(2)}) collective-permute-start(f32[3,1,10,130]{3,2,1,0:T(8,128)S(1)} %get-tuple-element.68), channel_id=1, source_target_pairs={{0,1},{1,2},{2,3},{4,5},{5,6},{6,7},{8,9},{9,10},{10,11},{12,13},{... | collective-permute-start | bytes 46808 | tf_op jit(solution)/shard_map/ppermute | solution.py:22
  87.0 3.4 %collective-permute-done.35 = f32[3,1,10,130]{3,2,1,0:T(8,128)S(1)} collective-permute-done((f32[3,1,10,130]{3,2,1,0:T(8,128)S(1)}, f32[3,1,10,130]{3,2,1,0:T(8,128)S(1)}, u32[]{:S(2)}, u32[]{:S(2)}) %collective-permute-start.35) | collective-permute-done | bytes 15632 | tf_op jit(solution)/shard_map/ppermute | solution.py:24
  93.4 4.0 %collective-permute-start.7 = (f32[6,8,8,1]{3,2,1,0:T(8,128)S(1)}, f32[6,8,8,1]{3,2,1,0:T(8,128)S(1)}, u32[]{:S(2)}, u32[]{:S(2)}) collective-permute-start(f32[6,8,8,1]{3,2,1,0:T(8,128)S(1)} %get-tuple-element.110), channel_id=1, source_target_pairs={{16,0},{17,1},{18,2},{19,3},{20,4},{21,5},{22,6},{23,7},{24,8},{25... | collective-permute-start | bytes 4616 | tf_op jit(solution)/shard_map/ppermute | solution.py:24
  100.1 5.4 %scatter_custom_fusion.2 = f32[3,8192]{0,1:T(8,128)} fusion(f32[3,8192]{0,1:T(8,128)} %bitcast.238, s32[4]{0:T(128)S(1)} %fusion.113, f32[]{:T(128)} %bitcast.77), kind=kCustom, calls=%fused_computation.351 | custom fusion | flops 12 | bytes 98816 | tf_op jit(solution)/shard_map/scatter-add | solution.py:112
  111.2 5.2 %scatter_custom_fusion.1 = f32[3,8192]{0,1:T(8,128)} fusion(f32[3,8192]{0,1:T(8,128)} %bitcast.234, s32[64]{0:T(128)S(1)} %fusion.111, f32[64]{0:T(128)S(1)} %get-tuple-element.127), kind=kCustom, calls=%fused_computation.340 | custom fusion | flops 192 | bytes 98816 | tf_op jit(solution)/shard_map/scatter-add | solution.py:112
  120.7 4.0 %collective-permute-start.37 = (f32[6,8,8,1]{3,2,1,0:T(8,128)S(1)}, f32[6,8,8,1]{3,2,1,0:T(8,128)S(1)}, u32[]{:S(2)}, u32[]{:S(2)}) collective-permute-start(f32[6,8,8,1]{3,2,1,0:T(8,128)S(1)} %get-tuple-element.93), channel_id=1, source_target_pairs={{16,0},{17,1},{18,2},{19,3},{20,4},{21,5},{22,6},{23,7},{24,8},{25... | collective-permute-start | bytes 4616 | tf_op jit(solution)/shard_map/ppermute | solution.py:24
  132.7 3.4 %collective-permute-start.39 = (f32[6,8,1,130]{3,2,1,0:T(1,128)S(1)}, f32[6,8,1,130]{3,2,1,0:T(1,128)S(1)}, u32[]{:S(2)}, u32[]{:S(2)}) collective-permute-start(f32[6,8,1,130]{3,2,1,0:T(1,128)S(1)} %get-tuple-element.47), channel_id=1, source_target_pairs={{4,0},{8,4},{12,8},{5,1},{9,5},{13,9},{6,2},{10,6},{14,10},{7,3},{... | collective-permute-start | bytes 74888 | tf_op jit(solution)/shard_map/ppermute | solution.py:24
  136.3 4.1 %collective-permute-start.10 = (f32[6,1,10,130]{3,2,1,0:T(8,128)S(1)}, f32[6,1,10,130]{3,2,1,0:T(8,128)S(1)}, u32[]{:S(2)}, u32[]{:S(2)}) collective-permute-start(f32[6,1,10,130]{3,2,1,0:T(8,128)S(1)} %get-tuple-element.44), channel_id=1, source_target_pairs={{0,1},{1,2},{2,3},{4,5},{5,6},{6,7},{8,9},{9,10},{10,11},{12,13},{... | collective-permute-start | bytes 93608 | tf_op jit(solution)/shard_map/ppermute | solution.py:22
  142.5 3.6 %collective-permute-start.40 = (f32[6,1,10,130]{3,2,1,0:T(8,128)S(1)}, f32[6,1,10,130]{3,2,1,0:T(8,128)S(1)}, u32[]{:S(2)}, u32[]{:S(2)}) collective-permute-start(f32[6,1,10,130]{3,2,1,0:T(8,128)S(1)} %get-tuple-element.38), channel_id=1, source_target_pairs={{0,1},{1,2},{2,3},{4,5},{5,6},{6,7},{8,9},{9,10},{10,11},{12,13},{... | collective-permute-start | bytes 93608 | tf_op jit(solution)/shard_map/ppermute | solution.py:22
  150.2 4.0 %collective-permute-start.13 = (f32[3,8,8,1]{3,2,1,0:T(8,128)S(1)}, f32[3,8,8,1]{3,2,1,0:T(8,128)S(1)}, u32[]{:S(2)}, u32[]{:S(2)}) collective-permute-start(f32[3,8,8,1]{3,2,1,0:T(8,128)S(1)} %get-tuple-element.118), channel_id=1, source_target_pairs={{16,0},{17,1},{18,2},{19,3},{20,4},{21,5},{22,6},{23,7},{24,8},{25... | collective-permute-start | bytes 2312 | tf_op jit(solution)/shard_map/ppermute | solution.py:24
  156.3 4.0 %collective-permute-start.43 = (f32[3,8,8,1]{3,2,0,1:T(8,128)S(1)}, f32[3,8,8,1]{3,2,0,1:T(8,128)S(1)}, u32[]{:S(2)}, u32[]{:S(2)}) collective-permute-start(f32[3,8,8,1]{3,2,0,1:T(8,128)S(1)} %get-tuple-element.114), channel_id=1, source_target_pairs={{16,0},{17,1},{18,2},{19,3},{20,4},{21,5},{22,6},{23,7},{24,8},{25... | collective-permute-start | bytes 2312 | tf_op jit(solution)/shard_map/ppermute | solution.py:24
  168.2 3.4 %collective-permute-start.45 = (f32[3,8,1,130]{3,2,0,1:T(1,128)S(1)}, f32[3,8,1,130]{3,2,0,1:T(1,128)S(1)}, u32[]{:S(2)}, u32[]{:S(2)}) collective-permute-start(f32[3,8,1,130]{3,2,0,1:T(1,128)S(1)} %get-tuple-element.75), channel_id=1, source_target_pairs={{4,0},{8,4},{12,8},{5,1},{9,5},{13,9},{6,2},{10,6},{14,10},{7,3},{... | collective-permute-start | bytes 37448 | tf_op jit(solution)/shard_map/ppermute | solution.py:24
  171.7 5.9 %collective-permute-start.16 = (f32[3,1,10,130]{3,2,1,0:T(8,128)S(1)}, f32[3,1,10,130]{3,2,1,0:T(8,128)S(1)}, u32[]{:S(2)}, u32[]{:S(2)}) collective-permute-start(f32[3,1,10,130]{3,2,1,0:T(8,128)S(1)} %get-tuple-element.70), channel_id=1, source_target_pairs={{0,1},{1,2},{2,3},{4,5},{5,6},{6,7},{8,9},{9,10},{10,11},{12,13},{... | collective-permute-start | bytes 46808 | tf_op jit(solution)/shard_map/ppermute | solution.py:22
  179.7 3.6 %collective-permute-start.46 = (f32[3,1,10,130]{3,2,0,1:T(8,128)S(1)}, f32[3,1,10,130]{3,2,0,1:T(8,128)S(1)}, u32[]{:S(2)}, u32[]{:S(2)}) collective-permute-start(f32[3,1,10,130]{3,2,0,1:T(8,128)S(1)} %get-tuple-element.66), channel_id=1, source_target_pairs={{0,1},{1,2},{2,3},{4,5},{5,6},{6,7},{8,9},{9,10},{10,11},{12,13},{... | collective-permute-start | bytes 46808 | tf_op jit(solution)/shard_map/ppermute | solution.py:22
  191.6 4.0 %collective-permute-start.19 = (f32[6,8,8,1]{3,2,1,0:T(8,128)S(1)}, f32[6,8,8,1]{3,2,1,0:T(8,128)S(1)}, u32[]{:S(2)}, u32[]{:S(2)}) collective-permute-start(f32[6,8,8,1]{3,2,1,0:T(8,128)S(1)} %get-tuple-element.103), channel_id=1, source_target_pairs={{16,0},{17,1},{18,2},{19,3},{20,4},{21,5},{22,6},{23,7},{24,8},{25... | collective-permute-start | bytes 4616 | tf_op jit(solution)/shard_map/ppermute | solution.py:24
  198.3 5.4 %scatter_custom_fusion.3 = f32[3,8192]{0,1:T(8,128)} fusion(f32[3,8192]{0,1:T(8,128)} %bitcast.240, s32[4]{0:T(128)S(1)} %fusion.113, f32[]{:T(128)} %bitcast.98), kind=kCustom, calls=%fused_computation.349 | custom fusion | flops 12 | bytes 98816 | tf_op jit(solution)/shard_map/scatter-add | solution.py:112
  209.3 28.2 %add_reduce_fusion.1 = (f32[8192]{0:T(1024)S(1)}, f32[8192]{0:T(1024)}, f32[8192]{0:T(1024)S(1)}) fusion(f32[3,8192]{0,1:T(8,128)} %scatter_custom_fusion, f32[3,8192]{0,1:T(8,128)} %scatter_custom_fusion.3, f32[3,8192]{0,1:T(8,128)} %scatter_custom_fusion.1, f32[3,8192]{0,1:T(8,128)} %scatter_custom_fusion.2), kind=kLoop, calls=%fused_computation.6 | loop fusion | flops 172032 | bytes 491520 | tf_op jit(solution)/shard_map/add | solution.py:89
  (182 shorter events, 111.5 us)
Async XLA Ops:
  1.7 51.6 %collective-permute-start = (f32[3,8,8,1]{3,2,1,0:T(8,128)S(1)}, f32[3,8,8,1]{3,2,1,0:T(8,128)S(1)}, u32[]{:S(2)}, u32[]{:S(2)}) collective-permute-start(f32[3,8,8,1]{3,2,1,0:T(8,128)S(1)} %get-tuple-element.87), channel_id=1, source_target_pairs={{0,16},{1,17},{2,18},{3,19},{4,20},{5,21},{6,22},{7,23},{8,24},{9,... | collective-permute-start | bytes 2312 | tf_op jit(solution)/shard_map/ppermute | solution.py:22
  3.0 50.3 %collective-permute-start.1 = (f32[3,8,8,1]{3,2,1,0:T(8,128)S(1)}, f32[3,8,8,1]{3,2,1,0:T(8,128)S(1)}, u32[]{:S(2)}, u32[]{:S(2)}) collective-permute-start(f32[3,8,8,1]{3,2,1,0:T(8,128)S(1)} %get-tuple-element.88), channel_id=1, source_target_pairs={{16,0},{17,1},{18,2},{19,3},{20,4},{21,5},{22,6},{23,7},{24,8},{25... | collective-permute-start | bytes 2312 | tf_op jit(solution)/shard_map/ppermute | solution.py:24
  17.3 12.9 %collective-permute-start.24 = (f32[6,8,8,1]{3,2,0,1:T(8,128)S(1)}, f32[6,8,8,1]{3,2,0,1:T(8,128)S(1)}, u32[]{:S(2)}, u32[]{:S(2)}) collective-permute-start(f32[6,8,8,1]{3,2,0,1:T(8,128)S(1)} %get-tuple-element.78), channel_id=1, source_target_pairs={{0,16},{1,17},{2,18},{3,19},{4,20},{5,21},{6,22},{7,23},{8,24},{9,... | collective-permute-start | bytes 4616 | tf_op jit(solution)/shard_map/ppermute | solution.py:22
  18.6 11.6 %collective-permute-start.25 = (f32[6,8,8,1]{3,2,0,1:T(8,128)S(1)}, f32[6,8,8,1]{3,2,0,1:T(8,128)S(1)}, u32[]{:S(2)}, u32[]{:S(2)}) collective-permute-start(f32[6,8,8,1]{3,2,0,1:T(8,128)S(1)} %get-tuple-element.79), channel_id=1, source_target_pairs={{16,0},{17,1},{18,2},{19,3},{20,4},{21,5},{22,6},{23,7},{24,8},{25... | collective-permute-start | bytes 4616 | tf_op jit(solution)/shard_map/ppermute | solution.py:24
  30.5 17.2 %collective-permute-start.26 = (f32[6,8,1,130]{3,2,1,0:T(1,128)S(1)}, f32[6,8,1,130]{3,2,1,0:T(1,128)S(1)}, u32[]{:S(2)}, u32[]{:S(2)}) collective-permute-start(f32[6,8,1,130]{3,2,1,0:T(1,128)S(1)} %get-tuple-element.48), channel_id=1, source_target_pairs={{0,4},{4,8},{8,12},{1,5},{5,9},{9,13},{2,6},{6,10},{10,14},{3,7},{... | collective-permute-start | bytes 74888 | tf_op jit(solution)/shard_map/ppermute | solution.py:22
  33.7 14.0 %collective-permute-start.27 = (f32[6,8,1,130]{3,2,1,0:T(1,128)S(1)}, f32[6,8,1,130]{3,2,1,0:T(1,128)S(1)}, u32[]{:S(2)}, u32[]{:S(2)}) collective-permute-start(f32[6,8,1,130]{3,2,1,0:T(1,128)S(1)} %get-tuple-element.49), channel_id=1, source_target_pairs={{4,0},{8,4},{12,8},{5,1},{9,5},{13,9},{6,2},{10,6},{14,10},{7,3},{... | collective-permute-start | bytes 74888 | tf_op jit(solution)/shard_map/ppermute | solution.py:24
  53.5 11.4 %collective-permute-start.2 = (f32[3,8,1,130]{3,2,1,0:T(1,128)S(1)}, f32[3,8,1,130]{3,2,1,0:T(1,128)S(1)}, u32[]{:S(2)}, u32[]{:S(2)}) collective-permute-start(f32[3,8,1,130]{3,2,1,0:T(1,128)S(1)} %get-tuple-element.85), channel_id=1, source_target_pairs={{0,4},{4,8},{8,12},{1,5},{5,9},{9,13},{2,6},{6,10},{10,14},{3,7},{... | collective-permute-start | bytes 37448 | tf_op jit(solution)/shard_map/ppermute | solution.py:22
  59.7 12.1 %collective-permute-start.30 = (f32[3,8,8,1]{3,2,1,0:T(8,128)S(1)}, f32[3,8,8,1]{3,2,1,0:T(8,128)S(1)}, u32[]{:S(2)}, u32[]{:S(2)}) collective-permute-start(f32[3,8,8,1]{3,2,1,0:T(8,128)S(1)} %get-tuple-element.115), channel_id=1, source_target_pairs={{0,16},{1,17},{2,18},{3,19},{4,20},{5,21},{6,22},{7,23},{8,24},{9,... | collective-permute-start | bytes 2312 | tf_op jit(solution)/shard_map/ppermute | solution.py:22
  65.1 12.2 %collective-permute-start.4 = (f32[3,1,10,130]{3,2,1,0:T(8,128)S(1)}, f32[3,1,10,130]{3,2,1,0:T(8,128)S(1)}, u32[]{:S(2)}, u32[]{:S(2)}) collective-permute-start(f32[3,1,10,130]{3,2,1,0:T(8,128)S(1)} %get-tuple-element.72), channel_id=1, source_target_pairs={{0,1},{1,2},{2,3},{4,5},{5,6},{6,7},{8,9},{9,10},{10,11},{12,13},{... | collective-permute-start | bytes 46808 | tf_op jit(solution)/shard_map/ppermute | solution.py:22
  92.1 32.6 %collective-permute-start.6 = (f32[6,8,8,1]{3,2,1,0:T(8,128)S(1)}, f32[6,8,8,1]{3,2,1,0:T(8,128)S(1)}, u32[]{:S(2)}, u32[]{:S(2)}) collective-permute-start(f32[6,8,8,1]{3,2,1,0:T(8,128)S(1)} %get-tuple-element.109), channel_id=1, source_target_pairs={{0,16},{1,17},{2,18},{3,19},{4,20},{5,21},{6,22},{7,23},{8,24},{9,... | collective-permute-start | bytes 4616 | tf_op jit(solution)/shard_map/ppermute | solution.py:22
  93.4 31.4 %collective-permute-start.7 = (f32[6,8,8,1]{3,2,1,0:T(8,128)S(1)}, f32[6,8,8,1]{3,2,1,0:T(8,128)S(1)}, u32[]{:S(2)}, u32[]{:S(2)}) collective-permute-start(f32[6,8,8,1]{3,2,1,0:T(8,128)S(1)} %get-tuple-element.110), channel_id=1, source_target_pairs={{16,0},{17,1},{18,2},{19,3},{20,4},{21,5},{22,6},{23,7},{24,8},{25... | collective-permute-start | bytes 4616 | tf_op jit(solution)/shard_map/ppermute | solution.py:24
  119.3 11.1 %collective-permute-start.36 = (f32[6,8,8,1]{3,2,1,0:T(8,128)S(1)}, f32[6,8,8,1]{3,2,1,0:T(8,128)S(1)}, u32[]{:S(2)}, u32[]{:S(2)}) collective-permute-start(f32[6,8,8,1]{3,2,1,0:T(8,128)S(1)} %get-tuple-element.92), channel_id=1, source_target_pairs={{0,16},{1,17},{2,18},{3,19},{4,20},{5,21},{6,22},{7,23},{8,24},{9,... | collective-permute-start | bytes 4616 | tf_op jit(solution)/shard_map/ppermute | solution.py:22
  130.8 11.5 %collective-permute-start.38 = (f32[6,8,1,130]{3,2,1,0:T(1,128)S(1)}, f32[6,8,1,130]{3,2,1,0:T(1,128)S(1)}, u32[]{:S(2)}, u32[]{:S(2)}) collective-permute-start(f32[6,8,1,130]{3,2,1,0:T(1,128)S(1)} %get-tuple-element.46), channel_id=1, source_target_pairs={{0,4},{4,8},{8,12},{1,5},{5,9},{9,13},{2,6},{6,10},{10,14},{3,7},{... | collective-permute-start | bytes 74888 | tf_op jit(solution)/shard_map/ppermute | solution.py:22
  136.3 11.8 %collective-permute-start.10 = (f32[6,1,10,130]{3,2,1,0:T(8,128)S(1)}, f32[6,1,10,130]{3,2,1,0:T(8,128)S(1)}, u32[]{:S(2)}, u32[]{:S(2)}) collective-permute-start(f32[6,1,10,130]{3,2,1,0:T(8,128)S(1)} %get-tuple-element.44), channel_id=1, source_target_pairs={{0,1},{1,2},{2,3},{4,5},{5,6},{6,7},{8,9},{9,10},{10,11},{12,13},{... | collective-permute-start | bytes 93608 | tf_op jit(solution)/shard_map/ppermute | solution.py:22
  142.5 11.7 %collective-permute-start.40 = (f32[6,1,10,130]{3,2,1,0:T(8,128)S(1)}, f32[6,1,10,130]{3,2,1,0:T(8,128)S(1)}, u32[]{:S(2)}, u32[]{:S(2)}) collective-permute-start(f32[6,1,10,130]{3,2,1,0:T(8,128)S(1)} %get-tuple-element.38), channel_id=1, source_target_pairs={{0,1},{1,2},{2,3},{4,5},{5,6},{6,7},{8,9},{9,10},{10,11},{12,13},{... | collective-permute-start | bytes 93608 | tf_op jit(solution)/shard_map/ppermute | solution.py:22
  148.9 11.4 %collective-permute-start.12 = (f32[3,8,8,1]{3,2,1,0:T(8,128)S(1)}, f32[3,8,8,1]{3,2,1,0:T(8,128)S(1)}, u32[]{:S(2)}, u32[]{:S(2)}) collective-permute-start(f32[3,8,8,1]{3,2,1,0:T(8,128)S(1)} %get-tuple-element.117), channel_id=1, source_target_pairs={{0,16},{1,17},{2,18},{3,19},{4,20},{5,21},{6,22},{7,23},{8,24},{9,... | collective-permute-start | bytes 2312 | tf_op jit(solution)/shard_map/ppermute | solution.py:22
  160.5 11.1 %collective-permute-start.14 = (f32[3,8,1,130]{3,2,1,0:T(1,128)S(1)}, f32[3,8,1,130]{3,2,1,0:T(1,128)S(1)}, u32[]{:S(2)}, u32[]{:S(2)}) collective-permute-start(f32[3,8,1,130]{3,2,1,0:T(1,128)S(1)} %get-tuple-element.80), channel_id=1, source_target_pairs={{0,4},{4,8},{8,12},{1,5},{5,9},{9,13},{2,6},{6,10},{10,14},{3,7},{... | collective-permute-start | bytes 37448 | tf_op jit(solution)/shard_map/ppermute | solution.py:22
  166.1 13.4 %collective-permute-start.44 = (f32[3,8,1,130]{3,2,0,1:T(1,128)S(1)}, f32[3,8,1,130]{3,2,0,1:T(1,128)S(1)}, u32[]{:S(2)}, u32[]{:S(2)}) collective-permute-start(f32[3,8,1,130]{3,2,0,1:T(1,128)S(1)} %get-tuple-element.74), channel_id=1, source_target_pairs={{0,4},{4,8},{8,12},{1,5},{5,9},{9,13},{2,6},{6,10},{10,14},{3,7},{... | collective-permute-start | bytes 37448 | tf_op jit(solution)/shard_map/ppermute | solution.py:22
  168.2 11.3 %collective-permute-start.45 = (f32[3,8,1,130]{3,2,0,1:T(1,128)S(1)}, f32[3,8,1,130]{3,2,0,1:T(1,128)S(1)}, u32[]{:S(2)}, u32[]{:S(2)}) collective-permute-start(f32[3,8,1,130]{3,2,0,1:T(1,128)S(1)} %get-tuple-element.75), channel_id=1, source_target_pairs={{4,0},{8,4},{12,8},{5,1},{9,5},{13,9},{6,2},{10,6},{14,10},{7,3},{... | collective-permute-start | bytes 37448 | tf_op jit(solution)/shard_map/ppermute | solution.py:24
  171.7 13.5 %collective-permute-start.16 = (f32[3,1,10,130]{3,2,1,0:T(8,128)S(1)}, f32[3,1,10,130]{3,2,1,0:T(8,128)S(1)}, u32[]{:S(2)}, u32[]{:S(2)}) collective-permute-start(f32[3,1,10,130]{3,2,1,0:T(8,128)S(1)} %get-tuple-element.70), channel_id=1, source_target_pairs={{0,1},{1,2},{2,3},{4,5},{5,6},{6,7},{8,9},{9,10},{10,11},{12,13},{... | collective-permute-start | bytes 46808 | tf_op jit(solution)/shard_map/ppermute | solution.py:22
  190.3 13.4 %collective-permute-start.18 = (f32[6,8,8,1]{3,2,1,0:T(8,128)S(1)}, f32[6,8,8,1]{3,2,1,0:T(8,128)S(1)}, u32[]{:S(2)}, u32[]{:S(2)}) collective-permute-start(f32[6,8,8,1]{3,2,1,0:T(8,128)S(1)} %get-tuple-element.102), channel_id=1, source_target_pairs={{0,16},{1,17},{2,18},{3,19},{4,20},{5,21},{6,22},{7,23},{8,24},{9,... | collective-permute-start | bytes 4616 | tf_op jit(solution)/shard_map/ppermute | solution.py:22
  191.6 12.1 %collective-permute-start.19 = (f32[6,8,8,1]{3,2,1,0:T(8,128)S(1)}, f32[6,8,8,1]{3,2,1,0:T(8,128)S(1)}, u32[]{:S(2)}, u32[]{:S(2)}) collective-permute-start(f32[6,8,8,1]{3,2,1,0:T(8,128)S(1)} %get-tuple-element.103), channel_id=1, source_target_pairs={{16,0},{17,1},{18,2},{19,3},{20,4},{21,5},{22,6},{23,7},{24,8},{25... | collective-permute-start | bytes 4616 | tf_op jit(solution)/shard_map/ppermute | solution.py:24
  204.0 33.5 %collective-permute-start.20 = (f32[6,8,1,130]{3,2,1,0:T(1,128)S(1)}, f32[6,8,1,130]{3,2,1,0:T(1,128)S(1)}, u32[]{:S(2)}, u32[]{:S(2)}) collective-permute-start(f32[6,8,1,130]{3,2,1,0:T(1,128)S(1)} %get-tuple-element.50), channel_id=1, source_target_pairs={{0,4},{4,8},{8,12},{1,5},{5,9},{9,13},{2,6},{6,10},{10,14},{3,7},{... | collective-permute-start | bytes 74888 | tf_op jit(solution)/shard_map/ppermute | solution.py:22
  205.9 31.6 %collective-permute-start.21 = (f32[6,8,1,130]{3,2,1,0:T(1,128)S(1)}, f32[6,8,1,130]{3,2,1,0:T(1,128)S(1)}, u32[]{:S(2)}, u32[]{:S(2)}) collective-permute-start(f32[6,8,1,130]{3,2,1,0:T(1,128)S(1)} %get-tuple-element.51), channel_id=1, source_target_pairs={{4,0},{8,4},{12,8},{5,1},{9,5},{13,9},{6,2},{10,6},{14,10},{7,3},{... | collective-permute-start | bytes 74888 | tf_op jit(solution)/shard_map/ppermute | solution.py:24
  (29 other events, 308.3 us)
where the time goes:
time: 250 us; the launch traced here: 248 us
  starting transfers between devices  134 us (54%)
  other arithmetic  61.7 us (25%)
  local copies, waits for them, and re-layouts  25.7 us (10%)
  waiting for transfers between devices  12.3 us (5%)
  blocking collectives  8.81 us (4%)
  between operations  5.73 us (2%)
    ppermute x24, starting transfers between devices, padded_2(): lax.ppermute(head, axis, [((i + 1) % count, i) for i in range(ends)])  70.4 us
    ppermute x24, starting transfers between devices, padded_2(): lax.ppermute(tail, axis, [(i, (i + 1) % count) for i in range(ends)])  63.4 us
    add x1, other arithmetic, imaging_terms(): forward_stress[0] * adjoint_stress[0]  28.2 us
    scatter-add x4, other arithmetic, inject(): flat = normal.reshape(3, -1).at[:, cells].add(values).reshape(normal.shape)  21 us
    reshape x5, local copies, waits for them, and re-layouts, inject(): flat = normal.reshape(3, -1).at[:, cells].add(values).reshape(normal.shape)  13.9 us
    ppermute x24, waiting for transfers between devices, padded_2(): lax.ppermute(head, axis, [((i + 1) % count, i) for i in range(ends)])  12.2 us
    all_gather x1, blocking collectives, restore(): everything = lax.all_gather(checkpoint_store, 'gz', axis=0, tiled=True)  8.81 us
    slice x5, local copies, waits for them, and re-layouts, inject(): normal = stress[:3]  6.46 us
  transfers between devices with their start and end apart: 48, of which 4 were waited for; matrix products, arithmetic and copies ran while one was open for 33% of the time, Pallas kernels for 0%

commit v1 on v0

v1 whole, which is shorter than its diff:
```python
import functools

import jax
import jax.numpy as jnp
from jax import lax
from jax.experimental import pallas as pl
from jax.experimental.pallas import tpu as pltpu
from jax.sharding import PartitionSpec as P

VX, VY, VZ, SXX, SYY, SZZ, SXY, SXZ, SYZ = range(9)
FWD, ADJ, BUOY, LAM, MU, INJ, SRC = 0, 9, 18, 19, 20, 21, 22
FIELDS = 23
HALO = 2

ADJ_Y = {VX: (2, 2), VY: (2, 2), VZ: (2, 2), SXX: (1, 1), SYY: (1, 2), SZZ: (1, 1), SXY: (2, 1), SXZ: (1, 1), SYZ: (2, 1)}
ADJ_Z = {VX: (2, 2), VY: (2, 2), VZ: (2, 2), SXX: (1, 1), SYY: (1, 1), SZZ: (1, 2), SXY: (1, 1), SXZ: (2, 1), SYZ: (2, 1)}
FWD_Y = {VX: (1, 2), VY: (2, 1), VZ: (1, 2), SXX: (1, 2), SYY: (2, 2), SZZ: (1, 2), SXY: (2, 2), SXZ: (1, 2), SYZ: (2, 2)}
OTHER = {BUOY: (2, 2), LAM: (1, 2), MU: (2, 2), INJ: (0, 1), SRC: (1, 1)}

F32_Y = {**{ADJ + f: c for f, c in ADJ_Y.items()}, **OTHER}
F32_Z = {**{ADJ + f: c for f, c in ADJ_Z.items()}, **OTHER}

VMEM_LIMIT = 48 * 1024 * 1024


def params():
    return pltpu.CompilerParams(vmem_limit_bytes=VMEM_LIMIT)


def vmem():
    return pl.BlockSpec(memory_space=pltpu.VMEM)


def smem():
    return pl.BlockSpec(memory_space=pltpu.SMEM)


def lo_cells(table, count):
    return [(f, count - d, -d) for f in sorted(table) for d in range(table[f][0], 0, -1)]


def hi_cells(table, count):
    return [(f, d, count + d) for f in sorted(table) for d in range(table[f][1])]


def split(value):
    high = value.astype(jnp.bfloat16)
    low = (value - high.astype(jnp.float32)).astype(jnp.bfloat16)
    return high, low


def joined(high, low):
    return high.astype(jnp.float32) + low.astype(jnp.float32)


def start_kernel(cz, store, adjoint, lam, mu, buoy, source, wavelet, receiver, traces, plan, out, inj):
    rows, lanes = cz * adjoint.shape[2], adjoint.shape[3]
    cells = receiver[...]
    count = cells.shape[1]
    row_hot = (lax.broadcasted_iota(jnp.int32, (rows, count), 0) == cells // lanes).astype(jnp.float32)
    lane_hit = lax.broadcasted_iota(jnp.int32, (lanes, count), 0) == cells % lanes
    for index, step in ((0, 1), (1, 0)):
        sample = traces[pl.ds(plan[step], 1), :]
        field = lax.dot_general(
            row_hot,
            jnp.where(lane_hit, sample, 0.0),
            (((1,), (1,)), ((), ())),
            precision=lax.Precision.HIGHEST,
            preferred_element_type=jnp.float32,
        )
        inj[index] = field.reshape(inj.shape[1:])
    flat = lax.broadcasted_iota(jnp.int32, (rows, lanes), 0) * lanes + lax.broadcasted_iota(jnp.int32, (rows, lanes), 1)
    for step in range(2):
        value = wavelet[plan[step]]
        field = jnp.zeros((rows, lanes), jnp.float32)
        for j in range(source.shape[3]):
            field = field + jnp.where(flat == source[0, 0, 0, j], value, 0.0)
        inj[2 + step] = field.reshape(inj.shape[1:])

    def own(field, layer):
        if field == BUOY:
            return buoy[layer]
        if field == LAM:
            return lam[layer]
        if field == MU:
            return mu[layer]
        if field == INJ:
            return inj[1, layer]
        if field == SRC:
            return inj[2, layer]
        value = adjoint[field - ADJ, layer]
        if SXX <= field - ADJ <= SZZ:
            value = value + inj[0, layer]
        return value

    slots, nine = store.shape[0], store.shape[1]
    for s in range(slots):
        for f in range(nine):
            out[s * nine + f] = store[s, f, 0]
    base = slots * nine
    faces = lo_cells(F32_Z, cz) + hi_cells(F32_Z, cz)
    for i, (field, layer, _) in enumerate(faces):
        high, low = split(own(field, layer))
        out[base + i] = high
        out[base + len(faces) + i] = low


def column_kernel(cz, gathered, peer, slot, place, adjoint, lam, mu, buoy, inj, main, strip, send):
    lanes = main.shape[3]
    layers = cz + 2 * HALO
    pieces = slot.shape[1]
    me, count = place[2], place[3]
    below, above = jnp.maximum(me - 1, 0), jnp.minimum(me + 1, count - 1)
    has_below = (me > 0).astype(jnp.float32)
    has_above = (me < count - 1).astype(jnp.float32)
    base = pieces * 9

    for z in range(layers):
        if z < HALO:
            brick, piece, keep = below, cz - HALO + z, has_below
        elif z < HALO + cz:
            brick, piece, keep = me, z - HALO, None
        else:
            brick, piece, keep = above, z - HALO - cz, has_above
        holder = peer[brick, piece]
        row = slot[brick, piece] * 9
        for f in range(9):
            value = gathered[holder, row + f].astype(jnp.float32)
            main[FWD + f, z] = value if keep is None else value * keep
    own = {BUOY: buoy, LAM: lam, MU: mu, INJ: inj.at[1], SRC: inj.at[2]}
    for z in range(cz):
        for f in range(9):
            value = adjoint[f, z]
            if SXX <= f <= SZZ:
                value = value + inj[0, z]
            main[ADJ + f, HALO + z] = value
        for f, ref in own.items():
            main[f, HALO + z] = ref[z]
    lo, hi = lo_cells(F32_Z, cz), hi_cells(F32_Z, cz)
    total = len(lo) + len(hi)
    zero = jnp.zeros(main.shape[2:], jnp.float32)
    have = {}
    for i, (field, _, index) in enumerate(lo + hi):
        have[field, HALO + index] = i
    for f in range(ADJ, FIELDS):
        for z in (0, 1, layers - 2, layers - 1):
            if (f, z) in have:
                i = have[f, z]
                source, keep = (below, has_below) if z < HALO else (above, has_above)
                main[f, z] = joined(gathered[source, base + i], gathered[source, base + total + i]) * keep
            else:
                main[f, z] = zero

    lane = lax.broadcasted_iota(jnp.int32, main.shape[2:], 1)
    position = lane % 8
    group = lane // 8
    for f in range(FIELDS):
        tile = zero
        for z in range(layers):
            value = main[f, z]
            tail = pltpu.roll(value, (8 * z + 2) % lanes, 1)
            head = pltpu.roll(value, (8 * z + 6) % lanes, 1)
            here = group == z
            tile = jnp.where(here & (position < 2), tail, jnp.where(here & (position >= 6), head, tile))
        strip[f] = tile
        high, low = split(tile)
        send[f] = high
        if f >= ADJ:
            send[FIELDS + f - ADJ] = low


def rows_kernel(cz, cy, main, strip, from_left, from_right, place, strips, up, down, packed):
    lanes = main.shape[3]
    layers = cz + 2 * HALO
    has_left = (place[0] > 0).astype(jnp.float32)
    has_right = (place[0] < place[1] - 1).astype(jnp.float32)
    lane = lax.broadcasted_iota(jnp.int32, main.shape[2:], 1)
    position = lane % 8
    for f in range(FIELDS):
        left, right = from_left[f].astype(jnp.float32), from_right[f].astype(jnp.float32)
        if f >= ADJ:
            left = left + from_left[FIELDS + f - ADJ].astype(jnp.float32)
            right = right + from_right[FIELDS + f - ADJ].astype(jnp.float32)
        left = pltpu.roll(left * has_left, 4, 1)
        right = pltpu.roll(right * has_right, lanes - 4, 1)
        tile = jnp.where((position == 4) | (position == 5), left, strip[f])
        tile = jnp.where((position == 2) | (position == 3), right, tile)
        strips[f] = tile
    for out, cells in ((up, lo_cells), (down, hi_cells)):
        tiles = 0
        for table, narrow in ((FWD_Y, True), (F32_Y, False)):
            rows = [(f, z, y) for f, y, _ in cells(table, cy) for z in range(layers + 1)]
            for r, (f, z, y) in enumerate(rows):
                value = strips[f, y : y + 1, :] if z == layers else main[f, z, y : y + 1, :]
                packed[r // 8, r % 8 : r % 8 + 1, :] = value
            used = -(-len(rows) // 8)
            for t in range(used):
                high, low = split(packed[t])
                out[tiles + t] = high
                if not narrow:
                    out[tiles + used + t] = low
            tiles += used if narrow else 2 * used


def row_tiles(cells, cz, cy):
    layers = cz + 2 * HALO
    narrow = -(-len(cells(FWD_Y, cy)) * (layers + 1) // 8)
    wide = -(-len(cells(F32_Y, cy)) * (layers + 1) // 8)
    return narrow + 2 * wide


def window_kernel(cz, cy, main, strips, from_lower, from_upper, inj, final, image_lam, image_mu, ring, packed, keep):
    lanes = main.shape[3]
    layers = cz + 2 * HALO
    ring_rows = ring.shape[2]
    for f in range(FIELDS):
        for z in range(layers + 1):
            ring[f, z, 0:cy, :] = strips[f] if z == layers else main[f, z]
            ring[f, z, cy:ring_rows, :] = jnp.zeros((ring_rows - cy, lanes), jnp.float32)
    for source, cells in ((from_lower, lo_cells), (from_upper, hi_cells)):
        tiles = 0
        for table, narrow in ((FWD_Y, True), (F32_Y, False)):
            rows = [(f, z, y % ring_rows) for f, _, y in cells(table, cy) for z in range(layers + 1)]
            used = -(-len(rows) // 8)
            for t in range(used):
                value = source[tiles + t].astype(jnp.float32)
                if not narrow:
                    value = value + source[tiles + used + t].astype(jnp.float32)
                packed[t] = value
            for r, (f, z, y) in enumerate(rows):
                ring[f, z, y : y + 1, :] = packed[r // 8, r % 8 : r % 8 + 1, :]
            tiles += used if narrow else 2 * used

    lane = lax.broadcasted_iota(jnp.int32, (ring_rows, lanes), 1)
    first_lane, last_lane = lane == 0, lane == lanes - 1
    edge = layers

    def at(f, z):
        return ring[f, z]

    def x_next(f, z):
        value = at(f, z)
        if z == edge:
            return pltpu.roll(value, lanes - 1, 1)
        beyond = pltpu.roll(at(f, edge), (lanes - 1 - (8 * z + 2)) % lanes, 1)
        return jnp.where(last_lane, beyond, pltpu.roll(value, lanes - 1, 1))

    def x_prev(f, z):
        value = at(f, z)
        if z == edge:
            return pltpu.roll(value, 1, 1)
        beyond = pltpu.roll(at(f, edge), (lanes - (8 * z + 5)) % lanes, 1)
        return jnp.where(first_lane, beyond, pltpu.roll(value, 1, 1))

    def y_next(f, z):
        return pltpu.roll(at(f, z), ring_rows - 1, 0)

    def y_prev(f, z):
        return pltpu.roll(at(f, z), 1, 0)

    def z_next(f, z):
        return pltpu.roll(at(f, edge), lanes - 8, 1) if z == edge else at(f, z + 1)

    def z_prev(f, z):
        return pltpu.roll(at(f, edge), 8, 1) if z == edge else at(f, z - 1)

    def velocity_rates(base, z, want):
        buoy = at(BUOY, z)
        sxx, syy, szz = (functools.partial(at, base + f) for f in (SXX, SYY, SZZ))
        sxy, sxz, syz = (functools.partial(at, base + f) for f in (SXY, SXZ, SYZ))
        out = {}
        if VX in want:
            out[VX] = buoy * (
                (x_next(base + SXX, z) - sxx(z)) + (sxy(z) - y_prev(base + SXY, z)) + (sxz(z) - z_prev(base + SXZ, z))
            )
        if VY in want:
            out[VY] = buoy * (
                (sxy(z) - x_prev(base + SXY, z)) + (y_next(base + SYY, z) - syy(z)) + (syz(z) - z_prev(base + SYZ, z))
            )
        if VZ in want:
            out[VZ] = buoy * (
                (sxz(z) - x_prev(base + SXZ, z)) + (syz(z) - y_prev(base + SYZ, z)) + (z_next(base + SZZ, z) - szz(z))
            )
        return out

    def stress_rates(base, z, want):
        lam, mu = at(LAM, z), at(MU, z)
        vx, vy, vz = at(base + VX, z), at(base + VY, z), at(base + VZ, z)
        out = {}
        if SXX in want:
            exx = vx - x_prev(base + VX, z)
            eyy = vy - y_prev(base + VY, z)
            ezz = vz - z_prev(base + VZ, z)
            common = lam * (exx + eyy + ezz)
            twice = 2.0 * mu
            out[SXX] = common + twice * exx
            out[SYY] = common + twice * eyy
            out[SZZ] = common + twice * ezz
        if SXY in want:
            out[SXY] = mu * ((y_next(base + VX, z) - vx) + (x_next(base + VY, z) - vy))
        if SXZ in want:
            out[SXZ] = mu * ((z_next(base + VX, z) - vx) + (x_next(base + VZ, z) - vz))
            out[SYZ] = mu * ((z_next(base + VY, z) - vy) + (y_next(base + VZ, z) - vz))
        return out

    def spread(ranges):
        for z in list(range(layers)) + [edge]:
            want = {f for f, (a, b) in ranges.items() if z == edge or a <= z < b}
            if want:
                yield z, want

    def velocity_step(base, sign, ranges):
        for z, want in spread(ranges):
            for f, rate in velocity_rates(base, z, want).items():
                ring[base + f, z] = at(base + f, z) + rate if sign > 0 else at(base + f, z) - rate

    def stress_step(base, sign, ranges, before=None, after=None):
        for z, want in spread(ranges):
            for f, rate in stress_rates(base, z, want).items():
                value, normal = at(base + f, z), f in (SXX, SYY, SZZ)
                if before is not None and normal:
                    value = value + at(before, z)
                value = value + rate if sign > 0 else value - rate
                if after is not None and normal:
                    value = value + at(after, z)
                ring[base + f, z] = value

    def terms(f, a):
        term_lam = (f[0] + f[1] + f[2]) * (a[0] + a[1] + a[2])
        term_mu = f[0] * a[0] + f[1] * a[1] + f[2] * a[2] + 2.0 * (f[3] * a[3] + f[4] * a[4] + f[5] * a[5])
        return term_lam, term_mu

    inner = (HALO, HALO + cz)
    n = layers
    stress_step(ADJ, -1, {SXX: (1, n), SXY: (0, n), SXZ: (0, n - 1)})
    velocity_step(FWD, 1, {VX: (1, n), VY: (1, n), VZ: (0, n - 1)})
    stress_step(FWD, 1, {SXX: (1, n - 1), SXY: (1, n - 1), SXZ: (1, n - 1)}, after=SRC)
    for z in range(*inner):
        f = [ring[FWD + s, z, 0:cy, :] for s in range(SXX, SYZ + 1)]
        a = [ring[ADJ + s, z, 0:cy, :] for s in range(SXX, SYZ + 1)]
        a = [value + ring[INJ, z, 0:cy, :] for value in a[:3]] + a[3:]
        keep[0, z - HALO], keep[1, z - HALO] = terms(f, a)
    velocity_step(FWD, 1, {VX: (2, n - 1), VY: (2, n - 1), VZ: (1, n - 2)})
    everything = set(range(SXX, SYZ + 1))
    for z in range(*inner):
        rates = stress_rates(FWD, z, everything)
        f = []
        for s in range(SXX, SYZ + 1):
            value = (at(FWD + s, z) + rates[s])[0:cy, :]
            f.append(value + inj[3, z - HALO] if s <= SZZ else value)
        a = [main[ADJ + s, z] for s in range(SXX, SYZ + 1)]
        term_lam, term_mu = terms(f, a)
        image_lam[z - HALO] = term_lam + keep[0, z - HALO]
        image_mu[z - HALO] = term_mu + keep[1, z - HALO]
    velocity_step(ADJ, -1, {VX: (1, n - 1), VY: (1, n - 1), VZ: (1, n - 1)})
    stress_step(ADJ, -1, {SXX: (2, n - 1), SXY: (1, n - 1), SXZ: (1, n - 2)}, before=INJ)
    for z in range(*inner):
        rates = velocity_rates(ADJ, z, {VX, VY, VZ})
        for f in (VX, VY, VZ):
            final[f, z - HALO] = (at(ADJ + f, z) - rates[f])[0:cy, :]
        for s in range(SXX, SYZ + 1):
            final[s, z - HALO] = ring[ADJ + s, z, 0:cy, :]


def exchange(value, axis):
    count = lax.axis_size(axis)
    if count == 2:
        other = lax.ppermute(value, axis, [(0, 1), (1, 0)])
        return other, other
    return (
        lax.ppermute(value, axis, [(i, i + 1) for i in range(count - 1)]),
        lax.ppermute(value, axis, [(i + 1, i) for i in range(count - 1)]),
    )


def on_device(
    checkpoint_store,
    holder_peer,
    holder_slot,
    adjoint_state,
    lame_lambda,
    lame_mu,
    buoyancy,
    source_cell,
    wavelet,
    receiver_cell,
    traces,
    plan,
):
    cz, cy, cx = lame_mu.shape
    layers = cz + 2 * HALO
    bf16, f32 = jnp.bfloat16, jnp.float32
    slots = checkpoint_store.shape[0]
    faces = len(lo_cells(F32_Z, cz)) + len(hi_cells(F32_Z, cz))
    place = jnp.stack([
        lax.axis_index("gx"), jnp.int32(lax.axis_size("gx")), lax.axis_index("gz"), jnp.int32(lax.axis_size("gz")),
    ]).astype(jnp.int32)

    outgoing, inj = pl.pallas_call(
        functools.partial(start_kernel, cz),
        out_shape=(
            jax.ShapeDtypeStruct((slots * 9 + 2 * faces, cy, cx), bf16),
            jax.ShapeDtypeStruct((4, cz, cy, cx), f32),
        ),
        in_specs=[vmem()] * 5 + [smem(), smem(), vmem(), vmem(), smem()],
        out_specs=(vmem(), vmem()),
        compiler_params=params(),
    )(
        checkpoint_store,
        adjoint_state,
        lame_lambda,
        lame_mu,
        buoyancy,
        source_cell,
        wavelet,
        receiver_cell.reshape(1, -1),
        traces.reshape(traces.shape[-2:]),
        plan,
    )
    gathered = lax.all_gather(outgoing, "gz", axis=0)

    main, strip, send = pl.pallas_call(
        functools.partial(column_kernel, cz),
        out_shape=(
            jax.ShapeDtypeStruct((FIELDS, layers, cy, cx), f32),
            jax.ShapeDtypeStruct((FIELDS, cy, cx), f32),
            jax.ShapeDtypeStruct((2 * FIELDS - ADJ, cy, cx), bf16),
        ),
        in_specs=[vmem(), smem(), smem(), smem()] + [vmem()] * 5,
        out_specs=(vmem(), vmem(), vmem()),
        compiler_params=params(),
    )(gathered, holder_peer[0, 0], holder_slot[0, 0], place, adjoint_state, lame_lambda, lame_mu, buoyancy, inj)
    from_left, from_right = exchange(send, "gx")

    most = max(-(-len(cells(table, cy)) * (layers + 1) // 8) for cells in (lo_cells, hi_cells) for table in (FWD_Y, F32_Y))
    strips, up, down = pl.pallas_call(
        functools.partial(rows_kernel, cz, cy),
        out_shape=(
            jax.ShapeDtypeStruct((FIELDS, cy, cx), f32),
            jax.ShapeDtypeStruct((row_tiles(lo_cells, cz, cy), cy, cx), bf16),
            jax.ShapeDtypeStruct((row_tiles(hi_cells, cz, cy), cy, cx), bf16),
        ),
        in_specs=[vmem()] * 4 + [smem()],
        out_specs=(vmem(), vmem(), vmem()),
        scratch_shapes=[pltpu.VMEM((most, 8, cx), f32)],
        compiler_params=params(),
    )(main, strip, from_left, from_right, place)
    count = lax.axis_size("gy")
    from_lower = lax.ppermute(up, "gy", [(i, i + 1) for i in range(count - 1)])
    from_upper = lax.ppermute(down, "gy", [(i + 1, i) for i in range(count - 1)])

    return pl.pallas_call(
        functools.partial(window_kernel, cz, cy),
        out_shape=(
            jax.ShapeDtypeStruct((9, cz, cy, cx), f32),
            jax.ShapeDtypeStruct((cz, cy, cx), f32),
            jax.ShapeDtypeStruct((cz, cy, cx), f32),
        ),
        in_specs=[vmem()] * 5,
        out_specs=(vmem(), vmem(), vmem()),
        scratch_shapes=[
            pltpu.VMEM((FIELDS, layers + 1, 2 * cy, cx), f32),
            pltpu.VMEM((most, 8, cx), f32),
            pltpu.VMEM((2, cz, cy, cx), f32),
        ],
        compiler_params=params(),
    )(main, strips, from_lower, from_upper, inj)


def solution(mesh):
    return jax.shard_map(
        on_device,
        mesh=mesh,
        in_specs=(
            P("gz", None, None, "gy", "gx"),
            P("gx", "gy", None, None),
            P("gx", "gy", None, None),
            P(None, "gz", "gy", "gx"),
            P("gz", "gy", "gx"),
            P("gz", "gy", "gx"),
            P("gz", "gy", "gx"),
            P("gz", "gy", "gx", None),
            P(),
            P("gz", "gy", "gx", None),
            P("gz", "gy", "gx", None, None),
            P(),
        ),
        out_specs=(P(None, "gz", "gy", "gx"), P("gz", "gy", "gx"), P("gz", "gy", "gx")),
        check_vma=False,
    )
```

time: 250 us -> 68.8 us (0.28)
  the two profiles are of different devices: /device:TPU:21 before, /device:TPU:0 now
where the time goes in v1:
time: 68.8 us; the launch traced here: 68 us
  waiting for transfers between devices  26.8 us (39%)
  between operations  14.1 us (20%)
  local copies, waits for them, and re-layouts  13.4 us (19%)
  starting transfers between devices  7.43 us (11%)
  Pallas kernels  6.21 us (9%)
    all_gather x1, waiting for transfers between devices, on_device(): gathered = lax.all_gather(outgoing, 'gz', axis=0)  20.7 us
    unnamed x34, local copies, waits for them, and re-layouts  13.4 us
    ppermute x1, starting transfers between devices, on_device(): from_lower = lax.ppermute(up, 'gy', [(i, i + 1) for i in range(count - 1)])  4.56 us
    ppermute x1, waiting for transfers between devices, on_device(): from_lower = lax.ppermute(up, 'gy', [(i, i + 1) for i in range(count - 1)])  3.08 us
    ppermute x1, waiting for transfers between devices, exchange(): other = lax.ppermute(value, axis, [(0, 1), (1, 0)])  2.98 us
    pallas_call x1, Pallas kernels, on_device(): pl.pallas_call(functools.partial(window_kernel, cz, cy), out_shape=(jax.S...  2.42 us
    pallas_call x1, Pallas kernels, on_device(): pl.pallas_call(functools.partial(start_kernel, cz), out_shape=(jax.ShapeD...  1.63 us
    ppermute x1, starting transfers between devices, exchange(): other = lax.ppermute(value, axis, [(0, 1), (1, 0)])  1.54 us
  transfers between devices with their start and end apart: 4, of which 3 were waited for; matrix products, arithmetic and copies ran while one was open for 0% of the time, Pallas kernels for 0%

profile of v1, /device:TPU:0, one launch (start us, length us, event | category | flops | bytes accessed | tf_op | source)
XLA Modules:
  0.0 68.0 jit_solution(8574272024784509292)
XLA Ops:
  7.2 1.0 %copy-done.1 = f32[9,8,8,128]{3,2,1,0:T(8,128)S(1)} copy-done((f32[9,8,8,128]{3,2,1,0:T(8,128)S(1)}, f32[9,8,8,128]{3,2,1,0:T(8,128)}, u32[]{:S(2)}) %copy-start.1) | copy-done | bytes 294936
  8.2 0.9 %copy-done.3 = bf16[8,9,1,8,128]{4,3,2,1,0:T(8,128)(2,1)S(1)} copy-done((bf16[8,9,1,8,128]{4,3,2,1,0:T(8,128)(2,1)S(1)}, bf16[8,9,1,8,128]{4,3,2,1,0:T(8,128)(2,1)}, u32[]{:S(2)}) %copy-start.3) | copy-done | bytes 147480
  9.1 0.8 %copy-done.4 = f32[8,8,128]{2,1,0:T(8,128)S(1)} copy-done((f32[8,8,128]{2,1,0:T(8,128)S(1)}, f32[8,8,128]{2,1,0:T(8,128)}, u32[]{:S(2)}) %copy-start.4) | copy-done | bytes 32792
  9.8 0.8 %copy-done.6 = f32[8,8,128]{2,1,0:T(8,128)S(1)} copy-done((f32[8,8,128]{2,1,0:T(8,128)S(1)}, f32[8,8,128]{2,1,0:T(8,128)}, u32[]{:S(2)}) %copy-start.6) | copy-done | bytes 32792
  10.6 0.8 %copy-done.8 = f32[8,8,128]{2,1,0:T(8,128)S(1)} copy-done((f32[8,8,128]{2,1,0:T(8,128)S(1)}, f32[8,8,128]{2,1,0:T(8,128)}, u32[]{:S(2)}) %copy-start.8) | copy-done | bytes 32792
  11.4 0.8 %copy-done.10 = f32[1,1,1,64,64]{4,3,2,1,0:T(8,128)S(1)} copy-done((f32[1,1,1,64,64]{4,3,2,1,0:T(8,128)S(1)}, f32[1,1,1,64,64]{4,3,2,1,0:T(8,128)}, u32[]{:S(2)}) %copy-start.10) | copy-done | bytes 16408
  12.1 0.7 copy-done.13
  14.7 1.6 %shard_map.139 = (bf16[154,8,128]{2,1,0:T(8,128)(2,1)}, f32[4,8,8,128]{3,2,1,0:T(8,128)S(1)}) custom-call(bf16[8,9,1,8,128]{4,3,2,1,0:T(8,128)(2,1)S(1)} %copy-done.3, f32[9,8,8,128]{3,2,1,0:T(8,128)S(1)} %copy-done.1, f32[8,8,128]{2,1,0:T(8,128)S(1)} %copy-done.4, f32[8,8,128]{2,1,0:T(8,128)S(1)} %copy-done.6, f32[8,8,128]{2,1,0:T(8,128)S(1)} %copy-done.8, ...), custom_call_target="tpu_custom_call" | custom-call | tf_op jit(solution)/shard_map/pallas_call | solution.py:399
  16.5 20.7 %all-gather.3.cloned.1.call-done = bf16[616,8,128]{2,1,0:T(8,128)(2,1)} async-done(((bf16[154,8,128]{2,1,0:T(8,128)(2,1)}), bf16[616,8,128]{2,1,0:T(8,128)(2,1)}) %all-gather.3.cloned.1.call-update) | async-done | bytes 1261584 | tf_op jit(solution)/shard_map/all_gather | solution.py:420
  37.2 1.3 %copy-done = bf16[616,8,128]{2,1,0:T(8,128)(2,1)S(1)} copy-done((bf16[616,8,128]{2,1,0:T(8,128)(2,1)S(1)}, bf16[616,8,128]{2,1,0:T(8,128)(2,1)}, u32[]{:S(2)}) %copy-start) | copy-done | bytes 1261592
  38.5 1.0 %copy-done.2 = f32[9,8,8,128]{3,2,1,0:T(8,128)S(1)} copy-done((f32[9,8,8,128]{3,2,1,0:T(8,128)S(1)}, f32[9,8,8,128]{3,2,1,0:T(8,128)}, u32[]{:S(2)}) %copy-start.2) | copy-done | bytes 294936
  39.4 0.8 %copy-done.5 = f32[8,8,128]{2,1,0:T(8,128)S(1)} copy-done((f32[8,8,128]{2,1,0:T(8,128)S(1)}, f32[8,8,128]{2,1,0:T(8,128)}, u32[]{:S(2)}) %copy-start.5) | copy-done | bytes 32792
  40.2 0.8 %copy-done.7 = f32[8,8,128]{2,1,0:T(8,128)S(1)} copy-done((f32[8,8,128]{2,1,0:T(8,128)S(1)}, f32[8,8,128]{2,1,0:T(8,128)}, u32[]{:S(2)}) %copy-start.7) | copy-done | bytes 32792
  41.0 0.8 %copy-done.9 = f32[8,8,128]{2,1,0:T(8,128)S(1)} copy-done((f32[8,8,128]{2,1,0:T(8,128)S(1)}, f32[8,8,128]{2,1,0:T(8,128)}, u32[]{:S(2)}) %copy-start.9) | copy-done | bytes 32792
  41.7 0.7 copy-done.11
  42.4 0.7 copy-done.12
  43.1 1.2 %shard_map.140 = (f32[23,12,8,128]{3,2,1,0:T(8,128)S(1)}, f32[23,8,128]{2,1,0:T(8,128)S(1)}, bf16[37,8,128]{2,1,0:T(8,128)(2,1)S(1)}) custom-call(bf16[4,154,8,128]{3,2,1,0:T(8,128)(2,1)S(1)} %bitcast.7, s32[4,8]{1,0:T(4,128)S(1)} %bitcast.9, s32[4,8]{1,0:T(4,128)S(1)} %bitcast.10, s32[4]{0:T(128)S(1)} %pad_add_fusion.place, f32[9,8,8,128]{3,2,1,0:T(8,128)S(1)} %copy-done.2, ...), custom_call_target="tpu_custom_call" | custom-call | tf_op jit(solution)/shard_map/pallas_call | solution.py:422
  44.3 1.5 %collective-permute-start = (bf16[37,8,128]{2,1,0:T(8,128)(2,1)S(1)}, bf16[37,8,128]{2,1,0:T(8,128)(2,1)S(1)}, u32[]{:S(2)}, u32[]{:S(2)}) collective-permute-start(bf16[37,8,128]{2,1,0:T(8,128)(2,1)S(1)} %get-tuple-element.15), channel_id=1, source_target_pairs={{0,16},{16,0},{1,17},{17,1},{2,18},{18,2},{3,19},{19,3},{4,20},{20... | collective-permute-start | bytes 227336 | tf_op jit(solution)/shard_map/ppermute | solution.py:368
  45.8 3.0 %collective-permute-done.from_left.from_right = bf16[37,8,128]{2,1,0:T(8,128)(2,1)S(1)} collective-permute-done((bf16[37,8,128]{2,1,0:T(8,128)(2,1)S(1)}, bf16[37,8,128]{2,1,0:T(8,128)(2,1)S(1)}, u32[]{:S(2)}, u32[]{:S(2)}) %collective-permute-start) | collective-permute-done | bytes 75808 | tf_op jit(solution)/shard_map/ppermute | solution.py:368
  48.8 1.0 %shard_map.141 = (f32[23,8,128]{2,1,0:T(8,128)S(1)}, bf16[88,8,128]{2,1,0:T(8,128)(2,1)S(1)}, bf16[98,8,128]{2,1,0:T(8,128)(2,1)S(1)}) custom-call(f32[23,12,8,128]{3,2,1,0:T(8,128)S(1)} %get-tuple-element.13.main, f32[23,8,128]{2,1,0:T(8,128)S(1)} %get-tuple-element.14.strip, bf16[37,8,128]{2,1,0:T(8,128)(2,1)S(1)} %collective-permute-done.from_left.from_right, ...), custom_call_target="tpu_custom_call" | custom-call | tf_op jit(solution)/shard_map/pallas_call | solution.py:436
  49.8 1.3 %collective-permute-start.2 = (bf16[98,8,128]{2,1,0:T(8,128)(2,1)S(1)}, bf16[98,8,128]{2,1,0:T(8,128)(2,1)S(1)}, u32[]{:S(2)}, u32[]{:S(2)}) collective-permute-start(bf16[98,8,128]{2,1,0:T(8,128)(2,1)S(1)} %get-tuple-element.18), channel_id=1, source_target_pairs={{4,0},{8,4},{12,8},{5,1},{9,5},{13,9},{6,2},{10,6},{14,10},{7,3},{... | collective-permute-start | bytes 602120 | tf_op jit(solution)/shard_map/ppermute | solution.py:450
  51.1 4.6 %collective-permute-start.1 = (bf16[88,8,128]{2,1,0:T(8,128)(2,1)S(1)}, bf16[88,8,128]{2,1,0:T(8,128)(2,1)S(1)}, u32[]{:S(2)}, u32[]{:S(2)}) collective-permute-start(bf16[88,8,128]{2,1,0:T(8,128)(2,1)S(1)} %get-tuple-element.17), channel_id=1, source_target_pairs={{0,4},{4,8},{8,12},{1,5},{5,9},{9,13},{2,6},{6,10},{10,14},{3,7},{... | collective-permute-start | bytes 540680 | tf_op jit(solution)/shard_map/ppermute | solution.py:449
  55.6 3.1 %collective-permute-done.1.from_lower = bf16[88,8,128]{2,1,0:T(8,128)(2,1)S(1)} collective-permute-done((bf16[88,8,128]{2,1,0:T(8,128)(2,1)S(1)}, bf16[88,8,128]{2,1,0:T(8,128)(2,1)S(1)}, u32[]{:S(2)}, u32[]{:S(2)}) %collective-permute-start.1) | collective-permute-done | bytes 180256 | tf_op jit(solution)/shard_map/ppermute | solution.py:449
  58.7 2.4 %shard_map.142 = (f32[9,8,8,128]{3,2,1,0:T(8,128)}, f32[8,8,128]{2,1,0:T(8,128)}, f32[8,8,128]{2,1,0:T(8,128)}) custom-call(f32[23,12,8,128]{3,2,1,0:T(8,128)S(1)} %get-tuple-element.13.main, f32[23,8,128]{2,1,0:T(8,128)S(1)} %get-tuple-element.16.strips, bf16[88,8,128]{2,1,0:T(8,128)(2,1)S(1)} %collective-permute-done.1.from_lower, ...), custom_call_target="tpu_custom_call" | custom-call | tf_op jit(solution)/shard_map/pallas_call | solution.py:452
  (24 shorter events, 2.1 us)
Async XLA Ops:
  7.2 30.0 %all-gather.3.cloned.1.call-start = ((), (), s32[]{:S(2)}) async-start(), calls=%async_computation | async-start | bytes 1576960 | tf_op jit(solution)/shard_map/all_gather | solution.py:420
  7.2 1.0 %copy-start.1 = (f32[9,8,8,128]{3,2,1,0:T(8,128)S(1)}, f32[9,8,8,128]{3,2,1,0:T(8,128)}, u32[]{:S(2)}) copy-start(f32[9,8,8,128]{3,2,1,0:T(8,128)} %adjoint.3) | copy-start | bytes 884740
  8.2 0.9 %copy-start.3 = (bf16[8,9,1,8,128]{4,3,2,1,0:T(8,128)(2,1)S(1)}, bf16[8,9,1,8,128]{4,3,2,1,0:T(8,128)(2,1)}, u32[]{:S(2)}) copy-start(bf16[8,9,1,8,128]{4,3,2,1,0:T(8,128)(2,1)} %store.1) | copy-start | bytes 442372
  9.1 0.8 %copy-start.4 = (f32[8,8,128]{2,1,0:T(8,128)S(1)}, f32[8,8,128]{2,1,0:T(8,128)}, u32[]{:S(2)}) copy-start(f32[8,8,128]{2,1,0:T(8,128)} %lam.3) | copy-start | bytes 98308
  9.8 0.8 %copy-start.6 = (f32[8,8,128]{2,1,0:T(8,128)S(1)}, f32[8,8,128]{2,1,0:T(8,128)}, u32[]{:S(2)}) copy-start(f32[8,8,128]{2,1,0:T(8,128)} %mu.3) | copy-start | bytes 98308
  10.6 0.8 %copy-start.8 = (f32[8,8,128]{2,1,0:T(8,128)S(1)}, f32[8,8,128]{2,1,0:T(8,128)}, u32[]{:S(2)}) copy-start(f32[8,8,128]{2,1,0:T(8,128)} %buoy.3) | copy-start | bytes 98308
  11.4 0.8 %copy-start.10 = (f32[1,1,1,64,64]{4,3,2,1,0:T(8,128)S(1)}, f32[1,1,1,64,64]{4,3,2,1,0:T(8,128)}, u32[]{:S(2)}) copy-start(f32[1,1,1,64,64]{4,3,2,1,0:T(8,128)} %param.22) | copy-start | bytes 49156
  12.1 0.7 copy-start.13
  12.8 0.7 copy-start.14
  13.4 0.7 copy-start.15
  14.1 0.7 copy-start.16
  37.2 1.3 %copy-start = (bf16[616,8,128]{2,1,0:T(8,128)(2,1)S(1)}, bf16[616,8,128]{2,1,0:T(8,128)(2,1)}, u32[]{:S(2)}) copy-start(bf16[616,8,128]{2,1,0:T(8,128)(2,1)} %all-gather.3.cloned.1.call-done) | copy-start | bytes 3784708
  38.5 1.0 %copy-start.2 = (f32[9,8,8,128]{3,2,1,0:T(8,128)S(1)}, f32[9,8,8,128]{3,2,1,0:T(8,128)}, u32[]{:S(2)}) copy-start(f32[9,8,8,128]{3,2,1,0:T(8,128)} %adjoint.3) | copy-start | bytes 884740
  39.4 0.8 %copy-start.5 = (f32[8,8,128]{2,1,0:T(8,128)S(1)}, f32[8,8,128]{2,1,0:T(8,128)}, u32[]{:S(2)}) copy-start(f32[8,8,128]{2,1,0:T(8,128)} %lam.3) | copy-start | bytes 98308
  40.2 0.8 %copy-start.7 = (f32[8,8,128]{2,1,0:T(8,128)S(1)}, f32[8,8,128]{2,1,0:T(8,128)}, u32[]{:S(2)}) copy-start(f32[8,8,128]{2,1,0:T(8,128)} %mu.3) | copy-start | bytes 98308
  40.9 0.8 %copy-start.9 = (f32[8,8,128]{2,1,0:T(8,128)S(1)}, f32[8,8,128]{2,1,0:T(8,128)}, u32[]{:S(2)}) copy-start(f32[8,8,128]{2,1,0:T(8,128)} %buoy.3) | copy-start | bytes 98308
  41.7 0.7 %copy-start.11 = (s32[1,1,4,8]{3,2,1,0:T(4,128)S(1)}, s32[1,1,4,8]{3,2,1,0:T(4,128)}, u32[]{:S(2)}) copy-start(s32[1,1,4,8]{3,2,1,0:T(4,128)} %param.13) | copy-start | bytes 388
  42.4 0.7 %copy-start.12 = (s32[1,1,4,8]{3,2,1,0:T(4,128)S(1)}, s32[1,1,4,8]{3,2,1,0:T(4,128)}, u32[]{:S(2)}) copy-start(s32[1,1,4,8]{3,2,1,0:T(4,128)} %param.14) | copy-start | bytes 388
  44.3 4.5 %collective-permute-start = (bf16[37,8,128]{2,1,0:T(8,128)(2,1)S(1)}, bf16[37,8,128]{2,1,0:T(8,128)(2,1)S(1)}, u32[]{:S(2)}, u32[]{:S(2)}) collective-permute-start(bf16[37,8,128]{2,1,0:T(8,128)(2,1)S(1)} %get-tuple-element.15), channel_id=1, source_target_pairs={{0,16},{16,0},{1,17},{17,1},{2,18},{18,2},{3,19},{19,3},{4,20},{20... | collective-permute-start | bytes 227336 | tf_op jit(solution)/shard_map/ppermute | solution.py:368
  49.8 8.9 %collective-permute-start.2 = (bf16[98,8,128]{2,1,0:T(8,128)(2,1)S(1)}, bf16[98,8,128]{2,1,0:T(8,128)(2,1)S(1)}, u32[]{:S(2)}, u32[]{:S(2)}) collective-permute-start(bf16[98,8,128]{2,1,0:T(8,128)(2,1)S(1)} %get-tuple-element.18), channel_id=1, source_target_pairs={{4,0},{8,4},{12,8},{5,1},{9,5},{13,9},{6,2},{10,6},{14,10},{7,3},{... | collective-permute-start | bytes 602120 | tf_op jit(solution)/shard_map/ppermute | solution.py:450
  51.1 7.6 %collective-permute-start.1 = (bf16[88,8,128]{2,1,0:T(8,128)(2,1)S(1)}, bf16[88,8,128]{2,1,0:T(8,128)(2,1)S(1)}, u32[]{:S(2)}, u32[]{:S(2)}) collective-permute-start(bf16[88,8,128]{2,1,0:T(8,128)(2,1)S(1)} %get-tuple-element.17), channel_id=1, source_target_pairs={{0,4},{4,8},{8,12},{1,5},{5,9},{9,13},{2,6},{6,10},{10,14},{3,7},{... | collective-permute-start | bytes 540680 | tf_op jit(solution)/shard_map/ppermute | solution.py:449
Sparse Core Ops, SparseCore 0:
  16.5 20.6 all-gather.2

commit v2 on v1

v2 whole, which is shorter than its diff:
```python
import functools

import jax
import jax.numpy as jnp
from jax import lax
from jax.experimental import pallas as pl
from jax.experimental.pallas import tpu as pltpu
from jax.sharding import PartitionSpec as P

VX, VY, VZ, SXX, SYY, SZZ, SXY, SXZ, SYZ = range(9)
FWD, ADJ, BUOY, LAM, MU, INJ, SRC = 0, 9, 18, 19, 20, 21, 22
FIELDS = 23
HALO = 2

ADJ_Z = {VX: (2, 2), VY: (2, 2), VZ: (2, 2), SXX: (1, 1), SYY: (1, 1), SZZ: (1, 2), SXY: (1, 1), SXZ: (2, 1), SYZ: (2, 1)}
OTHER_Z = {BUOY: (2, 2), LAM: (1, 2), MU: (2, 2), INJ: (0, 1), SRC: (1, 1)}
F32_Z = {**{ADJ + f: c for f, c in ADJ_Z.items()}, **OTHER_Z}

Y_ROWS = {
    FWD + VX: (None, (2, -1, 1), (1, -1, 1), (2, -2, 0)),
    FWD + VY: ((2, -2, 0), (1, -1, 1), (2, -1, 1), None),
    FWD + VZ: (None, (1, -2, 1), (1, -1, 1), (2, -2, 0)),
    FWD + SXX: (None, (2, -1, 1), (1, -1, 1), (2, -2, 1)),
    FWD + SYY: ((2, -2, 0), (1, -1, 1), (1, 0, 1), (2, -1, 1)),
    FWD + SZZ: (None, (1, -1, 1), (1, 0, 1), (2, -1, 0)),
    FWD + SXY: ((2, -1, 1), (1, 0, 1), (1, -1, 1), (2, -2, 0)),
    FWD + SXZ: (None, (1, -1, 1), (0, -1, 1), (1, -2, 1)),
    FWD + SYZ: ((1, -2, 1), (0, -1, 1), (1, -1, 1), (2, -2, 0)),
    ADJ + VX: ((2, -2, 0), (1, -1, 1), (1, -1, 1), (2, -2, 1)),
    ADJ + VY: ((2, -1, 1), (1, 0, 1), (1, -1, 1), (2, -2, 0)),
    ADJ + VZ: ((2, -2, 0), (1, -1, 1), (0, -1, 1), (1, -2, 0)),
    ADJ + SXX: (None, (2, -2, 1), (2, -2, 1), None),
    ADJ + SYY: (None, (2, -1, 1), (1, -1, 1), (2, -2, 0)),
    ADJ + SZZ: (None, (2, -1, 0), (1, -1, 0), None),
    ADJ + SXY: ((2, -2, 0), (1, -1, 1), (2, -2, 1), None),
    ADJ + SXZ: (None, (1, -2, 1), (1, -2, 1), None),
    ADJ + SYZ: ((2, -2, 0), (1, -1, 1), (1, -2, 0), None),
    BUOY: ((2, -2, 0), (1, -1, 1), (1, -1, 1), (2, -2, 0)),
    LAM: (None, (2, -1, 1), (1, -1, 1), (2, -2, 0)),
    MU: ((2, -2, 0), (1, -1, 1), (1, -1, 1), (2, -2, 0)),
    INJ: (None, None, (2, -2, 0), None),
    SRC: (None, (2, -2, 0), (2, -1, 1), None),
}

VMEM_LIMIT = 48 * 1024 * 1024


def vmem():
    return pl.BlockSpec(memory_space=pltpu.VMEM)


def hbm():
    return pl.BlockSpec(memory_space=pl.ANY)


def faces(cz, up):
    near, far = [], []
    for f in sorted(F32_Z):
        before, after = F32_Z[f]
        depth = before if up else after
        for d in range(depth):
            layer = cz - 1 - d if up else d
            (far if d else near).append((f, layer, HALO - 1 - d if up else HALO + cz + d))
    return near, far


def face_counts(cz):
    sides = [faces(cz, up) for up in (True, False)]
    return max(len(s[0]) for s in sides), max(len(s[1]) for s in sides)


def y_rows(cz, cy, up):
    layers = cz + 2 * HALO
    narrow, wide = [], []
    for f in sorted(Y_ROWS):
        for offset in (-1, -2) if up else (0, 1):
            spec = Y_ROWS[f][offset + HALO]
            if spec is None:
                continue
            source = cy + offset if up else offset
            target = 2 * cy + offset if up else cy + offset
            listed = list(range(spec[0], layers + spec[1])) + [layers] * spec[2]
            near = offset in (-1, 0)
            (wide if f >= ADJ and near else narrow).extend((f, z, source, target) for z in listed)
    return narrow, wide


def row_counts(cz, cy):
    sides = [y_rows(cz, cy, up) for up in (True, False)]
    return tuple(max(-(-len(s[i]) // 8) for s in sides) for i in (0, 1))


def split(value):
    high = value.astype(jnp.bfloat16)
    low = (value - high.astype(jnp.float32)).astype(jnp.bfloat16)
    return high, low


def joined(high, low):
    return high.astype(jnp.float32) + low.astype(jnp.float32)


def even_mask(axis, shape):
    return jnp.full(shape, lax.rem(lax.axis_index(axis), 2), jnp.int32) == 0


def copies(sems, *pairs):
    out = [pltpu.make_async_copy(source, target, sems.at[i]) for i, (source, target) in enumerate(pairs)]
    for copy in out:
        copy.start()
    return out


def start_kernel(
    cz, store, adjoint, lam, mu, buoy, source, wavelet, receiver, traces, plan,
    near_out, far_out, own, cells, samples, spots, wave, steps, sems,
):
    cy, lanes = own.shape[2], own.shape[3]
    rows = cz * cy
    tiles = store.shape[0]
    small = copies(sems, (plan, steps), (wavelet, wave), (source, spots), (receiver, cells), (traces, samples))
    large = copies(
        sems.at[pl.ds(len(small), 5)],
        (adjoint, own.at[pl.ds(0, 9)]),
        (buoy, own.at[BUOY - ADJ]),
        (lam, own.at[LAM - ADJ]),
        (mu, own.at[MU - ADJ]),
        (store, near_out.at[pl.ds(0, tiles)]),
    )
    for copy in small:
        copy.wait()
    listed = cells[...]
    count = listed.shape[1]
    row_hot = (lax.broadcasted_iota(jnp.int32, (rows, count), 0) == listed // lanes).astype(jnp.float32)
    lane_hit = lax.broadcasted_iota(jnp.int32, (lanes, count), 0) == listed % lanes
    injected = []
    for step in (1, 0):
        sample = samples[pl.ds(steps[step], 1), :]
        field = lax.dot_general(
            row_hot,
            jnp.where(lane_hit, sample, 0.0),
            (((1,), (1,)), ((), ())),
            precision=lax.Precision.HIGHEST,
            preferred_element_type=jnp.float32,
        )
        injected.append(field.reshape(cz, cy, lanes))
    own[INJ - ADJ] = injected[1]
    flat = lax.broadcasted_iota(jnp.int32, (rows, lanes), 0) * lanes + lax.broadcasted_iota(jnp.int32, (rows, lanes), 1)
    for step in range(2):
        value = wave[steps[step]]
        field = jnp.zeros((rows, lanes), jnp.float32)
        for j in range(source.shape[1]):
            field = field + jnp.where(flat == spots[0, j], value, 0.0)
        own[SRC - ADJ + step] = field.reshape(cz, cy, lanes)
    for copy in large:
        copy.wait()
    for f in (SXX, SYY, SZZ):
        own[f] = own[f] + injected[0]

    even = even_mask("gz", (cy, lanes))
    near, far = face_counts(cz)
    up, down = faces(cz, True), faces(cz, False)
    zero = jnp.zeros((cy, lanes), jnp.float32)

    def tile(side, i):
        return own[side[i][0] - ADJ, side[i][1]] if i < len(side) else zero

    for i in range(near):
        above, below = tile(up[0], i), tile(down[0], i)
        for out, base, value in (
            (near_out, tiles, jnp.where(even, above, below)),
            (far_out, 0, jnp.where(even, below, above)),
        ):
            out[base + i], out[base + near + i] = split(value)
    for i in range(far):
        above, below = tile(up[1], i), tile(down[1], i)
        near_out[tiles + 2 * near + i] = jnp.where(even, above, below).astype(jnp.bfloat16)
        far_out[2 * near + i] = jnp.where(even, below, above).astype(jnp.bfloat16)


def column_kernel(
    cz, store, core, chip, both, far, peer, slot, own, main, strip, send_a, send_b, stores, peers, slots, sems
):
    cy, lanes = main.shape[2], main.shape[3]
    layers = cz + 2 * HALO
    tiles = store.shape[0]
    me = lax.axis_index("gz")
    count = lax.axis_size("gz")
    moves = copies(
        sems,
        (peer, peers),
        (slot, slots),
        (store, stores.at[me]),
        (core.at[pl.ds(0, tiles)], stores.at[me ^ 1]),
        (chip, stores.at[me ^ 2]),
        (both, stores.at[me ^ 3]),
    )
    for z in range(cz):
        for f in range(ADJ, FIELDS):
            main[f, HALO + z] = own[f - ADJ, z]
    near, _ = face_counts(cz)
    even = even_mask("gz", (cy, lanes))
    zero = jnp.zeros((cy, lanes), jnp.float32)
    filled = set()
    for up in (True, False):
        for depth, listed in enumerate(faces(cz, up)):
            for i, (f, _, z) in enumerate(listed):
                values = []
                for ref, base in ((core, tiles), (far, 0)):
                    if depth == 0:
                        values.append(joined(ref[base + i], ref[base + near + i]))
                    else:
                        values.append(ref[base + 2 * near + i].astype(jnp.float32))
                main[f, z] = jnp.where(even, values[1], values[0]) if up else jnp.where(even, values[0], values[1])
                filled.add((f, z))
    for f in range(ADJ, FIELDS):
        for z in (0, 1, layers - 2, layers - 1):
            if (f, z) not in filled:
                main[f, z] = zero

    lane = lax.broadcasted_iota(jnp.int32, (cy, lanes), 1)
    position = lane % 8
    group = lane // 8

    def make_strip(f):
        tile = zero
        for z in range(layers):
            value = main[f, z]
            tail = pltpu.roll(value, (8 * z + 2) % lanes, 1)
            head = pltpu.roll(value, (8 * z + 6) % lanes, 1)
            here = group == z
            tile = jnp.where(here & (position < 2), tail, jnp.where(here & (position >= 6), head, tile))
        strip[f] = tile

    for f in range(ADJ, FIELDS):
        make_strip(f)
    for move in moves:
        move.wait()
    below, above = jnp.maximum(me - 1, 0), jnp.minimum(me + 1, count - 1)
    has_below = (me > 0).astype(jnp.float32)
    has_above = (me < count - 1).astype(jnp.float32)
    for z in range(layers):
        if z < HALO:
            brick, piece, keep = below, cz - HALO + z, has_below
        elif z < HALO + cz:
            brick, piece, keep = me, z - HALO, None
        else:
            brick, piece, keep = above, z - HALO - cz, has_above
        holder = peers[brick, piece]
        row = slots[brick, piece] * 9
        for f in range(9):
            value = stores[holder, row + f].astype(jnp.float32)
            main[FWD + f, z] = value if keep is None else value * keep
    for f in range(9):
        make_strip(f)
    even_x = even_mask("gx", (cy, lanes))
    for out, tail_from_even in ((send_a, True), (send_b, False)):
        if out is None:
            continue
        place = 0
        for fields, narrow in ((range(ADJ), True), (range(ADJ, FIELDS), False)):
            quads = [fields[i : i + 4] for i in range(0, len(fields), 4)]
            for i, quad in enumerate(quads):
                tile = zero
                for g, f in enumerate(quad):
                    tail, head = strip[f], pltpu.roll(strip[f], lanes - 6, 1)
                    value = jnp.where(even_x, tail, head) if tail_from_even else jnp.where(even_x, head, tail)
                    value = value if g == 0 else pltpu.roll(value, 2 * g, 1)
                    tile = jnp.where(position // 2 == g, value, tile)
                high, low = split(tile)
                out[place + i] = high
                if not narrow:
                    out[place + len(quads) + i] = low
            place += len(quads) if narrow else 2 * len(quads)


def x_tiles():
    return -(-ADJ // 4) + 2 * -(-(FIELDS - ADJ) // 4)


def rows_kernel(cz, main, strip, from_a, from_b, strips, send_a, send_b, packed):
    cy, lanes = main.shape[2], main.shape[3]
    layers = cz + 2 * HALO
    lane = lax.broadcasted_iota(jnp.int32, (cy, lanes), 1)
    position = lane % 8
    even_x = even_mask("gx", (cy, lanes))
    zero = jnp.zeros((cy, lanes), jnp.float32)
    place = 0
    for fields, narrow in ((range(ADJ), True), (range(ADJ, FIELDS), False)):
        quads = [fields[i : i + 4] for i in range(0, len(fields), 4)]
        for i, quad in enumerate(quads):
            got = []
            for ref in (from_a, from_b):
                if ref is None:
                    got.append(zero)
                elif narrow:
                    got.append(ref[place + i].astype(jnp.float32))
                else:
                    got.append(joined(ref[place + i], ref[place + len(quads) + i]))
            right, left = jnp.where(even_x, got[0], got[1]), jnp.where(even_x, got[1], got[0])
            for g, f in enumerate(quad):
                tile = jnp.where(position // 2 == 1, pltpu.roll(right, (2 - 2 * g) % lanes, 1), strip[f])
                strips[f] = jnp.where(position // 2 == 2, pltpu.roll(left, (4 - 2 * g) % lanes, 1), tile)
        place += len(quads) if narrow else 2 * len(quads)
    narrow, wide = row_counts(cz, cy)
    for side, up in enumerate((True, False)):
        for base, listed in zip((0, narrow), y_rows(cz, cy, up)):
            for r, (f, z, y, _) in enumerate(listed):
                value = strips[f, y : y + 1, :] if z == layers else main[f, z, y : y + 1, :]
                packed[side, base + r // 8, r % 8 : r % 8 + 1, :] = value
    even_y = even_mask("gy", (cy, lanes))
    for t in range(narrow + wide):
        up, down = packed[0, t], packed[1, t]
        for out, value in ((send_a, jnp.where(even_y, up, down)), (send_b, jnp.where(even_y, down, up))):
            if out is None:
                continue
            if t < narrow:
                out[t] = value.astype(jnp.bfloat16)
            else:
                out[t], out[wide + t] = split(value)


def window_kernel(cz, main, strips, from_a, from_b, own, final, image_lam, image_mu, ring, packed, keep):
    cy, lanes = main.shape[2], main.shape[3]
    layers = cz + 2 * HALO
    ring_rows = ring.shape[2]
    even_y = even_mask("gy", (cy, lanes))
    zero = jnp.zeros((cy, lanes), jnp.float32)
    for f in range(FIELDS):
        for z in range(layers + 1):
            ring[f, z, 0:cy, :] = strips[f] if z == layers else main[f, z]
            ring[f, z, cy:ring_rows, :] = jnp.zeros((ring_rows - cy, lanes), jnp.float32)
    narrow, wide = row_counts(cz, cy)
    for t in range(narrow + wide):
        got = []
        for ref in (from_a, from_b):
            if ref is None:
                got.append(zero)
            elif t < narrow:
                got.append(ref[t].astype(jnp.float32))
            else:
                got.append(joined(ref[t], ref[wide + t]))
        packed[0, t] = jnp.where(even_y, got[1], got[0])
        packed[1, t] = jnp.where(even_y, got[0], got[1])
    for side, up in enumerate((True, False)):
        for base, listed in zip((0, narrow), y_rows(cz, cy, up)):
            for r, (f, z, _, y) in enumerate(listed):
                ring[f, z, y : y + 1, :] = packed[side, base + r // 8, r % 8 : r % 8 + 1, :]

    lane = lax.broadcasted_iota(jnp.int32, (ring_rows, lanes), 1)
    first_lane, last_lane = lane == 0, lane == lanes - 1
    edge = layers

    def at(f, z):
        return ring[f, z]

    def x_next(f, z):
        value = at(f, z)
        if z == edge:
            return pltpu.roll(value, lanes - 1, 1)
        beyond = pltpu.roll(at(f, edge), (lanes - 1 - (8 * z + 2)) % lanes, 1)
        return jnp.where(last_lane, beyond, pltpu.roll(value, lanes - 1, 1))

    def x_prev(f, z):
        value = at(f, z)
        if z == edge:
            return pltpu.roll(value, 1, 1)
        beyond = pltpu.roll(at(f, edge), (lanes - (8 * z + 5)) % lanes, 1)
        return jnp.where(first_lane, beyond, pltpu.roll(value, 1, 1))

    def y_next(f, z):
        return pltpu.roll(at(f, z), ring_rows - 1, 0)

    def y_prev(f, z):
        return pltpu.roll(at(f, z), 1, 0)

    def z_next(f, z):
        return pltpu.roll(at(f, edge), lanes - 8, 1) if z == edge else at(f, z + 1)

    def z_prev(f, z):
        return pltpu.roll(at(f, edge), 8, 1) if z == edge else at(f, z - 1)

    def velocity_rates(base, z, want):
        buoy = at(BUOY, z)
        sxx, syy, szz = (functools.partial(at, base + f) for f in (SXX, SYY, SZZ))
        sxy, sxz, syz = (functools.partial(at, base + f) for f in (SXY, SXZ, SYZ))
        out = {}
        if VX in want:
            out[VX] = buoy * (
                (x_next(base + SXX, z) - sxx(z)) + (sxy(z) - y_prev(base + SXY, z)) + (sxz(z) - z_prev(base + SXZ, z))
            )
        if VY in want:
            out[VY] = buoy * (
                (sxy(z) - x_prev(base + SXY, z)) + (y_next(base + SYY, z) - syy(z)) + (syz(z) - z_prev(base + SYZ, z))
            )
        if VZ in want:
            out[VZ] = buoy * (
                (sxz(z) - x_prev(base + SXZ, z)) + (syz(z) - y_prev(base + SYZ, z)) + (z_next(base + SZZ, z) - szz(z))
            )
        return out

    def stress_rates(base, z, want):
        lam, mu = at(LAM, z), at(MU, z)
        vx, vy, vz = at(base + VX, z), at(base + VY, z), at(base + VZ, z)
        out = {}
        if SXX in want:
            exx = vx - x_prev(base + VX, z)
            eyy = vy - y_prev(base + VY, z)
            ezz = vz - z_prev(base + VZ, z)
            common = lam * (exx + eyy + ezz)
            twice = 2.0 * mu
            out[SXX] = common + twice * exx
            out[SYY] = common + twice * eyy
            out[SZZ] = common + twice * ezz
        if SXY in want:
            out[SXY] = mu * ((y_next(base + VX, z) - vx) + (x_next(base + VY, z) - vy))
        if SXZ in want:
            out[SXZ] = mu * ((z_next(base + VX, z) - vx) + (x_next(base + VZ, z) - vz))
            out[SYZ] = mu * ((z_next(base + VY, z) - vy) + (y_next(base + VZ, z) - vz))
        return out

    def spread(ranges):
        for z in list(range(layers)) + [edge]:
            want = {f for f, (a, b) in ranges.items() if z == edge or a <= z < b}
            if want:
                yield z, want

    def velocity_step(base, sign, ranges):
        for z, want in spread(ranges):
            for f, rate in velocity_rates(base, z, want).items():
                ring[base + f, z] = at(base + f, z) + rate if sign > 0 else at(base + f, z) - rate

    def stress_step(base, sign, ranges, before=None, after=None):
        for z, want in spread(ranges):
            for f, rate in stress_rates(base, z, want).items():
                value, normal = at(base + f, z), f in (SXX, SYY, SZZ)
                if before is not None and normal:
                    value = value + at(before, z)
                value = value + rate if sign > 0 else value - rate
                if after is not None and normal:
                    value = value + at(after, z)
                ring[base + f, z] = value

    def terms(f, a):
        term_lam = (f[0] + f[1] + f[2]) * (a[0] + a[1] + a[2])
        term_mu = f[0] * a[0] + f[1] * a[1] + f[2] * a[2] + 2.0 * (f[3] * a[3] + f[4] * a[4] + f[5] * a[5])
        return term_lam, term_mu

    inner = (HALO, HALO + cz)
    n = layers
    stress_step(ADJ, -1, {SXX: (1, n), SXY: (0, n), SXZ: (0, n - 1)})
    velocity_step(FWD, 1, {VX: (1, n), VY: (1, n), VZ: (0, n - 1)})
    stress_step(FWD, 1, {SXX: (1, n - 1), SXY: (1, n - 1), SXZ: (1, n - 1)}, after=SRC)
    for z in range(*inner):
        f = [ring[FWD + s, z, 0:cy, :] for s in range(SXX, SYZ + 1)]
        a = [ring[ADJ + s, z, 0:cy, :] for s in range(SXX, SYZ + 1)]
        a = [value + ring[INJ, z, 0:cy, :] for value in a[:3]] + a[3:]
        keep[0, z - HALO], keep[1, z - HALO] = terms(f, a)
    velocity_step(FWD, 1, {VX: (2, n - 1), VY: (2, n - 1), VZ: (1, n - 2)})
    everything = set(range(SXX, SYZ + 1))
    for z in range(*inner):
        rates = stress_rates(FWD, z, everything)
        f = []
        for s in range(SXX, SYZ + 1):
            value = (at(FWD + s, z) + rates[s])[0:cy, :]
            f.append(value + own[SRC - ADJ + 1, z - HALO] if s <= SZZ else value)
        a = [own[s, z - HALO] for s in range(SXX, SYZ + 1)]
        term_lam, term_mu = terms(f, a)
        image_lam[z - HALO] = term_lam + keep[0, z - HALO]
        image_mu[z - HALO] = term_mu + keep[1, z - HALO]
    velocity_step(ADJ, -1, {VX: (1, n - 1), VY: (1, n - 1), VZ: (1, n - 1)})
    stress_step(ADJ, -1, {SXX: (2, n - 1), SXY: (1, n - 1), SXZ: (1, n - 2)}, before=INJ)
    for z in range(*inner):
        rates = velocity_rates(ADJ, z, {VX, VY, VZ})
        for f in (VX, VY, VZ):
            final[f, z - HALO] = (at(ADJ + f, z) - rates[f])[0:cy, :]
        for s in range(SXX, SYZ + 1):
            final[s, z - HALO] = ring[ADJ + s, z, 0:cy, :]


def swap_pairs(count, first):
    return [(i + d, i + 1 - d) for i in range(first, count - 1, 2) for d in (0, 1)]


def swapped(value_a, value_b, axis):
    count = lax.axis_size(axis)
    got_a = lax.ppermute(value_a, axis, swap_pairs(count, 0))
    return got_a, None if value_b is None else lax.ppermute(value_b, axis, swap_pairs(count, 1))


def stay(value, spec):
    return pltpu.with_memory_space_constraint(value, pltpu.HBM) if spec.memory_space == pl.ANY else value


def kernel_call(body, args, in_specs, out_shape, scratch_shapes=()):
    here = [a is not None for a in args]
    there = [o is not None for o in out_shape]

    def run(*refs):
        refs = iter(refs)
        full = [next(refs) if h else None for h in here + there]
        body(*full, *refs)

    out = iter(
        pl.pallas_call(
            run,
            out_shape=tuple(o for o in out_shape if o is not None),
            in_specs=[s for s, h in zip(in_specs, here) if h],
            out_specs=tuple(vmem() for h in there if h),
            scratch_shapes=list(scratch_shapes),
            compiler_params=pltpu.CompilerParams(vmem_limit_bytes=VMEM_LIMIT),
        )(*[stay(a, s) for a, s in zip(args, in_specs) if a is not None])
    )
    return tuple(next(out) if h else None for h in there)


def on_device(
    checkpoint_store,
    holder_peer,
    holder_slot,
    adjoint_state,
    lame_lambda,
    lame_mu,
    buoyancy,
    source_cell,
    wavelet,
    receiver_cell,
    traces,
    plan,
):
    cz, cy, cx = lame_mu.shape
    layers = cz + 2 * HALO
    bf16, f32 = jnp.bfloat16, jnp.float32
    store = checkpoint_store.reshape(-1, cy, cx)
    tiles = store.shape[0]
    peer, slot = holder_peer[0, 0], holder_slot[0, 0]
    source, receiver = source_cell.reshape(1, -1), receiver_cell.reshape(1, -1)
    traces = traces.reshape(traces.shape[-2:])
    holders = lax.axis_size("gz")
    assert holders == 4
    near, far = face_counts(cz)
    face = 2 * near + far

    def shape(*dims, dtype=f32):
        return jax.ShapeDtypeStruct(dims, dtype)

    chip = lax.ppermute(store, "gz", [(i, i ^ 2) for i in range(holders)])
    to_core, to_far, own = kernel_call(
        functools.partial(start_kernel, cz),
        (store, adjoint_state, lame_lambda, lame_mu, buoyancy, source, wavelet, receiver, traces, plan),
        [hbm()] * 10,
        (shape(tiles + face, cy, cx, dtype=bf16), shape(face, cy, cx, dtype=bf16), shape(15, cz, cy, cx)),
        [
            pltpu.VMEM(receiver.shape, jnp.int32),
            pltpu.VMEM(traces.shape, f32),
            pltpu.SMEM(source.shape, jnp.int32),
            pltpu.SMEM(wavelet.shape, f32),
            pltpu.SMEM(plan.shape, jnp.int32),
            pltpu.SemaphoreType.DMA((10,)),
        ],
    )
    core, far_face = swapped(to_core, to_far, "gz")
    both = lax.ppermute(chip, "gz", [(i, i ^ 1) for i in range(holders)])

    wide_x, wide_y = lax.axis_size("gx") > 2, lax.axis_size("gy") > 2
    x_send = shape(x_tiles(), cy, cx, dtype=bf16)
    main, strip, x_a, x_b = kernel_call(
        functools.partial(column_kernel, cz),
        (store, core, chip, both, far_face, peer, slot, own),
        [hbm()] + [vmem()] * 4 + [hbm()] * 2 + [vmem()],
        (shape(FIELDS, layers, cy, cx), shape(FIELDS, cy, cx), x_send, x_send if wide_x else None),
        [
            pltpu.VMEM((holders, tiles, cy, cx), bf16),
            pltpu.SMEM(peer.shape, jnp.int32),
            pltpu.SMEM(slot.shape, jnp.int32),
            pltpu.SemaphoreType.DMA((6,)),
        ],
    )
    from_a, from_b = swapped(x_a, x_b, "gx")

    narrow, wide = row_counts(cz, cy)
    y_send = shape(narrow + 2 * wide, cy, cx, dtype=bf16)
    strips, y_a, y_b = kernel_call(
        functools.partial(rows_kernel, cz),
        (main, strip, from_a, from_b),
        [vmem()] * 4,
        (shape(FIELDS, cy, cx), y_send, y_send if wide_y else None),
        [pltpu.VMEM((2, narrow + wide, 8, cx), f32)],
    )
    from_a, from_b = swapped(y_a, y_b, "gy")

    return kernel_call(
        functools.partial(window_kernel, cz),
        (main, strips, from_a, from_b, own),
        [vmem()] * 5,
        (shape(9, cz, cy, cx), shape(cz, cy, cx), shape(cz, cy, cx)),
        [
            pltpu.VMEM((FIELDS, layers + 1, 2 * cy, cx), f32),
            pltpu.VMEM((2, narrow + wide, 8, cx), f32),
            pltpu.VMEM((2, cz, cy, cx), f32),
        ],
    )


def solution(mesh):
    return jax.shard_map(
        on_device,
        mesh=mesh,
        in_specs=(
            P("gz", None, None, "gy", "gx"),
            P("gx", "gy", None, None),
            P("gx", "gy", None, None),
            P(None, "gz", "gy", "gx"),
            P("gz", "gy", "gx"),
            P("gz", "gy", "gx"),
            P("gz", "gy", "gx"),
            P("gz", "gy", "gx", None),
            P(),
            P("gz", "gy", "gx", None),
            P("gz", "gy", "gx", None, None),
            P(),
        ),
        out_specs=(P(None, "gz", "gy", "gx"), P("gz", "gy", "gx"), P("gz", "gy", "gx")),
        check_vma=False,
    )
```

time: 68.8 us -> 28.9 us (0.42)
  the two profiles are of different devices: /device:TPU:0 before, /device:TPU:18 now
where the time goes in v2:
time: 28.9 us; the launch traced here: 28.7 us
  waiting for transfers between devices  14.2 us (49%)
  starting transfers between devices  8.35 us (29%)
  Pallas kernels  5.41 us (19%)
  between operations  0.68 us (2%)
    ppermute x2, waiting for transfers between devices, swapped(): lax.ppermute(value_b, axis, swap_pairs(count, 1))  6.55 us
    pallas_call x4, Pallas kernels, kernel_call(): pl.pallas_call(run, out_shape=tuple((o for o in out_shape if o is not Non...  5.41 us
    ppermute x2, starting transfers between devices, swapped(): lax.ppermute(value_b, axis, swap_pairs(count, 1))  4.45 us
    ppermute x1, waiting for transfers between devices, on_device(): chip = lax.ppermute(store, 'gz', [(i, i ^ 2) for i in range(holders)])  3.9 us
    ppermute x3, waiting for transfers between devices, swapped(): got_a = lax.ppermute(value_a, axis, swap_pairs(count, 0))  3.78 us
    ppermute x3, starting transfers between devices, swapped(): got_a = lax.ppermute(value_a, axis, swap_pairs(count, 0))  3.3 us
    ppermute x1, starting transfers between devices, on_device(): chip = lax.ppermute(store, 'gz', [(i, i ^ 2) for i in range(holders)])  0.6 us
  transfers between devices with their start and end apart: 7, of which 5 were waited for; matrix products, arithmetic and copies ran while one was open for 0% of the time, Pallas kernels for 4%

profile of v2, /device:TPU:18, one launch (start us, length us, event | category | flops | bytes accessed | tf_op | source)
XLA Modules:
  0.0 28.7 jit_solution(5477300750667796191)
XLA Ops:
  0.6 0.6 %collective-permute-start.1 = (bf16[72,8,128]{2,1,0:T(8,128)(2,1)}, bf16[72,8,128]{2,1,0:T(8,128)(2,1)S(1)}, u32[]{:S(2)}, u32[]{:S(2)}) collective-permute-start(bf16[72,8,128]{2,1,0:T(8,128)(2,1)} %bitcast.6), channel_id=1, source_target_pairs={{0,2},{1,3},{2,0},{3,1},{4,6},{5,7},{6,4},{7,5},{8,10},{9,11},{10,... | collective-permute-start | bytes 442376 | tf_op jit(solution)/shard_map/ppermute | solution.py:547
  1.2 1.3 %shard_map.139 = (bf16[107,8,128]{2,1,0:T(8,128)(2,1)S(1)}, bf16[35,8,128]{2,1,0:T(8,128)(2,1)S(1)}, f32[15,8,8,128]{3,2,1,0:T(8,128)S(1)}) custom-call(bf16[72,8,128]{2,1,0:T(8,128)(2,1)} %bitcast.7, f32[9,8,8,128]{3,2,1,0:T(8,128)} %refs_1_.1, f32[8,8,128]{2,1,0:T(8,128)} %refs_2_.1, f32[8,8,128]{2,1,0:T(8,128)} %refs_3_.1, f32[8,8,128]{2,1,0:T(8,128)} %refs_4_.1, ...), custom_call_target="tpu_custom_call" | custom-call | tf_op jit(solution)/shard_map/pallas_call | solution.py:505
  2.5 0.1 collective-permute-start
  2.6 3.9 %collective-permute-done.1.refs_2_ = bf16[72,8,128]{2,1,0:T(8,128)(2,1)S(1)} collective-permute-done((bf16[72,8,128]{2,1,0:T(8,128)(2,1)}, bf16[72,8,128]{2,1,0:T(8,128)(2,1)S(1)}, u32[]{:S(2)}, u32[]{:S(2)}) %collective-permute-start.1) | collective-permute-done | bytes 147488 | tf_op jit(solution)/shard_map/ppermute | solution.py:547
  6.5 0.0 collective-permute-start.2
  6.5 2.5 %collective-permute-start.3 = (bf16[35,8,128]{2,1,0:T(8,128)(2,1)S(1)}, bf16[35,8,128]{2,1,0:T(8,128)(2,1)S(1)}, u32[]{:S(2)}, u32[]{:S(2)}) collective-permute-start(bf16[35,8,128]{2,1,0:T(8,128)(2,1)S(1)} %get-tuple-element.13), channel_id=1, source_target_pairs={{1,2},{2,1},{5,6},{6,5},{9,10},{10,9},{13,14},{14,13},{17,18},{18,... | collective-permute-start | bytes 215048 | tf_op jit(solution)/shard_map/ppermute | solution.py:488
  9.1 3.1 %collective-permute-done.3.refs_4_ = bf16[35,8,128]{2,1,0:T(8,128)(2,1)S(1)} collective-permute-done((bf16[35,8,128]{2,1,0:T(8,128)(2,1)S(1)}, bf16[35,8,128]{2,1,0:T(8,128)(2,1)S(1)}, u32[]{:S(2)}, u32[]{:S(2)}) %collective-permute-start.3) | collective-permute-done | bytes 71712 | tf_op jit(solution)/shard_map/ppermute | solution.py:488
  12.1 0.0 collective-permute-done.refs_1_
  12.1 0.0 collective-permute-done.2.refs_3_
  12.1 1.5 %shard_map.140 = (f32[23,12,8,128]{3,2,1,0:T(8,128)S(1)}, f32[23,8,128]{2,1,0:T(8,128)S(1)}, bf16[11,8,128]{2,1,0:T(8,128)(2,1)S(1)}) custom-call(bf16[72,8,128]{2,1,0:T(8,128)(2,1)} %bitcast.8, bf16[107,8,128]{2,1,0:T(8,128)(2,1)S(1)} %collective-permute-done.refs_1_, bf16[72,8,128]{2,1,0:T(8,128)(2,1)S(1)} %collective-permute-done.1.refs_2_, ...), custom_call_target="tpu_custom_call" | custom-call | tf_op jit(solution)/shard_map/pallas_call | solution.py:505
  13.7 1.6 %collective-permute-start.4 = (bf16[11,8,128]{2,1,0:T(8,128)(2,1)S(1)}, bf16[11,8,128]{2,1,0:T(8,128)(2,1)S(1)}, u32[]{:S(2)}, u32[]{:S(2)}) collective-permute-start(bf16[11,8,128]{2,1,0:T(8,128)(2,1)S(1)} %get-tuple-element.17), channel_id=1, source_target_pairs={{0,16},{16,0},{1,17},{17,1},{2,18},{18,2},{3,19},{19,3},{4,20},{20... | collective-permute-start | bytes 67592 | tf_op jit(solution)/shard_map/ppermute | solution.py:487
  15.2 2.3 %collective-permute-done.4.refs_2_ = bf16[11,8,128]{2,1,0:T(8,128)(2,1)S(1)} collective-permute-done((bf16[11,8,128]{2,1,0:T(8,128)(2,1)S(1)}, bf16[11,8,128]{2,1,0:T(8,128)(2,1)S(1)}, u32[]{:S(2)}, u32[]{:S(2)}) %collective-permute-start.4) | collective-permute-done | bytes 22560 | tf_op jit(solution)/shard_map/ppermute | solution.py:487
  17.5 0.3 %shard_map.141 = (f32[23,8,128]{2,1,0:T(8,128)S(1)}, bf16[65,8,128]{2,1,0:T(8,128)(2,1)S(1)}, bf16[65,8,128]{2,1,0:T(8,128)(2,1)S(1)}) custom-call(f32[23,12,8,128]{3,2,1,0:T(8,128)S(1)} %get-tuple-element.15.refs_0_, f32[23,8,128]{2,1,0:T(8,128)S(1)} %get-tuple-element.16.refs_1_, bf16[11,8,128]{2,1,0:T(8,128)(2,1)S(1)} %collective-permute-done.4.refs_2_), custom_call_target="tpu_custom_call" | custom-call | tf_op jit(solution)/shard_map/pallas_call | solution.py:505
  17.8 1.6 %collective-permute-start.5 = (bf16[65,8,128]{2,1,0:T(8,128)(2,1)S(1)}, bf16[65,8,128]{2,1,0:T(8,128)(2,1)S(1)}, u32[]{:S(2)}, u32[]{:S(2)}) collective-permute-start(bf16[65,8,128]{2,1,0:T(8,128)(2,1)S(1)} %get-tuple-element.19), channel_id=1, source_target_pairs={{0,4},{4,0},{8,12},{12,8},{1,5},{5,1},{9,13},{13,9},{2,6},{6,2},{1... | collective-permute-start | bytes 399368 | tf_op jit(solution)/shard_map/ppermute | solution.py:487
  19.5 1.9 %collective-permute-start.6 = (bf16[65,8,128]{2,1,0:T(8,128)(2,1)S(1)}, bf16[65,8,128]{2,1,0:T(8,128)(2,1)S(1)}, u32[]{:S(2)}, u32[]{:S(2)}) collective-permute-start(bf16[65,8,128]{2,1,0:T(8,128)(2,1)S(1)} %get-tuple-element.20), channel_id=1, source_target_pairs={{4,8},{8,4},{5,9},{9,5},{6,10},{10,6},{7,11},{11,7},{20,24},{24,20... | collective-permute-start | bytes 399368 | tf_op jit(solution)/shard_map/ppermute | solution.py:488
  21.4 1.5 %collective-permute-done.5.refs_2_ = bf16[65,8,128]{2,1,0:T(8,128)(2,1)S(1)} collective-permute-done((bf16[65,8,128]{2,1,0:T(8,128)(2,1)S(1)}, bf16[65,8,128]{2,1,0:T(8,128)(2,1)S(1)}, u32[]{:S(2)}, u32[]{:S(2)}) %collective-permute-start.5) | collective-permute-done | bytes 133152 | tf_op jit(solution)/shard_map/ppermute | solution.py:487
  22.9 3.5 %collective-permute-done.6.refs_3_ = bf16[65,8,128]{2,1,0:T(8,128)(2,1)S(1)} collective-permute-done((bf16[65,8,128]{2,1,0:T(8,128)(2,1)S(1)}, bf16[65,8,128]{2,1,0:T(8,128)(2,1)S(1)}, u32[]{:S(2)}, u32[]{:S(2)}) %collective-permute-start.6) | collective-permute-done | bytes 133152 | tf_op jit(solution)/shard_map/ppermute | solution.py:488
  26.3 2.3 %shard_map.142 = (f32[9,8,8,128]{3,2,1,0:T(8,128)}, f32[8,8,128]{2,1,0:T(8,128)}, f32[8,8,128]{2,1,0:T(8,128)}) custom-call(f32[23,12,8,128]{3,2,1,0:T(8,128)S(1)} %get-tuple-element.15.refs_0_, f32[23,8,128]{2,1,0:T(8,128)S(1)} %get-tuple-element.18.refs_1_, bf16[65,8,128]{2,1,0:T(8,128)(2,1)S(1)} %collective-permute-done.5.refs_2_, ...), custom_call_target="tpu_custom_call" | custom-call | tf_op jit(solution)/shard_map/pallas_call | solution.py:505
Async XLA Ops:
  0.6 5.9 %collective-permute-start.1 = (bf16[72,8,128]{2,1,0:T(8,128)(2,1)}, bf16[72,8,128]{2,1,0:T(8,128)(2,1)S(1)}, u32[]{:S(2)}, u32[]{:S(2)}) collective-permute-start(bf16[72,8,128]{2,1,0:T(8,128)(2,1)} %bitcast.6), channel_id=1, source_target_pairs={{0,2},{1,3},{2,0},{3,1},{4,6},{5,7},{6,4},{7,5},{8,10},{9,11},{10,... | collective-permute-start | bytes 442376 | tf_op jit(solution)/shard_map/ppermute | solution.py:547
  2.5 9.6 %collective-permute-start = (bf16[107,8,128]{2,1,0:T(8,128)(2,1)S(1)}, bf16[107,8,128]{2,1,0:T(8,128)(2,1)S(1)}, u32[]{:S(2)}, u32[]{:S(2)}) collective-permute-start(bf16[107,8,128]{2,1,0:T(8,128)(2,1)S(1)} %get-tuple-element.12), channel_id=1, source_target_pairs={{0,1},{1,0},{2,3},{3,2},{4,5},{5,4},{6,7},{7,6},{8,9},{9,8},{10,11... | collective-permute-start | bytes 657416 | tf_op jit(solution)/shard_map/ppermute | solution.py:487
  6.5 5.6 %collective-permute-start.2 = (bf16[72,8,128]{2,1,0:T(8,128)(2,1)S(1)}, bf16[72,8,128]{2,1,0:T(8,128)(2,1)S(1)}, u32[]{:S(2)}, u32[]{:S(2)}) collective-permute-start(bf16[72,8,128]{2,1,0:T(8,128)(2,1)S(1)} %collective-permute-done.1.refs_2_), channel_id=1, source_target_pairs={{0,1},{1,0},{2,3},{3,2},{4,5},{5,4},{6,7},{7,6},{8,9},{9,8},{10,11... | collective-permute-start | bytes 442376 | tf_op jit(solution)/shard_map/ppermute | solution.py:563
  6.5 5.6 %collective-permute-start.3 = (bf16[35,8,128]{2,1,0:T(8,128)(2,1)S(1)}, bf16[35,8,128]{2,1,0:T(8,128)(2,1)S(1)}, u32[]{:S(2)}, u32[]{:S(2)}) collective-permute-start(bf16[35,8,128]{2,1,0:T(8,128)(2,1)S(1)} %get-tuple-element.13), channel_id=1, source_target_pairs={{1,2},{2,1},{5,6},{6,5},{9,10},{10,9},{13,14},{14,13},{17,18},{18,... | collective-permute-start | bytes 215048 | tf_op jit(solution)/shard_map/ppermute | solution.py:488
  13.7 3.9 %collective-permute-start.4 = (bf16[11,8,128]{2,1,0:T(8,128)(2,1)S(1)}, bf16[11,8,128]{2,1,0:T(8,128)(2,1)S(1)}, u32[]{:S(2)}, u32[]{:S(2)}) collective-permute-start(bf16[11,8,128]{2,1,0:T(8,128)(2,1)S(1)} %get-tuple-element.17), channel_id=1, source_target_pairs={{0,16},{16,0},{1,17},{17,1},{2,18},{18,2},{3,19},{19,3},{4,20},{20... | collective-permute-start | bytes 67592 | tf_op jit(solution)/shard_map/ppermute | solution.py:487
  17.8 5.1 %collective-permute-start.5 = (bf16[65,8,128]{2,1,0:T(8,128)(2,1)S(1)}, bf16[65,8,128]{2,1,0:T(8,128)(2,1)S(1)}, u32[]{:S(2)}, u32[]{:S(2)}) collective-permute-start(bf16[65,8,128]{2,1,0:T(8,128)(2,1)S(1)} %get-tuple-element.19), channel_id=1, source_target_pairs={{0,4},{4,0},{8,12},{12,8},{1,5},{5,1},{9,13},{13,9},{2,6},{6,2},{1... | collective-permute-start | bytes 399368 | tf_op jit(solution)/shard_map/ppermute | solution.py:487
  19.5 6.9 %collective-permute-start.6 = (bf16[65,8,128]{2,1,0:T(8,128)(2,1)S(1)}, bf16[65,8,128]{2,1,0:T(8,128)(2,1)S(1)}, u32[]{:S(2)}, u32[]{:S(2)}) collective-permute-start(bf16[65,8,128]{2,1,0:T(8,128)(2,1)S(1)} %get-tuple-element.20), channel_id=1, source_target_pairs={{4,8},{8,4},{5,9},{9,5},{6,10},{10,6},{7,11},{11,7},{20,24},{24,20... | collective-permute-start | bytes 399368 | tf_op jit(solution)/shard_map/ppermute | solution.py:488

commit v3 on v2

--- a/solution.py
+++ b/solution.py
@@ -100,8 +100,9 @@
     return high.astype(jnp.float32) + low.astype(jnp.float32)
 
 
-def even_mask(axis, shape):
-    return jnp.full(shape, lax.rem(lax.axis_index(axis), 2), jnp.int32) == 0
+def even_mask(axes, shape):
+    total = sum(lax.axis_index(a) for a in ((axes,) if isinstance(axes, str) else axes))
+    return jnp.full(shape, lax.rem(total, 2), jnp.int32) == 0
 
 
 def copies(sems, *pairs):
@@ -111,21 +112,57 @@
     return out
 
 
+def pack_rows(cz, cy, row_of, packed, send_a, send_b):
+    narrow, wide = row_counts(cz, cy)
+    for side, up in enumerate((True, False)):
+        for base, listed in zip((0, narrow), y_rows(cz, cy, up)):
+            for r, (f, z, y, _) in enumerate(listed):
+                packed[side, base + r // 8, r % 8 : r % 8 + 1, :] = row_of(f, z, y)
+    even = even_mask(("gy", "gz"), packed.shape[2:])
+    for t in range(narrow + wide):
+        up, down = packed[0, t], packed[1, t]
+        for out, value in ((send_a, jnp.where(even, up, down)), (send_b, jnp.where(even, down, up))):
+            if out is None:
+                continue
+            if t < narrow:
+                out[t] = value.astype(jnp.bfloat16)
+            else:
+                out[t], out[wide + t] = split(value)
+
+
+def unpack_rows(cz, cy, from_a, from_b, packed, put_row):
+    narrow, wide = row_counts(cz, cy)
+    even = even_mask(("gy", "gz"), packed.shape[2:])
+    for t in range(narrow + wide):
+        got = []
+        for ref in (from_a, from_b):
+            if ref is None:
+                got.append(jnp.zeros(packed.shape[2:], jnp.float32))
+            elif t < narrow:
+                got.append(ref[t].astype(jnp.float32))
+            else:
+                got.append(joined(ref[t], ref[wide + t]))
+        packed[0, t] = jnp.where(even, got[1], got[0])
+        packed[1, t] = jnp.where(even, got[0], got[1])
+    for side, up in enumerate((True, False)):
+        for base, listed in zip((0, narrow), y_rows(cz, cy, up)):
+            for r, (f, z, _, y) in enumerate(listed):
+                put_row(f, z, y, packed[side, base + r // 8, r % 8 : r % 8 + 1, :])
+
+
 def start_kernel(
-    cz, store, adjoint, lam, mu, buoy, source, wavelet, receiver, traces, plan,
-    near_out, far_out, own, cells, samples, spots, wave, steps, sems,
+    cz, adjoint, lam, mu, buoy, source, wavelet, receiver, traces, plan,
+    out, own, cells, samples, spots, wave, steps, sems,
 ):
     cy, lanes = own.shape[2], own.shape[3]
     rows = cz * cy
-    tiles = store.shape[0]
     small = copies(sems, (plan, steps), (wavelet, wave), (source, spots), (receiver, cells), (traces, samples))
     large = copies(
-        sems.at[pl.ds(len(small), 5)],
+        sems.at[pl.ds(len(small), 4)],
         (adjoint, own.at[pl.ds(0, 9)]),
         (buoy, own.at[BUOY - ADJ]),
         (lam, own.at[LAM - ADJ]),
         (mu, own.at[MU - ADJ]),
-        (store, near_out.at[pl.ds(0, tiles)]),
     )
     for copy in small:
         copy.wait()
@@ -165,24 +202,69 @@
     def tile(side, i):
         return own[side[i][0] - ADJ, side[i][1]] if i < len(side) else zero
 
+    face = 2 * near + far
     for i in range(near):
         above, below = tile(up[0], i), tile(down[0], i)
-        for out, base, value in (
-            (near_out, tiles, jnp.where(even, above, below)),
-            (far_out, 0, jnp.where(even, below, above)),
-        ):
+        for base, value in ((0, jnp.where(even, above, below)), (face, jnp.where(even, below, above))):
             out[base + i], out[base + near + i] = split(value)
     for i in range(far):
         above, below = tile(up[1], i), tile(down[1], i)
-        near_out[tiles + 2 * near + i] = jnp.where(even, above, below).astype(jnp.bfloat16)
-        far_out[2 * near + i] = jnp.where(even, below, above).astype(jnp.bfloat16)
+        out[2 * near + i] = jnp.where(even, above, below).astype(jnp.bfloat16)
+        out[face + 2 * near + i] = jnp.where(even, below, above).astype(jnp.bfloat16)
+
+
+def strip_of(main, layers):
+    cy, lanes = main(0).shape
+    lane = lax.broadcasted_iota(jnp.int32, (cy, lanes), 1)
+    position = lane % 8
+    group = lane // 8
+    tile = jnp.zeros((cy, lanes), jnp.float32)
+    for z in range(layers):
+        tail = pltpu.roll(main(z), (8 * z + 2) % lanes, 1)
+        head = pltpu.roll(main(z), (8 * z + 6) % lanes, 1)
+        here = group == z
+        tile = jnp.where(here & (position < 2), tail, jnp.where(here & (position >= 6), head, tile))
+    return tile
+
+
+def halo_kernel(cz, core, far, own, ring):
+    cy, lanes = own.shape[2], own.shape[3]
+    layers = cz + 2 * HALO
+    ring_rows = ring.shape[2]
+    near, _ = face_counts(cz)
+    even = even_mask("gz", (cy, lanes))
+    zero = jnp.zeros((cy, lanes), jnp.float32)
+    for f in range(ring.shape[0]):
+        for z in range(cz):
+            ring[f, HALO + z, 0:cy, :] = own[f, z]
+    filled = set()
+    for up in (True, False):
+        for depth, listed in enumerate(faces(cz, up)):
+            for i, (f, _, z) in enumerate(listed):
+                values = []
+                for ref in (core, far):
+                    if depth == 0:
+                        values.append(joined(ref[i], ref[near + i]))
+                    else:
+                        values.append(ref[2 * near + i].astype(jnp.float32))
+                value = jnp.where(even, values[1], values[0]) if up else jnp.where(even, values[0], values[1])
+                ring[f - ADJ, z, 0:cy, :] = value
+                filled.add((f - ADJ, z))
+    for f in range(ring.shape[0]):
+        for z in (0, 1, layers - 2, layers - 1):
+            if (f, z) not in filled:
+                ring[f, z, 0:cy, :] = zero
+        ring[f, layers, 0:cy, :] = strip_of(lambda z: ring[f, z, 0:cy, :], layers)
+        for z in range(layers + 1):
+            ring[f, z, cy:ring_rows, :] = jnp.zeros((ring_rows - cy, lanes), jnp.float32)
 
 
 def column_kernel(
-    cz, store, core, chip, both, far, peer, slot, own, main, strip, send_a, send_b, stores, peers, slots, sems
+    cz, store, core, chip, both, peer, slot, ring_w, ring, send_a, send_b, stores, peers, slots, sems
 ):
-    cy, lanes = main.shape[2], main.shape[3]
+    cy, lanes = core.shape[1], core.shape[2]
     layers = cz + 2 * HALO
+    ring_rows = ring.shape[2]
     tiles = store.shape[0]
     me = lax.axis_index("gz")
     count = lax.axis_size("gz")
@@ -191,49 +273,14 @@
         (peer, peers),
         (slot, slots),
         (store, stores.at[me]),
-        (core.at[pl.ds(0, tiles)], stores.at[me ^ 1]),
+        (core, stores.at[me ^ 1]),
         (chip, stores.at[me ^ 2]),
         (both, stores.at[me ^ 3]),
     )
-    for z in range(cz):
-        for f in range(ADJ, FIELDS):
-            main[f, HALO + z] = own[f - ADJ, z]
-    near, _ = face_counts(cz)
-    even = even_mask("gz", (cy, lanes))
     zero = jnp.zeros((cy, lanes), jnp.float32)
-    filled = set()
-    for up in (True, False):
-        for depth, listed in enumerate(faces(cz, up)):
-            for i, (f, _, z) in enumerate(listed):
-                values = []
-                for ref, base in ((core, tiles), (far, 0)):
-                    if depth == 0:
-                        values.append(joined(ref[base + i], ref[base + near + i]))
-                    else:
-                        values.append(ref[base + 2 * near + i].astype(jnp.float32))
-                main[f, z] = jnp.where(even, values[1], values[0]) if up else jnp.where(even, values[0], values[1])
-                filled.add((f, z))
-    for f in range(ADJ, FIELDS):
-        for z in (0, 1, layers - 2, layers - 1):
-            if (f, z) not in filled:
-                main[f, z] = zero
-
-    lane = lax.broadcasted_iota(jnp.int32, (cy, lanes), 1)
-    position = lane % 8
-    group = lane // 8
-
-    def make_strip(f):
-        tile = zero
-        for z in range(layers):
-            value = main[f, z]
-            tail = pltpu.roll(value, (8 * z + 2) % lanes, 1)
-            head = pltpu.roll(value, (8 * z + 6) % lanes, 1)
-            here = group == z
-            tile = jnp.where(here & (position < 2), tail, jnp.where(here & (position >= 6), head, tile))
-        strip[f] = tile
-
-    for f in range(ADJ, FIELDS):
-        make_strip(f)
+    for f in range(9):
+        for z in range(layers + 1):
+            ring[f, z, cy:ring_rows, :] = jnp.zeros((ring_rows - cy, lanes), jnp.float32)
     for move in moves:
         move.wait()
     below, above = jnp.maximum(me - 1, 0), jnp.minimum(me + 1, count - 1)
@@ -250,9 +297,12 @@
         row = slots[brick, piece] * 9
         for f in range(9):
             value = stores[holder, row + f].astype(jnp.float32)
-            main[FWD + f, z] = value if keep is None else value * keep
+            ring[f, z, 0:cy, :] = value if keep is None else value * keep
     for f in range(9):
-        make_strip(f)
+        ring[f, layers, 0:cy, :] = strip_of(lambda z: ring[f, z, 0:cy, :], layers)
+    strip = [ring[f, layers, 0:cy, :] for f in range(9)]
+    strip += [ring_w[f, layers, 0:cy, :] for f in range(ring_w.shape[0])]
+    position = lax.broadcasted_iota(jnp.int32, (cy, lanes), 1) % 8
     even_x = even_mask("gx", (cy, lanes))
     for out, tail_from_even in ((send_a, True), (send_b, False)):
         if out is None:
@@ -278,11 +328,12 @@
     return -(-ADJ // 4) + 2 * -(-(FIELDS - ADJ) // 4)
 
 
-def rows_kernel(cz, main, strip, from_a, from_b, strips, send_a, send_b, packed):
-    cy, lanes = main.shape[2], main.shape[3]
+def rows_kernel(cz, ring_f, ring_w, from_a, from_b, strips, send_a, send_b, packed):
+    cy, lanes = strips.shape[1], strips.shape[2]
     layers = cz + 2 * HALO
-    lane = lax.broadcasted_iota(jnp.int32, (cy, lanes), 1)
-    position = lane % 8
+    strip = [ring_f[f, layers, 0:cy, :] for f in range(9)]
+    strip += [ring_w[f, layers, 0:cy, :] for f in range(ring_w.shape[0])]
+    position = lax.broadcasted_iota(jnp.int32, (cy, lanes), 1) % 8
     even_x = even_mask("gx", (cy, lanes))
     zero = jnp.zeros((cy, lanes), jnp.float32)
     place = 0
@@ -302,50 +353,45 @@
                 tile = jnp.where(position // 2 == 1, pltpu.roll(right, (2 - 2 * g) % lanes, 1), strip[f])
                 strips[f] = jnp.where(position // 2 == 2, pltpu.roll(left, (4 - 2 * g) % lanes, 1), tile)
         place += len(quads) if narrow else 2 * len(quads)
-    narrow, wide = row_counts(cz, cy)
-    for side, up in enumerate((True, False)):
-        for base, listed in zip((0, narrow), y_rows(cz, cy, up)):
-            for r, (f, z, y, _) in enumerate(listed):
-                value = strips[f, y : y + 1, :] if z == layers else main[f, z, y : y + 1, :]
-                packed[side, base + r // 8, r % 8 : r % 8 + 1, :] = value
-    even_y = even_mask("gy", (cy, lanes))
-    for t in range(narrow + wide):
-        up, down = packed[0, t], packed[1, t]
-        for out, value in ((send_a, jnp.where(even_y, up, down)), (send_b, jnp.where(even_y, down, up))):
-            if out is None:
-                continue
-            if t < narrow:
-                out[t] = value.astype(jnp.bfloat16)
-            else:
-                out[t], out[wide + t] = split(value)
-
-
-def window_kernel(cz, main, strips, from_a, from_b, own, final, image_lam, image_mu, ring, packed, keep):
-    cy, lanes = main.shape[2], main.shape[3]
+
+    def row_of(f, z, y):
+        if z == layers:
+            return strips[f, y : y + 1, :]
+        return ring_f[f, z, y : y + 1, :] if f < ADJ else ring_w[f - ADJ, z, y : y + 1, :]
+
+    pack_rows(cz, cy, row_of, packed, send_a, send_b)
+
+
+class Ring:
+    def __init__(self, ring_f, ring_w):
+        self.parts = ring_f, ring_w
+
+    def __getitem__(self, key):
+        f = key[0]
+        return self.parts[0][key] if f < ADJ else self.parts[1][(f - ADJ, *key[1:])]
+
+    def __setitem__(self, key, value):
+        f = key[0]
+        if f < ADJ:
+            self.parts[0][key] = value
+        else:
+            self.parts[1][(f - ADJ, *key[1:])] = value
+
+
+def window_kernel(
+    cz, ring_f_in, ring_w_in, strips, from_a, from_b, own, final, image_lam, image_mu, ring_f, ring_w, packed, keep
+):
+    cy, lanes = own.shape[2], own.shape[3]
     layers = cz + 2 * HALO
-    ring_rows = ring.shape[2]
-    even_y = even_mask("gy", (cy, lanes))
-    zero = jnp.zeros((cy, lanes), jnp.float32)
+    ring_rows = ring_f.shape[2]
+    ring = Ring(ring_f, ring_w)
     for f in range(FIELDS):
-        for z in range(layers + 1):
-            ring[f, z, 0:cy, :] = strips[f] if z == layers else main[f, z]
-            ring[f, z, cy:ring_rows, :] = jnp.zeros((ring_rows - cy, lanes), jnp.float32)
-    narrow, wide = row_counts(cz, cy)
-    for t in range(narrow + wide):
-        got = []
-        for ref in (from_a, from_b):
-            if ref is None:
-                got.append(zero)
-            elif t < narrow:
-                got.append(ref[t].astype(jnp.float32))
-            else:
-                got.append(joined(ref[t], ref[wide + t]))
-        packed[0, t] = jnp.where(even_y, got[1], got[0])
-        packed[1, t] = jnp.where(even_y, got[0], got[1])
-    for side, up in enumerate((True, False)):
-        for base, listed in zip((0, narrow), y_rows(cz, cy, up)):
-            for r, (f, z, _, y) in enumerate(listed):
-                ring[f, z, y : y + 1, :] = packed[side, base + r // 8, r % 8 : r % 8 + 1, :]
+        ring[f, layers, 0:cy, :] = strips[f]
+
+    def put_row(f, z, y, value):
+        ring[f, z, y : y + 1, :] = value
+
+    unpack_rows(cz, cy, from_a, from_b, packed, put_row)
 
     lane = lax.broadcasted_iota(jnp.int32, (ring_rows, lanes), 1)
     first_lane, last_lane = lane == 0, lane == lanes - 1
@@ -492,7 +538,7 @@
     return pltpu.with_memory_space_constraint(value, pltpu.HBM) if spec.memory_space == pl.ANY else value
 
 
-def kernel_call(body, args, in_specs, out_shape, scratch_shapes=()):
+def kernel_call(body, args, in_specs, out_shape, scratch_shapes=(), aliases=None):
     here = [a is not None for a in args]
     there = [o is not None for o in out_shape]
 
@@ -508,6 +554,7 @@
             in_specs=[s for s, h in zip(in_specs, here) if h],
             out_specs=tuple(vmem() for h in there if h),
             scratch_shapes=list(scratch_shapes),
+            input_output_aliases=aliases or {},
             compiler_params=pltpu.CompilerParams(vmem_limit_bytes=VMEM_LIMIT),
         )(*[stay(a, s) for a, s in zip(args, in_specs) if a is not None])
     )
@@ -544,31 +591,39 @@
     def shape(*dims, dtype=f32):
         return jax.ShapeDtypeStruct(dims, dtype)
 
+    wide_x = lax.axis_size("gx") > 2
     chip = lax.ppermute(store, "gz", [(i, i ^ 2) for i in range(holders)])
-    to_core, to_far, own = kernel_call(
+    core = lax.ppermute(store, "gz", [(i, i ^ 1) for i in range(holders)])
+    to_core, own = kernel_call(
         functools.partial(start_kernel, cz),
-        (store, adjoint_state, lame_lambda, lame_mu, buoyancy, source, wavelet, receiver, traces, plan),
-        [hbm()] * 10,
-        (shape(tiles + face, cy, cx, dtype=bf16), shape(face, cy, cx, dtype=bf16), shape(15, cz, cy, cx)),
+        (adjoint_state, lame_lambda, lame_mu, buoyancy, source, wavelet, receiver, traces, plan),
+        [hbm()] * 9,
+        (shape(2 * face, cy, cx, dtype=bf16), shape(15, cz, cy, cx)),
         [
             pltpu.VMEM(receiver.shape, jnp.int32),
             pltpu.VMEM(traces.shape, f32),
             pltpu.SMEM(source.shape, jnp.int32),
             pltpu.SMEM(wavelet.shape, f32),
             pltpu.SMEM(plan.shape, jnp.int32),
-            pltpu.SemaphoreType.DMA((10,)),
+            pltpu.SemaphoreType.DMA((9,)),
         ],
     )
-    core, far_face = swapped(to_core, to_far, "gz")
+    core_faces = lax.ppermute(to_core, "gz", [(i, i ^ 1) for i in range(holders)])
+    far_face = lax.ppermute(core_faces[face:], "gz", [(0, 2), (3, 1)])
     both = lax.ppermute(chip, "gz", [(i, i ^ 1) for i in range(holders)])
 
-    wide_x, wide_y = lax.axis_size("gx") > 2, lax.axis_size("gy") > 2
+    (ring_w,) = kernel_call(
+        functools.partial(halo_kernel, cz),
+        (core_faces, far_face, own),
+        [vmem()] * 3,
+        (shape(FIELDS - ADJ, layers + 1, 2 * cy, cx),),
+    )
     x_send = shape(x_tiles(), cy, cx, dtype=bf16)
-    main, strip, x_a, x_b = kernel_call(
+    ring_f, x_a, x_b = kernel_call(
         functools.partial(column_kernel, cz),
-        (store, core, chip, both, far_face, peer, slot, own),
-        [hbm()] + [vmem()] * 4 + [hbm()] * 2 + [vmem()],
-        (shape(FIELDS, layers, cy, cx), shape(FIELDS, cy, cx), x_send, x_send if wide_x else None),
+        (store, core, chip, both, peer, slot, ring_w),
+        [hbm()] + [vmem()] * 3 + [hbm()] * 2 + [vmem()],
+        (shape(ADJ, layers + 1, 2 * cy, cx), x_send, x_send if wide_x else None),
         [
             pltpu.VMEM((holders, tiles, cy, cx), bf16),
             pltpu.SMEM(peer.shape, jnp.int32),
@@ -582,24 +637,41 @@
     y_send = shape(narrow + 2 * wide, cy, cx, dtype=bf16)
     strips, y_a, y_b = kernel_call(
         functools.partial(rows_kernel, cz),
-        (main, strip, from_a, from_b),
+        (ring_f, ring_w, from_a, from_b),
         [vmem()] * 4,
-        (shape(FIELDS, cy, cx), y_send, y_send if wide_y else None),
+        (shape(FIELDS, cy, cx), y_send, y_send),
         [pltpu.VMEM((2, narrow + wide, 8, cx), f32)],
     )
-    from_a, from_b = swapped(y_a, y_b, "gy")
-
-    return kernel_call(
+    gy = lax.axis_size("gy")
+    turns = [
+        [
+            (i * holders + c, j * holders + c)
+            for c in range(holders)
+            for i, j in swap_pairs(gy, (c + turn) % 2)
+        ]
+        for turn in (0, 1)
+    ]
+    from_a = lax.ppermute(y_a, ("gy", "gz"), turns[0])
+    from_b = lax.ppermute(y_b, ("gy", "gz"), turns[1])
+
+    result = kernel_call(
         functools.partial(window_kernel, cz),
-        (main, strips, from_a, from_b, own),
-        [vmem()] * 5,
-        (shape(9, cz, cy, cx), shape(cz, cy, cx), shape(cz, cy, cx)),
+        (ring_f, ring_w, strips, from_a, from_b, own),
+        [vmem()] * 6,
+        (
+            shape(9, cz, cy, cx),
+            shape(cz, cy, cx),
+            shape(cz, cy, cx),
+            shape(*ring_f.shape),
+            shape(*ring_w.shape),
+        ),
         [
-            pltpu.VMEM((FIELDS, layers + 1, 2 * cy, cx), f32),
             pltpu.VMEM((2, narrow + wide, 8, cx), f32),
             pltpu.VMEM((2, cz, cy, cx), f32),
         ],
-    )
+        {0: 3, 1: 4},
+    )
+    return result[:3]
 
 
 def solution(mesh):

time: 28.9 us -> 31.7 us (1.097)
  waiting for transfers between devices: 14.2 us -> 15.6 us
  starting transfers between devices: 8.35 us -> 9.45 us
    ppermute x2 -> x5, waiting for transfers between devices: 6.55 us -> 9.89 us  [the longest x1 4.93 us: on_device(): far_face = lax.ppermute(core_faces[face:], 'gz', [(0, 2), (3, 1)])]
    ppermute x2 -> x5, starting transfers between devices: 4.45 us -> 7.27 us  [the longest x1 3.48 us: on_device(): from_a = lax.ppermute(y_a, ('gy', 'gz'), turns[0])]
    ppermute x3 -> x1, starting transfers between devices: 3.3 us -> 1.58 us  [swapped(): got_a = lax.ppermute(value_a, axis, swap_pairs(count, 0))]
    ppermute x3 -> x1, waiting for transfers between devices: 3.78 us -> 2.28 us  [swapped(): got_a = lax.ppermute(value_a, axis, swap_pairs(count, 0))]
    ppermute x1, waiting for transfers between devices: 3.9 us -> 3.42 us  [on_device(): chip = lax.ppermute(store, 'gz', [(i, i ^ 2) for i in range(holders)])]
    pallas_call x4 -> x5, Pallas kernels: 5.41 us -> 5.69 us  [kernel_call(): pl.pallas_call(run, out_shape=tuple((o for o in out_shape if o is not Non...]
  transfers between devices with their start and end apart: 7 -> 8, of which waited for: 5 -> 5; matrix products, arithmetic and copies ran while one was open for 0% -> 0% of each run, Pallas kernels for 4% -> 5%
where the time goes in v3:
time: 31.7 us; the launch traced here: 31.5 us
  waiting for transfers between devices  15.6 us (49%)
  starting transfers between devices  9.45 us (30%)
  Pallas kernels  5.69 us (18%)
  between operations  0.71 us (2%)
    pallas_call x5, Pallas kernels, kernel_call(): pl.pallas_call(run, out_shape=tuple((o for o in out_shape if o is not Non...  5.69 us
    ppermute x1, waiting for transfers between devices, on_device(): far_face = lax.ppermute(core_faces[face:], 'gz', [(0, 2), (3, 1)])  4.93 us
    ppermute x1, waiting for transfers between devices, on_device(): from_b = lax.ppermute(y_b, ('gy', 'gz'), turns[1])  3.49 us
    ppermute x1, starting transfers between devices, on_device(): from_a = lax.ppermute(y_a, ('gy', 'gz'), turns[0])  3.48 us
    ppermute x1, waiting for transfers between devices, on_device(): chip = lax.ppermute(store, 'gz', [(i, i ^ 2) for i in range(holders)])  3.42 us
    ppermute x1, waiting for transfers between devices, swapped(): got_a = lax.ppermute(value_a, axis, swap_pairs(count, 0))  2.28 us
    ppermute x1, starting transfers between devices, on_device(): from_b = lax.ppermute(y_b, ('gy', 'gz'), turns[1])  1.92 us
    ppermute x1, starting transfers between devices, swapped(): got_a = lax.ppermute(value_a, axis, swap_pairs(count, 0))  1.58 us
  transfers between devices with their start and end apart: 8, of which 5 were waited for; matrix products, arithmetic and copies ran while one was open for 0% of the time, Pallas kernels for 5%

profile of v3, /device:TPU:18, one launch (start us, length us, event | category | flops | bytes accessed | tf_op | source)
XLA Modules:
  0.0 31.5 jit_solution(4128270349164537667)
XLA Ops:
  0.6 0.6 %collective-permute-start.1 = (bf16[72,8,128]{2,1,0:T(8,128)(2,1)}, bf16[72,8,128]{2,1,0:T(8,128)(2,1)S(1)}, u32[]{:S(2)}, u32[]{:S(2)}) collective-permute-start(bf16[72,8,128]{2,1,0:T(8,128)(2,1)} %bitcast.6), channel_id=1, source_target_pairs={{0,2},{1,3},{2,0},{3,1},{4,6},{5,7},{6,4},{7,5},{8,10},{9,11},{10,... | collective-permute-start | bytes 442376 | tf_op jit(solution)/shard_map/ppermute | solution.py:595
  1.2 1.3 %shard_map.139 = (bf16[70,8,128]{2,1,0:T(8,128)(2,1)S(1)}, f32[15,8,8,128]{3,2,1,0:T(8,128)S(1)}) custom-call(f32[9,8,8,128]{3,2,1,0:T(8,128)} %refs_0_.1, f32[8,8,128]{2,1,0:T(8,128)} %refs_1_.1, f32[8,8,128]{2,1,0:T(8,128)} %refs_2_.1, f32[8,8,128]{2,1,0:T(8,128)} %refs_3_.1, s32[1,4]{1,0:T(1,128)} %bitcast.12, f32[64]{0:T(128)} %refs_5_.1, ...), custom_call_target="tpu_custom_call" | custom-call | tf_op jit(solution)/shard_map/pallas_call | solution.py:551
  2.5 0.1 collective-permute-start.3
  2.6 0.5 %collective-permute-start = (bf16[72,8,128]{2,1,0:T(8,128)(2,1)}, bf16[72,8,128]{2,1,0:T(8,128)(2,1)S(1)}, u32[]{:S(2)}, u32[]{:S(2)}) collective-permute-start(bf16[72,8,128]{2,1,0:T(8,128)(2,1)} %bitcast.7), channel_id=1, source_target_pairs={{0,1},{1,0},{2,3},{3,2},{4,5},{5,4},{6,7},{7,6},{8,9},{9,8},{10,11... | collective-permute-start | bytes 442376 | tf_op jit(solution)/shard_map/ppermute | solution.py:596
  3.1 3.4 %collective-permute-done.1.refs_2_ = bf16[72,8,128]{2,1,0:T(8,128)(2,1)S(1)} collective-permute-done((bf16[72,8,128]{2,1,0:T(8,128)(2,1)}, bf16[72,8,128]{2,1,0:T(8,128)(2,1)S(1)}, u32[]{:S(2)}, u32[]{:S(2)}) %collective-permute-start.1) | collective-permute-done | bytes 147488 | tf_op jit(solution)/shard_map/ppermute | solution.py:595
  6.5 0.0 collective-permute-start.2
  6.5 0.0 collective-permute-done.3.refs_0_
  6.5 1.3 %collective-permute-start.4 = (bf16[35,8,128]{2,1,0:T(8,128)(2,1)S(1)}, bf16[35,8,128]{2,1,0:T(8,128)(2,1)S(1)}, u32[]{:S(2)}, u32[]{:S(2)}) collective-permute-start(bf16[35,8,128]{2,1,0:T(8,128)(2,1)S(1)} %slice.4), channel_id=1, source_target_pairs={{0,2},{3,1},{4,6},{7,5},{8,10},{11,9},{12,14},{15,13},{16,18},{19,... | collective-permute-start | bytes 215048 | tf_op jit(solution)/shard_map/ppermute | solution.py:612
  7.8 4.9 %collective-permute-done.4.refs_1_ = bf16[35,8,128]{2,1,0:T(8,128)(2,1)S(1)} collective-permute-done((bf16[35,8,128]{2,1,0:T(8,128)(2,1)S(1)}, bf16[35,8,128]{2,1,0:T(8,128)(2,1)S(1)}, u32[]{:S(2)}, u32[]{:S(2)}) %collective-permute-start.4) | collective-permute-done | bytes 71712 | tf_op jit(solution)/shard_map/ppermute | solution.py:612
  12.7 0.4 %shard_map.140.refs_6_.refs_1_ = f32[14,13,16,128]{3,2,1,0:T(8,128)S(1)} custom-call(bf16[70,8,128]{2,1,0:T(8,128)(2,1)S(1)} %collective-permute-done.3.refs_0_, bf16[35,8,128]{2,1,0:T(8,128)(2,1)S(1)} %collective-permute-done.4.refs_1_, f32[15,8,8,128]{3,2,1,0:T(8,128)S(1)} %get-tuple-element.14.refs_2_.refs_5_), custom_call_target="tpu_custom_call" | custom-call | tf_op jit(solution)/shard_map/pallas_call | solution.py:551
  13.2 0.0 collective-permute-done.refs_1_
  13.2 0.0 collective-permute-done.2.refs_3_
  13.2 1.4 %shard_map.141 = (f32[9,13,16,128]{3,2,1,0:T(8,128)S(1)}, bf16[11,8,128]{2,1,0:T(8,128)(2,1)S(1)}) custom-call(bf16[72,8,128]{2,1,0:T(8,128)(2,1)} %bitcast.8, bf16[72,8,128]{2,1,0:T(8,128)(2,1)S(1)} %collective-permute-done.refs_1_, bf16[72,8,128]{2,1,0:T(8,128)(2,1)S(1)} %collective-permute-done.1.refs_2_, ...), custom_call_target="tpu_custom_call" | custom-call | tf_op jit(solution)/shard_map/pallas_call | solution.py:551
  14.6 1.6 %collective-permute-start.5 = (bf16[11,8,128]{2,1,0:T(8,128)(2,1)S(1)}, bf16[11,8,128]{2,1,0:T(8,128)(2,1)S(1)}, u32[]{:S(2)}, u32[]{:S(2)}) collective-permute-start(bf16[11,8,128]{2,1,0:T(8,128)(2,1)S(1)} %get-tuple-element.16), channel_id=1, source_target_pairs={{0,16},{16,0},{1,17},{17,1},{2,18},{18,2},{3,19},{19,3},{4,20},{20... | collective-permute-start | bytes 67592 | tf_op jit(solution)/shard_map/ppermute | solution.py:533
  16.2 2.3 %collective-permute-done.5.refs_2_ = bf16[11,8,128]{2,1,0:T(8,128)(2,1)S(1)} collective-permute-done((bf16[11,8,128]{2,1,0:T(8,128)(2,1)S(1)}, bf16[11,8,128]{2,1,0:T(8,128)(2,1)S(1)}, u32[]{:S(2)}, u32[]{:S(2)}) %collective-permute-start.5) | collective-permute-done | bytes 22560 | tf_op jit(solution)/shard_map/ppermute | solution.py:533
  18.5 0.3 shard_map.142
  18.8 3.5 %collective-permute-start.6 = (bf16[65,8,128]{2,1,0:T(8,128)(2,1)S(1)}, bf16[65,8,128]{2,1,0:T(8,128)(2,1)S(1)}, u32[]{:S(2)}, u32[]{:S(2)}) collective-permute-start(bf16[65,8,128]{2,1,0:T(8,128)(2,1)S(1)} %get-tuple-element.18), channel_id=1, source_target_pairs={{0,4},{4,0},{8,12},{12,8},{5,9},{9,5},{2,6},{6,2},{10,14},{14,10},... | collective-permute-start | bytes 399368 | tf_op jit(solution)/shard_map/ppermute | solution.py:654
  22.3 1.9 %collective-permute-start.7 = (bf16[65,8,128]{2,1,0:T(8,128)(2,1)S(1)}, bf16[65,8,128]{2,1,0:T(8,128)(2,1)S(1)}, u32[]{:S(2)}, u32[]{:S(2)}) collective-permute-start(bf16[65,8,128]{2,1,0:T(8,128)(2,1)S(1)} %get-tuple-element.19), channel_id=1, source_target_pairs={{4,8},{8,4},{1,5},{5,1},{9,13},{13,9},{6,10},{10,6},{3,7},{7,3},{1... | collective-permute-start | bytes 399368 | tf_op jit(solution)/shard_map/ppermute | solution.py:655
  24.2 1.5 %collective-permute-done.6.refs_3_ = bf16[65,8,128]{2,1,0:T(8,128)(2,1)S(1)} collective-permute-done((bf16[65,8,128]{2,1,0:T(8,128)(2,1)S(1)}, bf16[65,8,128]{2,1,0:T(8,128)(2,1)S(1)}, u32[]{:S(2)}, u32[]{:S(2)}) %collective-permute-start.6) | collective-permute-done | bytes 133152 | tf_op jit(solution)/shard_map/ppermute | solution.py:654
  25.7 3.5 %collective-permute-done.7.refs_4_ = bf16[65,8,128]{2,1,0:T(8,128)(2,1)S(1)} collective-permute-done((bf16[65,8,128]{2,1,0:T(8,128)(2,1)S(1)}, bf16[65,8,128]{2,1,0:T(8,128)(2,1)S(1)}, u32[]{:S(2)}, u32[]{:S(2)}) %collective-permute-start.7) | collective-permute-done | bytes 133152 | tf_op jit(solution)/shard_map/ppermute | solution.py:655
  29.2 2.3 %shard_map.143 = (f32[9,8,8,128]{3,2,1,0:T(8,128)}, f32[8,8,128]{2,1,0:T(8,128)}, f32[8,8,128]{2,1,0:T(8,128)}, f32[9,13,16,128]{3,2,1,0:T(8,128)S(1)}, f32[14,13,16,128]{3,2,1,0:T(8,128)S(1)}) custom-call(f32[9,13,16,128]{3,2,1,0:T(8,128)S(1)} %get-tuple-element.15.refs_0_, ...), custom_call_target="tpu_custom_call", output_to_operand_aliasing={{3}: (0, {}), {4}: (1, {})} | custom-call | tf_op jit(solution)/shard_map/pallas_call | solution.py:551
  (1 shorter events, 0.0 us)
Async XLA Ops:
  0.6 5.9 %collective-permute-start.1 = (bf16[72,8,128]{2,1,0:T(8,128)(2,1)}, bf16[72,8,128]{2,1,0:T(8,128)(2,1)S(1)}, u32[]{:S(2)}, u32[]{:S(2)}) collective-permute-start(bf16[72,8,128]{2,1,0:T(8,128)(2,1)} %bitcast.6), channel_id=1, source_target_pairs={{0,2},{1,3},{2,0},{3,1},{4,6},{5,7},{6,4},{7,5},{8,10},{9,11},{10,... | collective-permute-start | bytes 442376 | tf_op jit(solution)/shard_map/ppermute | solution.py:595
  2.5 4.0 %collective-permute-start.3 = (bf16[70,8,128]{2,1,0:T(8,128)(2,1)S(1)}, bf16[70,8,128]{2,1,0:T(8,128)(2,1)S(1)}, u32[]{:S(2)}, u32[]{:S(2)}) collective-permute-start(bf16[70,8,128]{2,1,0:T(8,128)(2,1)S(1)} %get-tuple-element.13), channel_id=1, source_target_pairs={{0,1},{1,0},{2,3},{3,2},{4,5},{5,4},{6,7},{7,6},{8,9},{9,8},{10,11... | collective-permute-start | bytes 430088 | tf_op jit(solution)/shard_map/ppermute | solution.py:611
  2.6 10.6 %collective-permute-start = (bf16[72,8,128]{2,1,0:T(8,128)(2,1)}, bf16[72,8,128]{2,1,0:T(8,128)(2,1)S(1)}, u32[]{:S(2)}, u32[]{:S(2)}) collective-permute-start(bf16[72,8,128]{2,1,0:T(8,128)(2,1)} %bitcast.7), channel_id=1, source_target_pairs={{0,1},{1,0},{2,3},{3,2},{4,5},{5,4},{6,7},{7,6},{8,9},{9,8},{10,11... | collective-permute-start | bytes 442376 | tf_op jit(solution)/shard_map/ppermute | solution.py:596
  6.5 6.7 %collective-permute-start.2 = (bf16[72,8,128]{2,1,0:T(8,128)(2,1)S(1)}, bf16[72,8,128]{2,1,0:T(8,128)(2,1)S(1)}, u32[]{:S(2)}, u32[]{:S(2)}) collective-permute-start(bf16[72,8,128]{2,1,0:T(8,128)(2,1)S(1)} %collective-permute-done.1.refs_2_), channel_id=1, source_target_pairs={{0,1},{1,0},{2,3},{3,2},{4,5},{5,4},{6,7},{7,6},{8,9},{9,8},{10,11... | collective-permute-start | bytes 442376 | tf_op jit(solution)/shard_map/ppermute | solution.py:613
  6.5 6.2 %collective-permute-start.4 = (bf16[35,8,128]{2,1,0:T(8,128)(2,1)S(1)}, bf16[35,8,128]{2,1,0:T(8,128)(2,1)S(1)}, u32[]{:S(2)}, u32[]{:S(2)}) collective-permute-start(bf16[35,8,128]{2,1,0:T(8,128)(2,1)S(1)} %slice.4), channel_id=1, source_target_pairs={{0,2},{3,1},{4,6},{7,5},{8,10},{11,9},{12,14},{15,13},{16,18},{19,... | collective-permute-start | bytes 215048 | tf_op jit(solution)/shard_map/ppermute | solution.py:612
  14.6 3.9 %collective-permute-start.5 = (bf16[11,8,128]{2,1,0:T(8,128)(2,1)S(1)}, bf16[11,8,128]{2,1,0:T(8,128)(2,1)S(1)}, u32[]{:S(2)}, u32[]{:S(2)}) collective-permute-start(bf16[11,8,128]{2,1,0:T(8,128)(2,1)S(1)} %get-tuple-element.16), channel_id=1, source_target_pairs={{0,16},{16,0},{1,17},{17,1},{2,18},{18,2},{3,19},{19,3},{4,20},{20... | collective-permute-start | bytes 67592 | tf_op jit(solution)/shard_map/ppermute | solution.py:533
  18.8 6.9 %collective-permute-start.6 = (bf16[65,8,128]{2,1,0:T(8,128)(2,1)S(1)}, bf16[65,8,128]{2,1,0:T(8,128)(2,1)S(1)}, u32[]{:S(2)}, u32[]{:S(2)}) collective-permute-start(bf16[65,8,128]{2,1,0:T(8,128)(2,1)S(1)} %get-tuple-element.18), channel_id=1, source_target_pairs={{0,4},{4,0},{8,12},{12,8},{5,9},{9,5},{2,6},{6,2},{10,14},{14,10},... | collective-permute-start | bytes 399368 | tf_op jit(solution)/shard_map/ppermute | solution.py:654
  22.3 6.9 %collective-permute-start.7 = (bf16[65,8,128]{2,1,0:T(8,128)(2,1)S(1)}, bf16[65,8,128]{2,1,0:T(8,128)(2,1)S(1)}, u32[]{:S(2)}, u32[]{:S(2)}) collective-permute-start(bf16[65,8,128]{2,1,0:T(8,128)(2,1)S(1)} %get-tuple-element.19), channel_id=1, source_target_pairs={{4,8},{8,4},{1,5},{5,1},{9,13},{13,9},{6,10},{10,6},{3,7},{7,3},{1... | collective-permute-start | bytes 399368 | tf_op jit(solution)/shard_map/ppermute | solution.py:655

commit v4 on v3

--- a/solution.py
+++ b/solution.py
@@ -105,6 +105,11 @@
     return jnp.full(shape, lax.rem(total, 2), jnp.int32) == 0
 
 
+def has_neighbours(axis):
+    index = lax.axis_index(axis)
+    return (index > 0).astype(jnp.float32), (index < lax.axis_size(axis) - 1).astype(jnp.float32)
+
+
 def copies(sems, *pairs):
     out = [pltpu.make_async_copy(source, target, sems.at[i]) for i, (source, target) in enumerate(pairs)]
     for copy in out:
@@ -132,6 +137,7 @@
 
 def unpack_rows(cz, cy, from_a, from_b, packed, put_row):
     narrow, wide = row_counts(cz, cy)
+    has_lower, has_upper = has_neighbours("gy")
     even = even_mask(("gy", "gz"), packed.shape[2:])
     for t in range(narrow + wide):
         got = []
@@ -142,8 +148,8 @@
                 got.append(ref[t].astype(jnp.float32))
             else:
                 got.append(joined(ref[t], ref[wide + t]))
-        packed[0, t] = jnp.where(even, got[1], got[0])
-        packed[1, t] = jnp.where(even, got[0], got[1])
+        packed[0, t] = jnp.where(even, got[1], got[0]) * has_lower
+        packed[1, t] = jnp.where(even, got[0], got[1]) * has_upper
     for side, up in enumerate((True, False)):
         for base, listed in zip((0, narrow), y_rows(cz, cy, up)):
             for r, (f, z, _, y) in enumerate(listed):
@@ -151,18 +157,20 @@
 
 
 def start_kernel(
-    cz, adjoint, lam, mu, buoy, source, wavelet, receiver, traces, plan,
-    out, own, cells, samples, spots, wave, steps, sems,
+    cz, store, adjoint, lam, mu, buoy, source, wavelet, receiver, traces, plan,
+    near_out, far_out, own, cells, samples, spots, wave, steps, sems,
 ):
     cy, lanes = own.shape[2], own.shape[3]
     rows = cz * cy
+    tiles = store.shape[0]
     small = copies(sems, (plan, steps), (wavelet, wave), (source, spots), (receiver, cells), (traces, samples))
     large = copies(
-        sems.at[pl.ds(len(small), 4)],
+        sems.at[pl.ds(len(small), 5)],
         (adjoint, own.at[pl.ds(0, 9)]),
         (buoy, own.at[BUOY - ADJ]),
         (lam, own.at[LAM - ADJ]),
         (mu, own.at[MU - ADJ]),
+        (store, near_out.at[pl.ds(0, tiles)]),
     )
     for copy in small:
         copy.wait()
@@ -202,15 +210,19 @@
     def tile(side, i):
         return own[side[i][0] - ADJ, side[i][1]] if i < len(side) else zero
 
-    face = 2 * near + far
     for i in range(near):
         above, below = tile(up[0], i), tile(down[0], i)
-        for base, value in ((0, jnp.where(even, above, below)), (face, jnp.where(even, below, above))):
+        for out, base, value in (
+            (near_out, tiles, jnp.where(even, above, below)),
+            (far_out, 0, jnp.where(even, below, above)),
+        ):
             out[base + i], out[base + near + i] = split(value)
     for i in range(far):
         above, below = tile(up[1], i), tile(down[1], i)
-        out[2 * near + i] = jnp.where(even, above, below).astype(jnp.bfloat16)
-        out[face + 2 * near + i] = jnp.where(even, below, above).astype(jnp.bfloat16)
+        near_out[tiles + 2 * near + i] = jnp.where(even, above, below).astype(jnp.bfloat16)
+        far_out[2 * near + i] = jnp.where(even, below, above).astype(jnp.bfloat16)
+    for i in range(2 * near + far, far_out.shape[0]):
+        far_out[i] = zero.astype(jnp.bfloat16)
 
 
 def strip_of(main, layers):
@@ -227,12 +239,13 @@
     return tile
 
 
-def halo_kernel(cz, core, far, own, ring):
+def halo_kernel(cz, tiles, core, far, own, ring):
     cy, lanes = own.shape[2], own.shape[3]
     layers = cz + 2 * HALO
     ring_rows = ring.shape[2]
     near, _ = face_counts(cz)
     even = even_mask("gz", (cy, lanes))
+    has_below, has_above = has_neighbours("gz")
     zero = jnp.zeros((cy, lanes), jnp.float32)
     for f in range(ring.shape[0]):
         for z in range(cz):
@@ -242,13 +255,13 @@
         for depth, listed in enumerate(faces(cz, up)):
             for i, (f, _, z) in enumerate(listed):
                 values = []
-                for ref in (core, far):
+                for ref, base in ((core, tiles), (far, 0)):
                     if depth == 0:
-                        values.append(joined(ref[i], ref[near + i]))
+                        values.append(joined(ref[base + i], ref[base + near + i]))
                     else:
-                        values.append(ref[2 * near + i].astype(jnp.float32))
+                        values.append(ref[base + 2 * near + i].astype(jnp.float32))
                 value = jnp.where(even, values[1], values[0]) if up else jnp.where(even, values[0], values[1])
-                ring[f - ADJ, z, 0:cy, :] = value
+                ring[f - ADJ, z, 0:cy, :] = value * (has_below if up else has_above)
                 filled.add((f - ADJ, z))
     for f in range(ring.shape[0]):
         for z in (0, 1, layers - 2, layers - 1):
@@ -273,7 +286,7 @@
         (peer, peers),
         (slot, slots),
         (store, stores.at[me]),
-        (core, stores.at[me ^ 1]),
+        (core.at[pl.ds(0, tiles)], stores.at[me ^ 1]),
         (chip, stores.at[me ^ 2]),
         (both, stores.at[me ^ 3]),
     )
@@ -284,8 +297,7 @@
     for move in moves:
         move.wait()
     below, above = jnp.maximum(me - 1, 0), jnp.minimum(me + 1, count - 1)
-    has_below = (me > 0).astype(jnp.float32)
-    has_above = (me < count - 1).astype(jnp.float32)
+    has_below, has_above = has_neighbours("gz")
     for z in range(layers):
         if z < HALO:
             brick, piece, keep = below, cz - HALO + z, has_below
@@ -335,6 +347,7 @@
     strip += [ring_w[f, layers, 0:cy, :] for f in range(ring_w.shape[0])]
     position = lax.broadcasted_iota(jnp.int32, (cy, lanes), 1) % 8
     even_x = even_mask("gx", (cy, lanes))
+    has_left, has_right = has_neighbours("gx")
     zero = jnp.zeros((cy, lanes), jnp.float32)
     place = 0
     for fields, narrow in ((range(ADJ), True), (range(ADJ, FIELDS), False)):
@@ -348,7 +361,8 @@
                     got.append(ref[place + i].astype(jnp.float32))
                 else:
                     got.append(joined(ref[place + i], ref[place + len(quads) + i]))
-            right, left = jnp.where(even_x, got[0], got[1]), jnp.where(even_x, got[1], got[0])
+            right = jnp.where(even_x, got[0], got[1]) * has_right
+            left = jnp.where(even_x, got[1], got[0]) * has_left
             for g, f in enumerate(quad):
                 tile = jnp.where(position // 2 == 1, pltpu.roll(right, (2 - 2 * g) % lanes, 1), strip[f])
                 strips[f] = jnp.where(position // 2 == 2, pltpu.roll(left, (4 - 2 * g) % lanes, 1), tile)
@@ -525,7 +539,8 @@
 
 
 def swap_pairs(count, first):
-    return [(i + d, i + 1 - d) for i in range(first, count - 1, 2) for d in (0, 1)]
+    pairs = [(i + d, i + 1 - d) for i in range(first, count - 1, 2) for d in (0, 1)]
+    return pairs + [(i, i) for i in range(count) if i not in dict(pairs)]
 
 
 def swapped(value_a, value_b, axis):
@@ -593,28 +608,27 @@
 
     wide_x = lax.axis_size("gx") > 2
     chip = lax.ppermute(store, "gz", [(i, i ^ 2) for i in range(holders)])
-    core = lax.ppermute(store, "gz", [(i, i ^ 1) for i in range(holders)])
-    to_core, own = kernel_call(
+    to_core, to_far, own = kernel_call(
         functools.partial(start_kernel, cz),
-        (adjoint_state, lame_lambda, lame_mu, buoyancy, source, wavelet, receiver, traces, plan),
-        [hbm()] * 9,
-        (shape(2 * face, cy, cx, dtype=bf16), shape(15, cz, cy, cx)),
+        (store, adjoint_state, lame_lambda, lame_mu, buoyancy, source, wavelet, receiver, traces, plan),
+        [hbm()] * 10,
+        (shape(tiles + face, cy, cx, dtype=bf16), shape(tiles + 4, cy, cx, dtype=bf16), shape(15, cz, cy, cx)),
         [
             pltpu.VMEM(receiver.shape, jnp.int32),
             pltpu.VMEM(traces.shape, f32),
             pltpu.SMEM(source.shape, jnp.int32),
             pltpu.SMEM(wavelet.shape, f32),
             pltpu.SMEM(plan.shape, jnp.int32),
-            pltpu.SemaphoreType.DMA((9,)),
+            pltpu.SemaphoreType.DMA((10,)),
         ],
     )
-    core_faces = lax.ppermute(to_core, "gz", [(i, i ^ 1) for i in range(holders)])
-    far_face = lax.ppermute(core_faces[face:], "gz", [(0, 2), (3, 1)])
+    core = lax.ppermute(to_core, "gz", [(i, i ^ 1) for i in range(holders)])
+    far_face = lax.ppermute(to_far, "gz", swap_pairs(holders, 1))
     both = lax.ppermute(chip, "gz", [(i, i ^ 1) for i in range(holders)])
 
     (ring_w,) = kernel_call(
-        functools.partial(halo_kernel, cz),
-        (core_faces, far_face, own),
+        functools.partial(halo_kernel, cz, tiles),
+        (core, far_face, own),
         [vmem()] * 3,
         (shape(FIELDS - ADJ, layers + 1, 2 * cy, cx),),
     )

time: 31.7 us -> 28.1 us (0.89)
  the two profiles are of different devices: /device:TPU:18 before, /device:TPU:22 now
where the time goes in v4:
time: 28.1 us; the launch traced here: 27.9 us
  waiting for transfers between devices  11.3 us (40%)
  starting transfers between devices  10.1 us (36%)
  Pallas kernels  5.7 us (20%)
  between operations  0.7 us (2%)
    pallas_call x5, Pallas kernels, kernel_call(): pl.pallas_call(run, out_shape=tuple((o for o in out_shape if o is not Non...  5.7 us
    ppermute x1, waiting for transfers between devices, on_device(): from_b = lax.ppermute(y_b, ('gy', 'gz'), turns[1])  3.49 us
    ppermute x1, starting transfers between devices, on_device(): far_face = lax.ppermute(to_far, 'gz', swap_pairs(holders, 1))  3.49 us
    ppermute x1, starting transfers between devices, on_device(): from_a = lax.ppermute(y_a, ('gy', 'gz'), turns[0])  3.48 us
    ppermute x1, waiting for transfers between devices, swapped(): got_a = lax.ppermute(value_a, axis, swap_pairs(count, 0))  3.3 us
    ppermute x1, waiting for transfers between devices, on_device(): far_face = lax.ppermute(to_far, 'gz', swap_pairs(holders, 1))  2.65 us
    ppermute x1, starting transfers between devices, on_device(): from_b = lax.ppermute(y_b, ('gy', 'gz'), turns[1])  1.92 us
    ppermute x1, waiting for transfers between devices, on_device(): from_a = lax.ppermute(y_a, ('gy', 'gz'), turns[0])  1.46 us
  transfers between devices with their start and end apart: 7, of which 5 were waited for; matrix products, arithmetic and copies ran while one was open for 0% of the time, Pallas kernels for 6%

profile of v4, /device:TPU:22, one launch (start us, length us, event | category | flops | bytes accessed | tf_op | source)
XLA Modules:
  0.0 27.9 jit_solution(16076725292826341214)
XLA Ops:
  0.6 0.6 %collective-permute-start.1 = (bf16[72,8,128]{2,1,0:T(8,128)(2,1)}, bf16[72,8,128]{2,1,0:T(8,128)(2,1)S(1)}, u32[]{:S(2)}, u32[]{:S(2)}) collective-permute-start(bf16[72,8,128]{2,1,0:T(8,128)(2,1)} %bitcast.6), channel_id=1, source_target_pairs={{0,2},{1,3},{2,0},{3,1},{4,6},{5,7},{6,4},{7,5},{8,10},{9,11},{10,... | collective-permute-start | bytes 442376 | tf_op jit(solution)/shard_map/ppermute | solution.py:610
  1.2 1.3 %shard_map.139 = (bf16[107,8,128]{2,1,0:T(8,128)(2,1)S(1)}, bf16[76,8,128]{2,1,0:T(8,128)(2,1)S(1)}, f32[15,8,8,128]{3,2,1,0:T(8,128)S(1)}) custom-call(bf16[72,8,128]{2,1,0:T(8,128)(2,1)} %bitcast.7, f32[9,8,8,128]{3,2,1,0:T(8,128)} %refs_1_.1, f32[8,8,128]{2,1,0:T(8,128)} %refs_2_.1, f32[8,8,128]{2,1,0:T(8,128)} %refs_3_.1, f32[8,8,128]{2,1,0:T(8,128)} %refs_4_.1, ...), custom_call_target="tpu_custom_call" | custom-call | tf_op jit(solution)/shard_map/pallas_call | solution.py:566
  2.5 0.1 collective-permute-start
  2.6 3.5 %collective-permute-start.3 = (bf16[76,8,128]{2,1,0:T(8,128)(2,1)S(1)}, bf16[76,8,128]{2,1,0:T(8,128)(2,1)S(1)}, u32[]{:S(2)}, u32[]{:S(2)}) collective-permute-start(bf16[76,8,128]{2,1,0:T(8,128)(2,1)S(1)} %get-tuple-element.15), channel_id=1, source_target_pairs={{1,2},{2,1},{0,0},{3,3},{5,6},{6,5},{4,4},{7,7},{9,10},{10,9},{8,8... | collective-permute-start | bytes 466952 | tf_op jit(solution)/shard_map/ppermute | solution.py:626
  6.1 0.4 %collective-permute-done.1.refs_2_ = bf16[72,8,128]{2,1,0:T(8,128)(2,1)S(1)} collective-permute-done((bf16[72,8,128]{2,1,0:T(8,128)(2,1)}, bf16[72,8,128]{2,1,0:T(8,128)(2,1)S(1)}, u32[]{:S(2)}, u32[]{:S(2)}) %collective-permute-start.1) | collective-permute-done | bytes 147488 | tf_op jit(solution)/shard_map/ppermute | solution.py:610
  6.5 0.0 collective-permute-start.2
  6.5 2.6 %collective-permute-done.3.refs_1_ = bf16[76,8,128]{2,1,0:T(8,128)(2,1)S(1)} collective-permute-done((bf16[76,8,128]{2,1,0:T(8,128)(2,1)S(1)}, bf16[76,8,128]{2,1,0:T(8,128)(2,1)S(1)}, u32[]{:S(2)}, u32[]{:S(2)}) %collective-permute-start.3) | collective-permute-done | bytes 155680 | tf_op jit(solution)/shard_map/ppermute | solution.py:626
  9.1 0.0 collective-permute-done.refs_0_.refs_1_
  9.2 0.4 %shard_map.140.refs_6_.refs_1_ = f32[14,13,16,128]{3,2,1,0:T(8,128)S(1)} custom-call(bf16[107,8,128]{2,1,0:T(8,128)(2,1)S(1)} %collective-permute-done.refs_0_.refs_1_, bf16[76,8,128]{2,1,0:T(8,128)(2,1)S(1)} %collective-permute-done.3.refs_1_, f32[15,8,8,128]{3,2,1,0:T(8,128)S(1)} %get-tuple-element.16.refs_2_.refs_5_), custom_call_target="tpu_custom_call" | custom-call | tf_op jit(solution)/shard_map/pallas_call | solution.py:566
  9.6 0.0 collective-permute-done.2.refs_3_
  9.6 1.4 %shard_map.141 = (f32[9,13,16,128]{3,2,1,0:T(8,128)S(1)}, bf16[11,8,128]{2,1,0:T(8,128)(2,1)S(1)}) custom-call(bf16[72,8,128]{2,1,0:T(8,128)(2,1)} %bitcast.8, bf16[107,8,128]{2,1,0:T(8,128)(2,1)S(1)} %collective-permute-done.refs_0_.refs_1_, bf16[72,8,128]{2,1,0:T(8,128)(2,1)S(1)} %collective-permute-done.1.refs_2_, ...), custom_call_target="tpu_custom_call" | custom-call | tf_op jit(solution)/shard_map/pallas_call | solution.py:566
  11.0 0.6 %collective-permute-start.4 = (bf16[11,8,128]{2,1,0:T(8,128)(2,1)S(1)}, bf16[11,8,128]{2,1,0:T(8,128)(2,1)S(1)}, u32[]{:S(2)}, u32[]{:S(2)}) collective-permute-start(bf16[11,8,128]{2,1,0:T(8,128)(2,1)S(1)} %get-tuple-element.18), channel_id=1, source_target_pairs={{0,16},{16,0},{1,17},{17,1},{2,18},{18,2},{3,19},{19,3},{4,20},{20... | collective-permute-start | bytes 67592 | tf_op jit(solution)/shard_map/ppermute | solution.py:548
  11.6 3.3 %collective-permute-done.4.refs_2_ = bf16[11,8,128]{2,1,0:T(8,128)(2,1)S(1)} collective-permute-done((bf16[11,8,128]{2,1,0:T(8,128)(2,1)S(1)}, bf16[11,8,128]{2,1,0:T(8,128)(2,1)S(1)}, u32[]{:S(2)}, u32[]{:S(2)}) %collective-permute-start.4) | collective-permute-done | bytes 22560 | tf_op jit(solution)/shard_map/ppermute | solution.py:548
  14.9 0.3 %shard_map.142 = (f32[23,8,128]{2,1,0:T(8,128)S(1)}, bf16[65,8,128]{2,1,0:T(8,128)(2,1)S(1)}, bf16[65,8,128]{2,1,0:T(8,128)(2,1)S(1)}) custom-call(f32[9,13,16,128]{3,2,1,0:T(8,128)S(1)} %get-tuple-element.17.refs_0_, f32[14,13,16,128]{3,2,1,0:T(8,128)S(1)} %shard_map.140.refs_6_.refs_1_, bf16[11,8,128]{2,1,0:T(8,128)(2,1)S(1)} %collective-permute-done.4.refs_2_), custom_call_target="tpu_custom_call" | custom-call | tf_op jit(solution)/shard_map/pallas_call | solution.py:566
  15.2 3.5 %collective-permute-start.5 = (bf16[65,8,128]{2,1,0:T(8,128)(2,1)S(1)}, bf16[65,8,128]{2,1,0:T(8,128)(2,1)S(1)}, u32[]{:S(2)}, u32[]{:S(2)}) collective-permute-start(bf16[65,8,128]{2,1,0:T(8,128)(2,1)S(1)} %get-tuple-element.20), channel_id=1, source_target_pairs={{0,4},{4,0},{8,12},{12,8},{5,9},{9,5},{1,1},{13,13},{2,6},{6,2},{1... | collective-permute-start | bytes 399368 | tf_op jit(solution)/shard_map/ppermute | solution.py:668
  18.7 1.9 %collective-permute-start.6 = (bf16[65,8,128]{2,1,0:T(8,128)(2,1)S(1)}, bf16[65,8,128]{2,1,0:T(8,128)(2,1)S(1)}, u32[]{:S(2)}, u32[]{:S(2)}) collective-permute-start(bf16[65,8,128]{2,1,0:T(8,128)(2,1)S(1)} %get-tuple-element.21), channel_id=1, source_target_pairs={{4,8},{8,4},{0,0},{12,12},{1,5},{5,1},{9,13},{13,9},{6,10},{10,6},... | collective-permute-start | bytes 399368 | tf_op jit(solution)/shard_map/ppermute | solution.py:669
  20.6 1.5 %collective-permute-done.5.refs_3_ = bf16[65,8,128]{2,1,0:T(8,128)(2,1)S(1)} collective-permute-done((bf16[65,8,128]{2,1,0:T(8,128)(2,1)S(1)}, bf16[65,8,128]{2,1,0:T(8,128)(2,1)S(1)}, u32[]{:S(2)}, u32[]{:S(2)}) %collective-permute-start.5) | collective-permute-done | bytes 133152 | tf_op jit(solution)/shard_map/ppermute | solution.py:668
  22.1 3.5 %collective-permute-done.6.refs_4_ = bf16[65,8,128]{2,1,0:T(8,128)(2,1)S(1)} collective-permute-done((bf16[65,8,128]{2,1,0:T(8,128)(2,1)S(1)}, bf16[65,8,128]{2,1,0:T(8,128)(2,1)S(1)}, u32[]{:S(2)}, u32[]{:S(2)}) %collective-permute-start.6) | collective-permute-done | bytes 133152 | tf_op jit(solution)/shard_map/ppermute | solution.py:669
  25.5 2.3 %shard_map.143 = (f32[9,8,8,128]{3,2,1,0:T(8,128)}, f32[8,8,128]{2,1,0:T(8,128)}, f32[8,8,128]{2,1,0:T(8,128)}, f32[9,13,16,128]{3,2,1,0:T(8,128)S(1)}, f32[14,13,16,128]{3,2,1,0:T(8,128)S(1)}) custom-call(f32[9,13,16,128]{3,2,1,0:T(8,128)S(1)} %get-tuple-element.17.refs_0_, ...), custom_call_target="tpu_custom_call", output_to_operand_aliasing={{3}: (0, {}), {4}: (1, {})} | custom-call | tf_op jit(solution)/shard_map/pallas_call | solution.py:566
Async XLA Ops:
  0.6 5.9 %collective-permute-start.1 = (bf16[72,8,128]{2,1,0:T(8,128)(2,1)}, bf16[72,8,128]{2,1,0:T(8,128)(2,1)S(1)}, u32[]{:S(2)}, u32[]{:S(2)}) collective-permute-start(bf16[72,8,128]{2,1,0:T(8,128)(2,1)} %bitcast.6), channel_id=1, source_target_pairs={{0,2},{1,3},{2,0},{3,1},{4,6},{5,7},{6,4},{7,5},{8,10},{9,11},{10,... | collective-permute-start | bytes 442376 | tf_op jit(solution)/shard_map/ppermute | solution.py:610
  2.5 6.6 %collective-permute-start = (bf16[107,8,128]{2,1,0:T(8,128)(2,1)S(1)}, bf16[107,8,128]{2,1,0:T(8,128)(2,1)S(1)}, u32[]{:S(2)}, u32[]{:S(2)}) collective-permute-start(bf16[107,8,128]{2,1,0:T(8,128)(2,1)S(1)} %get-tuple-element.14), channel_id=1, source_target_pairs={{0,1},{1,0},{2,3},{3,2},{4,5},{5,4},{6,7},{7,6},{8,9},{9,8},{10,11... | collective-permute-start | bytes 657416 | tf_op jit(solution)/shard_map/ppermute | solution.py:625
  2.6 6.5 %collective-permute-start.3 = (bf16[76,8,128]{2,1,0:T(8,128)(2,1)S(1)}, bf16[76,8,128]{2,1,0:T(8,128)(2,1)S(1)}, u32[]{:S(2)}, u32[]{:S(2)}) collective-permute-start(bf16[76,8,128]{2,1,0:T(8,128)(2,1)S(1)} %get-tuple-element.15), channel_id=1, source_target_pairs={{1,2},{2,1},{0,0},{3,3},{5,6},{6,5},{4,4},{7,7},{9,10},{10,9},{8,8... | collective-permute-start | bytes 466952 | tf_op jit(solution)/shard_map/ppermute | solution.py:626
  6.5 3.1 %collective-permute-start.2 = (bf16[72,8,128]{2,1,0:T(8,128)(2,1)S(1)}, bf16[72,8,128]{2,1,0:T(8,128)(2,1)S(1)}, u32[]{:S(2)}, u32[]{:S(2)}) collective-permute-start(bf16[72,8,128]{2,1,0:T(8,128)(2,1)S(1)} %collective-permute-done.1.refs_2_), channel_id=1, source_target_pairs={{0,1},{1,0},{2,3},{3,2},{4,5},{5,4},{6,7},{7,6},{8,9},{9,8},{10,11... | collective-permute-start | bytes 442376 | tf_op jit(solution)/shard_map/ppermute | solution.py:627
  11.0 3.9 %collective-permute-start.4 = (bf16[11,8,128]{2,1,0:T(8,128)(2,1)S(1)}, bf16[11,8,128]{2,1,0:T(8,128)(2,1)S(1)}, u32[]{:S(2)}, u32[]{:S(2)}) collective-permute-start(bf16[11,8,128]{2,1,0:T(8,128)(2,1)S(1)} %get-tuple-element.18), channel_id=1, source_target_pairs={{0,16},{16,0},{1,17},{17,1},{2,18},{18,2},{3,19},{19,3},{4,20},{20... | collective-permute-start | bytes 67592 | tf_op jit(solution)/shard_map/ppermute | solution.py:548
  15.2 6.9 %collective-permute-start.5 = (bf16[65,8,128]{2,1,0:T(8,128)(2,1)S(1)}, bf16[65,8,128]{2,1,0:T(8,128)(2,1)S(1)}, u32[]{:S(2)}, u32[]{:S(2)}) collective-permute-start(bf16[65,8,128]{2,1,0:T(8,128)(2,1)S(1)} %get-tuple-element.20), channel_id=1, source_target_pairs={{0,4},{4,0},{8,12},{12,8},{5,9},{9,5},{1,1},{13,13},{2,6},{6,2},{1... | collective-permute-start | bytes 399368 | tf_op jit(solution)/shard_map/ppermute | solution.py:668
  18.7 6.9 %collective-permute-start.6 = (bf16[65,8,128]{2,1,0:T(8,128)(2,1)S(1)}, bf16[65,8,128]{2,1,0:T(8,128)(2,1)S(1)}, u32[]{:S(2)}, u32[]{:S(2)}) collective-permute-start(bf16[65,8,128]{2,1,0:T(8,128)(2,1)S(1)} %get-tuple-element.21), channel_id=1, source_target_pairs={{4,8},{8,4},{0,0},{12,12},{1,5},{5,1},{9,13},{13,9},{6,10},{10,6},... | collective-permute-start | bytes 399368 | tf_op jit(solution)/shard_map/ppermute | solution.py:669

commit v5 on v4

--- a/solution.py
+++ b/solution.py
@@ -273,7 +273,7 @@
 
 
 def column_kernel(
-    cz, store, core, chip, both, peer, slot, ring_w, ring, send_a, send_b, stores, peers, slots, sems
+    cz, store, core, chip, both_a, both_b, peer, slot, ring_w, ring, send_a, send_b, stores, peers, slots, sems
 ):
     cy, lanes = core.shape[1], core.shape[2]
     layers = cz + 2 * HALO
@@ -288,7 +288,8 @@
         (store, stores.at[me]),
         (core.at[pl.ds(0, tiles)], stores.at[me ^ 1]),
         (chip, stores.at[me ^ 2]),
-        (both, stores.at[me ^ 3]),
+        (both_a, stores.at[me ^ 3, pl.ds(0, both_a.shape[0])]),
+        (both_b, stores.at[me ^ 3, pl.ds(both_a.shape[0], both_b.shape[0])]),
     )
     zero = jnp.zeros((cy, lanes), jnp.float32)
     for f in range(9):
@@ -602,6 +603,7 @@
     assert holders == 4
     near, far = face_counts(cz)
     face = 2 * near + far
+    half = tiles // 2
 
     def shape(*dims, dtype=f32):
         return jax.ShapeDtypeStruct(dims, dtype)
@@ -612,7 +614,7 @@
         functools.partial(start_kernel, cz),
         (store, adjoint_state, lame_lambda, lame_mu, buoyancy, source, wavelet, receiver, traces, plan),
         [hbm()] * 10,
-        (shape(tiles + face, cy, cx, dtype=bf16), shape(tiles + 4, cy, cx, dtype=bf16), shape(15, cz, cy, cx)),
+        (shape(tiles + face, cy, cx, dtype=bf16), shape(max(face, half) + 4, cy, cx, dtype=bf16), shape(15, cz, cy, cx)),
         [
             pltpu.VMEM(receiver.shape, jnp.int32),
             pltpu.VMEM(traces.shape, f32),
@@ -623,8 +625,8 @@
         ],
     )
     core = lax.ppermute(to_core, "gz", [(i, i ^ 1) for i in range(holders)])
-    far_face = lax.ppermute(to_far, "gz", swap_pairs(holders, 1))
-    both = lax.ppermute(chip, "gz", [(i, i ^ 1) for i in range(holders)])
+    far_face = lax.ppermute(to_far, "gz", [(i, i ^ 3) for i in range(holders)])
+    both = [lax.ppermute(part, "gz", [(i, i ^ 1) for i in range(holders)]) for part in (chip[:half], chip[half:])]
 
     (ring_w,) = kernel_call(
         functools.partial(halo_kernel, cz, tiles),
@@ -635,14 +637,14 @@
     x_send = shape(x_tiles(), cy, cx, dtype=bf16)
     ring_f, x_a, x_b = kernel_call(
         functools.partial(column_kernel, cz),
-        (store, core, chip, both, peer, slot, ring_w),
-        [hbm()] + [vmem()] * 3 + [hbm()] * 2 + [vmem()],
+        (store, core, chip, *both, peer, slot, ring_w),
+        [hbm()] + [vmem()] * 4 + [hbm()] * 2 + [vmem()],
         (shape(ADJ, layers + 1, 2 * cy, cx), x_send, x_send if wide_x else None),
         [
             pltpu.VMEM((holders, tiles, cy, cx), bf16),
             pltpu.SMEM(peer.shape, jnp.int32),
             pltpu.SMEM(slot.shape, jnp.int32),
-            pltpu.SemaphoreType.DMA((6,)),
+            pltpu.SemaphoreType.DMA((7,)),
         ],
     )
     from_a, from_b = swapped(x_a, x_b, "gx")
@@ -657,14 +659,12 @@
         [pltpu.VMEM((2, narrow + wide, 8, cx), f32)],
     )
     gy = lax.axis_size("gy")
-    turns = [
-        [
-            (i * holders + c, j * holders + c)
-            for c in range(holders)
-            for i, j in swap_pairs(gy, (c + turn) % 2)
-        ]
-        for turn in (0, 1)
-    ]
+    turns = [[], []]
+    for turn, pairs in enumerate(turns):
+        for c in range(holders):
+            first = (c + turn) % 2
+            change = dict(swap_pairs(gy, first))
+            pairs.extend((i * holders + c, (i * holders + (c ^ 2)) if j == i else (j * holders + c)) for i, j in change.items())
     from_a = lax.ppermute(y_a, ("gy", "gz"), turns[0])
     from_b = lax.ppermute(y_b, ("gy", "gz"), turns[1])
 

time: 28.1 us -> 24.9 us (0.89)
  the two profiles are of different devices: /device:TPU:22 before, /device:TPU:0 now
where the time goes in v5:
time: 24.9 us; the launch traced here: 24.7 us
  starting transfers between devices  9.13 us (37%)
  waiting for transfers between devices  9.13 us (37%)
  Pallas kernels  5.71 us (23%)
  between operations  0.7 us (3%)
    pallas_call x5, Pallas kernels, kernel_call(): pl.pallas_call(run, out_shape=tuple((o for o in out_shape if o is not Non...  5.71 us
    ppermute x1, starting transfers between devices, on_device(): chip = lax.ppermute(store, 'gz', [(i, i ^ 2) for i in range(holders)])  3 us
    ppermute x1, waiting for transfers between devices, on_device(): chip = lax.ppermute(store, 'gz', [(i, i ^ 2) for i in range(holders)])  2.82 us
    ppermute x1, waiting for transfers between devices, on_device(): from_a = lax.ppermute(y_a, ('gy', 'gz'), turns[0])  2.79 us
    ppermute x1, waiting for transfers between devices, swapped(): got_a = lax.ppermute(value_a, axis, swap_pairs(count, 0))  2.05 us
    ppermute x1, starting transfers between devices, on_device(): from_a = lax.ppermute(y_a, ('gy', 'gz'), turns[0])  1.88 us
    ppermute x1, starting transfers between devices, swapped(): got_a = lax.ppermute(value_a, axis, swap_pairs(count, 0))  1.82 us
    ppermute x1, starting transfers between devices, on_device(): from_b = lax.ppermute(y_b, ('gy', 'gz'), turns[1])  1.66 us
  transfers between devices with their start and end apart: 8, of which 5 were waited for; matrix products, arithmetic and copies ran while one was open for 0% of the time, Pallas kernels for 7%

profile of v5, /device:TPU:0, one launch (start us, length us, event | category | flops | bytes accessed | tf_op | source)
XLA Modules:
  0.0 24.7 jit_solution(10804140625860188566)
XLA Ops:
  0.6 3.0 %collective-permute-start.1 = (bf16[72,8,128]{2,1,0:T(8,128)(2,1)}, bf16[72,8,128]{2,1,0:T(8,128)(2,1)S(1)}, u32[]{:S(2)}, u32[]{:S(2)}) collective-permute-start(bf16[72,8,128]{2,1,0:T(8,128)(2,1)} %bitcast.6), channel_id=1, source_target_pairs={{0,2},{1,3},{2,0},{3,1},{4,6},{5,7},{6,4},{7,5},{8,10},{9,11},{10,... | collective-permute-start | bytes 442376 | tf_op jit(solution)/shard_map/ppermute | solution.py:612
  3.6 1.3 %shard_map.139 = (bf16[107,8,128]{2,1,0:T(8,128)(2,1)S(1)}, bf16[40,8,128]{2,1,0:T(8,128)(2,1)S(1)}, f32[15,8,8,128]{3,2,1,0:T(8,128)S(1)}) custom-call(bf16[72,8,128]{2,1,0:T(8,128)(2,1)} %bitcast.7, f32[9,8,8,128]{3,2,1,0:T(8,128)} %refs_1_.1, f32[8,8,128]{2,1,0:T(8,128)} %refs_2_.1, f32[8,8,128]{2,1,0:T(8,128)} %refs_3_.1, f32[8,8,128]{2,1,0:T(8,128)} %refs_4_.1, ...), custom_call_target="tpu_custom_call" | custom-call | tf_op jit(solution)/shard_map/pallas_call | solution.py:567
  4.9 0.1 collective-permute-start.4
  5.0 0.1 collective-permute-start
  5.1 2.8 %collective-permute-done.1.refs_2_ = bf16[72,8,128]{2,1,0:T(8,128)(2,1)S(1)} collective-permute-done((bf16[72,8,128]{2,1,0:T(8,128)(2,1)}, bf16[72,8,128]{2,1,0:T(8,128)(2,1)S(1)}, u32[]{:S(2)}, u32[]{:S(2)}) %collective-permute-start.1) | collective-permute-done | bytes 147488 | tf_op jit(solution)/shard_map/ppermute | solution.py:612
  8.0 0.1 collective-permute-start.3
  8.0 0.5 %collective-permute-start.2 = (bf16[36,8,128]{2,1,0:T(8,128)(2,1)S(1)}, bf16[36,8,128]{2,1,0:T(8,128)(2,1)S(1)}, u32[]{:S(2)}, u32[]{:S(2)}) collective-permute-start(bf16[36,8,128]{2,1,0:T(8,128)(2,1)S(1)} %get-tuple-element.26), channel_id=1, source_target_pairs={{0,1},{1,0},{2,3},{3,2},{4,5},{5,4},{6,7},{7,6},{8,9},{9,8},{10,11... | collective-permute-start | bytes 221192 | tf_op jit(solution)/shard_map/ppermute | solution.py:629
  8.5 0.9 %collective-permute-done.4.refs_1_ = bf16[40,8,128]{2,1,0:T(8,128)(2,1)S(1)} collective-permute-done((bf16[40,8,128]{2,1,0:T(8,128)(2,1)S(1)}, bf16[40,8,128]{2,1,0:T(8,128)(2,1)S(1)}, u32[]{:S(2)}, u32[]{:S(2)}) %collective-permute-start.4) | collective-permute-done | bytes 81952 | tf_op jit(solution)/shard_map/ppermute | solution.py:628
  9.5 0.0 collective-permute-done.refs_0_.refs_1_
  9.5 0.4 %shard_map.140.refs_7_.refs_1_ = f32[14,13,16,128]{3,2,1,0:T(8,128)S(1)} custom-call(bf16[107,8,128]{2,1,0:T(8,128)(2,1)S(1)} %collective-permute-done.refs_0_.refs_1_, bf16[40,8,128]{2,1,0:T(8,128)(2,1)S(1)} %collective-permute-done.4.refs_1_, f32[15,8,8,128]{3,2,1,0:T(8,128)S(1)} %get-tuple-element.16.refs_2_.refs_5_), custom_call_target="tpu_custom_call" | custom-call | tf_op jit(solution)/shard_map/pallas_call | solution.py:567
  9.9 0.0 collective-permute-done.3.refs_4_
  9.9 0.0 collective-permute-done.2.refs_3_
  9.9 1.4 %shard_map.141 = (f32[9,13,16,128]{3,2,1,0:T(8,128)S(1)}, bf16[11,8,128]{2,1,0:T(8,128)(2,1)S(1)}) custom-call(bf16[72,8,128]{2,1,0:T(8,128)(2,1)} %bitcast.8, bf16[107,8,128]{2,1,0:T(8,128)(2,1)S(1)} %collective-permute-done.refs_0_.refs_1_, bf16[72,8,128]{2,1,0:T(8,128)(2,1)S(1)} %collective-permute-done.1.refs_2_, ...), custom_call_target="tpu_custom_call" | custom-call | tf_op jit(solution)/shard_map/pallas_call | solution.py:567
  11.3 1.8 %collective-permute-start.5 = (bf16[11,8,128]{2,1,0:T(8,128)(2,1)S(1)}, bf16[11,8,128]{2,1,0:T(8,128)(2,1)S(1)}, u32[]{:S(2)}, u32[]{:S(2)}) collective-permute-start(bf16[11,8,128]{2,1,0:T(8,128)(2,1)S(1)} %get-tuple-element.18), channel_id=1, source_target_pairs={{0,16},{16,0},{1,17},{17,1},{2,18},{18,2},{3,19},{19,3},{4,20},{20... | collective-permute-start | bytes 67592 | tf_op jit(solution)/shard_map/ppermute | solution.py:549
  13.2 2.0 %collective-permute-done.5.refs_2_ = bf16[11,8,128]{2,1,0:T(8,128)(2,1)S(1)} collective-permute-done((bf16[11,8,128]{2,1,0:T(8,128)(2,1)S(1)}, bf16[11,8,128]{2,1,0:T(8,128)(2,1)S(1)}, u32[]{:S(2)}, u32[]{:S(2)}) %collective-permute-start.5) | collective-permute-done | bytes 22560 | tf_op jit(solution)/shard_map/ppermute | solution.py:549
  15.2 0.3 %shard_map.142 = (f32[23,8,128]{2,1,0:T(8,128)S(1)}, bf16[65,8,128]{2,1,0:T(8,128)(2,1)S(1)}, bf16[65,8,128]{2,1,0:T(8,128)(2,1)S(1)}) custom-call(f32[9,13,16,128]{3,2,1,0:T(8,128)S(1)} %get-tuple-element.17.refs_0_, f32[14,13,16,128]{3,2,1,0:T(8,128)S(1)} %shard_map.140.refs_7_.refs_1_, bf16[11,8,128]{2,1,0:T(8,128)(2,1)S(1)} %collective-permute-done.5.refs_2_), custom_call_target="tpu_custom_call" | custom-call | tf_op jit(solution)/shard_map/pallas_call | solution.py:567
  15.5 1.9 %collective-permute-start.6 = (bf16[65,8,128]{2,1,0:T(8,128)(2,1)S(1)}, bf16[65,8,128]{2,1,0:T(8,128)(2,1)S(1)}, u32[]{:S(2)}, u32[]{:S(2)}) collective-permute-start(bf16[65,8,128]{2,1,0:T(8,128)(2,1)S(1)} %get-tuple-element.20), channel_id=1, source_target_pairs={{0,4},{4,0},{8,12},{12,8},{5,9},{9,5},{1,3},{13,15},{2,6},{6,2},{1... | collective-permute-start | bytes 399368 | tf_op jit(solution)/shard_map/ppermute | solution.py:668
  17.4 1.7 %collective-permute-start.7 = (bf16[65,8,128]{2,1,0:T(8,128)(2,1)S(1)}, bf16[65,8,128]{2,1,0:T(8,128)(2,1)S(1)}, u32[]{:S(2)}, u32[]{:S(2)}) collective-permute-start(bf16[65,8,128]{2,1,0:T(8,128)(2,1)S(1)} %get-tuple-element.21), channel_id=1, source_target_pairs={{4,8},{8,4},{0,2},{12,14},{1,5},{5,1},{9,13},{13,9},{6,10},{10,6},... | collective-permute-start | bytes 399368 | tf_op jit(solution)/shard_map/ppermute | solution.py:669
  19.0 2.8 %collective-permute-done.6.refs_3_ = bf16[65,8,128]{2,1,0:T(8,128)(2,1)S(1)} collective-permute-done((bf16[65,8,128]{2,1,0:T(8,128)(2,1)S(1)}, bf16[65,8,128]{2,1,0:T(8,128)(2,1)S(1)}, u32[]{:S(2)}, u32[]{:S(2)}) %collective-permute-start.6) | collective-permute-done | bytes 133152 | tf_op jit(solution)/shard_map/ppermute | solution.py:668
  21.8 0.5 %collective-permute-done.7.refs_4_ = bf16[65,8,128]{2,1,0:T(8,128)(2,1)S(1)} collective-permute-done((bf16[65,8,128]{2,1,0:T(8,128)(2,1)S(1)}, bf16[65,8,128]{2,1,0:T(8,128)(2,1)S(1)}, u32[]{:S(2)}, u32[]{:S(2)}) %collective-permute-start.7) | collective-permute-done | bytes 133152 | tf_op jit(solution)/shard_map/ppermute | solution.py:669
  22.4 2.3 %shard_map.143 = (f32[9,8,8,128]{3,2,1,0:T(8,128)}, f32[8,8,128]{2,1,0:T(8,128)}, f32[8,8,128]{2,1,0:T(8,128)}, f32[9,13,16,128]{3,2,1,0:T(8,128)S(1)}, f32[14,13,16,128]{3,2,1,0:T(8,128)S(1)}) custom-call(f32[9,13,16,128]{3,2,1,0:T(8,128)S(1)} %get-tuple-element.17.refs_0_, ...), custom_call_target="tpu_custom_call", output_to_operand_aliasing={{3}: (0, {}), {4}: (1, {})} | custom-call | tf_op jit(solution)/shard_map/pallas_call | solution.py:567
  (1 shorter events, 0.0 us)
Async XLA Ops:
  0.6 7.3 %collective-permute-start.1 = (bf16[72,8,128]{2,1,0:T(8,128)(2,1)}, bf16[72,8,128]{2,1,0:T(8,128)(2,1)S(1)}, u32[]{:S(2)}, u32[]{:S(2)}) collective-permute-start(bf16[72,8,128]{2,1,0:T(8,128)(2,1)} %bitcast.6), channel_id=1, source_target_pairs={{0,2},{1,3},{2,0},{3,1},{4,6},{5,7},{6,4},{7,5},{8,10},{9,11},{10,... | collective-permute-start | bytes 442376 | tf_op jit(solution)/shard_map/ppermute | solution.py:612
  4.9 4.5 %collective-permute-start.4 = (bf16[40,8,128]{2,1,0:T(8,128)(2,1)S(1)}, bf16[40,8,128]{2,1,0:T(8,128)(2,1)S(1)}, u32[]{:S(2)}, u32[]{:S(2)}) collective-permute-start(bf16[40,8,128]{2,1,0:T(8,128)(2,1)S(1)} %get-tuple-element.15), channel_id=1, source_target_pairs={{0,3},{1,2},{2,1},{3,0},{4,7},{5,6},{6,5},{7,4},{8,11},{9,10},{10,... | collective-permute-start | bytes 245768 | tf_op jit(solution)/shard_map/ppermute | solution.py:628
  5.0 4.5 %collective-permute-start = (bf16[107,8,128]{2,1,0:T(8,128)(2,1)S(1)}, bf16[107,8,128]{2,1,0:T(8,128)(2,1)S(1)}, u32[]{:S(2)}, u32[]{:S(2)}) collective-permute-start(bf16[107,8,128]{2,1,0:T(8,128)(2,1)S(1)} %get-tuple-element.14), channel_id=1, source_target_pairs={{0,1},{1,0},{2,3},{3,2},{4,5},{5,4},{6,7},{7,6},{8,9},{9,8},{10,11... | collective-permute-start | bytes 657416 | tf_op jit(solution)/shard_map/ppermute | solution.py:627
  8.0 1.9 %collective-permute-start.3 = (bf16[36,8,128]{2,1,0:T(8,128)(2,1)S(1)}, bf16[36,8,128]{2,1,0:T(8,128)(2,1)S(1)}, u32[]{:S(2)}, u32[]{:S(2)}) collective-permute-start(bf16[36,8,128]{2,1,0:T(8,128)(2,1)S(1)} %get-tuple-element.25), channel_id=1, source_target_pairs={{0,1},{1,0},{2,3},{3,2},{4,5},{5,4},{6,7},{7,6},{8,9},{9,8},{10,11... | collective-permute-start | bytes 221192 | tf_op jit(solution)/shard_map/ppermute | solution.py:629
  8.0 1.9 %collective-permute-start.2 = (bf16[36,8,128]{2,1,0:T(8,128)(2,1)S(1)}, bf16[36,8,128]{2,1,0:T(8,128)(2,1)S(1)}, u32[]{:S(2)}, u32[]{:S(2)}) collective-permute-start(bf16[36,8,128]{2,1,0:T(8,128)(2,1)S(1)} %get-tuple-element.26), channel_id=1, source_target_pairs={{0,1},{1,0},{2,3},{3,2},{4,5},{5,4},{6,7},{7,6},{8,9},{9,8},{10,11... | collective-permute-start | bytes 221192 | tf_op jit(solution)/shard_map/ppermute | solution.py:629
  11.3 3.9 %collective-permute-start.5 = (bf16[11,8,128]{2,1,0:T(8,128)(2,1)S(1)}, bf16[11,8,128]{2,1,0:T(8,128)(2,1)S(1)}, u32[]{:S(2)}, u32[]{:S(2)}) collective-permute-start(bf16[11,8,128]{2,1,0:T(8,128)(2,1)S(1)} %get-tuple-element.18), channel_id=1, source_target_pairs={{0,16},{16,0},{1,17},{17,1},{2,18},{18,2},{3,19},{19,3},{4,20},{20... | collective-permute-start | bytes 67592 | tf_op jit(solution)/shard_map/ppermute | solution.py:549
  15.5 6.3 %collective-permute-start.6 = (bf16[65,8,128]{2,1,0:T(8,128)(2,1)S(1)}, bf16[65,8,128]{2,1,0:T(8,128)(2,1)S(1)}, u32[]{:S(2)}, u32[]{:S(2)}) collective-permute-start(bf16[65,8,128]{2,1,0:T(8,128)(2,1)S(1)} %get-tuple-element.20), channel_id=1, source_target_pairs={{0,4},{4,0},{8,12},{12,8},{5,9},{9,5},{1,3},{13,15},{2,6},{6,2},{1... | collective-permute-start | bytes 399368 | tf_op jit(solution)/shard_map/ppermute | solution.py:668
  17.4 5.0 %collective-permute-start.7 = (bf16[65,8,128]{2,1,0:T(8,128)(2,1)S(1)}, bf16[65,8,128]{2,1,0:T(8,128)(2,1)S(1)}, u32[]{:S(2)}, u32[]{:S(2)}) collective-permute-start(bf16[65,8,128]{2,1,0:T(8,128)(2,1)S(1)} %get-tuple-element.21), channel_id=1, source_target_pairs={{4,8},{8,4},{0,2},{12,14},{1,5},{5,1},{9,13},{13,9},{6,10},{10,6},... | collective-permute-start | bytes 399368 | tf_op jit(solution)/shard_map/ppermute | solution.py:669

commit v6 on v5

--- a/solution.py
+++ b/solution.py
@@ -42,6 +42,9 @@
     SRC: (None, (2, -2, 0), (2, -1, 1), None),
 }
 
+EXACT_ROWS = {-1: (ADJ + VY, ADJ + SXY, ADJ + SYZ, BUOY, SRC), 0: (ADJ + SYY, LAM, INJ, SRC)}
+
+PAD = 1
 VMEM_LIMIT = 48 * 1024 * 1024
 
 
@@ -80,14 +83,17 @@
             source = cy + offset if up else offset
             target = 2 * cy + offset if up else cy + offset
             listed = list(range(spec[0], layers + spec[1])) + [layers] * spec[2]
-            near = offset in (-1, 0)
-            (wide if f >= ADJ and near else narrow).extend((f, z, source, target) for z in listed)
+            exact = f in EXACT_ROWS.get(offset, ())
+            (wide if exact else narrow).extend((f, z, source, target) for z in listed)
     return narrow, wide
 
 
-def row_counts(cz, cy):
-    sides = [y_rows(cz, cy, up) for up in (True, False)]
-    return tuple(max(-(-len(s[i]) // 8) for s in sides) for i in (0, 1))
+def row_counts(cz, cy, up):
+    return tuple(-(-len(rows) // 8) for rows in y_rows(cz, cy, up))
+
+
+def row_tiles(cz, cy):
+    return max(narrow + 2 * wide for narrow, wide in (row_counts(cz, cy, up) for up in (True, False)))
 
 
 def split(value):
@@ -118,39 +124,33 @@
 
 
 def pack_rows(cz, cy, row_of, packed, send_a, send_b):
-    narrow, wide = row_counts(cz, cy)
+    coded = []
     for side, up in enumerate((True, False)):
+        narrow, wide = row_counts(cz, cy, up)
         for base, listed in zip((0, narrow), y_rows(cz, cy, up)):
             for r, (f, z, y, _) in enumerate(listed):
                 packed[side, base + r // 8, r % 8 : r % 8 + 1, :] = row_of(f, z, y)
+        rest = [split(packed[side, narrow + t])[1].astype(jnp.float32) for t in range(wide)]
+        coded.append([packed[side, t] for t in range(narrow + wide)] + rest)
     even = even_mask(("gy", "gz"), packed.shape[2:])
-    for t in range(narrow + wide):
-        up, down = packed[0, t], packed[1, t]
-        for out, value in ((send_a, jnp.where(even, up, down)), (send_b, jnp.where(even, down, up))):
-            if out is None:
-                continue
-            if t < narrow:
-                out[t] = value.astype(jnp.bfloat16)
-            else:
-                out[t], out[wide + t] = split(value)
+    for t in range(send_a.shape[0]):
+        up, down = (tiles[min(t, len(tiles) - 1)] for tiles in coded)
+        send_a[t] = jnp.where(even, up, down).astype(jnp.bfloat16)
+        send_b[t] = jnp.where(even, down, up).astype(jnp.bfloat16)
 
 
 def unpack_rows(cz, cy, from_a, from_b, packed, put_row):
-    narrow, wide = row_counts(cz, cy)
     has_lower, has_upper = has_neighbours("gy")
     even = even_mask(("gy", "gz"), packed.shape[2:])
-    for t in range(narrow + wide):
-        got = []
-        for ref in (from_a, from_b):
-            if ref is None:
-                got.append(jnp.zeros(packed.shape[2:], jnp.float32))
-            elif t < narrow:
-                got.append(ref[t].astype(jnp.float32))
-            else:
-                got.append(joined(ref[t], ref[wide + t]))
-        packed[0, t] = jnp.where(even, got[1], got[0]) * has_lower
-        packed[1, t] = jnp.where(even, got[0], got[1]) * has_upper
-    for side, up in enumerate((True, False)):
+    for side, (up, keep) in enumerate(((True, has_lower), (False, has_upper))):
+        narrow, wide = row_counts(cz, cy, up)
+
+        def got(t):
+            a, b = from_a[t].astype(jnp.float32), from_b[t].astype(jnp.float32)
+            return (jnp.where(even, b, a) if up else jnp.where(even, a, b)) * keep
+
+        for t in range(narrow + wide):
+            packed[side, t] = got(t) if t < narrow else got(t) + got(wide + t)
         for base, listed in zip((0, narrow), y_rows(cz, cy, up)):
             for r, (f, z, _, y) in enumerate(listed):
                 put_row(f, z, y, packed[side, base + r // 8, r % 8 : r % 8 + 1, :])
@@ -239,10 +239,26 @@
     return tile
 
 
-def halo_kernel(cz, tiles, core, far, own, ring):
+def column_kernel(
+    cz, store, core, chip, both_a, both_b, far, peer, slot, own,
+    ring_f, ring, send_a, send_b, stores, peers, slots, sems,
+):
     cy, lanes = own.shape[2], own.shape[3]
     layers = cz + 2 * HALO
     ring_rows = ring.shape[2]
+    tiles = store.shape[0]
+    me = lax.axis_index("gz")
+    count = lax.axis_size("gz")
+    moves = copies(
+        sems,
+        (peer, peers),
+        (slot, slots),
+        (store, stores.at[me]),
+        (core.at[pl.ds(0, tiles)], stores.at[me ^ 1]),
+        (chip, stores.at[me ^ 2]),
+        (both_a, stores.at[me ^ 3, pl.ds(0, both_a.shape[0])]),
+        (both_b, stores.at[me ^ 3, pl.ds(both_a.shape[0], both_b.shape[0])]),
+    )
     near, _ = face_counts(cz)
     even = even_mask("gz", (cy, lanes))
     has_below, has_above = has_neighbours("gz")
@@ -270,35 +286,13 @@
         ring[f, layers, 0:cy, :] = strip_of(lambda z: ring[f, z, 0:cy, :], layers)
         for z in range(layers + 1):
             ring[f, z, cy:ring_rows, :] = jnp.zeros((ring_rows - cy, lanes), jnp.float32)
-
-
-def column_kernel(
-    cz, store, core, chip, both_a, both_b, peer, slot, ring_w, ring, send_a, send_b, stores, peers, slots, sems
-):
-    cy, lanes = core.shape[1], core.shape[2]
-    layers = cz + 2 * HALO
-    ring_rows = ring.shape[2]
-    tiles = store.shape[0]
-    me = lax.axis_index("gz")
-    count = lax.axis_size("gz")
-    moves = copies(
-        sems,
-        (peer, peers),
-        (slot, slots),
-        (store, stores.at[me]),
-        (core.at[pl.ds(0, tiles)], stores.at[me ^ 1]),
-        (chip, stores.at[me ^ 2]),
-        (both_a, stores.at[me ^ 3, pl.ds(0, both_a.shape[0])]),
-        (both_b, stores.at[me ^ 3, pl.ds(both_a.shape[0], both_b.shape[0])]),
-    )
-    zero = jnp.zeros((cy, lanes), jnp.float32)
-    for f in range(9):
+    for f in range(ring_f.shape[0]):
         for z in range(layers + 1):
-            ring[f, z, cy:ring_rows, :] = jnp.zeros((ring_rows - cy, lanes), jnp.float32)
+            ring_f[f, z, cy:ring_rows, :] = jnp.zeros((ring_rows - cy, lanes), jnp.float32)
+    strip = [ring[f, layers, 0:cy, :] for f in range(ring.shape[0])]
     for move in moves:
         move.wait()
     below, above = jnp.maximum(me - 1, 0), jnp.minimum(me + 1, count - 1)
-    has_below, has_above = has_neighbours("gz")
     for z in range(layers):
         if z < HALO:
             brick, piece, keep = below, cz - HALO + z, has_below
@@ -310,11 +304,10 @@
         row = slots[brick, piece] * 9
         for f in range(9):
             value = stores[holder, row + f].astype(jnp.float32)
-            ring[f, z, 0:cy, :] = value if keep is None else value * keep
+            ring_f[f, z, 0:cy, :] = value if keep is None else value * keep
     for f in range(9):
-        ring[f, layers, 0:cy, :] = strip_of(lambda z: ring[f, z, 0:cy, :], layers)
-    strip = [ring[f, layers, 0:cy, :] for f in range(9)]
-    strip += [ring_w[f, layers, 0:cy, :] for f in range(ring_w.shape[0])]
+        ring_f[f, layers, 0:cy, :] = strip_of(lambda z: ring_f[f, z, 0:cy, :], layers)
+    strip = [ring_f[f, layers, 0:cy, :] for f in range(9)] + strip
     position = lax.broadcasted_iota(jnp.int32, (cy, lanes), 1) % 8
     even_x = even_mask("gx", (cy, lanes))
     for out, tail_from_even in ((send_a, True), (send_b, False)):
@@ -394,7 +387,8 @@
 
 
 def window_kernel(
-    cz, ring_f_in, ring_w_in, strips, from_a, from_b, own, final, image_lam, image_mu, ring_f, ring_w, packed, keep
+    cz, ring_f_in, ring_w_in, strips, from_a, from_b, own, final, image_lam, image_mu, ring_f, ring_w,
+    packed, keep, images, speeds, sems,
 ):
     cy, lanes = own.shape[2], own.shape[3]
     layers = cz + 2 * HALO
@@ -527,16 +521,20 @@
             f.append(value + own[SRC - ADJ + 1, z - HALO] if s <= SZZ else value)
         a = [own[s, z - HALO] for s in range(SXX, SYZ + 1)]
         term_lam, term_mu = terms(f, a)
-        image_lam[z - HALO] = term_lam + keep[0, z - HALO]
-        image_mu[z - HALO] = term_mu + keep[1, z - HALO]
+        images[0, z - HALO] = term_lam + keep[0, z - HALO]
+        images[1, z - HALO] = term_mu + keep[1, z - HALO]
+    moves = copies(sems, (images.at[0], image_lam), (images.at[1], image_mu))
     velocity_step(ADJ, -1, {VX: (1, n - 1), VY: (1, n - 1), VZ: (1, n - 1)})
     stress_step(ADJ, -1, {SXX: (2, n - 1), SXY: (1, n - 1), SXZ: (1, n - 2)}, before=INJ)
+    stresses = ring_w.at[pl.ds(SXX, SYZ + 1 - SXX), pl.ds(HALO, cz), pl.ds(0, cy)]
+    moves += copies(sems.at[pl.ds(2, 1)], (stresses, final.at[pl.ds(SXX, SYZ + 1 - SXX)]))
     for z in range(*inner):
         rates = velocity_rates(ADJ, z, {VX, VY, VZ})
         for f in (VX, VY, VZ):
-            final[f, z - HALO] = (at(ADJ + f, z) - rates[f])[0:cy, :]
-        for s in range(SXX, SYZ + 1):
-            final[s, z - HALO] = ring[ADJ + s, z, 0:cy, :]
+            speeds[f, z - HALO] = (at(ADJ + f, z) - rates[f])[0:cy, :]
+    moves += copies(sems.at[pl.ds(3, 1)], (speeds, final.at[pl.ds(VX, VZ + 1 - VX)]))
+    for move in moves:
+        move.wait()
 
 
 def swap_pairs(count, first):
@@ -554,7 +552,7 @@
     return pltpu.with_memory_space_constraint(value, pltpu.HBM) if spec.memory_space == pl.ANY else value
 
 
-def kernel_call(body, args, in_specs, out_shape, scratch_shapes=(), aliases=None):
+def kernel_call(body, args, in_specs, out_shape, scratch_shapes=(), aliases=None, out_specs=None):
     here = [a is not None for a in args]
     there = [o is not None for o in out_shape]
 
@@ -568,7 +566,7 @@
             run,
             out_shape=tuple(o for o in out_shape if o is not None),
             in_specs=[s for s, h in zip(in_specs, here) if h],
-            out_specs=tuple(vmem() for h in there if h),
+            out_specs=out_specs or tuple(vmem() for h in there if h),
             scratch_shapes=list(scratch_shapes),
             input_output_aliases=aliases or {},
             compiler_params=pltpu.CompilerParams(vmem_limit_bytes=VMEM_LIMIT),
@@ -614,7 +612,7 @@
         functools.partial(start_kernel, cz),
         (store, adjoint_state, lame_lambda, lame_mu, buoyancy, source, wavelet, receiver, traces, plan),
         [hbm()] * 10,
-        (shape(tiles + face, cy, cx, dtype=bf16), shape(max(face, half) + 4, cy, cx, dtype=bf16), shape(15, cz, cy, cx)),
+        (shape(tiles + face, cy, cx, dtype=bf16), shape(max(face, half) + PAD, cy, cx, dtype=bf16), shape(15, cz, cy, cx)),
         [
             pltpu.VMEM(receiver.shape, jnp.int32),
             pltpu.VMEM(traces.shape, f32),
@@ -625,21 +623,27 @@
         ],
     )
     core = lax.ppermute(to_core, "gz", [(i, i ^ 1) for i in range(holders)])
-    far_face = lax.ppermute(to_far, "gz", [(i, i ^ 3) for i in range(holders)])
+    gy = lax.axis_size("gy")
+    across = {
+        (i, c): (i, 3 - c) if c in (1, 2) else (i ^ 1, c)
+        for i in range(gy) for c in range(holders)
+    }
+    far_face = lax.ppermute(
+        to_far, ("gy", "gz"), [(a[0] * holders + a[1], b[0] * holders + b[1]) for a, b in across.items()]
+    )
     both = [lax.ppermute(part, "gz", [(i, i ^ 1) for i in range(holders)]) for part in (chip[:half], chip[half:])]
 
-    (ring_w,) = kernel_call(
-        functools.partial(halo_kernel, cz, tiles),
-        (core, far_face, own),
-        [vmem()] * 3,
-        (shape(FIELDS - ADJ, layers + 1, 2 * cy, cx),),
-    )
     x_send = shape(x_tiles(), cy, cx, dtype=bf16)
-    ring_f, x_a, x_b = kernel_call(
+    ring_f, ring_w, x_a, x_b = kernel_call(
         functools.partial(column_kernel, cz),
-        (store, core, chip, *both, peer, slot, ring_w),
-        [hbm()] + [vmem()] * 4 + [hbm()] * 2 + [vmem()],
-        (shape(ADJ, layers + 1, 2 * cy, cx), x_send, x_send if wide_x else None),
+        (store, core, chip, *both, far_face, peer, slot, own),
+        [hbm()] + [vmem()] * 5 + [hbm()] * 2 + [vmem()],
+        (
+            shape(ADJ, layers + 1, 2 * cy, cx),
+            shape(FIELDS - ADJ, layers + 1, 2 * cy, cx),
+            x_send,
+            x_send if wide_x else None,
+        ),
         [
             pltpu.VMEM((holders, tiles, cy, cx), bf16),
             pltpu.SMEM(peer.shape, jnp.int32),
@@ -649,16 +653,15 @@
     )
     from_a, from_b = swapped(x_a, x_b, "gx")
 
-    narrow, wide = row_counts(cz, cy)
-    y_send = shape(narrow + 2 * wide, cy, cx, dtype=bf16)
+    y_send = shape(row_tiles(cz, cy), cy, cx, dtype=bf16)
+    row_scratch = pltpu.VMEM((2, max(sum(row_counts(cz, cy, up)) for up in (True, False)), 8, cx), f32)
     strips, y_a, y_b = kernel_call(
         functools.partial(rows_kernel, cz),
         (ring_f, ring_w, from_a, from_b),
         [vmem()] * 4,
         (shape(FIELDS, cy, cx), y_send, y_send),
-        [pltpu.VMEM((2, narrow + wide, 8, cx), f32)],
-    )
-    gy = lax.axis_size("gy")
+        [row_scratch],
+    )
     turns = [[], []]
     for turn, pairs in enumerate(turns):
         for c in range(holders):
@@ -680,10 +683,14 @@
             shape(*ring_w.shape),
         ),
         [
-            pltpu.VMEM((2, narrow + wide, 8, cx), f32),
+            row_scratch,
             pltpu.VMEM((2, cz, cy, cx), f32),
+            pltpu.VMEM((2, cz, cy, cx), f32),
+            pltpu.VMEM((3, cz, cy, cx), f32),
+            pltpu.SemaphoreType.DMA((4,)),
         ],
         {0: 3, 1: 4},
+        (hbm(),) * 3 + (vmem(),) * 2,
     )
     return result[:3]
 

time: 24.9 us -> 24.2 us (0.972)
  waiting for transfers between devices: 9.13 us -> 7.14 us
  starting transfers between devices: 9.13 us -> 10.8 us
  Pallas kernels: 5.71 us -> 5.43 us
    ppermute x1, starting transfers between devices: 0.07 us -> 1.64 us  [on_device(): lax.ppermute(to_far, ('gy', 'gz'), [(a[0] * holders + a[1], b[0] * holder...]
    ppermute x1, waiting for transfers between devices: 2.82 us -> 1.31 us  [on_device(): chip = lax.ppermute(store, 'gz', [(i, i ^ 2) for i in range(holders)])]
    ppermute x1, waiting for transfers between devices: 2.79 us -> 1.62 us  [on_device(): from_a = lax.ppermute(y_a, ('gy', 'gz'), turns[0])]
    ppermute x1, starting transfers between devices: 1.66 us -> 2.3 us  [on_device(): from_b = lax.ppermute(y_b, ('gy', 'gz'), turns[1])]
    ppermute x1, waiting for transfers between devices: 0.53 us -> 1.06 us  [on_device(): from_b = lax.ppermute(y_b, ('gy', 'gz'), turns[1])]
    pallas_call x5 -> x4, Pallas kernels: 5.71 us -> 5.43 us  [kernel_call(): pl.pallas_call(run, out_shape=tuple((o for o in out_shape if o is not Non...]
  transfers between devices with their start and end apart: 8 -> 8, of which waited for: 5 -> 5; matrix products, arithmetic and copies ran while one was open for 0% -> 0% of each run, Pallas kernels for 7% -> 5%
where the time goes in v6:
time: 24.2 us; the launch traced here: 24.1 us
  starting transfers between devices  10.8 us (45%)
  waiting for transfers between devices  7.14 us (30%)
  Pallas kernels  5.43 us (22%)
  between operations  0.67 us (3%)
    pallas_call x4, Pallas kernels, kernel_call(): pl.pallas_call(run, out_shape=tuple((o for o in out_shape if o is not Non...  5.43 us
    ppermute x1, starting transfers between devices, on_device(): chip = lax.ppermute(store, 'gz', [(i, i ^ 2) for i in range(holders)])  3 us
    ppermute x1, starting transfers between devices, on_device(): from_b = lax.ppermute(y_b, ('gy', 'gz'), turns[1])  2.3 us
    ppermute x1, waiting for transfers between devices, swapped(): got_a = lax.ppermute(value_a, axis, swap_pairs(count, 0))  2.24 us
    ppermute x1, starting transfers between devices, on_device(): from_a = lax.ppermute(y_a, ('gy', 'gz'), turns[0])  1.69 us
    ppermute x1, starting transfers between devices, on_device(): lax.ppermute(to_far, ('gy', 'gz'), [(a[0] * holders + a[1], b[0] * holder...  1.64 us
    ppermute x1, starting transfers between devices, swapped(): got_a = lax.ppermute(value_a, axis, swap_pairs(count, 0))  1.63 us
    ppermute x1, waiting for transfers between devices, on_device(): from_a = lax.ppermute(y_a, ('gy', 'gz'), turns[0])  1.62 us
  transfers between devices with their start and end apart: 8, of which 5 were waited for; matrix products, arithmetic and copies ran while one was open for 0% of the time, Pallas kernels for 5%

profile of v6, /device:TPU:0, one launch (start us, length us, event | category | flops | bytes accessed | tf_op | source)
XLA Modules:
  0.0 24.1 jit_solution(17467928054799748251)
XLA Ops:
  0.6 3.0 %collective-permute-start.1 = (bf16[72,8,128]{2,1,0:T(8,128)(2,1)}, bf16[72,8,128]{2,1,0:T(8,128)(2,1)S(1)}, u32[]{:S(2)}, u32[]{:S(2)}) collective-permute-start(bf16[72,8,128]{2,1,0:T(8,128)(2,1)} %bitcast.6), channel_id=1, source_target_pairs={{0,2},{1,3},{2,0},{3,1},{4,6},{5,7},{6,4},{7,5},{8,10},{9,11},{10,... | collective-permute-start | bytes 442376 | tf_op jit(solution)/shard_map/ppermute | solution.py:610
  3.6 1.3 %shard_map.139 = (bf16[107,8,128]{2,1,0:T(8,128)(2,1)S(1)}, bf16[37,8,128]{2,1,0:T(8,128)(2,1)S(1)}, f32[15,8,8,128]{3,2,1,0:T(8,128)S(1)}) custom-call(bf16[72,8,128]{2,1,0:T(8,128)(2,1)} %bitcast.7, f32[9,8,8,128]{3,2,1,0:T(8,128)} %refs_1_.1, f32[8,8,128]{2,1,0:T(8,128)} %refs_2_.1, f32[8,8,128]{2,1,0:T(8,128)} %refs_3_.1, f32[8,8,128]{2,1,0:T(8,128)} %refs_4_.1, ...), custom_call_target="tpu_custom_call" | custom-call | tf_op jit(solution)/shard_map/pallas_call | solution.py:565
  4.9 1.6 %collective-permute-start.4 = (bf16[37,8,128]{2,1,0:T(8,128)(2,1)S(1)}, bf16[37,8,128]{2,1,0:T(8,128)(2,1)S(1)}, u32[]{:S(2)}, u32[]{:S(2)}) collective-permute-start(bf16[37,8,128]{2,1,0:T(8,128)(2,1)S(1)} %get-tuple-element.16), channel_id=1, source_target_pairs={{0,4},{1,2},{2,1},{3,7},{4,0},{5,6},{6,5},{7,3},{8,12},{9,10},{10,... | collective-permute-start | bytes 227336 | tf_op jit(solution)/shard_map/ppermute | solution.py:631
  6.6 0.0 collective-permute-start
  6.6 1.3 %collective-permute-done.1.refs_2_ = bf16[72,8,128]{2,1,0:T(8,128)(2,1)S(1)} collective-permute-done((bf16[72,8,128]{2,1,0:T(8,128)(2,1)}, bf16[72,8,128]{2,1,0:T(8,128)(2,1)S(1)}, u32[]{:S(2)}, u32[]{:S(2)}) %collective-permute-start.1) | collective-permute-done | bytes 147488 | tf_op jit(solution)/shard_map/ppermute | solution.py:610
  7.9 0.1 collective-permute-start.3
  8.0 0.5 %collective-permute-start.2 = (bf16[36,8,128]{2,1,0:T(8,128)(2,1)S(1)}, bf16[36,8,128]{2,1,0:T(8,128)(2,1)S(1)}, u32[]{:S(2)}, u32[]{:S(2)}) collective-permute-start(bf16[36,8,128]{2,1,0:T(8,128)(2,1)S(1)} %get-tuple-element.28), channel_id=1, source_target_pairs={{0,1},{1,0},{2,3},{3,2},{4,5},{5,4},{6,7},{7,6},{8,9},{9,8},{10,11... | collective-permute-start | bytes 221192 | tf_op jit(solution)/shard_map/ppermute | solution.py:634
  8.5 0.9 %collective-permute-done.4.refs_5_ = bf16[37,8,128]{2,1,0:T(8,128)(2,1)S(1)} collective-permute-done((bf16[37,8,128]{2,1,0:T(8,128)(2,1)S(1)}, bf16[37,8,128]{2,1,0:T(8,128)(2,1)S(1)}, u32[]{:S(2)}, u32[]{:S(2)}) %collective-permute-start.4) | collective-permute-done | bytes 75808 | tf_op jit(solution)/shard_map/ppermute | solution.py:631
  9.4 0.0 collective-permute-done.refs_1_
  9.4 0.0 collective-permute-done.3.refs_4_
  9.4 0.0 collective-permute-done.2.refs_3_
  9.4 1.5 %shard_map.140 = (f32[9,13,16,128]{3,2,1,0:T(8,128)S(1)}, f32[14,13,16,128]{3,2,1,0:T(8,128)S(1)}, bf16[11,8,128]{2,1,0:T(8,128)(2,1)S(1)}) custom-call(bf16[72,8,128]{2,1,0:T(8,128)(2,1)} %bitcast.8, bf16[107,8,128]{2,1,0:T(8,128)(2,1)S(1)} %collective-permute-done.refs_1_, bf16[72,8,128]{2,1,0:T(8,128)(2,1)S(1)} %collective-permute-done.1.refs_2_, ...), custom_call_target="tpu_custom_call" | custom-call | tf_op jit(solution)/shard_map/pallas_call | solution.py:565
  10.9 1.6 %collective-permute-start.5 = (bf16[11,8,128]{2,1,0:T(8,128)(2,1)S(1)}, bf16[11,8,128]{2,1,0:T(8,128)(2,1)S(1)}, u32[]{:S(2)}, u32[]{:S(2)}) collective-permute-start(bf16[11,8,128]{2,1,0:T(8,128)(2,1)S(1)} %get-tuple-element.20), channel_id=1, source_target_pairs={{0,16},{16,0},{1,17},{17,1},{2,18},{18,2},{3,19},{19,3},{4,20},{20... | collective-permute-start | bytes 67592 | tf_op jit(solution)/shard_map/ppermute | solution.py:547
  12.6 2.2 %collective-permute-done.5.refs_2_ = bf16[11,8,128]{2,1,0:T(8,128)(2,1)S(1)} collective-permute-done((bf16[11,8,128]{2,1,0:T(8,128)(2,1)S(1)}, bf16[11,8,128]{2,1,0:T(8,128)(2,1)S(1)}, u32[]{:S(2)}, u32[]{:S(2)}) %collective-permute-start.5) | collective-permute-done | bytes 22560 | tf_op jit(solution)/shard_map/ppermute | solution.py:547
  14.8 0.3 %shard_map.141 = (f32[23,8,128]{2,1,0:T(8,128)S(1)}, bf16[52,8,128]{2,1,0:T(8,128)(2,1)S(1)}, bf16[52,8,128]{2,1,0:T(8,128)(2,1)S(1)}) custom-call(f32[9,13,16,128]{3,2,1,0:T(8,128)S(1)} %get-tuple-element.18.refs_0_, f32[14,13,16,128]{3,2,1,0:T(8,128)S(1)} %get-tuple-element.19.refs_1_, bf16[11,8,128]{2,1,0:T(8,128)(2,1)S(1)} %collective-permute-done.5.refs_2_), custom_call_target="tpu_custom_call" | custom-call | tf_op jit(solution)/shard_map/pallas_call | solution.py:565
  15.1 1.7 %collective-permute-start.6 = (bf16[52,8,128]{2,1,0:T(8,128)(2,1)S(1)}, bf16[52,8,128]{2,1,0:T(8,128)(2,1)S(1)}, u32[]{:S(2)}, u32[]{:S(2)}) collective-permute-start(bf16[52,8,128]{2,1,0:T(8,128)(2,1)S(1)} %get-tuple-element.22), channel_id=1, source_target_pairs={{0,4},{4,0},{8,12},{12,8},{5,9},{9,5},{1,3},{13,15},{2,6},{6,2},{1... | collective-permute-start | bytes 319496 | tf_op jit(solution)/shard_map/ppermute | solution.py:671
  16.8 2.3 %collective-permute-start.7 = (bf16[52,8,128]{2,1,0:T(8,128)(2,1)S(1)}, bf16[52,8,128]{2,1,0:T(8,128)(2,1)S(1)}, u32[]{:S(2)}, u32[]{:S(2)}) collective-permute-start(bf16[52,8,128]{2,1,0:T(8,128)(2,1)S(1)} %get-tuple-element.23), channel_id=1, source_target_pairs={{4,8},{8,4},{0,2},{12,14},{1,5},{5,1},{9,13},{13,9},{6,10},{10,6},... | collective-permute-start | bytes 319496 | tf_op jit(solution)/shard_map/ppermute | solution.py:672
  19.1 1.6 %collective-permute-done.6.refs_3_ = bf16[52,8,128]{2,1,0:T(8,128)(2,1)S(1)} collective-permute-done((bf16[52,8,128]{2,1,0:T(8,128)(2,1)S(1)}, bf16[52,8,128]{2,1,0:T(8,128)(2,1)S(1)}, u32[]{:S(2)}, u32[]{:S(2)}) %collective-permute-start.6) | collective-permute-done | bytes 106528 | tf_op jit(solution)/shard_map/ppermute | solution.py:671
  20.7 1.1 %collective-permute-done.7.refs_4_ = bf16[52,8,128]{2,1,0:T(8,128)(2,1)S(1)} collective-permute-done((bf16[52,8,128]{2,1,0:T(8,128)(2,1)S(1)}, bf16[52,8,128]{2,1,0:T(8,128)(2,1)S(1)}, u32[]{:S(2)}, u32[]{:S(2)}) %collective-permute-start.7) | collective-permute-done | bytes 106528 | tf_op jit(solution)/shard_map/ppermute | solution.py:672
  21.8 2.3 %shard_map.142 = (f32[9,8,8,128]{3,2,1,0:T(8,128)}, f32[8,8,128]{2,1,0:T(8,128)}, f32[8,8,128]{2,1,0:T(8,128)}, f32[9,13,16,128]{3,2,1,0:T(8,128)S(1)}, f32[14,13,16,128]{3,2,1,0:T(8,128)S(1)}) custom-call(f32[9,13,16,128]{3,2,1,0:T(8,128)S(1)} %get-tuple-element.18.refs_0_, ...), custom_call_target="tpu_custom_call", output_to_operand_aliasing={{3}: (0, {}), {4}: (1, {})} | custom-call | tf_op jit(solution)/shard_map/pallas_call | solution.py:565
  (1 shorter events, 0.0 us)
Async XLA Ops:
  0.6 7.2 %collective-permute-start.1 = (bf16[72,8,128]{2,1,0:T(8,128)(2,1)}, bf16[72,8,128]{2,1,0:T(8,128)(2,1)S(1)}, u32[]{:S(2)}, u32[]{:S(2)}) collective-permute-start(bf16[72,8,128]{2,1,0:T(8,128)(2,1)} %bitcast.6), channel_id=1, source_target_pairs={{0,2},{1,3},{2,0},{3,1},{4,6},{5,7},{6,4},{7,5},{8,10},{9,11},{10,... | collective-permute-start | bytes 442376 | tf_op jit(solution)/shard_map/ppermute | solution.py:610
  4.9 4.4 %collective-permute-start.4 = (bf16[37,8,128]{2,1,0:T(8,128)(2,1)S(1)}, bf16[37,8,128]{2,1,0:T(8,128)(2,1)S(1)}, u32[]{:S(2)}, u32[]{:S(2)}) collective-permute-start(bf16[37,8,128]{2,1,0:T(8,128)(2,1)S(1)} %get-tuple-element.16), channel_id=1, source_target_pairs={{0,4},{1,2},{2,1},{3,7},{4,0},{5,6},{6,5},{7,3},{8,12},{9,10},{10,... | collective-permute-start | bytes 227336 | tf_op jit(solution)/shard_map/ppermute | solution.py:631
  6.6 2.8 %collective-permute-start = (bf16[107,8,128]{2,1,0:T(8,128)(2,1)S(1)}, bf16[107,8,128]{2,1,0:T(8,128)(2,1)S(1)}, u32[]{:S(2)}, u32[]{:S(2)}) collective-permute-start(bf16[107,8,128]{2,1,0:T(8,128)(2,1)S(1)} %get-tuple-element.15), channel_id=1, source_target_pairs={{0,1},{1,0},{2,3},{3,2},{4,5},{5,4},{6,7},{7,6},{8,9},{9,8},{10,11... | collective-permute-start | bytes 657416 | tf_op jit(solution)/shard_map/ppermute | solution.py:625
  7.9 1.5 %collective-permute-start.3 = (bf16[36,8,128]{2,1,0:T(8,128)(2,1)S(1)}, bf16[36,8,128]{2,1,0:T(8,128)(2,1)S(1)}, u32[]{:S(2)}, u32[]{:S(2)}) collective-permute-start(bf16[36,8,128]{2,1,0:T(8,128)(2,1)S(1)} %get-tuple-element.27), channel_id=1, source_target_pairs={{0,1},{1,0},{2,3},{3,2},{4,5},{5,4},{6,7},{7,6},{8,9},{9,8},{10,11... | collective-permute-start | bytes 221192 | tf_op jit(solution)/shard_map/ppermute | solution.py:634
  8.0 1.4 %collective-permute-start.2 = (bf16[36,8,128]{2,1,0:T(8,128)(2,1)S(1)}, bf16[36,8,128]{2,1,0:T(8,128)(2,1)S(1)}, u32[]{:S(2)}, u32[]{:S(2)}) collective-permute-start(bf16[36,8,128]{2,1,0:T(8,128)(2,1)S(1)} %get-tuple-element.28), channel_id=1, source_target_pairs={{0,1},{1,0},{2,3},{3,2},{4,5},{5,4},{6,7},{7,6},{8,9},{9,8},{10,11... | collective-permute-start | bytes 221192 | tf_op jit(solution)/shard_map/ppermute | solution.py:634
  10.9 3.9 %collective-permute-start.5 = (bf16[11,8,128]{2,1,0:T(8,128)(2,1)S(1)}, bf16[11,8,128]{2,1,0:T(8,128)(2,1)S(1)}, u32[]{:S(2)}, u32[]{:S(2)}) collective-permute-start(bf16[11,8,128]{2,1,0:T(8,128)(2,1)S(1)} %get-tuple-element.20), channel_id=1, source_target_pairs={{0,16},{16,0},{1,17},{17,1},{2,18},{18,2},{3,19},{19,3},{4,20},{20... | collective-permute-start | bytes 67592 | tf_op jit(solution)/shard_map/ppermute | solution.py:547
  15.1 5.6 %collective-permute-start.6 = (bf16[52,8,128]{2,1,0:T(8,128)(2,1)S(1)}, bf16[52,8,128]{2,1,0:T(8,128)(2,1)S(1)}, u32[]{:S(2)}, u32[]{:S(2)}) collective-permute-start(bf16[52,8,128]{2,1,0:T(8,128)(2,1)S(1)} %get-tuple-element.22), channel_id=1, source_target_pairs={{0,4},{4,0},{8,12},{12,8},{5,9},{9,5},{1,3},{13,15},{2,6},{6,2},{1... | collective-permute-start | bytes 319496 | tf_op jit(solution)/shard_map/ppermute | solution.py:671
  16.8 5.0 %collective-permute-start.7 = (bf16[52,8,128]{2,1,0:T(8,128)(2,1)S(1)}, bf16[52,8,128]{2,1,0:T(8,128)(2,1)S(1)}, u32[]{:S(2)}, u32[]{:S(2)}) collective-permute-start(bf16[52,8,128]{2,1,0:T(8,128)(2,1)S(1)} %get-tuple-element.23), channel_id=1, source_target_pairs={{4,8},{8,4},{0,2},{12,14},{1,5},{5,1},{9,13},{13,9},{6,10},{10,6},... | collective-permute-start | bytes 319496 | tf_op jit(solution)/shard_map/ppermute | solution.py:672

commit v7 on v6

--- a/solution.py
+++ b/solution.py
@@ -74,7 +74,7 @@
 
 def y_rows(cz, cy, up):
     layers = cz + 2 * HALO
-    narrow, wide = [], []
+    narrow, wide, strip = [], [], []
     for f in sorted(Y_ROWS):
         for offset in (-1, -2) if up else (0, 1):
             spec = Y_ROWS[f][offset + HALO]
@@ -82,10 +82,11 @@
                 continue
             source = cy + offset if up else offset
             target = 2 * cy + offset if up else cy + offset
-            listed = list(range(spec[0], layers + spec[1])) + [layers] * spec[2]
             exact = f in EXACT_ROWS.get(offset, ())
-            (wide if exact else narrow).extend((f, z, source, target) for z in listed)
-    return narrow, wide
+            (wide if exact else narrow).extend((f, z, source, target) for z in range(spec[0], layers + spec[1]))
+            if spec[2]:
+                strip.append((f, layers, source, target))
+    return narrow, wide, strip
 
 
 def row_counts(cz, cy, up):
@@ -93,7 +94,8 @@
 
 
 def row_tiles(cz, cy):
-    return max(narrow + 2 * wide for narrow, wide in (row_counts(cz, cy, up) for up in (True, False)))
+    sides = [row_counts(cz, cy, up) for up in (True, False)]
+    return max(n + 2 * w + c for n, w, c in sides), max(c for _, _, c in sides)
 
 
 def split(value):
@@ -123,54 +125,71 @@
     return out
 
 
-def pack_rows(cz, cy, row_of, packed, send_a, send_b):
-    coded = []
+def pack_rows(cz, cy, row_of, packed, sends, diagonals):
+    coded, corners = [], []
     for side, up in enumerate((True, False)):
-        narrow, wide = row_counts(cz, cy, up)
-        for base, listed in zip((0, narrow), y_rows(cz, cy, up)):
+        narrow, wide, strip = row_counts(cz, cy, up)
+        for base, listed in zip((0, narrow, narrow + wide), y_rows(cz, cy, up)):
             for r, (f, z, y, _) in enumerate(listed):
                 packed[side, base + r // 8, r % 8 : r % 8 + 1, :] = row_of(f, z, y)
         rest = [split(packed[side, narrow + t])[1].astype(jnp.float32) for t in range(wide)]
-        coded.append([packed[side, t] for t in range(narrow + wide)] + rest)
+        coded.append([packed[side, t] for t in range(narrow + wide + strip)] + rest)
+        corners.append([packed[side, narrow + wide + t] for t in range(strip)])
     even = even_mask(("gy", "gz"), packed.shape[2:])
-    for t in range(send_a.shape[0]):
-        up, down = (tiles[min(t, len(tiles) - 1)] for tiles in coded)
-        send_a[t] = jnp.where(even, up, down).astype(jnp.bfloat16)
-        send_b[t] = jnp.where(even, down, up).astype(jnp.bfloat16)
-
-
-def unpack_rows(cz, cy, from_a, from_b, packed, put_row):
+    for outs, tiles in ((sends, coded), (diagonals, corners)):
+        for t in range(outs[0].shape[0]):
+            up, down = (side[min(t, len(side) - 1)] for side in tiles)
+            outs[0][t] = jnp.where(even, up, down).astype(jnp.bfloat16)
+            outs[1][t] = jnp.where(even, down, up).astype(jnp.bfloat16)
+
+
+def unpack_rows(cz, cy, got, diagonals, packed, put_row):
+    lanes = packed.shape[3]
     has_lower, has_upper = has_neighbours("gy")
+    has_left, has_right = has_neighbours("gx")
     even = even_mask(("gy", "gz"), packed.shape[2:])
+    even_x = even_mask("gx", packed.shape[2:])
+    pair = lax.broadcasted_iota(jnp.int32, packed.shape[2:], 1) % 8 // 2
     for side, (up, keep) in enumerate(((True, has_lower), (False, has_upper))):
-        narrow, wide = row_counts(cz, cy, up)
-
-        def got(t):
-            a, b = from_a[t].astype(jnp.float32), from_b[t].astype(jnp.float32)
+        narrow, wide, strip = row_counts(cz, cy, up)
+
+        def of(two, t):
+            a, b = two[0][t].astype(jnp.float32), two[1][t].astype(jnp.float32)
             return (jnp.where(even, b, a) if up else jnp.where(even, a, b)) * keep
 
-        for t in range(narrow + wide):
-            packed[side, t] = got(t) if t < narrow else got(t) + got(wide + t)
-        for base, listed in zip((0, narrow), y_rows(cz, cy, up)):
+        for t in range(narrow + wide + strip):
+            value = of(got, t)
+            if narrow <= t < narrow + wide:
+                value = value + of(got, wide + strip + t)
+            if t >= narrow + wide:
+                for turn, two in enumerate(diagonals):
+                    corner = of(two, t - narrow - wide)
+                    right = jnp.where(pair == 1, pltpu.roll(corner * has_right, lanes - 4, 1), 0.0)
+                    left = jnp.where(pair == 2, pltpu.roll(corner * has_left, 4, 1), 0.0)
+                    value = value + (jnp.where(even_x, left, right) if turn else jnp.where(even_x, right, left))
+            packed[side, t] = value
+        for base, listed in zip((0, narrow, narrow + wide), y_rows(cz, cy, up)):
             for r, (f, z, _, y) in enumerate(listed):
                 put_row(f, z, y, packed[side, base + r // 8, r % 8 : r % 8 + 1, :])
 
 
 def start_kernel(
-    cz, store, adjoint, lam, mu, buoy, source, wavelet, receiver, traces, plan,
-    near_out, far_out, own, cells, samples, spots, wave, steps, sems,
+    cz, store, adjoint, lam, mu, buoy, source, wavelet, receiver, traces, plan, peer, slot,
+    near_out, far_out, own, peer_out, slot_out, cells, samples, spots, wave, steps, sems,
 ):
     cy, lanes = own.shape[2], own.shape[3]
     rows = cz * cy
     tiles = store.shape[0]
     small = copies(sems, (plan, steps), (wavelet, wave), (source, spots), (receiver, cells), (traces, samples))
     large = copies(
-        sems.at[pl.ds(len(small), 5)],
+        sems.at[pl.ds(len(small), 7)],
         (adjoint, own.at[pl.ds(0, 9)]),
         (buoy, own.at[BUOY - ADJ]),
         (lam, own.at[LAM - ADJ]),
         (mu, own.at[MU - ADJ]),
         (store, near_out.at[pl.ds(0, tiles)]),
+        (peer, peer_out),
+        (slot, slot_out),
     )
     for copy in small:
         copy.wait()
@@ -240,25 +259,17 @@
 
 
 def column_kernel(
-    cz, store, core, chip, both_a, both_b, far, peer, slot, own,
-    ring_f, ring, send_a, send_b, stores, peers, slots, sems,
+    cz, mine, core, chip, both_a, both_b, far, peer, slot, own,
+    ring_f, ring, x_a, x_b, y_a, y_b, corner_a, corner_b, packed, peers, slots, sems,
 ):
     cy, lanes = own.shape[2], own.shape[3]
     layers = cz + 2 * HALO
     ring_rows = ring.shape[2]
-    tiles = store.shape[0]
+    tiles = chip.shape[0]
+    half = both_a.shape[0]
     me = lax.axis_index("gz")
     count = lax.axis_size("gz")
-    moves = copies(
-        sems,
-        (peer, peers),
-        (slot, slots),
-        (store, stores.at[me]),
-        (core.at[pl.ds(0, tiles)], stores.at[me ^ 1]),
-        (chip, stores.at[me ^ 2]),
-        (both_a, stores.at[me ^ 3, pl.ds(0, both_a.shape[0])]),
-        (both_b, stores.at[me ^ 3, pl.ds(both_a.shape[0], both_b.shape[0])]),
-    )
+    moves = copies(sems, (peer, peers), (slot, slots))
     near, _ = face_counts(cz)
     even = even_mask("gz", (cy, lanes))
     has_below, has_above = has_neighbours("gz")
@@ -300,17 +311,22 @@
             brick, piece, keep = me, z - HALO, None
         else:
             brick, piece, keep = above, z - HALO - cz, has_above
-        holder = peers[brick, piece]
         row = slots[brick, piece] * 9
+        hops = jnp.full((cy, lanes), peers[brick, piece] ^ me, jnp.int32)
+        late = jnp.full((cy, lanes), row, jnp.int32) >= half
+        row_a, row_b = jnp.minimum(row, half - 9), jnp.maximum(row - half, 0)
         for f in range(9):
-            value = stores[holder, row + f].astype(jnp.float32)
+            parts = (mine[row + f], core[row + f], chip[row + f], both_a[row_a + f], both_b[row_b + f])
+            parts = [part.astype(jnp.float32) for part in parts]
+            value = jnp.where(late, parts[4], parts[3])
+            value = jnp.where(hops < 2, jnp.where(hops == 1, parts[1], parts[0]), jnp.where(hops == 2, parts[2], value))
             ring_f[f, z, 0:cy, :] = value if keep is None else value * keep
     for f in range(9):
         ring_f[f, layers, 0:cy, :] = strip_of(lambda z: ring_f[f, z, 0:cy, :], layers)
     strip = [ring_f[f, layers, 0:cy, :] for f in range(9)] + strip
     position = lax.broadcasted_iota(jnp.int32, (cy, lanes), 1) % 8
     even_x = even_mask("gx", (cy, lanes))
-    for out, tail_from_even in ((send_a, True), (send_b, False)):
+    for out, tail_from_even in ((x_a, True), (x_b, False)):
         if out is None:
             continue
         place = 0
@@ -329,17 +345,41 @@
                     out[place + len(quads) + i] = low
             place += len(quads) if narrow else 2 * len(quads)
 
+    def row_of(f, z, y):
+        return ring_f[f, z, y : y + 1, :] if f < ADJ else ring[f - ADJ, z, y : y + 1, :]
+
+    pack_rows(cz, cy, row_of, packed, (y_a, y_b), (corner_a, corner_b))
+
 
 def x_tiles():
     return -(-ADJ // 4) + 2 * -(-(FIELDS - ADJ) // 4)
 
 
-def rows_kernel(cz, ring_f, ring_w, from_a, from_b, strips, send_a, send_b, packed):
-    cy, lanes = strips.shape[1], strips.shape[2]
+class Ring:
+    def __init__(self, ring_f, ring_w):
+        self.parts = ring_f, ring_w
+
+    def __getitem__(self, key):
+        f = key[0]
+        return self.parts[0][key] if f < ADJ else self.parts[1][(f - ADJ, *key[1:])]
+
+    def __setitem__(self, key, value):
+        f = key[0]
+        if f < ADJ:
+            self.parts[0][key] = value
+        else:
+            self.parts[1][(f - ADJ, *key[1:])] = value
+
+
+def window_kernel(
+    cz, ring_f_in, ring_w_in, x_a, x_b, y_a, y_b, corner_aa, corner_ab, corner_ba, corner_bb, own,
+    final, image_lam, image_mu, ring_f, ring_w, packed, keep, images, speeds, sems,
+):
+    cy, lanes = own.shape[2], own.shape[3]
     layers = cz + 2 * HALO
-    strip = [ring_f[f, layers, 0:cy, :] for f in range(9)]
-    strip += [ring_w[f, layers, 0:cy, :] for f in range(ring_w.shape[0])]
-    position = lax.broadcasted_iota(jnp.int32, (cy, lanes), 1) % 8
+    ring_rows = ring_f.shape[2]
+    ring = Ring(ring_f, ring_w)
+    pair = lax.broadcasted_iota(jnp.int32, (cy, lanes), 1) % 8 // 2
     even_x = even_mask("gx", (cy, lanes))
     has_left, has_right = has_neighbours("gx")
     zero = jnp.zeros((cy, lanes), jnp.float32)
@@ -348,7 +388,7 @@
         quads = [fields[i : i + 4] for i in range(0, len(fields), 4)]
         for i, quad in enumerate(quads):
             got = []
-            for ref in (from_a, from_b):
+            for ref in (x_a, x_b):
                 if ref is None:
                     got.append(zero)
                 elif narrow:
@@ -358,49 +398,15 @@
             right = jnp.where(even_x, got[0], got[1]) * has_right
             left = jnp.where(even_x, got[1], got[0]) * has_left
             for g, f in enumerate(quad):
-                tile = jnp.where(position // 2 == 1, pltpu.roll(right, (2 - 2 * g) % lanes, 1), strip[f])
-                strips[f] = jnp.where(position // 2 == 2, pltpu.roll(left, (4 - 2 * g) % lanes, 1), tile)
+                tile = jnp.where(pair == 1, pltpu.roll(right, (2 - 2 * g) % lanes, 1), ring[f, layers, 0:cy, :])
+                ring[f, layers, 0:cy, :] = jnp.where(pair == 2, pltpu.roll(left, (4 - 2 * g) % lanes, 1), tile)
         place += len(quads) if narrow else 2 * len(quads)
-
-    def row_of(f, z, y):
-        if z == layers:
-            return strips[f, y : y + 1, :]
-        return ring_f[f, z, y : y + 1, :] if f < ADJ else ring_w[f - ADJ, z, y : y + 1, :]
-
-    pack_rows(cz, cy, row_of, packed, send_a, send_b)
-
-
-class Ring:
-    def __init__(self, ring_f, ring_w):
-        self.parts = ring_f, ring_w
-
-    def __getitem__(self, key):
-        f = key[0]
-        return self.parts[0][key] if f < ADJ else self.parts[1][(f - ADJ, *key[1:])]
-
-    def __setitem__(self, key, value):
-        f = key[0]
-        if f < ADJ:
-            self.parts[0][key] = value
-        else:
-            self.parts[1][(f - ADJ, *key[1:])] = value
-
-
-def window_kernel(
-    cz, ring_f_in, ring_w_in, strips, from_a, from_b, own, final, image_lam, image_mu, ring_f, ring_w,
-    packed, keep, images, speeds, sems,
-):
-    cy, lanes = own.shape[2], own.shape[3]
-    layers = cz + 2 * HALO
-    ring_rows = ring_f.shape[2]
-    ring = Ring(ring_f, ring_w)
-    for f in range(FIELDS):
-        ring[f, layers, 0:cy, :] = strips[f]
 
     def put_row(f, z, y, value):
         ring[f, z, y : y + 1, :] = value
 
-    unpack_rows(cz, cy, from_a, from_b, packed, put_row)
+    diagonals = [two for two in ((corner_aa, corner_ab), (corner_ba, corner_bb)) if two[0] is not None]
+    unpack_rows(cz, cy, (y_a, y_b), diagonals, packed, put_row)
 
     lane = lax.broadcasted_iota(jnp.int32, (ring_rows, lanes), 1)
     first_lane, last_lane = lane == 0, lane == lanes - 1
@@ -608,18 +614,19 @@
 
     wide_x = lax.axis_size("gx") > 2
     chip = lax.ppermute(store, "gz", [(i, i ^ 2) for i in range(holders)])
-    to_core, to_far, own = kernel_call(
+    to_core, to_far, own, peer, slot = kernel_call(
         functools.partial(start_kernel, cz),
-        (store, adjoint_state, lame_lambda, lame_mu, buoyancy, source, wavelet, receiver, traces, plan),
-        [hbm()] * 10,
-        (shape(tiles + face, cy, cx, dtype=bf16), shape(max(face, half) + PAD, cy, cx, dtype=bf16), shape(15, cz, cy, cx)),
+        (store, adjoint_state, lame_lambda, lame_mu, buoyancy, source, wavelet, receiver, traces, plan, peer, slot),
+        [hbm()] * 12,
+        (shape(tiles + face, cy, cx, dtype=bf16), shape(max(face, half) + PAD, cy, cx, dtype=bf16), shape(15, cz, cy, cx),
+         shape(*peer.shape, dtype=jnp.int32), shape(*slot.shape, dtype=jnp.int32)),
         [
             pltpu.VMEM(receiver.shape, jnp.int32),
             pltpu.VMEM(traces.shape, f32),
             pltpu.SMEM(source.shape, jnp.int32),
             pltpu.SMEM(wavelet.shape, f32),
             pltpu.SMEM(plan.shape, jnp.int32),
-            pltpu.SemaphoreType.DMA((10,)),
+            pltpu.SemaphoreType.DMA((12,)),
         ],
     )
     core = lax.ppermute(to_core, "gz", [(i, i ^ 1) for i in range(holders)])
@@ -634,47 +641,60 @@
     both = [lax.ppermute(part, "gz", [(i, i ^ 1) for i in range(holders)]) for part in (chip[:half], chip[half:])]
 
     x_send = shape(x_tiles(), cy, cx, dtype=bf16)
-    ring_f, ring_w, x_a, x_b = kernel_call(
+    y_size, corner_size = row_tiles(cz, cy)
+    y_send, corner_send = shape(y_size, cy, cx, dtype=bf16), shape(corner_size, cy, cx, dtype=bf16)
+    row_scratch = pltpu.VMEM((2, max(sum(row_counts(cz, cy, up)) for up in (True, False)), 8, cx), f32)
+    ring_f, ring_w, x_a, x_b, y_a, y_b, corner_a, corner_b = kernel_call(
         functools.partial(column_kernel, cz),
-        (store, core, chip, *both, far_face, peer, slot, own),
-        [hbm()] + [vmem()] * 5 + [hbm()] * 2 + [vmem()],
+        (to_core, core, chip, *both, far_face, peer, slot, own),
+        [vmem()] * 9,
         (
             shape(ADJ, layers + 1, 2 * cy, cx),
             shape(FIELDS - ADJ, layers + 1, 2 * cy, cx),
             x_send,
             x_send if wide_x else None,
+            y_send,
+            y_send,
+            corner_send,
+            corner_send,
         ),
         [
-            pltpu.VMEM((holders, tiles, cy, cx), bf16),
+            row_scratch,
             pltpu.SMEM(peer.shape, jnp.int32),
             pltpu.SMEM(slot.shape, jnp.int32),
-            pltpu.SemaphoreType.DMA((7,)),
+            pltpu.SemaphoreType.DMA((2,)),
         ],
     )
-    from_a, from_b = swapped(x_a, x_b, "gx")
-
-    y_send = shape(row_tiles(cz, cy), cy, cx, dtype=bf16)
-    row_scratch = pltpu.VMEM((2, max(sum(row_counts(cz, cy, up)) for up in (True, False)), 8, cx), f32)
-    strips, y_a, y_b = kernel_call(
-        functools.partial(rows_kernel, cz),
-        (ring_f, ring_w, from_a, from_b),
-        [vmem()] * 4,
-        (shape(FIELDS, cy, cx), y_send, y_send),
-        [row_scratch],
-    )
-    turns = [[], []]
-    for turn, pairs in enumerate(turns):
-        for c in range(holders):
-            first = (c + turn) % 2
-            change = dict(swap_pairs(gy, first))
-            pairs.extend((i * holders + c, (i * holders + (c ^ 2)) if j == i else (j * holders + c)) for i, j in change.items())
-    from_a = lax.ppermute(y_a, ("gy", "gz"), turns[0])
-    from_b = lax.ppermute(y_b, ("gy", "gz"), turns[1])
-
+    axes = ("gx", "gy", "gz")
+    gx = lax.axis_size("gx")
+
+    def partner(i, j, c, x_turn, y_turn):
+        if x_turn is not None:
+            i = dict(swap_pairs(gx, x_turn))[i]
+        if y_turn is not None:
+            other = dict(swap_pairs(gy, (c + y_turn) % 2))[j]
+            j, c = (j, c ^ 2) if other == j else (other, c)
+        return (i * gy + j) * holders + c
+
+    def swap(value, x_turn, y_turn):
+        if value is None:
+            return None
+        pairs = [
+            ((i * gy + j) * holders + c, partner(i, j, c, x_turn, y_turn))
+            for i in range(gx) for j in range(gy) for c in range(holders)
+        ]
+        return lax.ppermute(value, axes, pairs)
+
+    x_turns = (0, 1) if wide_x else (0,)
+    corners = [swap(v, t, u) for t in x_turns for u, v in enumerate((corner_a, corner_b))]
+    corners += [None] * (4 - len(corners))
     result = kernel_call(
         functools.partial(window_kernel, cz),
-        (ring_f, ring_w, strips, from_a, from_b, own),
-        [vmem()] * 6,
+        (
+            ring_f, ring_w, swap(x_a, 0, None), swap(x_b, 1, None), swap(y_a, None, 0), swap(y_b, None, 1),
+            *corners, own,
+        ),
+        [vmem()] * 11,
         (
             shape(9, cz, cy, cx),
             shape(cz, cy, cx),

time: 24.2 us -> 24.7 us (1.021)
  starting transfers between devices: 10.8 us -> 14.8 us
  waiting for transfers between devices: 7.14 us -> 3.83 us
    ppermute x3 -> x5, starting transfers between devices: 5.62 us -> 9.57 us  [swap(): return lax.ppermute(value, axes, pairs)]
    ppermute x3 -> x5, waiting for transfers between devices: 4.92 us -> 1.61 us  [swap(): return lax.ppermute(value, axes, pairs)]
    pallas_call x4 -> x3, Pallas kernels: 5.43 us -> 5.26 us  [kernel_call(): pl.pallas_call(run, out_shape=tuple((o for o in out_shape if o is not Non...]
  transfers between devices with their start and end apart: 8 -> 10, of which waited for: 5 -> 4; matrix products, arithmetic and copies ran while one was open for 0% -> 0% of each run, Pallas kernels for 5% -> 5%
where the time goes in v7:
time: 24.7 us; the launch traced here: 24.6 us
  starting transfers between devices  14.8 us (60%)
  Pallas kernels  5.26 us (21%)
  waiting for transfers between devices  3.83 us (16%)
  between operations  0.68 us (3%)
    ppermute x5, starting transfers between devices, swap(): return lax.ppermute(value, axes, pairs)  9.57 us
    pallas_call x3, Pallas kernels, kernel_call(): pl.pallas_call(run, out_shape=tuple((o for o in out_shape if o is not Non...  5.26 us
    ppermute x1, starting transfers between devices, on_device(): chip = lax.ppermute(store, 'gz', [(i, i ^ 2) for i in range(holders)])  3 us
    ppermute x1, starting transfers between devices, on_device(): lax.ppermute(to_far, ('gy', 'gz'), [(a[0] * holders + a[1], b[0] * holder...  1.64 us
    ppermute x5, waiting for transfers between devices, swap(): return lax.ppermute(value, axes, pairs)  1.61 us
    ppermute x1, waiting for transfers between devices, on_device(): chip = lax.ppermute(store, 'gz', [(i, i ^ 2) for i in range(holders)])  1.29 us
    ppermute x1, waiting for transfers between devices, on_device(): lax.ppermute(to_far, ('gy', 'gz'), [(a[0] * holders + a[1], b[0] * holder...  0.92 us
    ppermute x2, starting transfers between devices, on_device(): lax.ppermute(part, 'gz', [(i, i ^ 1) for i in range(holders)])  0.57 us
  transfers between devices with their start and end apart: 10, of which 4 were waited for; matrix products, arithmetic and copies ran while one was open for 0% of the time, Pallas kernels for 5%

profile of v7, /device:TPU:0, one launch (start us, length us, event | category | flops | bytes accessed | tf_op | source)
XLA Modules:
  0.0 24.6 jit_solution(2605163919676551463)
XLA Ops:
  0.6 3.0 %collective-permute-start.1 = (bf16[72,8,128]{2,1,0:T(8,128)(2,1)}, bf16[72,8,128]{2,1,0:T(8,128)(2,1)S(1)}, u32[]{:S(2)}, u32[]{:S(2)}) collective-permute-start(bf16[72,8,128]{2,1,0:T(8,128)(2,1)} %bitcast.6), channel_id=1, source_target_pairs={{0,2},{1,3},{2,0},{3,1},{4,6},{5,7},{6,4},{7,5},{8,10},{9,11},{10,... | collective-permute-start | bytes 442376 | tf_op jit(solution)/shard_map/ppermute | solution.py:616
  3.6 1.3 %shard_map.139 = (bf16[107,8,128]{2,1,0:T(8,128)(2,1)S(1)}, bf16[37,8,128]{2,1,0:T(8,128)(2,1)S(1)}, f32[15,8,8,128]{3,2,1,0:T(8,128)S(1)}, s32[4,8]{1,0:T(4,128)S(1)}, s32[4,8]{1,0:T(4,128)S(1)}) custom-call(bf16[72,8,128]{2,1,0:T(8,128)(2,1)} %bitcast.7, f32[9,8,8,128]{3,2,1,0:T(8,128)} %refs_1_.1, f32[8,8,128]{2,1,0:T(8,128)} %refs_2_.1, ...), custom_call_target="tpu_custom_call" | custom-call | tf_op jit(solution)/shard_map/pallas_call | solution.py:571
  4.9 1.6 %collective-permute-start.4 = (bf16[37,8,128]{2,1,0:T(8,128)(2,1)S(1)}, bf16[37,8,128]{2,1,0:T(8,128)(2,1)S(1)}, u32[]{:S(2)}, u32[]{:S(2)}) collective-permute-start(bf16[37,8,128]{2,1,0:T(8,128)(2,1)S(1)} %get-tuple-element.19), channel_id=1, source_target_pairs={{0,4},{1,2},{2,1},{3,7},{4,0},{5,6},{6,5},{7,3},{8,12},{9,10},{10,... | collective-permute-start | bytes 227336 | tf_op jit(solution)/shard_map/ppermute | solution.py:638
  6.6 0.0 collective-permute-start
  6.6 1.3 %collective-permute-done.1.refs_2_ = bf16[72,8,128]{2,1,0:T(8,128)(2,1)S(1)} collective-permute-done((bf16[72,8,128]{2,1,0:T(8,128)(2,1)}, bf16[72,8,128]{2,1,0:T(8,128)(2,1)S(1)}, u32[]{:S(2)}, u32[]{:S(2)}) %collective-permute-start.1) | collective-permute-done | bytes 147488 | tf_op jit(solution)/shard_map/ppermute | solution.py:616
  7.9 0.1 collective-permute-start.3
  8.0 0.5 %collective-permute-start.2 = (bf16[36,8,128]{2,1,0:T(8,128)(2,1)S(1)}, bf16[36,8,128]{2,1,0:T(8,128)(2,1)S(1)}, u32[]{:S(2)}, u32[]{:S(2)}) collective-permute-start(bf16[36,8,128]{2,1,0:T(8,128)(2,1)S(1)} %get-tuple-element.34), channel_id=1, source_target_pairs={{0,1},{1,0},{2,3},{3,2},{4,5},{5,4},{6,7},{7,6},{8,9},{9,8},{10,11... | collective-permute-start | bytes 221192 | tf_op jit(solution)/shard_map/ppermute | solution.py:641
  8.5 0.9 %collective-permute-done.4.refs_5_ = bf16[37,8,128]{2,1,0:T(8,128)(2,1)S(1)} collective-permute-done((bf16[37,8,128]{2,1,0:T(8,128)(2,1)S(1)}, bf16[37,8,128]{2,1,0:T(8,128)(2,1)S(1)}, u32[]{:S(2)}, u32[]{:S(2)}) %collective-permute-start.4) | collective-permute-done | bytes 75808 | tf_op jit(solution)/shard_map/ppermute | solution.py:638
  9.4 0.0 collective-permute-done.refs_1_
  9.4 0.0 collective-permute-done.3.refs_4_
  9.4 0.0 collective-permute-done.2.refs_3_
  9.4 1.5 %shard_map.140 = (f32[9,13,16,128]{3,2,1,0:T(8,128)S(1)}, f32[14,13,16,128]{3,2,1,0:T(8,128)S(1)}, bf16[11,8,128]{2,1,0:T(8,128)(2,1)S(1)}, bf16[52,8,128]{2,1,0...) custom-call(bf16[107,8,128]{2,1,0:T(8,128)(2,1)S(1)} %get-tuple-elem, ...), custom_call_target="tpu_custom_call" | custom-call | tf_op jit(solution)/shard_map/pallas_call | solution.py:571
  10.9 1.7 %collective-permute-start.6 = (bf16[52,8,128]{2,1,0:T(8,128)(2,1)S(1)}, bf16[52,8,128]{2,1,0:T(8,128)(2,1)S(1)}, u32[]{:S(2)}, u32[]{:S(2)}) collective-permute-start(bf16[52,8,128]{2,1,0:T(8,128)(2,1)S(1)} %get-tuple-element.26), channel_id=1, source_target_pairs={{0,4},{1,3},{2,6},{3,1},{4,0},{5,9},{6,2},{7,11},{8,12},{9,5},{10,... | collective-permute-start | bytes 319496 | tf_op jit(solution)/shard_map/ppermute | solution.py:686
  12.6 2.3 %collective-permute-start.7 = (bf16[52,8,128]{2,1,0:T(8,128)(2,1)S(1)}, bf16[52,8,128]{2,1,0:T(8,128)(2,1)S(1)}, u32[]{:S(2)}, u32[]{:S(2)}) collective-permute-start(bf16[52,8,128]{2,1,0:T(8,128)(2,1)S(1)} %get-tuple-element.27), channel_id=1, source_target_pairs={{0,2},{1,5},{2,0},{3,7},{4,8},{5,1},{6,10},{7,3},{8,4},{9,13},{10,... | collective-permute-start | bytes 319496 | tf_op jit(solution)/shard_map/ppermute | solution.py:686
  14.9 1.5 %collective-permute-start.5 = (bf16[11,8,128]{2,1,0:T(8,128)(2,1)S(1)}, bf16[11,8,128]{2,1,0:T(8,128)(2,1)S(1)}, u32[]{:S(2)}, u32[]{:S(2)}) collective-permute-start(bf16[11,8,128]{2,1,0:T(8,128)(2,1)S(1)} %get-tuple-element.25), channel_id=1, source_target_pairs={{0,16},{1,17},{2,18},{3,19},{4,20},{5,21},{6,22},{7,23},{8,24},{9,... | collective-permute-start | bytes 67592 | tf_op jit(solution)/shard_map/ppermute | solution.py:686
  16.4 0.8 %collective-permute-start.8 = (bf16[3,8,128]{2,1,0:T(8,128)(2,1)S(1)}, bf16[3,8,128]{2,1,0:T(8,128)(2,1)S(1)}, u32[]{:S(2)}, u32[]{:S(2)}) collective-permute-start(bf16[3,8,128]{2,1,0:T(8,128)(2,1)S(1)} %get-tuple-element.28), channel_id=1, source_target_pairs={{0,20},{1,19},{2,22},{3,17},{4,16},{5,25},{6,18},{7,27},{8,28},{9,... | collective-permute-start | bytes 18440 | tf_op jit(solution)/shard_map/ppermute | solution.py:686
  17.2 3.3 %collective-permute-start.9 = (bf16[3,8,128]{2,1,0:T(8,128)(2,1)S(1)}, bf16[3,8,128]{2,1,0:T(8,128)(2,1)S(1)}, u32[]{:S(2)}, u32[]{:S(2)}) collective-permute-start(bf16[3,8,128]{2,1,0:T(8,128)(2,1)S(1)} %get-tuple-element.29), channel_id=1, source_target_pairs={{0,18},{1,21},{2,16},{3,23},{4,24},{5,17},{6,26},{7,19},{8,20},{9,... | collective-permute-start | bytes 18440 | tf_op jit(solution)/shard_map/ppermute | solution.py:686
  20.5 0.5 %collective-permute-done.8.refs_5_ = bf16[3,8,128]{2,1,0:T(8,128)(2,1)S(1)} collective-permute-done((bf16[3,8,128]{2,1,0:T(8,128)(2,1)S(1)}, bf16[3,8,128]{2,1,0:T(8,128)(2,1)S(1)}, u32[]{:S(2)}, u32[]{:S(2)}) %collective-permute-start.8) | collective-permute-done | bytes 6176 | tf_op jit(solution)/shard_map/ppermute | solution.py:686
  21.0 1.1 %collective-permute-done.9.refs_6_ = bf16[3,8,128]{2,1,0:T(8,128)(2,1)S(1)} collective-permute-done((bf16[3,8,128]{2,1,0:T(8,128)(2,1)S(1)}, bf16[3,8,128]{2,1,0:T(8,128)(2,1)S(1)}, u32[]{:S(2)}, u32[]{:S(2)}) %collective-permute-start.9) | collective-permute-done | bytes 6176 | tf_op jit(solution)/shard_map/ppermute | solution.py:686
  22.1 0.0 collective-permute-done.5.refs_2_
  22.1 0.0 collective-permute-done.6.refs_3_
  22.1 0.0 collective-permute-done.7.refs_4_
  22.1 2.4 %shard_map.141 = (f32[9,8,8,128]{3,2,1,0:T(8,128)}, f32[8,8,128]{2,1,0:T(8,128)}, f32[8,8,128]{2,1,0:T(8,128)}, f32[9,13,16,128]{3,2,1,0:T(8,128)S(1)}, f32[14,13,16,128]{3,2,1,0:T(8,128)S(1)}) custom-call(f32[9,13,16,128]{3,2,1,0:T(8,128)S(1)} %get-tuple-element.23.refs_0_, ...), custom_call_target="tpu_custom_call", output_to_operand_aliasing={{3}: (0, {}), {4}: (1, {})} | custom-call | tf_op jit(solution)/shard_map/pallas_call | solution.py:571
  (1 shorter events, 0.0 us)
Async XLA Ops:
  0.6 7.2 %collective-permute-start.1 = (bf16[72,8,128]{2,1,0:T(8,128)(2,1)}, bf16[72,8,128]{2,1,0:T(8,128)(2,1)S(1)}, u32[]{:S(2)}, u32[]{:S(2)}) collective-permute-start(bf16[72,8,128]{2,1,0:T(8,128)(2,1)} %bitcast.6), channel_id=1, source_target_pairs={{0,2},{1,3},{2,0},{3,1},{4,6},{5,7},{6,4},{7,5},{8,10},{9,11},{10,... | collective-permute-start | bytes 442376 | tf_op jit(solution)/shard_map/ppermute | solution.py:616
  4.9 4.4 %collective-permute-start.4 = (bf16[37,8,128]{2,1,0:T(8,128)(2,1)S(1)}, bf16[37,8,128]{2,1,0:T(8,128)(2,1)S(1)}, u32[]{:S(2)}, u32[]{:S(2)}) collective-permute-start(bf16[37,8,128]{2,1,0:T(8,128)(2,1)S(1)} %get-tuple-element.19), channel_id=1, source_target_pairs={{0,4},{1,2},{2,1},{3,7},{4,0},{5,6},{6,5},{7,3},{8,12},{9,10},{10,... | collective-permute-start | bytes 227336 | tf_op jit(solution)/shard_map/ppermute | solution.py:638
  6.6 2.8 %collective-permute-start = (bf16[107,8,128]{2,1,0:T(8,128)(2,1)S(1)}, bf16[107,8,128]{2,1,0:T(8,128)(2,1)S(1)}, u32[]{:S(2)}, u32[]{:S(2)}) collective-permute-start(bf16[107,8,128]{2,1,0:T(8,128)(2,1)S(1)} %get-tuple-element.18.refs_0_), channel_id=1, source_target_pairs={{0,1},{1,0},{2,3},{3,2},{4,5},{5,4},{6,7},{7,6},{8,9},{9,8},{10,11... | collective-permute-start | bytes 657416 | tf_op jit(solution)/shard_map/ppermute | solution.py:632
  7.9 1.5 %collective-permute-start.3 = (bf16[36,8,128]{2,1,0:T(8,128)(2,1)S(1)}, bf16[36,8,128]{2,1,0:T(8,128)(2,1)S(1)}, u32[]{:S(2)}, u32[]{:S(2)}) collective-permute-start(bf16[36,8,128]{2,1,0:T(8,128)(2,1)S(1)} %get-tuple-element.33), channel_id=1, source_target_pairs={{0,1},{1,0},{2,3},{3,2},{4,5},{5,4},{6,7},{7,6},{8,9},{9,8},{10,11... | collective-permute-start | bytes 221192 | tf_op jit(solution)/shard_map/ppermute | solution.py:641
  8.0 1.4 %collective-permute-start.2 = (bf16[36,8,128]{2,1,0:T(8,128)(2,1)S(1)}, bf16[36,8,128]{2,1,0:T(8,128)(2,1)S(1)}, u32[]{:S(2)}, u32[]{:S(2)}) collective-permute-start(bf16[36,8,128]{2,1,0:T(8,128)(2,1)S(1)} %get-tuple-element.34), channel_id=1, source_target_pairs={{0,1},{1,0},{2,3},{3,2},{4,5},{5,4},{6,7},{7,6},{8,9},{9,8},{10,11... | collective-permute-start | bytes 221192 | tf_op jit(solution)/shard_map/ppermute | solution.py:641
  10.9 11.2 %collective-permute-start.6 = (bf16[52,8,128]{2,1,0:T(8,128)(2,1)S(1)}, bf16[52,8,128]{2,1,0:T(8,128)(2,1)S(1)}, u32[]{:S(2)}, u32[]{:S(2)}) collective-permute-start(bf16[52,8,128]{2,1,0:T(8,128)(2,1)S(1)} %get-tuple-element.26), channel_id=1, source_target_pairs={{0,4},{1,3},{2,6},{3,1},{4,0},{5,9},{6,2},{7,11},{8,12},{9,5},{10,... | collective-permute-start | bytes 319496 | tf_op jit(solution)/shard_map/ppermute | solution.py:686
  12.6 9.5 %collective-permute-start.7 = (bf16[52,8,128]{2,1,0:T(8,128)(2,1)S(1)}, bf16[52,8,128]{2,1,0:T(8,128)(2,1)S(1)}, u32[]{:S(2)}, u32[]{:S(2)}) collective-permute-start(bf16[52,8,128]{2,1,0:T(8,128)(2,1)S(1)} %get-tuple-element.27), channel_id=1, source_target_pairs={{0,2},{1,5},{2,0},{3,7},{4,8},{5,1},{6,10},{7,3},{8,4},{9,13},{10,... | collective-permute-start | bytes 319496 | tf_op jit(solution)/shard_map/ppermute | solution.py:686
  14.9 7.2 %collective-permute-start.5 = (bf16[11,8,128]{2,1,0:T(8,128)(2,1)S(1)}, bf16[11,8,128]{2,1,0:T(8,128)(2,1)S(1)}, u32[]{:S(2)}, u32[]{:S(2)}) collective-permute-start(bf16[11,8,128]{2,1,0:T(8,128)(2,1)S(1)} %get-tuple-element.25), channel_id=1, source_target_pairs={{0,16},{1,17},{2,18},{3,19},{4,20},{5,21},{6,22},{7,23},{8,24},{9,... | collective-permute-start | bytes 67592 | tf_op jit(solution)/shard_map/ppermute | solution.py:686
  16.4 4.5 %collective-permute-start.8 = (bf16[3,8,128]{2,1,0:T(8,128)(2,1)S(1)}, bf16[3,8,128]{2,1,0:T(8,128)(2,1)S(1)}, u32[]{:S(2)}, u32[]{:S(2)}) collective-permute-start(bf16[3,8,128]{2,1,0:T(8,128)(2,1)S(1)} %get-tuple-element.28), channel_id=1, source_target_pairs={{0,20},{1,19},{2,22},{3,17},{4,16},{5,25},{6,18},{7,27},{8,28},{9,... | collective-permute-start | bytes 18440 | tf_op jit(solution)/shard_map/ppermute | solution.py:686
  17.2 4.9 %collective-permute-start.9 = (bf16[3,8,128]{2,1,0:T(8,128)(2,1)S(1)}, bf16[3,8,128]{2,1,0:T(8,128)(2,1)S(1)}, u32[]{:S(2)}, u32[]{:S(2)}) collective-permute-start(bf16[3,8,128]{2,1,0:T(8,128)(2,1)S(1)} %get-tuple-element.29), channel_id=1, source_target_pairs={{0,18},{1,21},{2,16},{3,23},{4,24},{5,17},{6,26},{7,19},{8,20},{9,... | collective-permute-start | bytes 18440 | tf_op jit(solution)/shard_map/ppermute | solution.py:686

commit v8 on v7

--- a/solution.py
+++ b/solution.py
@@ -95,7 +95,7 @@
 
 def row_tiles(cz, cy):
     sides = [row_counts(cz, cy, up) for up in (True, False)]
-    return max(n + 2 * w + c for n, w, c in sides), max(c for _, _, c in sides)
+    return max(c for _, _, c in sides), max(n + 2 * w for n, w, _ in sides)
 
 
 def split(value):
@@ -125,50 +125,55 @@
     return out
 
 
-def pack_rows(cz, cy, row_of, packed, sends, diagonals):
-    coded, corners = [], []
+def scatter_rows(packed, listed, row_of):
+    for r, (f, z, y, _) in enumerate(listed):
+        packed[r // 8, r % 8 : r % 8 + 1, :] = row_of(f, z, y)
+
+
+def pack_tiles(sides, sends, first, count):
+    even = even_mask(("gy", "gz"), sends[0].shape[1:])
+    for t in range(count):
+        up, down = (side[min(t, len(side) - 1)] for side in sides)
+        sends[0][first + t] = jnp.where(even, up, down).astype(jnp.bfloat16)
+        sends[1][first + t] = jnp.where(even, down, up).astype(jnp.bfloat16)
+
+
+def layer_rows_kernel(cz, ring_f, ring_w, send_a, send_b, packed):
+    cy = ring_f.shape[2] // 2
+    strip_tiles, tiles = row_tiles(cz, cy)
+
+    def row_of(f, z, y):
+        return ring_f[f, z, y : y + 1, :] if f < ADJ else ring_w[f - ADJ, z, y : y + 1, :]
+
+    sides = []
     for side, up in enumerate((True, False)):
-        narrow, wide, strip = row_counts(cz, cy, up)
-        for base, listed in zip((0, narrow, narrow + wide), y_rows(cz, cy, up)):
-            for r, (f, z, y, _) in enumerate(listed):
-                packed[side, base + r // 8, r % 8 : r % 8 + 1, :] = row_of(f, z, y)
-        rest = [split(packed[side, narrow + t])[1].astype(jnp.float32) for t in range(wide)]
-        coded.append([packed[side, t] for t in range(narrow + wide + strip)] + rest)
-        corners.append([packed[side, narrow + wide + t] for t in range(strip)])
+        narrow, wide, _ = y_rows(cz, cy, up)
+        n, w, _ = row_counts(cz, cy, up)
+        scatter_rows(packed.at[side], narrow, row_of)
+        scatter_rows(packed.at[side, pl.ds(n, w)], wide, row_of)
+        rest = [split(packed[side, n + t])[1].astype(jnp.float32) for t in range(w)]
+        sides.append([packed[side, t] for t in range(n + w)] + rest)
+    pack_tiles(sides, (send_a, send_b), strip_tiles, tiles)
+
+
+def unpack_rows(cz, cy, got, packed, put_row):
+    has_lower, has_upper = has_neighbours("gy")
     even = even_mask(("gy", "gz"), packed.shape[2:])
-    for outs, tiles in ((sends, coded), (diagonals, corners)):
-        for t in range(outs[0].shape[0]):
-            up, down = (side[min(t, len(side) - 1)] for side in tiles)
-            outs[0][t] = jnp.where(even, up, down).astype(jnp.bfloat16)
-            outs[1][t] = jnp.where(even, down, up).astype(jnp.bfloat16)
-
-
-def unpack_rows(cz, cy, got, diagonals, packed, put_row):
-    lanes = packed.shape[3]
-    has_lower, has_upper = has_neighbours("gy")
-    has_left, has_right = has_neighbours("gx")
-    even = even_mask(("gy", "gz"), packed.shape[2:])
-    even_x = even_mask("gx", packed.shape[2:])
-    pair = lax.broadcasted_iota(jnp.int32, packed.shape[2:], 1) % 8 // 2
+    strip_tiles, _ = row_tiles(cz, cy)
     for side, (up, keep) in enumerate(((True, has_lower), (False, has_upper))):
-        narrow, wide, strip = row_counts(cz, cy, up)
-
-        def of(two, t):
-            a, b = two[0][t].astype(jnp.float32), two[1][t].astype(jnp.float32)
+        narrow, wide, strip = y_rows(cz, cy, up)
+        n, w, c = row_counts(cz, cy, up)
+
+        def of(t):
+            a, b = got[0][t].astype(jnp.float32), got[1][t].astype(jnp.float32)
             return (jnp.where(even, b, a) if up else jnp.where(even, a, b)) * keep
 
-        for t in range(narrow + wide + strip):
-            value = of(got, t)
-            if narrow <= t < narrow + wide:
-                value = value + of(got, wide + strip + t)
-            if t >= narrow + wide:
-                for turn, two in enumerate(diagonals):
-                    corner = of(two, t - narrow - wide)
-                    right = jnp.where(pair == 1, pltpu.roll(corner * has_right, lanes - 4, 1), 0.0)
-                    left = jnp.where(pair == 2, pltpu.roll(corner * has_left, 4, 1), 0.0)
-                    value = value + (jnp.where(even_x, left, right) if turn else jnp.where(even_x, right, left))
-            packed[side, t] = value
-        for base, listed in zip((0, narrow, narrow + wide), y_rows(cz, cy, up)):
+        for t in range(n + w):
+            value = of(strip_tiles + t)
+            packed[side, t] = value if t < n else value + of(strip_tiles + w + t)
+        for t in range(c):
+            packed[side, n + w + t] = of(t)
+        for base, listed in ((0, narrow), (n, wide), (n + w, strip)):
             for r, (f, z, _, y) in enumerate(listed):
                 put_row(f, z, y, packed[side, base + r // 8, r % 8 : r % 8 + 1, :])
 
@@ -244,27 +249,46 @@
         far_out[i] = zero.astype(jnp.bfloat16)
 
 
-def strip_of(main, layers):
-    cy, lanes = main(0).shape
-    lane = lax.broadcasted_iota(jnp.int32, (cy, lanes), 1)
-    position = lane % 8
-    group = lane // 8
-    tile = jnp.zeros((cy, lanes), jnp.float32)
-    for z in range(layers):
-        tail = pltpu.roll(main(z), (8 * z + 2) % lanes, 1)
-        head = pltpu.roll(main(z), (8 * z + 6) % lanes, 1)
-        here = group == z
-        tile = jnp.where(here & (position < 2), tail, jnp.where(here & (position >= 6), head, tile))
+def strip_part(tile, main, listed):
+    lanes = tile.shape[1]
+    lane = lax.broadcasted_iota(jnp.int32, tile.shape, 1)
+    for z in listed:
+        tile = jnp.where((lane >= 8 * z) & (lane < 8 * z + 4), pltpu.roll(main(z), (8 * z + 2) % lanes, 1), tile)
     return tile
 
 
-def column_kernel(
-    cz, mine, core, chip, both_a, both_b, far, peer, slot, own,
-    ring_f, ring, x_a, x_b, y_a, y_b, corner_a, corner_b, packed, peers, slots, sems,
-):
+def strip_whole(tile):
+    position = lax.broadcasted_iota(jnp.int32, tile.shape, 1) % 8
+    return jnp.where(position < 2, tile, jnp.where(position >= 6, pltpu.roll(tile, 4, 1), 0.0))
+
+
+def frame_kernel(cz, own, ring_f, ring):
     cy, lanes = own.shape[2], own.shape[3]
     layers = cz + 2 * HALO
     ring_rows = ring.shape[2]
+    zero = jnp.zeros((cy, lanes), jnp.float32)
+    beyond = jnp.zeros((ring_rows - cy, lanes), jnp.float32)
+    filled = {(f - ADJ, z) for up in (True, False) for listed in faces(cz, up) for f, _, z in listed}
+    for f in range(ring.shape[0]):
+        for z in range(cz):
+            ring[f, HALO + z, 0:cy, :] = own[f, z]
+        for z in (0, 1, layers - 2, layers - 1):
+            if (f, z) not in filled:
+                ring[f, z, 0:cy, :] = zero
+        ring[f, layers, 0:cy, :] = strip_part(zero, lambda z: own[f, z - HALO], range(HALO, HALO + cz))
+        for z in range(layers + 1):
+            ring[f, z, cy:ring_rows, :] = beyond
+    for f in range(ring_f.shape[0]):
+        for z in range(layers + 1):
+            ring_f[f, z, cy:ring_rows, :] = beyond
+
+
+def column_kernel(
+    cz, mine, core, chip, both_a, both_b, far, peer, slot, ring_f_in, ring_w_in,
+    ring_f, ring, x_a, x_b, peers, slots, sems,
+):
+    cy, lanes = chip.shape[1], chip.shape[2]
+    layers = cz + 2 * HALO
     tiles = chip.shape[0]
     half = both_a.shape[0]
     me = lax.axis_index("gz")
@@ -274,10 +298,7 @@
     even = even_mask("gz", (cy, lanes))
     has_below, has_above = has_neighbours("gz")
     zero = jnp.zeros((cy, lanes), jnp.float32)
-    for f in range(ring.shape[0]):
-        for z in range(cz):
-            ring[f, HALO + z, 0:cy, :] = own[f, z]
-    filled = set()
+    filled = {}
     for up in (True, False):
         for depth, listed in enumerate(faces(cz, up)):
             for i, (f, _, z) in enumerate(listed):
@@ -288,19 +309,15 @@
                     else:
                         values.append(ref[base + 2 * near + i].astype(jnp.float32))
                 value = jnp.where(even, values[1], values[0]) if up else jnp.where(even, values[0], values[1])
-                ring[f - ADJ, z, 0:cy, :] = value * (has_below if up else has_above)
-                filled.add((f - ADJ, z))
+                value = value * (has_below if up else has_above)
+                ring[f - ADJ, z, 0:cy, :] = value
+                filled.setdefault(f - ADJ, {})[z] = value
+    strip = []
     for f in range(ring.shape[0]):
-        for z in (0, 1, layers - 2, layers - 1):
-            if (f, z) not in filled:
-                ring[f, z, 0:cy, :] = zero
-        ring[f, layers, 0:cy, :] = strip_of(lambda z: ring[f, z, 0:cy, :], layers)
-        for z in range(layers + 1):
-            ring[f, z, cy:ring_rows, :] = jnp.zeros((ring_rows - cy, lanes), jnp.float32)
-    for f in range(ring_f.shape[0]):
-        for z in range(layers + 1):
-            ring_f[f, z, cy:ring_rows, :] = jnp.zeros((ring_rows - cy, lanes), jnp.float32)
-    strip = [ring[f, layers, 0:cy, :] for f in range(ring.shape[0])]
+        there = filled.get(f, {})
+        tile = strip_whole(strip_part(ring[f, layers, 0:cy, :], lambda z: there[z], sorted(there)))
+        ring[f, layers, 0:cy, :] = tile
+        strip.append(tile)
     for move in moves:
         move.wait()
     below, above = jnp.maximum(me - 1, 0), jnp.minimum(me + 1, count - 1)
@@ -322,7 +339,7 @@
             value = jnp.where(hops < 2, jnp.where(hops == 1, parts[1], parts[0]), jnp.where(hops == 2, parts[2], value))
             ring_f[f, z, 0:cy, :] = value if keep is None else value * keep
     for f in range(9):
-        ring_f[f, layers, 0:cy, :] = strip_of(lambda z: ring_f[f, z, 0:cy, :], layers)
+        ring_f[f, layers, 0:cy, :] = strip_whole(strip_part(zero, lambda z: ring_f[f, z, 0:cy, :], range(layers)))
     strip = [ring_f[f, layers, 0:cy, :] for f in range(9)] + strip
     position = lax.broadcasted_iota(jnp.int32, (cy, lanes), 1) % 8
     even_x = even_mask("gx", (cy, lanes))
@@ -345,11 +362,6 @@
                     out[place + len(quads) + i] = low
             place += len(quads) if narrow else 2 * len(quads)
 
-    def row_of(f, z, y):
-        return ring_f[f, z, y : y + 1, :] if f < ADJ else ring[f - ADJ, z, y : y + 1, :]
-
-    pack_rows(cz, cy, row_of, packed, (y_a, y_b), (corner_a, corner_b))
-
 
 def x_tiles():
     return -(-ADJ // 4) + 2 * -(-(FIELDS - ADJ) // 4)
@@ -371,14 +383,9 @@
             self.parts[1][(f - ADJ, *key[1:])] = value
 
 
-def window_kernel(
-    cz, ring_f_in, ring_w_in, x_a, x_b, y_a, y_b, corner_aa, corner_ab, corner_ba, corner_bb, own,
-    final, image_lam, image_mu, ring_f, ring_w, packed, keep, images, speeds, sems,
-):
-    cy, lanes = own.shape[2], own.shape[3]
+def strip_rows_kernel(cz, ring_f, ring_w, x_a, x_b, y_a_in, y_b_in, strips, y_a, y_b, packed):
+    cy, lanes = strips.shape[1], strips.shape[2]
     layers = cz + 2 * HALO
-    ring_rows = ring_f.shape[2]
-    ring = Ring(ring_f, ring_w)
     pair = lax.broadcasted_iota(jnp.int32, (cy, lanes), 1) % 8 // 2
     even_x = even_mask("gx", (cy, lanes))
     has_left, has_right = has_neighbours("gx")
@@ -398,15 +405,32 @@
             right = jnp.where(even_x, got[0], got[1]) * has_right
             left = jnp.where(even_x, got[1], got[0]) * has_left
             for g, f in enumerate(quad):
-                tile = jnp.where(pair == 1, pltpu.roll(right, (2 - 2 * g) % lanes, 1), ring[f, layers, 0:cy, :])
-                ring[f, layers, 0:cy, :] = jnp.where(pair == 2, pltpu.roll(left, (4 - 2 * g) % lanes, 1), tile)
+                strip = ring_f[f, layers, 0:cy, :] if f < ADJ else ring_w[f - ADJ, layers, 0:cy, :]
+                tile = jnp.where(pair == 1, pltpu.roll(right, (2 - 2 * g) % lanes, 1), strip)
+                strips[f] = jnp.where(pair == 2, pltpu.roll(left, (4 - 2 * g) % lanes, 1), tile)
         place += len(quads) if narrow else 2 * len(quads)
+    sides = []
+    for side, up in enumerate((True, False)):
+        scatter_rows(packed.at[side], y_rows(cz, cy, up)[2], lambda f, z, y: strips[f, y : y + 1, :])
+        sides.append([packed[side, t] for t in range(row_counts(cz, cy, up)[2])])
+    pack_tiles(sides, (y_a, y_b), 0, packed.shape[1])
+
+
+def window_kernel(
+    cz, ring_f_in, ring_w_in, strips, y_a, y_b, own,
+    final, image_lam, image_mu, ring_f, ring_w, packed, keep, images, speeds, sems,
+):
+    cy, lanes = own.shape[2], own.shape[3]
+    layers = cz + 2 * HALO
+    ring_rows = ring_f.shape[2]
+    ring = Ring(ring_f, ring_w)
+    for f in range(FIELDS):
+        ring[f, layers, 0:cy, :] = strips[f]
 
     def put_row(f, z, y, value):
         ring[f, z, y : y + 1, :] = value
 
-    diagonals = [two for two in ((corner_aa, corner_ab), (corner_ba, corner_bb)) if two[0] is not None]
-    unpack_rows(cz, cy, (y_a, y_b), diagonals, packed, put_row)
+    unpack_rows(cz, cy, (y_a, y_b), packed, put_row)
 
     lane = lax.broadcasted_iota(jnp.int32, (ring_rows, lanes), 1)
     first_lane, last_lane = lane == 0, lane == lanes - 1
@@ -640,30 +664,24 @@
     )
     both = [lax.ppermute(part, "gz", [(i, i ^ 1) for i in range(holders)]) for part in (chip[:half], chip[half:])]
 
+    ring_f, ring_w = kernel_call(
+        functools.partial(frame_kernel, cz),
+        (own,),
+        [vmem()],
+        (shape(ADJ, layers + 1, 2 * cy, cx), shape(FIELDS - ADJ, layers + 1, 2 * cy, cx)),
+    )
     x_send = shape(x_tiles(), cy, cx, dtype=bf16)
-    y_size, corner_size = row_tiles(cz, cy)
-    y_send, corner_send = shape(y_size, cy, cx, dtype=bf16), shape(corner_size, cy, cx, dtype=bf16)
-    row_scratch = pltpu.VMEM((2, max(sum(row_counts(cz, cy, up)) for up in (True, False)), 8, cx), f32)
-    ring_f, ring_w, x_a, x_b, y_a, y_b, corner_a, corner_b = kernel_call(
+    ring_f, ring_w, x_a, x_b = kernel_call(
         functools.partial(column_kernel, cz),
-        (to_core, core, chip, *both, far_face, peer, slot, own),
-        [vmem()] * 9,
-        (
-            shape(ADJ, layers + 1, 2 * cy, cx),
-            shape(FIELDS - ADJ, layers + 1, 2 * cy, cx),
-            x_send,
-            x_send if wide_x else None,
-            y_send,
-            y_send,
-            corner_send,
-            corner_send,
-        ),
+        (to_core, core, chip, *both, far_face, peer, slot, ring_f, ring_w),
+        [vmem()] * 10,
+        (shape(*ring_f.shape), shape(*ring_w.shape), x_send, x_send if wide_x else None),
         [
-            row_scratch,
             pltpu.SMEM(peer.shape, jnp.int32),
             pltpu.SMEM(slot.shape, jnp.int32),
             pltpu.SemaphoreType.DMA((2,)),
         ],
+        {8: 0, 9: 1},
     )
     axes = ("gx", "gy", "gz")
     gx = lax.axis_size("gx")
@@ -685,16 +703,28 @@
         ]
         return lax.ppermute(value, axes, pairs)
 
-    x_turns = (0, 1) if wide_x else (0,)
-    corners = [swap(v, t, u) for t in x_turns for u, v in enumerate((corner_a, corner_b))]
-    corners += [None] * (4 - len(corners))
+    strip_tiles, tiles = row_tiles(cz, cy)
+    y_send = shape(strip_tiles + tiles, cy, cx, dtype=bf16)
+    scratch_tiles = max(sum(row_counts(cz, cy, up)) for up in (True, False))
+    y_a, y_b = kernel_call(
+        functools.partial(layer_rows_kernel, cz),
+        (ring_f, ring_w),
+        [vmem()] * 2,
+        (y_send, y_send),
+        [pltpu.VMEM((2, scratch_tiles, 8, cx), f32)],
+    )
+    strips, y_a, y_b = kernel_call(
+        functools.partial(strip_rows_kernel, cz),
+        (ring_f, ring_w, swap(x_a, 0, None), swap(x_b, 1, None), y_a, y_b),
+        [vmem()] * 6,
+        (shape(FIELDS, cy, cx), y_send, y_send),
+        [pltpu.VMEM((2, strip_tiles, 8, cx), f32)],
+        {4 if wide_x else 3: 1, 5 if wide_x else 4: 2},
+    )
     result = kernel_call(
         functools.partial(window_kernel, cz),
-        (
-            ring_f, ring_w, swap(x_a, 0, None), swap(x_b, 1, None), swap(y_a, None, 0), swap(y_b, None, 1),
-            *corners, own,
-        ),
-        [vmem()] * 11,
+        (ring_f, ring_w, strips, swap(y_a, None, 0), swap(y_b, None, 1), own),
+        [vmem()] * 6,
         (
             shape(9, cz, cy, cx),
             shape(cz, cy, cx),
@@ -703,7 +733,7 @@
             shape(*ring_w.shape),
         ),
         [
-            row_scratch,
+            pltpu.VMEM((2, scratch_tiles, 8, cx), f32),
             pltpu.VMEM((2, cz, cy, cx), f32),
             pltpu.VMEM((2, cz, cy, cx), f32),
             pltpu.VMEM((3, cz, cy, cx), f32),

time: 24.7 us -> 23.6 us (0.955)
  starting transfers between devices: 14.8 us -> 10.8 us
  waiting for transfers between devices: 3.83 us -> 6.65 us
    ppermute x5 -> x3, starting transfers between devices: 9.57 us -> 5.63 us  [swap(): return lax.ppermute(value, axes, pairs)]
    ppermute x5 -> x3, waiting for transfers between devices: 1.61 us -> 4.64 us  [swap(): return lax.ppermute(value, axes, pairs)]
    pallas_call x3 -> x6, Pallas kernels: 5.26 us -> 5.26 us  [kernel_call(): pl.pallas_call(run, out_shape=tuple((o for o in out_shape if o is not Non...]
  transfers between devices with their start and end apart: 10 -> 8, of which waited for: 4 -> 5; matrix products, arithmetic and copies ran while one was open for 0% -> 0% of each run, Pallas kernels for 5% -> 8%
where the time goes in v8:
time: 23.6 us; the launch traced here: 23.5 us
  starting transfers between devices  10.8 us (46%)
  waiting for transfers between devices  6.65 us (28%)
  Pallas kernels  5.26 us (22%)
  between operations  0.68 us (3%)
    ppermute x3, starting transfers between devices, swap(): return lax.ppermute(value, axes, pairs)  5.63 us
    pallas_call x6, Pallas kernels, kernel_call(): pl.pallas_call(run, out_shape=tuple((o for o in out_shape if o is not Non...  5.26 us
    ppermute x3, waiting for transfers between devices, swap(): return lax.ppermute(value, axes, pairs)  4.64 us
    ppermute x1, starting transfers between devices, on_device(): chip = lax.ppermute(store, 'gz', [(i, i ^ 2) for i in range(holders)])  3 us
    ppermute x1, starting transfers between devices, on_device(): lax.ppermute(to_far, ('gy', 'gz'), [(a[0] * holders + a[1], b[0] * holder...  1.64 us
    ppermute x1, waiting for transfers between devices, on_device(): chip = lax.ppermute(store, 'gz', [(i, i ^ 2) for i in range(holders)])  1.29 us
    ppermute x1, waiting for transfers between devices, on_device(): lax.ppermute(to_far, ('gy', 'gz'), [(a[0] * holders + a[1], b[0] * holder...  0.72 us
    ppermute x2, starting transfers between devices, on_device(): lax.ppermute(part, 'gz', [(i, i ^ 1) for i in range(holders)])  0.57 us
  transfers between devices with their start and end apart: 8, of which 5 were waited for; matrix products, arithmetic and copies ran while one was open for 0% of the time, Pallas kernels for 8%

profile of v8, /device:TPU:0, one launch (start us, length us, event | category | flops | bytes accessed | tf_op | source)
XLA Modules:
  0.0 23.5 jit_solution(9232742340731073325)
XLA Ops:
  0.6 3.0 %collective-permute-start.1 = (bf16[72,8,128]{2,1,0:T(8,128)(2,1)}, bf16[72,8,128]{2,1,0:T(8,128)(2,1)S(1)}, u32[]{:S(2)}, u32[]{:S(2)}) collective-permute-start(bf16[72,8,128]{2,1,0:T(8,128)(2,1)} %bitcast.6), channel_id=1, source_target_pairs={{0,2},{1,3},{2,0},{3,1},{4,6},{5,7},{6,4},{7,5},{8,10},{9,11},{10,... | collective-permute-start | bytes 442376 | tf_op jit(solution)/shard_map/ppermute | solution.py:640
  3.6 1.3 %shard_map.139 = (bf16[107,8,128]{2,1,0:T(8,128)(2,1)S(1)}, bf16[37,8,128]{2,1,0:T(8,128)(2,1)S(1)}, f32[15,8,8,128]{3,2,1,0:T(8,128)S(1)}, s32[4,8]{1,0:T(4,128)S(1)}, s32[4,8]{1,0:T(4,128)S(1)}) custom-call(bf16[72,8,128]{2,1,0:T(8,128)(2,1)} %bitcast.7, f32[9,8,8,128]{3,2,1,0:T(8,128)} %refs_1_.1, f32[8,8,128]{2,1,0:T(8,128)} %refs_2_.1, ...), custom_call_target="tpu_custom_call" | custom-call | tf_op jit(solution)/shard_map/pallas_call | solution.py:595
  4.9 1.6 %collective-permute-start.4 = (bf16[37,8,128]{2,1,0:T(8,128)(2,1)S(1)}, bf16[37,8,128]{2,1,0:T(8,128)(2,1)S(1)}, u32[]{:S(2)}, u32[]{:S(2)}) collective-permute-start(bf16[37,8,128]{2,1,0:T(8,128)(2,1)S(1)} %get-tuple-element.22), channel_id=1, source_target_pairs={{0,4},{1,2},{2,1},{3,7},{4,0},{5,6},{6,5},{7,3},{8,12},{9,10},{10,... | collective-permute-start | bytes 227336 | tf_op jit(solution)/shard_map/ppermute | solution.py:662
  6.6 0.0 collective-permute-start
  6.6 1.3 %collective-permute-done.1.refs_2_ = bf16[72,8,128]{2,1,0:T(8,128)(2,1)S(1)} collective-permute-done((bf16[72,8,128]{2,1,0:T(8,128)(2,1)}, bf16[72,8,128]{2,1,0:T(8,128)(2,1)S(1)}, u32[]{:S(2)}, u32[]{:S(2)}) %collective-permute-start.1) | collective-permute-done | bytes 147488 | tf_op jit(solution)/shard_map/ppermute | solution.py:640
  7.9 0.1 collective-permute-start.3
  8.0 0.5 %collective-permute-start.2 = (bf16[36,8,128]{2,1,0:T(8,128)(2,1)S(1)}, bf16[36,8,128]{2,1,0:T(8,128)(2,1)S(1)}, u32[]{:S(2)}, u32[]{:S(2)}) collective-permute-start(bf16[36,8,128]{2,1,0:T(8,128)(2,1)S(1)} %get-tuple-element.40), channel_id=1, source_target_pairs={{0,1},{1,0},{2,3},{3,2},{4,5},{5,4},{6,7},{7,6},{8,9},{9,8},{10,11... | collective-permute-start | bytes 221192 | tf_op jit(solution)/shard_map/ppermute | solution.py:665
  8.5 0.2 shard_map.140
  8.7 0.7 %collective-permute-done.4.refs_5_ = bf16[37,8,128]{2,1,0:T(8,128)(2,1)S(1)} collective-permute-done((bf16[37,8,128]{2,1,0:T(8,128)(2,1)S(1)}, bf16[37,8,128]{2,1,0:T(8,128)(2,1)S(1)}, u32[]{:S(2)}, u32[]{:S(2)}) %collective-permute-start.4) | collective-permute-done | bytes 75808 | tf_op jit(solution)/shard_map/ppermute | solution.py:662
  9.4 0.0 collective-permute-done.refs_1_
  9.4 0.0 collective-permute-done.3.refs_4_
  9.4 0.0 collective-permute-done.2.refs_3_
  9.4 1.1 %shard_map.141 = (f32[9,13,16,128]{3,2,1,0:T(8,128)S(1)}, f32[14,13,16,128]{3,2,1,0:T(8,128)S(1)}, bf16[11,8,128]{2,1,0:T(8,128)(2,1)S(1)}) custom-call(bf16[107,8,128]{2,1,0:T(8,128)(2,1)S(1)} %get-tuple-element.21.refs_0_, bf16[107,8,128]{2,1,0:T(8,128)(2,1)S(1)} %collective-permute-done.refs_1_, ...), custom_call_target="tpu_custom_call", output_to_operand_aliasing={{0}: (8, {}), {1}: (9, {})} | custom-call | tf_op jit(solution)/shard_map/pallas_call | solution.py:595
  10.5 1.6 %collective-permute-start.5 = (bf16[11,8,128]{2,1,0:T(8,128)(2,1)S(1)}, bf16[11,8,128]{2,1,0:T(8,128)(2,1)S(1)}, u32[]{:S(2)}, u32[]{:S(2)}) collective-permute-start(bf16[11,8,128]{2,1,0:T(8,128)(2,1)S(1)} %get-tuple-element.30), channel_id=1, source_target_pairs={{0,16},{1,17},{2,18},{3,19},{4,20},{5,21},{6,22},{7,23},{8,24},{9,... | collective-permute-start | bytes 67592 | tf_op jit(solution)/shard_map/ppermute | solution.py:704
  12.1 0.3 %shard_map.142 = (bf16[52,8,128]{2,1,0:T(8,128)(2,1)S(1)}, bf16[52,8,128]{2,1,0:T(8,128)(2,1)S(1)}) custom-call(f32[9,13,16,128]{3,2,1,0:T(8,128)S(1)} %get-tuple-element.28.refs_0_, f32[14,13,16,128]{3,2,1,0:T(8,128)S(1)} %get-tuple-element.29.refs_1_), custom_call_target="tpu_custom_call" | custom-call | tf_op jit(solution)/shard_map/pallas_call | solution.py:595
  12.4 2.0 %collective-permute-done.5.refs_2_ = bf16[11,8,128]{2,1,0:T(8,128)(2,1)S(1)} collective-permute-done((bf16[11,8,128]{2,1,0:T(8,128)(2,1)S(1)}, bf16[11,8,128]{2,1,0:T(8,128)(2,1)S(1)}, u32[]{:S(2)}, u32[]{:S(2)}) %collective-permute-start.5) | collective-permute-done | bytes 22560 | tf_op jit(solution)/shard_map/ppermute | solution.py:704
  14.3 0.1 shard_map.143
  14.5 1.7 %collective-permute-start.6 = (bf16[52,8,128]{2,1,0:T(8,128)(2,1)S(1)}, bf16[52,8,128]{2,1,0:T(8,128)(2,1)S(1)}, u32[]{:S(2)}, u32[]{:S(2)}) collective-permute-start(bf16[52,8,128]{2,1,0:T(8,128)(2,1)S(1)} %get-tuple-element.34), channel_id=1, source_target_pairs={{0,4},{1,3},{2,6},{3,1},{4,0},{5,9},{6,2},{7,11},{8,12},{9,5},{10,... | collective-permute-start | bytes 319496 | tf_op jit(solution)/shard_map/ppermute | solution.py:704
  16.2 2.3 %collective-permute-start.7 = (bf16[52,8,128]{2,1,0:T(8,128)(2,1)S(1)}, bf16[52,8,128]{2,1,0:T(8,128)(2,1)S(1)}, u32[]{:S(2)}, u32[]{:S(2)}) collective-permute-start(bf16[52,8,128]{2,1,0:T(8,128)(2,1)S(1)} %get-tuple-element.35), channel_id=1, source_target_pairs={{0,2},{1,5},{2,0},{3,7},{4,8},{5,1},{6,10},{7,3},{8,4},{9,13},{10,... | collective-permute-start | bytes 319496 | tf_op jit(solution)/shard_map/ppermute | solution.py:704
  18.5 1.6 %collective-permute-done.6.refs_3_ = bf16[52,8,128]{2,1,0:T(8,128)(2,1)S(1)} collective-permute-done((bf16[52,8,128]{2,1,0:T(8,128)(2,1)S(1)}, bf16[52,8,128]{2,1,0:T(8,128)(2,1)S(1)}, u32[]{:S(2)}, u32[]{:S(2)}) %collective-permute-start.6) | collective-permute-done | bytes 106528 | tf_op jit(solution)/shard_map/ppermute | solution.py:704
  20.1 1.1 %collective-permute-done.7.refs_4_ = bf16[52,8,128]{2,1,0:T(8,128)(2,1)S(1)} collective-permute-done((bf16[52,8,128]{2,1,0:T(8,128)(2,1)S(1)}, bf16[52,8,128]{2,1,0:T(8,128)(2,1)S(1)}, u32[]{:S(2)}, u32[]{:S(2)}) %collective-permute-start.7) | collective-permute-done | bytes 106528 | tf_op jit(solution)/shard_map/ppermute | solution.py:704
  21.2 2.3 %shard_map.144 = (f32[9,8,8,128]{3,2,1,0:T(8,128)}, f32[8,8,128]{2,1,0:T(8,128)}, f32[8,8,128]{2,1,0:T(8,128)}, f32[9,13,16,128]{3,2,1,0:T(8,128)S(1)}, f32[14,13,16,128]{3,2,1,0:T(8,128)S(1)}) custom-call(f32[9,13,16,128]{3,2,1,0:T(8,128)S(1)} %get-tuple-element.28.refs_0_, ...), custom_call_target="tpu_custom_call", output_to_operand_aliasing={{3}: (0, {}), {4}: (1, {})} | custom-call | tf_op jit(solution)/shard_map/pallas_call | solution.py:595
  (1 shorter events, 0.0 us)
Async XLA Ops:
  0.6 7.2 %collective-permute-start.1 = (bf16[72,8,128]{2,1,0:T(8,128)(2,1)}, bf16[72,8,128]{2,1,0:T(8,128)(2,1)S(1)}, u32[]{:S(2)}, u32[]{:S(2)}) collective-permute-start(bf16[72,8,128]{2,1,0:T(8,128)(2,1)} %bitcast.6), channel_id=1, source_target_pairs={{0,2},{1,3},{2,0},{3,1},{4,6},{5,7},{6,4},{7,5},{8,10},{9,11},{10,... | collective-permute-start | bytes 442376 | tf_op jit(solution)/shard_map/ppermute | solution.py:640
  4.9 4.4 %collective-permute-start.4 = (bf16[37,8,128]{2,1,0:T(8,128)(2,1)S(1)}, bf16[37,8,128]{2,1,0:T(8,128)(2,1)S(1)}, u32[]{:S(2)}, u32[]{:S(2)}) collective-permute-start(bf16[37,8,128]{2,1,0:T(8,128)(2,1)S(1)} %get-tuple-element.22), channel_id=1, source_target_pairs={{0,4},{1,2},{2,1},{3,7},{4,0},{5,6},{6,5},{7,3},{8,12},{9,10},{10,... | collective-permute-start | bytes 227336 | tf_op jit(solution)/shard_map/ppermute | solution.py:662
  6.6 2.8 %collective-permute-start = (bf16[107,8,128]{2,1,0:T(8,128)(2,1)S(1)}, bf16[107,8,128]{2,1,0:T(8,128)(2,1)S(1)}, u32[]{:S(2)}, u32[]{:S(2)}) collective-permute-start(bf16[107,8,128]{2,1,0:T(8,128)(2,1)S(1)} %get-tuple-element.21.refs_0_), channel_id=1, source_target_pairs={{0,1},{1,0},{2,3},{3,2},{4,5},{5,4},{6,7},{7,6},{8,9},{9,8},{10,11... | collective-permute-start | bytes 657416 | tf_op jit(solution)/shard_map/ppermute | solution.py:656
  7.9 1.5 %collective-permute-start.3 = (bf16[36,8,128]{2,1,0:T(8,128)(2,1)S(1)}, bf16[36,8,128]{2,1,0:T(8,128)(2,1)S(1)}, u32[]{:S(2)}, u32[]{:S(2)}) collective-permute-start(bf16[36,8,128]{2,1,0:T(8,128)(2,1)S(1)} %get-tuple-element.39), channel_id=1, source_target_pairs={{0,1},{1,0},{2,3},{3,2},{4,5},{5,4},{6,7},{7,6},{8,9},{9,8},{10,11... | collective-permute-start | bytes 221192 | tf_op jit(solution)/shard_map/ppermute | solution.py:665
  8.0 1.4 %collective-permute-start.2 = (bf16[36,8,128]{2,1,0:T(8,128)(2,1)S(1)}, bf16[36,8,128]{2,1,0:T(8,128)(2,1)S(1)}, u32[]{:S(2)}, u32[]{:S(2)}) collective-permute-start(bf16[36,8,128]{2,1,0:T(8,128)(2,1)S(1)} %get-tuple-element.40), channel_id=1, source_target_pairs={{0,1},{1,0},{2,3},{3,2},{4,5},{5,4},{6,7},{7,6},{8,9},{9,8},{10,11... | collective-permute-start | bytes 221192 | tf_op jit(solution)/shard_map/ppermute | solution.py:665
  10.5 3.9 %collective-permute-start.5 = (bf16[11,8,128]{2,1,0:T(8,128)(2,1)S(1)}, bf16[11,8,128]{2,1,0:T(8,128)(2,1)S(1)}, u32[]{:S(2)}, u32[]{:S(2)}) collective-permute-start(bf16[11,8,128]{2,1,0:T(8,128)(2,1)S(1)} %get-tuple-element.30), channel_id=1, source_target_pairs={{0,16},{1,17},{2,18},{3,19},{4,20},{5,21},{6,22},{7,23},{8,24},{9,... | collective-permute-start | bytes 67592 | tf_op jit(solution)/shard_map/ppermute | solution.py:704
  14.5 5.6 %collective-permute-start.6 = (bf16[52,8,128]{2,1,0:T(8,128)(2,1)S(1)}, bf16[52,8,128]{2,1,0:T(8,128)(2,1)S(1)}, u32[]{:S(2)}, u32[]{:S(2)}) collective-permute-start(bf16[52,8,128]{2,1,0:T(8,128)(2,1)S(1)} %get-tuple-element.34), channel_id=1, source_target_pairs={{0,4},{1,3},{2,6},{3,1},{4,0},{5,9},{6,2},{7,11},{8,12},{9,5},{10,... | collective-permute-start | bytes 319496 | tf_op jit(solution)/shard_map/ppermute | solution.py:704
  16.2 5.0 %collective-permute-start.7 = (bf16[52,8,128]{2,1,0:T(8,128)(2,1)S(1)}, bf16[52,8,128]{2,1,0:T(8,128)(2,1)S(1)}, u32[]{:S(2)}, u32[]{:S(2)}) collective-permute-start(bf16[52,8,128]{2,1,0:T(8,128)(2,1)S(1)} %get-tuple-element.35), channel_id=1, source_target_pairs={{0,2},{1,5},{2,0},{3,7},{4,8},{5,1},{6,10},{7,3},{8,4},{9,13},{10,... | collective-permute-start | bytes 319496 | tf_op jit(solution)/shard_map/ppermute | solution.py:704

commit v9 on v8

--- a/solution.py
+++ b/solution.py
@@ -81,7 +81,7 @@
             if spec is None:
                 continue
             source = cy + offset if up else offset
-            target = 2 * cy + offset if up else cy + offset
+            target = cy - HALO + offset if up else HALO + offset
             exact = f in EXACT_ROWS.get(offset, ())
             (wide if exact else narrow).extend((f, z, source, target) for z in range(spec[0], layers + spec[1]))
             if spec[2]:
@@ -139,7 +139,7 @@
 
 
 def layer_rows_kernel(cz, ring_f, ring_w, send_a, send_b, packed):
-    cy = ring_f.shape[2] // 2
+    cy = ring_f.shape[2]
     strip_tiles, tiles = row_tiles(cz, cy)
 
     def row_of(f, z, y):
@@ -262,29 +262,22 @@
     return jnp.where(position < 2, tile, jnp.where(position >= 6, pltpu.roll(tile, 4, 1), 0.0))
 
 
-def frame_kernel(cz, own, ring_f, ring):
+def frame_kernel(cz, own, ring):
     cy, lanes = own.shape[2], own.shape[3]
     layers = cz + 2 * HALO
-    ring_rows = ring.shape[2]
     zero = jnp.zeros((cy, lanes), jnp.float32)
-    beyond = jnp.zeros((ring_rows - cy, lanes), jnp.float32)
     filled = {(f - ADJ, z) for up in (True, False) for listed in faces(cz, up) for f, _, z in listed}
     for f in range(ring.shape[0]):
         for z in range(cz):
-            ring[f, HALO + z, 0:cy, :] = own[f, z]
+            ring[f, HALO + z] = own[f, z]
         for z in (0, 1, layers - 2, layers - 1):
             if (f, z) not in filled:
-                ring[f, z, 0:cy, :] = zero
-        ring[f, layers, 0:cy, :] = strip_part(zero, lambda z: own[f, z - HALO], range(HALO, HALO + cz))
-        for z in range(layers + 1):
-            ring[f, z, cy:ring_rows, :] = beyond
-    for f in range(ring_f.shape[0]):
-        for z in range(layers + 1):
-            ring_f[f, z, cy:ring_rows, :] = beyond
+                ring[f, z] = zero
+        ring[f, layers] = strip_part(zero, lambda z: own[f, z - HALO], range(HALO, HALO + cz))
 
 
 def column_kernel(
-    cz, mine, core, chip, both_a, both_b, far, peer, slot, ring_f_in, ring_w_in,
+    cz, mine, core, chip, both_a, both_b, far, peer, slot, ring_w_in,
     ring_f, ring, x_a, x_b, peers, slots, sems,
 ):
     cy, lanes = chip.shape[1], chip.shape[2]
@@ -310,13 +303,13 @@
                         values.append(ref[base + 2 * near + i].astype(jnp.float32))
                 value = jnp.where(even, values[1], values[0]) if up else jnp.where(even, values[0], values[1])
                 value = value * (has_below if up else has_above)
-                ring[f - ADJ, z, 0:cy, :] = value
+                ring[f - ADJ, z] = value
                 filled.setdefault(f - ADJ, {})[z] = value
     strip = []
     for f in range(ring.shape[0]):
         there = filled.get(f, {})
-        tile = strip_whole(strip_part(ring[f, layers, 0:cy, :], lambda z: there[z], sorted(there)))
-        ring[f, layers, 0:cy, :] = tile
+        tile = strip_whole(strip_part(ring[f, layers], lambda z: there[z], sorted(there)))
+        ring[f, layers] = tile
         strip.append(tile)
     for move in moves:
         move.wait()
@@ -337,10 +330,10 @@
             parts = [part.astype(jnp.float32) for part in parts]
             value = jnp.where(late, parts[4], parts[3])
             value = jnp.where(hops < 2, jnp.where(hops == 1, parts[1], parts[0]), jnp.where(hops == 2, parts[2], value))
-            ring_f[f, z, 0:cy, :] = value if keep is None else value * keep
+            ring_f[f, z] = value if keep is None else value * keep
     for f in range(9):
-        ring_f[f, layers, 0:cy, :] = strip_whole(strip_part(zero, lambda z: ring_f[f, z, 0:cy, :], range(layers)))
-    strip = [ring_f[f, layers, 0:cy, :] for f in range(9)] + strip
+        ring_f[f, layers] = strip_whole(strip_part(zero, lambda z: ring_f[f, z], range(layers)))
+    strip = [ring_f[f, layers] for f in range(9)] + strip
     position = lax.broadcasted_iota(jnp.int32, (cy, lanes), 1) % 8
     even_x = even_mask("gx", (cy, lanes))
     for out, tail_from_even in ((x_a, True), (x_b, False)):
@@ -365,22 +358,6 @@
 
 def x_tiles():
     return -(-ADJ // 4) + 2 * -(-(FIELDS - ADJ) // 4)
-
-
-class Ring:
-    def __init__(self, ring_f, ring_w):
-        self.parts = ring_f, ring_w
-
-    def __getitem__(self, key):
-        f = key[0]
-        return self.parts[0][key] if f < ADJ else self.parts[1][(f - ADJ, *key[1:])]
-
-    def __setitem__(self, key, value):
-        f = key[0]
-        if f < ADJ:
-            self.parts[0][key] = value
-        else:
-            self.parts[1][(f - ADJ, *key[1:])] = value
 
 
 def strip_rows_kernel(cz, ring_f, ring_w, x_a, x_b, y_a_in, y_b_in, strips, y_a, y_b, packed):
@@ -405,7 +382,7 @@
             right = jnp.where(even_x, got[0], got[1]) * has_right
             left = jnp.where(even_x, got[1], got[0]) * has_left
             for g, f in enumerate(quad):
-                strip = ring_f[f, layers, 0:cy, :] if f < ADJ else ring_w[f - ADJ, layers, 0:cy, :]
+                strip = ring_f[f, layers] if f < ADJ else ring_w[f - ADJ, layers]
                 tile = jnp.where(pair == 1, pltpu.roll(right, (2 - 2 * g) % lanes, 1), strip)
                 strips[f] = jnp.where(pair == 2, pltpu.roll(left, (4 - 2 * g) % lanes, 1), tile)
         place += len(quads) if narrow else 2 * len(quads)
@@ -416,153 +393,208 @@
     pack_tiles(sides, (y_a, y_b), 0, packed.shape[1])
 
 
-def window_kernel(
-    cz, ring_f_in, ring_w_in, strips, y_a, y_b, own,
-    final, image_lam, image_mu, ring_f, ring_w, packed, keep, images, speeds, sems,
-):
-    cy, lanes = own.shape[2], own.shape[3]
+STAGE = {"fv": 0, "fs": 3, "fw": 9, "as": 12, "av": 18, "at": 21}
+STAGES = 27
+NORMAL = (SXX, SYY, SZZ)
+STRESS = range(SXX, SYZ + 1)
+
+
+def window(cz, base, stage, after, before, put):
     layers = cz + 2 * HALO
-    ring_rows = ring_f.shape[2]
-    ring = Ring(ring_f, ring_w)
-    for f in range(FIELDS):
-        ring[f, layers, 0:cy, :] = strips[f]
-
-    def put_row(f, z, y, value):
-        ring[f, z, y : y + 1, :] = value
-
-    unpack_rows(cz, cy, (y_a, y_b), packed, put_row)
-
-    lane = lax.broadcasted_iota(jnp.int32, (ring_rows, lanes), 1)
+    edge = layers
+    cy, lanes = stage.shape[2], stage.shape[3]
+    lane = lax.broadcasted_iota(jnp.int32, (cy, lanes), 1)
     first_lane, last_lane = lane == 0, lane == lanes - 1
-    edge = layers
-
-    def at(f, z):
-        return ring[f, z]
-
-    def x_next(f, z):
-        value = at(f, z)
+    inner = range(HALO, HALO + cz)
+
+    def start(field):
+        return lambda z: base(field, z)
+
+    def kept(name, field):
+        index = STAGE[name] + field
+        return lambda z: stage[index, z]
+
+    def x_next(of, z):
+        value = pltpu.roll(of(z), lanes - 1, 1)
         if z == edge:
-            return pltpu.roll(value, lanes - 1, 1)
-        beyond = pltpu.roll(at(f, edge), (lanes - 1 - (8 * z + 2)) % lanes, 1)
-        return jnp.where(last_lane, beyond, pltpu.roll(value, lanes - 1, 1))
-
-    def x_prev(f, z):
-        value = at(f, z)
+            return value
+        return jnp.where(last_lane, pltpu.roll(of(edge), (lanes - 1 - (8 * z + 2)) % lanes, 1), value)
+
+    def x_prev(of, z):
+        value = pltpu.roll(of(z), 1, 1)
         if z == edge:
-            return pltpu.roll(value, 1, 1)
-        beyond = pltpu.roll(at(f, edge), (lanes - (8 * z + 5)) % lanes, 1)
-        return jnp.where(first_lane, beyond, pltpu.roll(value, 1, 1))
-
-    def y_next(f, z):
-        return pltpu.roll(at(f, z), ring_rows - 1, 0)
-
-    def y_prev(f, z):
-        return pltpu.roll(at(f, z), 1, 0)
-
-    def z_next(f, z):
-        return pltpu.roll(at(f, edge), lanes - 8, 1) if z == edge else at(f, z + 1)
-
-    def z_prev(f, z):
-        return pltpu.roll(at(f, edge), 8, 1) if z == edge else at(f, z - 1)
-
-    def velocity_rates(base, z, want):
-        buoy = at(BUOY, z)
-        sxx, syy, szz = (functools.partial(at, base + f) for f in (SXX, SYY, SZZ))
-        sxy, sxz, syz = (functools.partial(at, base + f) for f in (SXY, SXZ, SYZ))
+            return value
+        return jnp.where(first_lane, pltpu.roll(of(edge), (lanes - (8 * z + 5)) % lanes, 1), value)
+
+    def z_next(of, z):
+        return pltpu.roll(of(edge), lanes - 8, 1) if z == edge else of(z + 1)
+
+    def z_prev(of, z):
+        return pltpu.roll(of(edge), 8, 1) if z == edge else of(z - 1)
+
+    def velocity_rates(k, s, z, want):
+        buoy = base(BUOY, z)
+        sxx, syy, szz, sxy, sxz, syz = s
         out = {}
         if VX in want:
+            xy = sxy(z)
             out[VX] = buoy * (
-                (x_next(base + SXX, z) - sxx(z)) + (sxy(z) - y_prev(base + SXY, z)) + (sxz(z) - z_prev(base + SXZ, z))
+                (x_next(sxx, z) - sxx(z)) + (xy - before(k, 0, z, xy)) + (sxz(z) - z_prev(sxz, z))
             )
         if VY in want:
+            yy = syy(z)
             out[VY] = buoy * (
-                (sxy(z) - x_prev(base + SXY, z)) + (y_next(base + SYY, z) - syy(z)) + (syz(z) - z_prev(base + SYZ, z))
+                (sxy(z) - x_prev(sxy, z)) + (after(k, 1, z, yy) - yy) + (syz(z) - z_prev(syz, z))
             )
         if VZ in want:
+            yz = syz(z)
             out[VZ] = buoy * (
-                (sxz(z) - x_prev(base + SXZ, z)) + (syz(z) - y_prev(base + SYZ, z)) + (z_next(base + SZZ, z) - szz(z))
+                (sxz(z) - x_prev(sxz, z)) + (yz - before(k, 2, z, yz)) + (z_next(szz, z) - szz(z))
             )
         return out
 
-    def stress_rates(base, z, want):
-        lam, mu = at(LAM, z), at(MU, z)
-        vx, vy, vz = at(base + VX, z), at(base + VY, z), at(base + VZ, z)
+    def stress_rates(k, v, z, want):
+        lam, mu = base(LAM, z), base(MU, z)
+        of_x, of_y, of_z = v
+        vx, vy, vz = of_x(z), of_y(z), of_z(z)
         out = {}
         if SXX in want:
-            exx = vx - x_prev(base + VX, z)
-            eyy = vy - y_prev(base + VY, z)
-            ezz = vz - z_prev(base + VZ, z)
+            exx = vx - x_prev(of_x, z)
+            eyy = vy - before(k, 0, z, vy)
+            ezz = vz - z_prev(of_z, z)
             common = lam * (exx + eyy + ezz)
             twice = 2.0 * mu
             out[SXX] = common + twice * exx
             out[SYY] = common + twice * eyy
             out[SZZ] = common + twice * ezz
         if SXY in want:
-            out[SXY] = mu * ((y_next(base + VX, z) - vx) + (x_next(base + VY, z) - vy))
+            out[SXY] = mu * ((after(k, 1, z, vx) - vx) + (x_next(of_y, z) - vy))
         if SXZ in want:
-            out[SXZ] = mu * ((z_next(base + VX, z) - vx) + (x_next(base + VZ, z) - vz))
-            out[SYZ] = mu * ((z_next(base + VY, z) - vy) + (y_next(base + VZ, z) - vz))
+            out[SXZ] = mu * ((z_next(of_x, z) - vx) + (x_next(of_z, z) - vz))
+            out[SYZ] = mu * ((z_next(of_y, z) - vy) + (after(k, 2, z, vz) - vz))
         return out
 
     def spread(ranges):
-        for z in list(range(layers)) + [edge]:
+        for z in range(layers + 1):
             want = {f for f, (a, b) in ranges.items() if z == edge or a <= z < b}
             if want:
                 yield z, want
 
-    def velocity_step(base, sign, ranges):
+    def velocity_step(k, name, v, s, sign, ranges):
         for z, want in spread(ranges):
-            for f, rate in velocity_rates(base, z, want).items():
-                ring[base + f, z] = at(base + f, z) + rate if sign > 0 else at(base + f, z) - rate
-
-    def stress_step(base, sign, ranges, before=None, after=None):
+            for f, rate in velocity_rates(k, s, z, want).items():
+                stage[STAGE[name] + f, z] = v[f](z) + rate if sign > 0 else v[f](z) - rate
+        return [kept(name, f) for f in (VX, VY, VZ)]
+
+    def stress_step(k, name, v, s, sign, ranges, ahead=None, behind=None):
         for z, want in spread(ranges):
-            for f, rate in stress_rates(base, z, want).items():
-                value, normal = at(base + f, z), f in (SXX, SYY, SZZ)
-                if before is not None and normal:
-                    value = value + at(before, z)
+            for f, rate in stress_rates(k, v, z, want).items():
+                value = s[f - SXX](z)
+                if ahead is not None and f in NORMAL:
+                    value = value + base(ahead, z)
                 value = value + rate if sign > 0 else value - rate
-                if after is not None and normal:
-                    value = value + at(after, z)
-                ring[base + f, z] = value
+                if behind is not None and f in NORMAL:
+                    value = value + base(behind, z)
+                stage[STAGE[name] + f - SXX, z] = value
+        return [kept(name, f - SXX) for f in STRESS]
 
     def terms(f, a):
         term_lam = (f[0] + f[1] + f[2]) * (a[0] + a[1] + a[2])
         term_mu = f[0] * a[0] + f[1] * a[1] + f[2] * a[2] + 2.0 * (f[3] * a[3] + f[4] * a[4] + f[5] * a[5])
         return term_lam, term_mu
 
-    inner = (HALO, HALO + cz)
     n = layers
-    stress_step(ADJ, -1, {SXX: (1, n), SXY: (0, n), SXZ: (0, n - 1)})
-    velocity_step(FWD, 1, {VX: (1, n), VY: (1, n), VZ: (0, n - 1)})
-    stress_step(FWD, 1, {SXX: (1, n - 1), SXY: (1, n - 1), SXZ: (1, n - 1)}, after=SRC)
-    for z in range(*inner):
-        f = [ring[FWD + s, z, 0:cy, :] for s in range(SXX, SYZ + 1)]
-        a = [ring[ADJ + s, z, 0:cy, :] for s in range(SXX, SYZ + 1)]
-        a = [value + ring[INJ, z, 0:cy, :] for value in a[:3]] + a[3:]
-        keep[0, z - HALO], keep[1, z - HALO] = terms(f, a)
-    velocity_step(FWD, 1, {VX: (2, n - 1), VY: (2, n - 1), VZ: (1, n - 2)})
-    everything = set(range(SXX, SYZ + 1))
-    for z in range(*inner):
-        rates = stress_rates(FWD, z, everything)
-        f = []
-        for s in range(SXX, SYZ + 1):
-            value = (at(FWD + s, z) + rates[s])[0:cy, :]
-            f.append(value + own[SRC - ADJ + 1, z - HALO] if s <= SZZ else value)
-        a = [own[s, z - HALO] for s in range(SXX, SYZ + 1)]
-        term_lam, term_mu = terms(f, a)
-        images[0, z - HALO] = term_lam + keep[0, z - HALO]
-        images[1, z - HALO] = term_mu + keep[1, z - HALO]
-    moves = copies(sems, (images.at[0], image_lam), (images.at[1], image_mu))
-    velocity_step(ADJ, -1, {VX: (1, n - 1), VY: (1, n - 1), VZ: (1, n - 1)})
-    stress_step(ADJ, -1, {SXX: (2, n - 1), SXY: (1, n - 1), SXZ: (1, n - 2)}, before=INJ)
-    stresses = ring_w.at[pl.ds(SXX, SYZ + 1 - SXX), pl.ds(HALO, cz), pl.ds(0, cy)]
-    moves += copies(sems.at[pl.ds(2, 1)], (stresses, final.at[pl.ds(SXX, SYZ + 1 - SXX)]))
-    for z in range(*inner):
-        rates = velocity_rates(ADJ, z, {VX, VY, VZ})
+    fv, fs = [start(FWD + f) for f in (VX, VY, VZ)], [start(FWD + f) for f in STRESS]
+    av, first = [start(ADJ + f) for f in (VX, VY, VZ)], [start(ADJ + f) for f in STRESS]
+    a_s = stress_step(0, "as", av, first, -1, {SXX: (1, n), SXY: (0, n), SXZ: (0, n - 1)})
+    fv = velocity_step(1, "fv", fv, fs, 1, {VX: (1, n), VY: (1, n), VZ: (0, n - 1)})
+    fs = stress_step(2, "fs", fv, fs, 1, {SXX: (1, n - 1), SXY: (1, n - 1), SXZ: (1, n - 1)}, behind=SRC)
+    fv = velocity_step(3, "fw", fv, fs, 1, {VX: (2, n - 1), VY: (2, n - 1), VZ: (1, n - 2)})
+    for z in inner:
+        rates = stress_rates(4, fv, z, set(STRESS))
+        now = [of(z) for of in fs]
+        later = [now[s - SXX] + rates[s] + (base(FIELDS, z) if s in NORMAL else 0.0) for s in STRESS]
+        lam_late, mu_late = terms(later, [of(z) for of in first])
+        with_traces = [of(z) + (base(INJ, z) if s in NORMAL else 0.0) for s, of in zip(STRESS, a_s)]
+        lam_early, mu_early = terms(now, with_traces)
+        put(9, z - HALO, lam_late + lam_early)
+        put(10, z - HALO, mu_late + mu_early)
+    av = velocity_step(5, "av", av, a_s, -1, {VX: (1, n - 1), VY: (1, n - 1), VZ: (1, n - 1)})
+    a_s = stress_step(6, "at", av, a_s, -1, {SXX: (2, n - 1), SXY: (1, n - 1), SXZ: (1, n - 2)}, ahead=INJ)
+    for s, of in zip(STRESS, a_s):
+        for z in inner:
+            put(s, z - HALO, of(z))
+    for z in inner:
+        rates = velocity_rates(7, a_s, z, {VX, VY, VZ})
         for f in (VX, VY, VZ):
-            speeds[f, z - HALO] = (at(ADJ + f, z) - rates[f])[0:cy, :]
-    moves += copies(sems.at[pl.ds(3, 1)], (speeds, final.at[pl.ds(VX, VZ + 1 - VX)]))
+            put(f, z - HALO, av[f](z) - rates[f])
+
+
+def middle_kernel(cz, ring_f, ring_w, strips, own, edges, sides, middle, stage):
+    cy, lanes = own.shape[2], own.shape[3]
+    layers = cz + 2 * HALO
+
+    def base(f, z):
+        if f == FIELDS:
+            return own[f - ADJ, z - HALO]
+        if z == layers:
+            return strips[f]
+        return ring_f[f, z] if f < ADJ else ring_w[f - ADJ, z]
+
+    row = lax.broadcasted_iota(jnp.int32, (cy, lanes), 0)
+    for f in range(FIELDS + 1):
+        for z in range(HALO, HALO + cz) if f == FIELDS else range(layers + 1):
+            tile = base(f, z)
+            tail, head = pltpu.roll(tile, HALO, 0), pltpu.roll(tile, cy - HALO, 0)
+            edges[f, z] = jnp.where(row < HALO, tail, jnp.where(row >= cy - HALO, head, 0.0))
+
+    def after(k, j, z, tile):
+        sides[k, j, z] = pltpu.roll(tile, cy - 1 - HALO, 0)
+        return pltpu.roll(tile, cy - 1, 0)
+
+    def before(k, j, z, tile):
+        sides[k, j, z] = pltpu.roll(tile, HALO + 1, 0)
+        return pltpu.roll(tile, 1, 0)
+
+    def put(i, z, value):
+        middle[i, z] = value
+
+    window(cz, base, stage, after, before, put)
+
+
+def edge_kernel(
+    cz, edges_in, sides, middle, y_a, y_b, final, image_lam, image_mu, edges, packed, stage, result, sems
+):
+    cy, lanes = middle.shape[2], middle.shape[3]
+
+    def put_row(f, z, y, value):
+        edges[f, z, y : y + 1, :] = value
+
+    unpack_rows(cz, cy, (y_a, y_b), packed, put_row)
+    row = lax.broadcasted_iota(jnp.int32, (cy, lanes), 0)
+
+    def after(k, j, z, tile):
+        return jnp.where(row == cy - 1, sides[k, j, z], pltpu.roll(tile, cy - 1, 0))
+
+    def before(k, j, z, tile):
+        return jnp.where(row == 0, sides[k, j, z], pltpu.roll(tile, 1, 0))
+
+    moves = []
+
+    def put(i, z, value):
+        tail, head = pltpu.roll(value, HALO, 0), pltpu.roll(value, cy - HALO, 0)
+        result[i, z] = jnp.where(row < HALO, tail, jnp.where(row >= cy - HALO, head, middle[i, z]))
+        if z == cz - 1:
+            if i == 10:
+                moves.extend(copies(sems, (result.at[9], image_lam), (result.at[10], image_mu)))
+            if i == SYZ:
+                part = pl.ds(SXX, SYZ + 1 - SXX)
+                moves.extend(copies(sems.at[pl.ds(2, 1)], (result.at[part], final.at[part])))
+            if i == VZ:
+                part = pl.ds(VX, VZ + 1 - VX)
+                moves.extend(copies(sems.at[pl.ds(3, 1)], (result.at[part], final.at[part])))
+
+    window(cz, lambda f, z: edges[f, z], stage, after, before, put)
     for move in moves:
         move.wait()
 
@@ -664,24 +696,21 @@
     )
     both = [lax.ppermute(part, "gz", [(i, i ^ 1) for i in range(holders)]) for part in (chip[:half], chip[half:])]
 
-    ring_f, ring_w = kernel_call(
-        functools.partial(frame_kernel, cz),
-        (own,),
-        [vmem()],
-        (shape(ADJ, layers + 1, 2 * cy, cx), shape(FIELDS - ADJ, layers + 1, 2 * cy, cx)),
+    (ring_w,) = kernel_call(
+        functools.partial(frame_kernel, cz), (own,), [vmem()], (shape(FIELDS - ADJ, layers + 1, cy, cx),)
     )
     x_send = shape(x_tiles(), cy, cx, dtype=bf16)
     ring_f, ring_w, x_a, x_b = kernel_call(
         functools.partial(column_kernel, cz),
-        (to_core, core, chip, *both, far_face, peer, slot, ring_f, ring_w),
-        [vmem()] * 10,
-        (shape(*ring_f.shape), shape(*ring_w.shape), x_send, x_send if wide_x else None),
+        (to_core, core, chip, *both, far_face, peer, slot, ring_w),
+        [vmem()] * 9,
+        (shape(ADJ, layers + 1, cy, cx), shape(*ring_w.shape), x_send, x_send if wide_x else None),
         [
             pltpu.SMEM(peer.shape, jnp.int32),
             pltpu.SMEM(slot.shape, jnp.int32),
             pltpu.SemaphoreType.DMA((2,)),
         ],
-        {8: 0, 9: 1},
+        {8: 1},
     )
     axes = ("gx", "gy", "gz")
     gx = lax.axis_size("gx")
@@ -721,26 +750,30 @@
         [pltpu.VMEM((2, strip_tiles, 8, cx), f32)],
         {4 if wide_x else 3: 1, 5 if wide_x else 4: 2},
     )
+    edges, sides, middle = kernel_call(
+        functools.partial(middle_kernel, cz),
+        (ring_f, ring_w, strips, own),
+        [vmem()] * 4,
+        (
+            shape(FIELDS + 1, layers + 1, cy, cx),
+            shape(8, 3, layers + 1, cy, cx),
+            shape(11, cz, cy, cx),
+        ),
+        [pltpu.VMEM((STAGES, layers + 1, cy, cx), f32)],
+    )
     result = kernel_call(
-        functools.partial(window_kernel, cz),
-        (ring_f, ring_w, strips, swap(y_a, None, 0), swap(y_b, None, 1), own),
-        [vmem()] * 6,
-        (
-            shape(9, cz, cy, cx),
-            shape(cz, cy, cx),
-            shape(cz, cy, cx),
-            shape(*ring_f.shape),
-            shape(*ring_w.shape),
-        ),
+        functools.partial(edge_kernel, cz),
+        (edges, sides, middle, swap(y_a, None, 0), swap(y_b, None, 1)),
+        [vmem()] * 5,
+        (shape(9, cz, cy, cx), shape(cz, cy, cx), shape(cz, cy, cx), shape(*edges.shape)),
         [
             pltpu.VMEM((2, scratch_tiles, 8, cx), f32),
-            pltpu.VMEM((2, cz, cy, cx), f32),
-            pltpu.VMEM((2, cz, cy, cx), f32),
-            pltpu.VMEM((3, cz, cy, cx), f32),
+            pltpu.VMEM((STAGES, layers + 1, cy, cx), f32),
+            pltpu.VMEM((11, cz, cy, cx), f32),
             pltpu.SemaphoreType.DMA((4,)),
         ],
-        {0: 3, 1: 4},
-        (hbm(),) * 3 + (vmem(),) * 2,
+        {0: 3},
+        (hbm(),) * 3 + (vmem(),),
     )
     return result[:3]
 

time: 23.6 us -> 23.1 us (0.979)
  waiting for transfers between devices: 6.65 us -> 5.63 us
  Pallas kernels: 5.26 us -> 5.74 us
    ppermute x3, waiting for transfers between devices: 4.64 us -> 3.61 us  [swap(): return lax.ppermute(value, axes, pairs)]
    pallas_call x6 -> x7, Pallas kernels: 5.26 us -> 5.74 us  [kernel_call(): pl.pallas_call(run, out_shape=tuple((o for o in out_shape if o is not Non...]
  transfers between devices with their start and end apart: 8 -> 8, of which waited for: 5 -> 5; matrix products, arithmetic and copies ran while one was open for 0% -> 0% of each run, Pallas kernels for 8% -> 12%
where the time goes in v9:
time: 23.1 us; the launch traced here: 22.9 us
  starting transfers between devices  10.8 us (47%)
  Pallas kernels  5.74 us (25%)
  waiting for transfers between devices  5.63 us (24%)
  between operations  0.69 us (3%)
    pallas_call x7, Pallas kernels, kernel_call(): pl.pallas_call(run, out_shape=tuple((o for o in out_shape if o is not Non...  5.74 us
    ppermute x3, starting transfers between devices, swap(): return lax.ppermute(value, axes, pairs)  5.62 us
    ppermute x3, waiting for transfers between devices, swap(): return lax.ppermute(value, axes, pairs)  3.61 us
    ppermute x1, starting transfers between devices, on_device(): chip = lax.ppermute(store, 'gz', [(i, i ^ 2) for i in range(holders)])  3 us
    ppermute x1, starting transfers between devices, on_device(): lax.ppermute(to_far, ('gy', 'gz'), [(a[0] * holders + a[1], b[0] * holder...  1.64 us
    ppermute x1, waiting for transfers between devices, on_device(): chip = lax.ppermute(store, 'gz', [(i, i ^ 2) for i in range(holders)])  1.29 us
    ppermute x1, waiting for transfers between devices, on_device(): lax.ppermute(to_far, ('gy', 'gz'), [(a[0] * holders + a[1], b[0] * holder...  0.72 us
    ppermute x2, starting transfers between devices, on_device(): lax.ppermute(part, 'gz', [(i, i ^ 1) for i in range(holders)])  0.57 us
  transfers between devices with their start and end apart: 8, of which 5 were waited for; matrix products, arithmetic and copies ran while one was open for 0% of the time, Pallas kernels for 12%

profile of v9, /device:TPU:0, one launch (start us, length us, event | category | flops | bytes accessed | tf_op | source)
XLA Modules:
  0.0 22.9 jit_solution(9857699850640564652)
XLA Ops:
  0.6 3.0 %collective-permute-start.1 = (bf16[72,8,128]{2,1,0:T(8,128)(2,1)}, bf16[72,8,128]{2,1,0:T(8,128)(2,1)S(1)}, u32[]{:S(2)}, u32[]{:S(2)}) collective-permute-start(bf16[72,8,128]{2,1,0:T(8,128)(2,1)} %bitcast.6), channel_id=1, source_target_pairs={{0,2},{1,3},{2,0},{3,1},{4,6},{5,7},{6,4},{7,5},{8,10},{9,11},{10,... | collective-permute-start | bytes 442376 | tf_op jit(solution)/shard_map/ppermute | solution.py:672
  3.6 1.3 %shard_map.139 = (bf16[107,8,128]{2,1,0:T(8,128)(2,1)S(1)}, bf16[37,8,128]{2,1,0:T(8,128)(2,1)S(1)}, f32[15,8,8,128]{3,2,1,0:T(8,128)S(1)}, s32[4,8]{1,0:T(4,128)S(1)}, s32[4,8]{1,0:T(4,128)S(1)}) custom-call(bf16[72,8,128]{2,1,0:T(8,128)(2,1)} %bitcast.7, f32[9,8,8,128]{3,2,1,0:T(8,128)} %refs_1_.1, f32[8,8,128]{2,1,0:T(8,128)} %refs_2_.1, ...), custom_call_target="tpu_custom_call" | custom-call | tf_op jit(solution)/shard_map/pallas_call | solution.py:627
  4.9 1.6 %collective-permute-start.4 = (bf16[37,8,128]{2,1,0:T(8,128)(2,1)S(1)}, bf16[37,8,128]{2,1,0:T(8,128)(2,1)S(1)}, u32[]{:S(2)}, u32[]{:S(2)}) collective-permute-start(bf16[37,8,128]{2,1,0:T(8,128)(2,1)S(1)} %get-tuple-element.23), channel_id=1, source_target_pairs={{0,4},{1,2},{2,1},{3,7},{4,0},{5,6},{6,5},{7,3},{8,12},{9,10},{10,... | collective-permute-start | bytes 227336 | tf_op jit(solution)/shard_map/ppermute | solution.py:694
  6.6 0.0 collective-permute-start
  6.6 1.3 %collective-permute-done.1.refs_2_ = bf16[72,8,128]{2,1,0:T(8,128)(2,1)S(1)} collective-permute-done((bf16[72,8,128]{2,1,0:T(8,128)(2,1)}, bf16[72,8,128]{2,1,0:T(8,128)(2,1)S(1)}, u32[]{:S(2)}, u32[]{:S(2)}) %collective-permute-start.1) | collective-permute-done | bytes 147488 | tf_op jit(solution)/shard_map/ppermute | solution.py:672
  7.9 0.1 collective-permute-start.3
  8.0 0.5 %collective-permute-start.2 = (bf16[36,8,128]{2,1,0:T(8,128)(2,1)S(1)}, bf16[36,8,128]{2,1,0:T(8,128)(2,1)S(1)}, u32[]{:S(2)}, u32[]{:S(2)}) collective-permute-start(bf16[36,8,128]{2,1,0:T(8,128)(2,1)S(1)} %get-tuple-element.42), channel_id=1, source_target_pairs={{0,1},{1,0},{2,3},{3,2},{4,5},{5,4},{6,7},{7,6},{8,9},{9,8},{10,11... | collective-permute-start | bytes 221192 | tf_op jit(solution)/shard_map/ppermute | solution.py:697
  8.5 0.2 shard_map.140.refs_8_
  8.7 0.7 %collective-permute-done.4.refs_5_ = bf16[37,8,128]{2,1,0:T(8,128)(2,1)S(1)} collective-permute-done((bf16[37,8,128]{2,1,0:T(8,128)(2,1)S(1)}, bf16[37,8,128]{2,1,0:T(8,128)(2,1)S(1)}, u32[]{:S(2)}, u32[]{:S(2)}) %collective-permute-start.4) | collective-permute-done | bytes 75808 | tf_op jit(solution)/shard_map/ppermute | solution.py:694
  9.4 0.0 collective-permute-done.refs_1_
  9.4 0.0 collective-permute-done.3.refs_4_
  9.4 0.0 collective-permute-done.2.refs_3_
  9.4 1.1 %shard_map.141 = (f32[9,13,8,128]{3,2,1,0:T(8,128)S(1)}, f32[14,13,8,128]{3,2,1,0:T(8,128)S(1)}, bf16[11,8,128]{2,1,0:T(8,128)(2,1)S(1)}) custom-call(bf16[107,8,128]{2,1,0:T(8,128)(2,1)S(1)} %get-tuple-element.22.refs_0_, bf16[107,8,128]{2,1,0:T(8,128)(2,1)S(1)} %collective-permute-done.refs_1_, ...), custom_call_target="tpu_custom_call", output_to_operand_aliasing={{1}: (8, {})} | custom-call | tf_op jit(solution)/shard_map/pallas_call | solution.py:627
  10.5 1.6 %collective-permute-start.5 = (bf16[11,8,128]{2,1,0:T(8,128)(2,1)S(1)}, bf16[11,8,128]{2,1,0:T(8,128)(2,1)S(1)}, u32[]{:S(2)}, u32[]{:S(2)}) collective-permute-start(bf16[11,8,128]{2,1,0:T(8,128)(2,1)S(1)} %get-tuple-element.29), channel_id=1, source_target_pairs={{0,16},{1,17},{2,18},{3,19},{4,20},{5,21},{6,22},{7,23},{8,24},{9,... | collective-permute-start | bytes 67592 | tf_op jit(solution)/shard_map/ppermute | solution.py:733
  12.1 0.3 %shard_map.142 = (bf16[52,8,128]{2,1,0:T(8,128)(2,1)S(1)}, bf16[52,8,128]{2,1,0:T(8,128)(2,1)S(1)}) custom-call(f32[9,13,8,128]{3,2,1,0:T(8,128)S(1)} %get-tuple-element.27.refs_0_, f32[14,13,8,128]{3,2,1,0:T(8,128)S(1)} %get-tuple-element.28.refs_1_), custom_call_target="tpu_custom_call" | custom-call | tf_op jit(solution)/shard_map/pallas_call | solution.py:627
  12.4 2.0 %collective-permute-done.5.refs_2_ = bf16[11,8,128]{2,1,0:T(8,128)(2,1)S(1)} collective-permute-done((bf16[11,8,128]{2,1,0:T(8,128)(2,1)S(1)}, bf16[11,8,128]{2,1,0:T(8,128)(2,1)S(1)}, u32[]{:S(2)}, u32[]{:S(2)}) %collective-permute-start.5) | collective-permute-done | bytes 22560 | tf_op jit(solution)/shard_map/ppermute | solution.py:733
  14.3 0.1 shard_map.143
  14.5 1.7 %collective-permute-start.6 = (bf16[52,8,128]{2,1,0:T(8,128)(2,1)S(1)}, bf16[52,8,128]{2,1,0:T(8,128)(2,1)S(1)}, u32[]{:S(2)}, u32[]{:S(2)}) collective-permute-start(bf16[52,8,128]{2,1,0:T(8,128)(2,1)S(1)} %get-tuple-element.36), channel_id=1, source_target_pairs={{0,4},{1,3},{2,6},{3,1},{4,0},{5,9},{6,2},{7,11},{8,12},{9,5},{10,... | collective-permute-start | bytes 319496 | tf_op jit(solution)/shard_map/ppermute | solution.py:733
  16.2 2.3 %collective-permute-start.7 = (bf16[52,8,128]{2,1,0:T(8,128)(2,1)S(1)}, bf16[52,8,128]{2,1,0:T(8,128)(2,1)S(1)}, u32[]{:S(2)}, u32[]{:S(2)}) collective-permute-start(bf16[52,8,128]{2,1,0:T(8,128)(2,1)S(1)} %get-tuple-element.37), channel_id=1, source_target_pairs={{0,2},{1,5},{2,0},{3,7},{4,8},{5,1},{6,10},{7,3},{8,4},{9,13},{10,... | collective-permute-start | bytes 319496 | tf_op jit(solution)/shard_map/ppermute | solution.py:733
  18.5 1.0 %shard_map.144 = (f32[24,13,8,128]{3,2,1,0:T(8,128)S(1)}, f32[8,3,13,8,128]{4,3,2,1,0:T(8,128)S(1)}, f32[11,8,8,128]{3,2,1,0:T(8,128)S(1)}) custom-call(f32[9,13,8,128]{3,2,1,0:T(8,128)S(1)} %get-tuple-element.27.refs_0_, f32[14,13,8,128]{3,2,1,0:T(8,128)S(1)} %get-tuple-element.28.refs_1_, f32[23,8,128]{2,1,0:T(8,128)S(1)} %get-tuple-element.32.refs_2_, ...), custom_call_target="tpu_custom_call" | custom-call | tf_op jit(solution)/shard_map/pallas_call | solution.py:627
  19.5 0.6 %collective-permute-done.6.refs_3_ = bf16[52,8,128]{2,1,0:T(8,128)(2,1)S(1)} collective-permute-done((bf16[52,8,128]{2,1,0:T(8,128)(2,1)S(1)}, bf16[52,8,128]{2,1,0:T(8,128)(2,1)S(1)}, u32[]{:S(2)}, u32[]{:S(2)}) %collective-permute-start.6) | collective-permute-done | bytes 106528 | tf_op jit(solution)/shard_map/ppermute | solution.py:733
  20.1 1.1 %collective-permute-done.7.refs_4_ = bf16[52,8,128]{2,1,0:T(8,128)(2,1)S(1)} collective-permute-done((bf16[52,8,128]{2,1,0:T(8,128)(2,1)S(1)}, bf16[52,8,128]{2,1,0:T(8,128)(2,1)S(1)}, u32[]{:S(2)}, u32[]{:S(2)}) %collective-permute-start.7) | collective-permute-done | bytes 106528 | tf_op jit(solution)/shard_map/ppermute | solution.py:733
  21.1 1.8 %shard_map.145 = (f32[9,8,8,128]{3,2,1,0:T(8,128)}, f32[8,8,128]{2,1,0:T(8,128)}, f32[8,8,128]{2,1,0:T(8,128)}, f32[24,13,8,128]{3,2,1,0:T(8,128)S(1)}) custom-call(f32[24,13,8,128]{3,2,1,0:T(8,128)S(1)} %get-tuple-element.33.refs_0_, f32[8,3,13,8,128]{4,3,2,1,0:T(8,128)S(1)} %get-tuple-element.34.refs_1_, ...), custom_call_target="tpu_custom_call", output_to_operand_aliasing={{3}: (0, {})} | custom-call | tf_op jit(solution)/shard_map/pallas_call | solution.py:627
  (1 shorter events, 0.0 us)
Async XLA Ops:
  0.6 7.2 %collective-permute-start.1 = (bf16[72,8,128]{2,1,0:T(8,128)(2,1)}, bf16[72,8,128]{2,1,0:T(8,128)(2,1)S(1)}, u32[]{:S(2)}, u32[]{:S(2)}) collective-permute-start(bf16[72,8,128]{2,1,0:T(8,128)(2,1)} %bitcast.6), channel_id=1, source_target_pairs={{0,2},{1,3},{2,0},{3,1},{4,6},{5,7},{6,4},{7,5},{8,10},{9,11},{10,... | collective-permute-start | bytes 442376 | tf_op jit(solution)/shard_map/ppermute | solution.py:672
  4.9 4.4 %collective-permute-start.4 = (bf16[37,8,128]{2,1,0:T(8,128)(2,1)S(1)}, bf16[37,8,128]{2,1,0:T(8,128)(2,1)S(1)}, u32[]{:S(2)}, u32[]{:S(2)}) collective-permute-start(bf16[37,8,128]{2,1,0:T(8,128)(2,1)S(1)} %get-tuple-element.23), channel_id=1, source_target_pairs={{0,4},{1,2},{2,1},{3,7},{4,0},{5,6},{6,5},{7,3},{8,12},{9,10},{10,... | collective-permute-start | bytes 227336 | tf_op jit(solution)/shard_map/ppermute | solution.py:694
  6.6 2.8 %collective-permute-start = (bf16[107,8,128]{2,1,0:T(8,128)(2,1)S(1)}, bf16[107,8,128]{2,1,0:T(8,128)(2,1)S(1)}, u32[]{:S(2)}, u32[]{:S(2)}) collective-permute-start(bf16[107,8,128]{2,1,0:T(8,128)(2,1)S(1)} %get-tuple-element.22.refs_0_), channel_id=1, source_target_pairs={{0,1},{1,0},{2,3},{3,2},{4,5},{5,4},{6,7},{7,6},{8,9},{9,8},{10,11... | collective-permute-start | bytes 657416 | tf_op jit(solution)/shard_map/ppermute | solution.py:688
  7.9 1.5 %collective-permute-start.3 = (bf16[36,8,128]{2,1,0:T(8,128)(2,1)S(1)}, bf16[36,8,128]{2,1,0:T(8,128)(2,1)S(1)}, u32[]{:S(2)}, u32[]{:S(2)}) collective-permute-start(bf16[36,8,128]{2,1,0:T(8,128)(2,1)S(1)} %get-tuple-element.41), channel_id=1, source_target_pairs={{0,1},{1,0},{2,3},{3,2},{4,5},{5,4},{6,7},{7,6},{8,9},{9,8},{10,11... | collective-permute-start | bytes 221192 | tf_op jit(solution)/shard_map/ppermute | solution.py:697
  8.0 1.4 %collective-permute-start.2 = (bf16[36,8,128]{2,1,0:T(8,128)(2,1)S(1)}, bf16[36,8,128]{2,1,0:T(8,128)(2,1)S(1)}, u32[]{:S(2)}, u32[]{:S(2)}) collective-permute-start(bf16[36,8,128]{2,1,0:T(8,128)(2,1)S(1)} %get-tuple-element.42), channel_id=1, source_target_pairs={{0,1},{1,0},{2,3},{3,2},{4,5},{5,4},{6,7},{7,6},{8,9},{9,8},{10,11... | collective-permute-start | bytes 221192 | tf_op jit(solution)/shard_map/ppermute | solution.py:697
  10.5 3.9 %collective-permute-start.5 = (bf16[11,8,128]{2,1,0:T(8,128)(2,1)S(1)}, bf16[11,8,128]{2,1,0:T(8,128)(2,1)S(1)}, u32[]{:S(2)}, u32[]{:S(2)}) collective-permute-start(bf16[11,8,128]{2,1,0:T(8,128)(2,1)S(1)} %get-tuple-element.29), channel_id=1, source_target_pairs={{0,16},{1,17},{2,18},{3,19},{4,20},{5,21},{6,22},{7,23},{8,24},{9,... | collective-permute-start | bytes 67592 | tf_op jit(solution)/shard_map/ppermute | solution.py:733
  14.5 5.6 %collective-permute-start.6 = (bf16[52,8,128]{2,1,0:T(8,128)(2,1)S(1)}, bf16[52,8,128]{2,1,0:T(8,128)(2,1)S(1)}, u32[]{:S(2)}, u32[]{:S(2)}) collective-permute-start(bf16[52,8,128]{2,1,0:T(8,128)(2,1)S(1)} %get-tuple-element.36), channel_id=1, source_target_pairs={{0,4},{1,3},{2,6},{3,1},{4,0},{5,9},{6,2},{7,11},{8,12},{9,5},{10,... | collective-permute-start | bytes 319496 | tf_op jit(solution)/shard_map/ppermute | solution.py:733
  16.2 5.0 %collective-permute-start.7 = (bf16[52,8,128]{2,1,0:T(8,128)(2,1)S(1)}, bf16[52,8,128]{2,1,0:T(8,128)(2,1)S(1)}, u32[]{:S(2)}, u32[]{:S(2)}) collective-permute-start(bf16[52,8,128]{2,1,0:T(8,128)(2,1)S(1)} %get-tuple-element.37), channel_id=1, source_target_pairs={{0,2},{1,5},{2,0},{3,7},{4,8},{5,1},{6,10},{7,3},{8,4},{9,13},{10,... | collective-permute-start | bytes 319496 | tf_op jit(solution)/shard_map/ppermute | solution.py:733

commit v10 on v9

--- a/solution.py
+++ b/solution.py
@@ -156,26 +156,36 @@
     pack_tiles(sides, (send_a, send_b), strip_tiles, tiles)
 
 
-def unpack_rows(cz, cy, got, packed, put_row):
+def unpack_rows(cz, cy, first, message, packed, edges):
     has_lower, has_upper = has_neighbours("gy")
-    even = even_mask(("gy", "gz"), packed.shape[2:])
     strip_tiles, _ = row_tiles(cz, cy)
-    for side, (up, keep) in enumerate(((True, has_lower), (False, has_upper))):
+    parity = lax.rem(lax.axis_index("gy") + lax.axis_index("gz"), 2)
+
+    def side(up, keep):
         narrow, wide, strip = y_rows(cz, cy, up)
         n, w, c = row_counts(cz, cy, up)
-
-        def of(t):
-            a, b = got[0][t].astype(jnp.float32), got[1][t].astype(jnp.float32)
-            return (jnp.where(even, b, a) if up else jnp.where(even, a, b)) * keep
-
         for t in range(n + w):
-            value = of(strip_tiles + t)
-            packed[side, t] = value if t < n else value + of(strip_tiles + w + t)
+            value = message[strip_tiles + t].astype(jnp.float32)
+            if t >= n:
+                value = value + message[strip_tiles + w + t].astype(jnp.float32)
+            packed[t] = value * keep
         for t in range(c):
-            packed[side, n + w + t] = of(t)
+            packed[n + w + t] = message[t].astype(jnp.float32) * keep
         for base, listed in ((0, narrow), (n, wide), (n + w, strip)):
             for r, (f, z, _, y) in enumerate(listed):
-                put_row(f, z, y, packed[side, base + r // 8, r % 8 : r % 8 + 1, :])
+                edges[f, z, y : y + 1, :] = packed[base + r // 8, r % 8 : r % 8 + 1, :]
+
+    @pl.when(parity == (1 if first else 0))
+    def _():
+        side(True, has_lower)
+
+    @pl.when(parity == (0 if first else 1))
+    def _():
+        side(False, has_upper)
+
+
+def first_rows_kernel(cz, message, edges_in, edges, packed):
+    unpack_rows(cz, edges.shape[2], True, message, packed, edges)
 
 
 def start_kernel(
@@ -563,14 +573,11 @@
 
 
 def edge_kernel(
-    cz, edges_in, sides, middle, y_a, y_b, final, image_lam, image_mu, edges, packed, stage, result, sems
+    cz, edges_in, sides, middle, message, final, image_lam, image_mu, edges, packed, stage, result, sems
 ):
     cy, lanes = middle.shape[2], middle.shape[3]
 
-    def put_row(f, z, y, value):
-        edges[f, z, y : y + 1, :] = value
-
-    unpack_rows(cz, cy, (y_a, y_b), packed, put_row)
+    unpack_rows(cz, cy, False, message, packed, edges)
     row = lax.broadcasted_iota(jnp.int32, (cy, lanes), 0)
 
     def after(k, j, z, tile):
@@ -720,7 +727,7 @@
             i = dict(swap_pairs(gx, x_turn))[i]
         if y_turn is not None:
             other = dict(swap_pairs(gy, (c + y_turn) % 2))[j]
-            j, c = (j, c ^ 2) if other == j else (other, c)
+            i, j = (i ^ 1, j) if other == j else (i, other)
         return (i * gy + j) * holders + c
 
     def swap(value, x_turn, y_turn):
@@ -761,13 +768,22 @@
         ),
         [pltpu.VMEM((STAGES, layers + 1, cy, cx), f32)],
     )
+    row_scratch = pltpu.VMEM((scratch_tiles, 8, cx), f32)
+    (edges,) = kernel_call(
+        functools.partial(first_rows_kernel, cz),
+        (swap(y_a, None, 0), edges),
+        [vmem()] * 2,
+        (shape(*edges.shape),),
+        [row_scratch],
+        {1: 0},
+    )
     result = kernel_call(
         functools.partial(edge_kernel, cz),
-        (edges, sides, middle, swap(y_a, None, 0), swap(y_b, None, 1)),
-        [vmem()] * 5,
+        (edges, sides, middle, swap(y_b, None, 1)),
+        [vmem()] * 4,
         (shape(9, cz, cy, cx), shape(cz, cy, cx), shape(cz, cy, cx), shape(*edges.shape)),
         [
-            pltpu.VMEM((2, scratch_tiles, 8, cx), f32),
+            row_scratch,
             pltpu.VMEM((STAGES, layers + 1, cy, cx), f32),
             pltpu.VMEM((11, cz, cy, cx), f32),
             pltpu.SemaphoreType.DMA((4,)),

time: 23.1 us -> 22.8 us (0.987)
  starting transfers between devices: 10.8 us -> 10.1 us
  waiting for transfers between devices: 5.63 us -> 5.98 us
    ppermute x3, starting transfers between devices: 5.62 us -> 4.85 us  [swap(): return lax.ppermute(value, axes, pairs)]
    ppermute x3, waiting for transfers between devices: 3.61 us -> 3.97 us  [swap(): return lax.ppermute(value, axes, pairs)]
    pallas_call x7 -> x8, Pallas kernels: 5.74 us -> 5.86 us  [kernel_call(): pl.pallas_call(run, out_shape=tuple((o for o in out_shape if o is not Non...]
  transfers between devices with their start and end apart: 8 -> 8, of which waited for: 5 -> 5; matrix products, arithmetic and copies ran while one was open for 0% -> 0% of each run, Pallas kernels for 12% -> 13%
where the time goes in v10:
time: 22.8 us; the launch traced here: 22.6 us
  starting transfers between devices  10.1 us (44%)
  waiting for transfers between devices  5.98 us (26%)
  Pallas kernels  5.86 us (26%)
  between operations  0.69 us (3%)
    pallas_call x8, Pallas kernels, kernel_call(): pl.pallas_call(run, out_shape=tuple((o for o in out_shape if o is not Non...  5.86 us
    ppermute x3, starting transfers between devices, swap(): return lax.ppermute(value, axes, pairs)  4.85 us
    ppermute x3, waiting for transfers between devices, swap(): return lax.ppermute(value, axes, pairs)  3.97 us
    ppermute x1, starting transfers between devices, on_device(): chip = lax.ppermute(store, 'gz', [(i, i ^ 2) for i in range(holders)])  3 us
    ppermute x1, starting transfers between devices, on_device(): lax.ppermute(to_far, ('gy', 'gz'), [(a[0] * holders + a[1], b[0] * holder...  1.64 us
    ppermute x1, waiting for transfers between devices, on_device(): chip = lax.ppermute(store, 'gz', [(i, i ^ 2) for i in range(holders)])  1.29 us
    ppermute x1, waiting for transfers between devices, on_device(): lax.ppermute(to_far, ('gy', 'gz'), [(a[0] * holders + a[1], b[0] * holder...  0.72 us
    ppermute x2, starting transfers between devices, on_device(): lax.ppermute(part, 'gz', [(i, i ^ 1) for i in range(holders)])  0.57 us
  transfers between devices with their start and end apart: 8, of which 5 were waited for; matrix products, arithmetic and copies ran while one was open for 0% of the time, Pallas kernels for 13%

profile of v10, /device:TPU:0, one launch (start us, length us, event | category | flops | bytes accessed | tf_op | source)
XLA Modules:
  0.0 22.6 jit_solution(12426085011083187918)
XLA Ops:
  0.6 3.0 %collective-permute-start.1 = (bf16[72,8,128]{2,1,0:T(8,128)(2,1)}, bf16[72,8,128]{2,1,0:T(8,128)(2,1)S(1)}, u32[]{:S(2)}, u32[]{:S(2)}) collective-permute-start(bf16[72,8,128]{2,1,0:T(8,128)(2,1)} %bitcast.6), channel_id=1, source_target_pairs={{0,2},{1,3},{2,0},{3,1},{4,6},{5,7},{6,4},{7,5},{8,10},{9,11},{10,... | collective-permute-start | bytes 442376 | tf_op jit(solution)/shard_map/ppermute | solution.py:679
  3.6 1.3 %shard_map.139 = (bf16[107,8,128]{2,1,0:T(8,128)(2,1)S(1)}, bf16[37,8,128]{2,1,0:T(8,128)(2,1)S(1)}, f32[15,8,8,128]{3,2,1,0:T(8,128)S(1)}, s32[4,8]{1,0:T(4,128)S(1)}, s32[4,8]{1,0:T(4,128)S(1)}) custom-call(bf16[72,8,128]{2,1,0:T(8,128)(2,1)} %bitcast.7, f32[9,8,8,128]{3,2,1,0:T(8,128)} %refs_1_.1, f32[8,8,128]{2,1,0:T(8,128)} %refs_2_.1, ...), custom_call_target="tpu_custom_call" | custom-call | tf_op jit(solution)/shard_map/pallas_call | solution.py:634
  4.9 1.6 %collective-permute-start.4 = (bf16[37,8,128]{2,1,0:T(8,128)(2,1)S(1)}, bf16[37,8,128]{2,1,0:T(8,128)(2,1)S(1)}, u32[]{:S(2)}, u32[]{:S(2)}) collective-permute-start(bf16[37,8,128]{2,1,0:T(8,128)(2,1)S(1)} %get-tuple-element.23), channel_id=1, source_target_pairs={{0,4},{1,2},{2,1},{3,7},{4,0},{5,6},{6,5},{7,3},{8,12},{9,10},{10,... | collective-permute-start | bytes 227336 | tf_op jit(solution)/shard_map/ppermute | solution.py:701
  6.6 0.0 collective-permute-start
  6.6 1.3 %collective-permute-done.1.refs_2_ = bf16[72,8,128]{2,1,0:T(8,128)(2,1)S(1)} collective-permute-done((bf16[72,8,128]{2,1,0:T(8,128)(2,1)}, bf16[72,8,128]{2,1,0:T(8,128)(2,1)S(1)}, u32[]{:S(2)}, u32[]{:S(2)}) %collective-permute-start.1) | collective-permute-done | bytes 147488 | tf_op jit(solution)/shard_map/ppermute | solution.py:679
  7.9 0.1 collective-permute-start.3
  8.0 0.5 %collective-permute-start.2 = (bf16[36,8,128]{2,1,0:T(8,128)(2,1)S(1)}, bf16[36,8,128]{2,1,0:T(8,128)(2,1)S(1)}, u32[]{:S(2)}, u32[]{:S(2)}) collective-permute-start(bf16[36,8,128]{2,1,0:T(8,128)(2,1)S(1)} %get-tuple-element.42), channel_id=1, source_target_pairs={{0,1},{1,0},{2,3},{3,2},{4,5},{5,4},{6,7},{7,6},{8,9},{9,8},{10,11... | collective-permute-start | bytes 221192 | tf_op jit(solution)/shard_map/ppermute | solution.py:704
  8.5 0.2 shard_map.140.refs_8_
  8.7 0.7 %collective-permute-done.4.refs_5_ = bf16[37,8,128]{2,1,0:T(8,128)(2,1)S(1)} collective-permute-done((bf16[37,8,128]{2,1,0:T(8,128)(2,1)S(1)}, bf16[37,8,128]{2,1,0:T(8,128)(2,1)S(1)}, u32[]{:S(2)}, u32[]{:S(2)}) %collective-permute-start.4) | collective-permute-done | bytes 75808 | tf_op jit(solution)/shard_map/ppermute | solution.py:701
  9.4 0.0 collective-permute-done.refs_1_
  9.4 0.0 collective-permute-done.3.refs_4_
  9.4 0.0 collective-permute-done.2.refs_3_
  9.4 1.1 %shard_map.141 = (f32[9,13,8,128]{3,2,1,0:T(8,128)S(1)}, f32[14,13,8,128]{3,2,1,0:T(8,128)S(1)}, bf16[11,8,128]{2,1,0:T(8,128)(2,1)S(1)}) custom-call(bf16[107,8,128]{2,1,0:T(8,128)(2,1)S(1)} %get-tuple-element.22.refs_0_, bf16[107,8,128]{2,1,0:T(8,128)(2,1)S(1)} %collective-permute-done.refs_1_, ...), custom_call_target="tpu_custom_call", output_to_operand_aliasing={{1}: (8, {})} | custom-call | tf_op jit(solution)/shard_map/pallas_call | solution.py:634
  10.5 1.6 %collective-permute-start.5 = (bf16[11,8,128]{2,1,0:T(8,128)(2,1)S(1)}, bf16[11,8,128]{2,1,0:T(8,128)(2,1)S(1)}, u32[]{:S(2)}, u32[]{:S(2)}) collective-permute-start(bf16[11,8,128]{2,1,0:T(8,128)(2,1)S(1)} %get-tuple-element.29), channel_id=1, source_target_pairs={{0,16},{1,17},{2,18},{3,19},{4,20},{5,21},{6,22},{7,23},{8,24},{9,... | collective-permute-start | bytes 67592 | tf_op jit(solution)/shard_map/ppermute | solution.py:740
  12.1 0.3 %shard_map.142 = (bf16[52,8,128]{2,1,0:T(8,128)(2,1)S(1)}, bf16[52,8,128]{2,1,0:T(8,128)(2,1)S(1)}) custom-call(f32[9,13,8,128]{3,2,1,0:T(8,128)S(1)} %get-tuple-element.27.refs_0_, f32[14,13,8,128]{3,2,1,0:T(8,128)S(1)} %get-tuple-element.28.refs_1_), custom_call_target="tpu_custom_call" | custom-call | tf_op jit(solution)/shard_map/pallas_call | solution.py:634
  12.4 2.0 %collective-permute-done.5.refs_2_ = bf16[11,8,128]{2,1,0:T(8,128)(2,1)S(1)} collective-permute-done((bf16[11,8,128]{2,1,0:T(8,128)(2,1)S(1)}, bf16[11,8,128]{2,1,0:T(8,128)(2,1)S(1)}, u32[]{:S(2)}, u32[]{:S(2)}) %collective-permute-start.5) | collective-permute-done | bytes 22560 | tf_op jit(solution)/shard_map/ppermute | solution.py:740
  14.3 0.1 shard_map.143
  14.5 1.7 %collective-permute-start.6 = (bf16[52,8,128]{2,1,0:T(8,128)(2,1)S(1)}, bf16[52,8,128]{2,1,0:T(8,128)(2,1)S(1)}, u32[]{:S(2)}, u32[]{:S(2)}) collective-permute-start(bf16[52,8,128]{2,1,0:T(8,128)(2,1)S(1)} %get-tuple-element.32), channel_id=1, source_target_pairs={{0,4},{1,17},{2,6},{3,19},{4,0},{5,9},{6,2},{7,11},{8,12},{9,5},{1... | collective-permute-start | bytes 319496 | tf_op jit(solution)/shard_map/ppermute | solution.py:740
  16.2 1.5 %collective-permute-start.7 = (bf16[52,8,128]{2,1,0:T(8,128)(2,1)S(1)}, bf16[52,8,128]{2,1,0:T(8,128)(2,1)S(1)}, u32[]{:S(2)}, u32[]{:S(2)}) collective-permute-start(bf16[52,8,128]{2,1,0:T(8,128)(2,1)S(1)} %get-tuple-element.37), channel_id=1, source_target_pairs={{0,16},{1,5},{2,18},{3,7},{4,8},{5,1},{6,10},{7,3},{8,4},{9,13},{1... | collective-permute-start | bytes 319496 | tf_op jit(solution)/shard_map/ppermute | solution.py:740
  17.7 1.0 %shard_map.144 = (f32[24,13,8,128]{3,2,1,0:T(8,128)S(1)}, f32[8,3,13,8,128]{4,3,2,1,0:T(8,128)S(1)}, f32[11,8,8,128]{3,2,1,0:T(8,128)S(1)}) custom-call(f32[9,13,8,128]{3,2,1,0:T(8,128)S(1)} %get-tuple-element.27.refs_0_, f32[14,13,8,128]{3,2,1,0:T(8,128)S(1)} %get-tuple-element.28.refs_1_, f32[23,8,128]{2,1,0:T(8,128)S(1)} %get-tuple-element.33.refs_2_, ...), custom_call_target="tpu_custom_call" | custom-call | tf_op jit(solution)/shard_map/pallas_call | solution.py:634
  18.7 1.2 %collective-permute-done.6.refs_0_ = bf16[52,8,128]{2,1,0:T(8,128)(2,1)S(1)} collective-permute-done((bf16[52,8,128]{2,1,0:T(8,128)(2,1)S(1)}, bf16[52,8,128]{2,1,0:T(8,128)(2,1)S(1)}, u32[]{:S(2)}, u32[]{:S(2)}) %collective-permute-start.6) | collective-permute-done | bytes 106528 | tf_op jit(solution)/shard_map/ppermute | solution.py:740
  19.9 0.1 shard_map.145.refs_0_
  20.1 0.8 %collective-permute-done.7.refs_3_ = bf16[52,8,128]{2,1,0:T(8,128)(2,1)S(1)} collective-permute-done((bf16[52,8,128]{2,1,0:T(8,128)(2,1)S(1)}, bf16[52,8,128]{2,1,0:T(8,128)(2,1)S(1)}, u32[]{:S(2)}, u32[]{:S(2)}) %collective-permute-start.7) | collective-permute-done | bytes 106528 | tf_op jit(solution)/shard_map/ppermute | solution.py:740
  20.9 1.7 %shard_map.146 = (f32[9,8,8,128]{3,2,1,0:T(8,128)}, f32[8,8,128]{2,1,0:T(8,128)}, f32[8,8,128]{2,1,0:T(8,128)}, f32[24,13,8,128]{3,2,1,0:T(8,128)S(1)}) custom-call(f32[24,13,8,128]{3,2,1,0:T(8,128)S(1)} %shard_map.145.refs_0_, f32[8,3,13,8,128]{4,3,2,1,0:T(8,128)S(1)} %get-tuple-element.35.refs_1_, ...), custom_call_target="tpu_custom_call", output_to_operand_aliasing={{3}: (0, {})} | custom-call | tf_op jit(solution)/shard_map/pallas_call | solution.py:634
  (1 shorter events, 0.0 us)
Async XLA Ops:
  0.6 7.2 %collective-permute-start.1 = (bf16[72,8,128]{2,1,0:T(8,128)(2,1)}, bf16[72,8,128]{2,1,0:T(8,128)(2,1)S(1)}, u32[]{:S(2)}, u32[]{:S(2)}) collective-permute-start(bf16[72,8,128]{2,1,0:T(8,128)(2,1)} %bitcast.6), channel_id=1, source_target_pairs={{0,2},{1,3},{2,0},{3,1},{4,6},{5,7},{6,4},{7,5},{8,10},{9,11},{10,... | collective-permute-start | bytes 442376 | tf_op jit(solution)/shard_map/ppermute | solution.py:679
  4.9 4.4 %collective-permute-start.4 = (bf16[37,8,128]{2,1,0:T(8,128)(2,1)S(1)}, bf16[37,8,128]{2,1,0:T(8,128)(2,1)S(1)}, u32[]{:S(2)}, u32[]{:S(2)}) collective-permute-start(bf16[37,8,128]{2,1,0:T(8,128)(2,1)S(1)} %get-tuple-element.23), channel_id=1, source_target_pairs={{0,4},{1,2},{2,1},{3,7},{4,0},{5,6},{6,5},{7,3},{8,12},{9,10},{10,... | collective-permute-start | bytes 227336 | tf_op jit(solution)/shard_map/ppermute | solution.py:701
  6.6 2.8 %collective-permute-start = (bf16[107,8,128]{2,1,0:T(8,128)(2,1)S(1)}, bf16[107,8,128]{2,1,0:T(8,128)(2,1)S(1)}, u32[]{:S(2)}, u32[]{:S(2)}) collective-permute-start(bf16[107,8,128]{2,1,0:T(8,128)(2,1)S(1)} %get-tuple-element.22.refs_0_), channel_id=1, source_target_pairs={{0,1},{1,0},{2,3},{3,2},{4,5},{5,4},{6,7},{7,6},{8,9},{9,8},{10,11... | collective-permute-start | bytes 657416 | tf_op jit(solution)/shard_map/ppermute | solution.py:695
  7.9 1.5 %collective-permute-start.3 = (bf16[36,8,128]{2,1,0:T(8,128)(2,1)S(1)}, bf16[36,8,128]{2,1,0:T(8,128)(2,1)S(1)}, u32[]{:S(2)}, u32[]{:S(2)}) collective-permute-start(bf16[36,8,128]{2,1,0:T(8,128)(2,1)S(1)} %get-tuple-element.41), channel_id=1, source_target_pairs={{0,1},{1,0},{2,3},{3,2},{4,5},{5,4},{6,7},{7,6},{8,9},{9,8},{10,11... | collective-permute-start | bytes 221192 | tf_op jit(solution)/shard_map/ppermute | solution.py:704
  8.0 1.4 %collective-permute-start.2 = (bf16[36,8,128]{2,1,0:T(8,128)(2,1)S(1)}, bf16[36,8,128]{2,1,0:T(8,128)(2,1)S(1)}, u32[]{:S(2)}, u32[]{:S(2)}) collective-permute-start(bf16[36,8,128]{2,1,0:T(8,128)(2,1)S(1)} %get-tuple-element.42), channel_id=1, source_target_pairs={{0,1},{1,0},{2,3},{3,2},{4,5},{5,4},{6,7},{7,6},{8,9},{9,8},{10,11... | collective-permute-start | bytes 221192 | tf_op jit(solution)/shard_map/ppermute | solution.py:704
  10.5 3.9 %collective-permute-start.5 = (bf16[11,8,128]{2,1,0:T(8,128)(2,1)S(1)}, bf16[11,8,128]{2,1,0:T(8,128)(2,1)S(1)}, u32[]{:S(2)}, u32[]{:S(2)}) collective-permute-start(bf16[11,8,128]{2,1,0:T(8,128)(2,1)S(1)} %get-tuple-element.29), channel_id=1, source_target_pairs={{0,16},{1,17},{2,18},{3,19},{4,20},{5,21},{6,22},{7,23},{8,24},{9,... | collective-permute-start | bytes 67592 | tf_op jit(solution)/shard_map/ppermute | solution.py:740
  14.5 5.4 %collective-permute-start.6 = (bf16[52,8,128]{2,1,0:T(8,128)(2,1)S(1)}, bf16[52,8,128]{2,1,0:T(8,128)(2,1)S(1)}, u32[]{:S(2)}, u32[]{:S(2)}) collective-permute-start(bf16[52,8,128]{2,1,0:T(8,128)(2,1)S(1)} %get-tuple-element.32), channel_id=1, source_target_pairs={{0,4},{1,17},{2,6},{3,19},{4,0},{5,9},{6,2},{7,11},{8,12},{9,5},{1... | collective-permute-start | bytes 319496 | tf_op jit(solution)/shard_map/ppermute | solution.py:740
  16.2 4.7 %collective-permute-start.7 = (bf16[52,8,128]{2,1,0:T(8,128)(2,1)S(1)}, bf16[52,8,128]{2,1,0:T(8,128)(2,1)S(1)}, u32[]{:S(2)}, u32[]{:S(2)}) collective-permute-start(bf16[52,8,128]{2,1,0:T(8,128)(2,1)S(1)} %get-tuple-element.37), channel_id=1, source_target_pairs={{0,16},{1,5},{2,18},{3,7},{4,8},{5,1},{6,10},{7,3},{8,4},{9,13},{1... | collective-permute-start | bytes 319496 | tf_op jit(solution)/shard_map/ppermute | solution.py:740

commit v11 on v10

--- a/solution.py
+++ b/solution.py
@@ -134,8 +134,8 @@
     even = even_mask(("gy", "gz"), sends[0].shape[1:])
     for t in range(count):
         up, down = (side[min(t, len(side) - 1)] for side in sides)
-        sends[0][first + t] = jnp.where(even, up, down).astype(jnp.bfloat16)
-        sends[1][first + t] = jnp.where(even, down, up).astype(jnp.bfloat16)
+        sends[0][first + t] = jnp.where(even, down, up).astype(jnp.bfloat16)
+        sends[1][first + t] = jnp.where(even, up, down).astype(jnp.bfloat16)
 
 
 def layer_rows_kernel(cz, ring_f, ring_w, send_a, send_b, packed):
@@ -175,11 +175,11 @@
             for r, (f, z, _, y) in enumerate(listed):
                 edges[f, z, y : y + 1, :] = packed[base + r // 8, r % 8 : r % 8 + 1, :]
 
-    @pl.when(parity == (1 if first else 0))
+    @pl.when(parity == (0 if first else 1))
     def _():
         side(True, has_lower)
 
-    @pl.when(parity == (0 if first else 1))
+    @pl.when(parity == (1 if first else 0))
     def _():
         side(False, has_upper)
 
@@ -272,7 +272,22 @@
     return jnp.where(position < 2, tile, jnp.where(position >= 6, pltpu.roll(tile, 4, 1), 0.0))
 
 
-def frame_kernel(cz, own, ring):
+def pieces(cz, peers, slots):
+    me, count = lax.axis_index("gz"), lax.axis_size("gz")
+    below, above = jnp.maximum(me - 1, 0), jnp.minimum(me + 1, count - 1)
+    has_below, has_above = has_neighbours("gz")
+    for z in range(cz + 2 * HALO):
+        if z < HALO:
+            brick, piece, keep = below, cz - HALO + z, has_below
+        elif z < HALO + cz:
+            brick, piece, keep = me, z - HALO, None
+        else:
+            brick, piece, keep = above, z - HALO - cz, has_above
+        yield z, peers[brick, piece] ^ me, slots[brick, piece] * 9, keep
+
+
+def frame_kernel(cz, mine, core, chip, peer, slot, own, ring_f, ring, peers, slots, sems):
+    moves = copies(sems, (peer, peers), (slot, slots))
     cy, lanes = own.shape[2], own.shape[3]
     layers = cz + 2 * HALO
     zero = jnp.zeros((cy, lanes), jnp.float32)
@@ -284,18 +299,24 @@
             if (f, z) not in filled:
                 ring[f, z] = zero
         ring[f, layers] = strip_part(zero, lambda z: own[f, z - HALO], range(HALO, HALO + cz))
+    for move in moves:
+        move.wait()
+    for z, hops, row, keep in pieces(cz, peers, slots):
+        hops = jnp.full((cy, lanes), hops, jnp.int32)
+        for f in range(9):
+            a, b, c = (ref[row + f].astype(jnp.float32) for ref in (mine, core, chip))
+            value = jnp.where(hops == 0, a, jnp.where(hops == 1, b, c))
+            ring_f[f, z] = value if keep is None else value * keep
 
 
 def column_kernel(
-    cz, mine, core, chip, both_a, both_b, far, peer, slot, ring_w_in,
+    cz, core, both_a, both_b, far, peer, slot, ring_f_in, ring_w_in,
     ring_f, ring, x_a, x_b, peers, slots, sems,
 ):
-    cy, lanes = chip.shape[1], chip.shape[2]
+    cy, lanes = core.shape[1], core.shape[2]
     layers = cz + 2 * HALO
-    tiles = chip.shape[0]
     half = both_a.shape[0]
-    me = lax.axis_index("gz")
-    count = lax.axis_size("gz")
+    tiles = half + both_b.shape[0]
     moves = copies(sems, (peer, peers), (slot, slots))
     near, _ = face_counts(cz)
     even = even_mask("gz", (cy, lanes))
@@ -323,24 +344,14 @@
         strip.append(tile)
     for move in moves:
         move.wait()
-    below, above = jnp.maximum(me - 1, 0), jnp.minimum(me + 1, count - 1)
-    for z in range(layers):
-        if z < HALO:
-            brick, piece, keep = below, cz - HALO + z, has_below
-        elif z < HALO + cz:
-            brick, piece, keep = me, z - HALO, None
-        else:
-            brick, piece, keep = above, z - HALO - cz, has_above
-        row = slots[brick, piece] * 9
-        hops = jnp.full((cy, lanes), peers[brick, piece] ^ me, jnp.int32)
+    for z, hops, row, keep in pieces(cz, peers, slots):
+        last = jnp.full((cy, lanes), hops, jnp.int32) == 3
         late = jnp.full((cy, lanes), row, jnp.int32) >= half
         row_a, row_b = jnp.minimum(row, half - 9), jnp.maximum(row - half, 0)
         for f in range(9):
-            parts = (mine[row + f], core[row + f], chip[row + f], both_a[row_a + f], both_b[row_b + f])
-            parts = [part.astype(jnp.float32) for part in parts]
-            value = jnp.where(late, parts[4], parts[3])
-            value = jnp.where(hops < 2, jnp.where(hops == 1, parts[1], parts[0]), jnp.where(hops == 2, parts[2], value))
-            ring_f[f, z] = value if keep is None else value * keep
+            a, b = both_a[row_a + f].astype(jnp.float32), both_b[row_b + f].astype(jnp.float32)
+            value = jnp.where(late, b, a)
+            ring_f[f, z] = jnp.where(last, value if keep is None else value * keep, ring_f[f, z])
     for f in range(9):
         ring_f[f, layers] = strip_whole(strip_part(zero, lambda z: ring_f[f, z], range(layers)))
     strip = [ring_f[f, layers] for f in range(9)] + strip
@@ -703,21 +714,26 @@
     )
     both = [lax.ppermute(part, "gz", [(i, i ^ 1) for i in range(holders)]) for part in (chip[:half], chip[half:])]
 
-    (ring_w,) = kernel_call(
-        functools.partial(frame_kernel, cz), (own,), [vmem()], (shape(FIELDS - ADJ, layers + 1, cy, cx),)
+    table_scratch = [
+        pltpu.SMEM(peer.shape, jnp.int32),
+        pltpu.SMEM(slot.shape, jnp.int32),
+        pltpu.SemaphoreType.DMA((2,)),
+    ]
+    ring_f, ring_w = kernel_call(
+        functools.partial(frame_kernel, cz),
+        (to_core, core, chip, peer, slot, own),
+        [vmem()] * 6,
+        (shape(ADJ, layers + 1, cy, cx), shape(FIELDS - ADJ, layers + 1, cy, cx)),
+        table_scratch,
     )
     x_send = shape(x_tiles(), cy, cx, dtype=bf16)
     ring_f, ring_w, x_a, x_b = kernel_call(
         functools.partial(column_kernel, cz),
-        (to_core, core, chip, *both, far_face, peer, slot, ring_w),
-        [vmem()] * 9,
-        (shape(ADJ, layers + 1, cy, cx), shape(*ring_w.shape), x_send, x_send if wide_x else None),
-        [
-            pltpu.SMEM(peer.shape, jnp.int32),
-            pltpu.SMEM(slot.shape, jnp.int32),
-            pltpu.SemaphoreType.DMA((2,)),
-        ],
-        {8: 1},
+        (core, *both, far_face, peer, slot, ring_f, ring_w),
+        [vmem()] * 8,
+        (shape(*ring_f.shape), shape(*ring_w.shape), x_send, x_send if wide_x else None),
+        table_scratch,
+        {6: 0, 7: 1},
     )
     axes = ("gx", "gy", "gz")
     gx = lax.axis_size("gx")
@@ -726,7 +742,7 @@
         if x_turn is not None:
             i = dict(swap_pairs(gx, x_turn))[i]
         if y_turn is not None:
-            other = dict(swap_pairs(gy, (c + y_turn) % 2))[j]
+            other = dict(swap_pairs(gy, (c + y_turn + 1) % 2))[j]
             i, j = (i ^ 1, j) if other == j else (i, other)
         return (i * gy + j) * holders + c
 

time: 22.8 us -> 22.8 us (level)
  waiting for transfers between devices: 5.98 us -> 5.22 us
  Pallas kernels: 5.86 us -> 6.55 us
    pallas_call x8, Pallas kernels: 5.86 us -> 6.55 us  [kernel_call(): pl.pallas_call(run, out_shape=tuple((o for o in out_shape if o is not Non...]
    ppermute x1, waiting for transfers between devices: 0.72 us -> 0.07 us  [on_device(): lax.ppermute(to_far, ('gy', 'gz'), [(a[0] * holders + a[1], b[0] * holder...]
  transfers between devices with their start and end apart: 8 -> 8, of which waited for: 5 -> 5; matrix products, arithmetic and copies ran while one was open for 0% -> 0% of each run, Pallas kernels for 13% -> 16%
where the time goes in v11:
time: 22.8 us; the launch traced here: 22.6 us
  starting transfers between devices  10.1 us (44%)
  Pallas kernels  6.55 us (29%)
  waiting for transfers between devices  5.22 us (23%)
  between operations  0.7 us (3%)
    pallas_call x8, Pallas kernels, kernel_call(): pl.pallas_call(run, out_shape=tuple((o for o in out_shape if o is not Non...  6.55 us
    ppermute x3, starting transfers between devices, swap(): return lax.ppermute(value, axes, pairs)  4.92 us
    ppermute x3, waiting for transfers between devices, swap(): return lax.ppermute(value, axes, pairs)  3.85 us
    ppermute x1, starting transfers between devices, on_device(): chip = lax.ppermute(store, 'gz', [(i, i ^ 2) for i in range(holders)])  3 us
    ppermute x1, starting transfers between devices, on_device(): lax.ppermute(to_far, ('gy', 'gz'), [(a[0] * holders + a[1], b[0] * holder...  1.64 us
    ppermute x1, waiting for transfers between devices, on_device(): chip = lax.ppermute(store, 'gz', [(i, i ^ 2) for i in range(holders)])  1.29 us
    ppermute x2, starting transfers between devices, on_device(): lax.ppermute(part, 'gz', [(i, i ^ 1) for i in range(holders)])  0.57 us
  transfers between devices with their start and end apart: 8, of which 5 were waited for; matrix products, arithmetic and copies ran while one was open for 0% of the time, Pallas kernels for 16%

profile of v11, /device:TPU:0, one launch (start us, length us, event | category | flops | bytes accessed | tf_op | source)
XLA Modules:
  0.0 22.6 jit_solution(9776871376819709848)
XLA Ops:
  0.6 3.0 %collective-permute-start.1 = (bf16[72,8,128]{2,1,0:T(8,128)(2,1)}, bf16[72,8,128]{2,1,0:T(8,128)(2,1)S(1)}, u32[]{:S(2)}, u32[]{:S(2)}) collective-permute-start(bf16[72,8,128]{2,1,0:T(8,128)(2,1)} %bitcast.6), channel_id=1, source_target_pairs={{0,2},{1,3},{2,0},{3,1},{4,6},{5,7},{6,4},{7,5},{8,10},{9,11},{10,... | collective-permute-start | bytes 442376 | tf_op jit(solution)/shard_map/ppermute | solution.py:690
  3.6 1.3 %shard_map.139 = (bf16[107,8,128]{2,1,0:T(8,128)(2,1)S(1)}, bf16[37,8,128]{2,1,0:T(8,128)(2,1)S(1)}, f32[15,8,8,128]{3,2,1,0:T(8,128)S(1)}, s32[4,8]{1,0:T(4,128)S(1)}, s32[4,8]{1,0:T(4,128)S(1)}) custom-call(bf16[72,8,128]{2,1,0:T(8,128)(2,1)} %bitcast.7, f32[9,8,8,128]{3,2,1,0:T(8,128)} %refs_1_.1, f32[8,8,128]{2,1,0:T(8,128)} %refs_2_.1, ...), custom_call_target="tpu_custom_call" | custom-call | tf_op jit(solution)/shard_map/pallas_call | solution.py:645
  4.9 1.6 %collective-permute-start.4 = (bf16[37,8,128]{2,1,0:T(8,128)(2,1)S(1)}, bf16[37,8,128]{2,1,0:T(8,128)(2,1)S(1)}, u32[]{:S(2)}, u32[]{:S(2)}) collective-permute-start(bf16[37,8,128]{2,1,0:T(8,128)(2,1)S(1)} %get-tuple-element.25), channel_id=1, source_target_pairs={{0,4},{1,2},{2,1},{3,7},{4,0},{5,6},{6,5},{7,3},{8,12},{9,10},{10,... | collective-permute-start | bytes 227336 | tf_op jit(solution)/shard_map/ppermute | solution.py:712
  6.6 0.0 collective-permute-start
  6.6 1.3 %collective-permute-done.1.refs_2_ = bf16[72,8,128]{2,1,0:T(8,128)(2,1)S(1)} collective-permute-done((bf16[72,8,128]{2,1,0:T(8,128)(2,1)}, bf16[72,8,128]{2,1,0:T(8,128)(2,1)S(1)}, u32[]{:S(2)}, u32[]{:S(2)}) %collective-permute-start.1) | collective-permute-done | bytes 147488 | tf_op jit(solution)/shard_map/ppermute | solution.py:690
  7.9 0.1 collective-permute-start.3
  8.0 0.5 %collective-permute-start.2 = (bf16[36,8,128]{2,1,0:T(8,128)(2,1)S(1)}, bf16[36,8,128]{2,1,0:T(8,128)(2,1)S(1)}, u32[]{:S(2)}, u32[]{:S(2)}) collective-permute-start(bf16[36,8,128]{2,1,0:T(8,128)(2,1)S(1)} %get-tuple-element.46), channel_id=1, source_target_pairs={{0,1},{1,0},{2,3},{3,2},{4,5},{5,4},{6,7},{7,6},{8,9},{9,8},{10,11... | collective-permute-start | bytes 221192 | tf_op jit(solution)/shard_map/ppermute | solution.py:715
  8.5 0.0 collective-permute-done.refs_1_.refs_0_
  8.5 0.8 %shard_map.140 = (f32[9,13,8,128]{3,2,1,0:T(8,128)S(1)}, f32[14,13,8,128]{3,2,1,0:T(8,128)S(1)}) custom-call(bf16[107,8,128]{2,1,0:T(8,128)(2,1)S(1)} %get-tuple-element.24.refs_0_, bf16[107,8,128]{2,1,0:T(8,128)(2,1)S(1)} %collective-permute-done.refs_1_.refs_0_, bf16[72,8,128]{2,1,0:T(8,128)(2,1)S(1)} %collective-permute-done.1.refs_2_, ...), custom_call_target="tpu_custom_call" | custom-call | tf_op jit(solution)/shard_map/pallas_call | solution.py:645
  9.3 0.1 collective-permute-done.4.refs_3_
  9.4 0.0 collective-permute-done.3.refs_2_
  9.4 0.0 collective-permute-done.2.refs_1_
  9.4 1.1 %shard_map.141 = (f32[9,13,8,128]{3,2,1,0:T(8,128)S(1)}, f32[14,13,8,128]{3,2,1,0:T(8,128)S(1)}, bf16[11,8,128]{2,1,0:T(8,128)(2,1)S(1)}) custom-call(bf16[107,8,128]{2,1,0:T(8,128)(2,1)S(1)} %collective-permute-done.refs_1_.refs_0_, bf16[36,8,128]{2,1,0:T(8,128)(2,1)S(1)} %collective-permute-done.2.refs_1_, ...), custom_call_target="tpu_custom_call", output_to_operand_aliasing={{0}: (6, {}), {1}: (7, {})} | custom-call | tf_op jit(solution)/shard_map/pallas_call | solution.py:645
  10.4 1.6 %collective-permute-start.5 = (bf16[11,8,128]{2,1,0:T(8,128)(2,1)S(1)}, bf16[11,8,128]{2,1,0:T(8,128)(2,1)S(1)}, u32[]{:S(2)}, u32[]{:S(2)}) collective-permute-start(bf16[11,8,128]{2,1,0:T(8,128)(2,1)S(1)} %get-tuple-element.33), channel_id=1, source_target_pairs={{0,16},{1,17},{2,18},{3,19},{4,20},{5,21},{6,22},{7,23},{8,24},{9,... | collective-permute-start | bytes 67592 | tf_op jit(solution)/shard_map/ppermute | solution.py:756
  12.1 0.3 %shard_map.142 = (bf16[52,8,128]{2,1,0:T(8,128)(2,1)S(1)}, bf16[52,8,128]{2,1,0:T(8,128)(2,1)S(1)}) custom-call(f32[9,13,8,128]{3,2,1,0:T(8,128)S(1)} %get-tuple-element.31.refs_0_, f32[14,13,8,128]{3,2,1,0:T(8,128)S(1)} %get-tuple-element.32.refs_1_), custom_call_target="tpu_custom_call" | custom-call | tf_op jit(solution)/shard_map/pallas_call | solution.py:645
  12.4 2.0 %collective-permute-done.5.refs_2_ = bf16[11,8,128]{2,1,0:T(8,128)(2,1)S(1)} collective-permute-done((bf16[11,8,128]{2,1,0:T(8,128)(2,1)S(1)}, bf16[11,8,128]{2,1,0:T(8,128)(2,1)S(1)}, u32[]{:S(2)}, u32[]{:S(2)}) %collective-permute-start.5) | collective-permute-done | bytes 22560 | tf_op jit(solution)/shard_map/ppermute | solution.py:756
  14.3 0.1 shard_map.143
  14.4 1.6 %collective-permute-start.6 = (bf16[52,8,128]{2,1,0:T(8,128)(2,1)S(1)}, bf16[52,8,128]{2,1,0:T(8,128)(2,1)S(1)}, u32[]{:S(2)}, u32[]{:S(2)}) collective-permute-start(bf16[52,8,128]{2,1,0:T(8,128)(2,1)S(1)} %get-tuple-element.36), channel_id=1, source_target_pairs={{0,16},{1,5},{2,18},{3,7},{4,8},{5,1},{6,10},{7,3},{8,4},{9,13},{1... | collective-permute-start | bytes 319496 | tf_op jit(solution)/shard_map/ppermute | solution.py:756
  16.1 1.6 %collective-permute-start.7 = (bf16[52,8,128]{2,1,0:T(8,128)(2,1)S(1)}, bf16[52,8,128]{2,1,0:T(8,128)(2,1)S(1)}, u32[]{:S(2)}, u32[]{:S(2)}) collective-permute-start(bf16[52,8,128]{2,1,0:T(8,128)(2,1)S(1)} %get-tuple-element.41), channel_id=1, source_target_pairs={{0,4},{1,17},{2,6},{3,19},{4,0},{5,9},{6,2},{7,11},{8,12},{9,5},{1... | collective-permute-start | bytes 319496 | tf_op jit(solution)/shard_map/ppermute | solution.py:756
  17.7 1.0 %shard_map.144 = (f32[24,13,8,128]{3,2,1,0:T(8,128)S(1)}, f32[8,3,13,8,128]{4,3,2,1,0:T(8,128)S(1)}, f32[11,8,8,128]{3,2,1,0:T(8,128)S(1)}) custom-call(f32[9,13,8,128]{3,2,1,0:T(8,128)S(1)} %get-tuple-element.31.refs_0_, f32[14,13,8,128]{3,2,1,0:T(8,128)S(1)} %get-tuple-element.32.refs_1_, f32[23,8,128]{2,1,0:T(8,128)S(1)} %get-tuple-element.37.refs_2_, ...), custom_call_target="tpu_custom_call" | custom-call | tf_op jit(solution)/shard_map/pallas_call | solution.py:645
  18.8 1.2 %collective-permute-done.6.refs_0_ = bf16[52,8,128]{2,1,0:T(8,128)(2,1)S(1)} collective-permute-done((bf16[52,8,128]{2,1,0:T(8,128)(2,1)S(1)}, bf16[52,8,128]{2,1,0:T(8,128)(2,1)S(1)}, u32[]{:S(2)}, u32[]{:S(2)}) %collective-permute-start.6) | collective-permute-done | bytes 106528 | tf_op jit(solution)/shard_map/ppermute | solution.py:756
  20.0 0.1 shard_map.145.refs_0_
  20.1 0.7 %collective-permute-done.7.refs_3_ = bf16[52,8,128]{2,1,0:T(8,128)(2,1)S(1)} collective-permute-done((bf16[52,8,128]{2,1,0:T(8,128)(2,1)S(1)}, bf16[52,8,128]{2,1,0:T(8,128)(2,1)S(1)}, u32[]{:S(2)}, u32[]{:S(2)}) %collective-permute-start.7) | collective-permute-done | bytes 106528 | tf_op jit(solution)/shard_map/ppermute | solution.py:756
  20.8 1.8 %shard_map.146 = (f32[9,8,8,128]{3,2,1,0:T(8,128)}, f32[8,8,128]{2,1,0:T(8,128)}, f32[8,8,128]{2,1,0:T(8,128)}, f32[24,13,8,128]{3,2,1,0:T(8,128)S(1)}) custom-call(f32[24,13,8,128]{3,2,1,0:T(8,128)S(1)} %shard_map.145.refs_0_, f32[8,3,13,8,128]{4,3,2,1,0:T(8,128)S(1)} %get-tuple-element.39.refs_1_, ...), custom_call_target="tpu_custom_call", output_to_operand_aliasing={{3}: (0, {})} | custom-call | tf_op jit(solution)/shard_map/pallas_call | solution.py:645
  (1 shorter events, 0.0 us)
Async XLA Ops:
  0.6 7.2 %collective-permute-start.1 = (bf16[72,8,128]{2,1,0:T(8,128)(2,1)}, bf16[72,8,128]{2,1,0:T(8,128)(2,1)S(1)}, u32[]{:S(2)}, u32[]{:S(2)}) collective-permute-start(bf16[72,8,128]{2,1,0:T(8,128)(2,1)} %bitcast.6), channel_id=1, source_target_pairs={{0,2},{1,3},{2,0},{3,1},{4,6},{5,7},{6,4},{7,5},{8,10},{9,11},{10,... | collective-permute-start | bytes 442376 | tf_op jit(solution)/shard_map/ppermute | solution.py:690
  4.9 4.4 %collective-permute-start.4 = (bf16[37,8,128]{2,1,0:T(8,128)(2,1)S(1)}, bf16[37,8,128]{2,1,0:T(8,128)(2,1)S(1)}, u32[]{:S(2)}, u32[]{:S(2)}) collective-permute-start(bf16[37,8,128]{2,1,0:T(8,128)(2,1)S(1)} %get-tuple-element.25), channel_id=1, source_target_pairs={{0,4},{1,2},{2,1},{3,7},{4,0},{5,6},{6,5},{7,3},{8,12},{9,10},{10,... | collective-permute-start | bytes 227336 | tf_op jit(solution)/shard_map/ppermute | solution.py:712
  6.6 1.9 %collective-permute-start = (bf16[107,8,128]{2,1,0:T(8,128)(2,1)S(1)}, bf16[107,8,128]{2,1,0:T(8,128)(2,1)S(1)}, u32[]{:S(2)}, u32[]{:S(2)}) collective-permute-start(bf16[107,8,128]{2,1,0:T(8,128)(2,1)S(1)} %get-tuple-element.24.refs_0_), channel_id=1, source_target_pairs={{0,1},{1,0},{2,3},{3,2},{4,5},{5,4},{6,7},{7,6},{8,9},{9,8},{10,11... | collective-permute-start | bytes 657416 | tf_op jit(solution)/shard_map/ppermute | solution.py:706
  7.9 1.5 %collective-permute-start.3 = (bf16[36,8,128]{2,1,0:T(8,128)(2,1)S(1)}, bf16[36,8,128]{2,1,0:T(8,128)(2,1)S(1)}, u32[]{:S(2)}, u32[]{:S(2)}) collective-permute-start(bf16[36,8,128]{2,1,0:T(8,128)(2,1)S(1)} %get-tuple-element.45), channel_id=1, source_target_pairs={{0,1},{1,0},{2,3},{3,2},{4,5},{5,4},{6,7},{7,6},{8,9},{9,8},{10,11... | collective-permute-start | bytes 221192 | tf_op jit(solution)/shard_map/ppermute | solution.py:715
  8.0 1.4 %collective-permute-start.2 = (bf16[36,8,128]{2,1,0:T(8,128)(2,1)S(1)}, bf16[36,8,128]{2,1,0:T(8,128)(2,1)S(1)}, u32[]{:S(2)}, u32[]{:S(2)}) collective-permute-start(bf16[36,8,128]{2,1,0:T(8,128)(2,1)S(1)} %get-tuple-element.46), channel_id=1, source_target_pairs={{0,1},{1,0},{2,3},{3,2},{4,5},{5,4},{6,7},{7,6},{8,9},{9,8},{10,11... | collective-permute-start | bytes 221192 | tf_op jit(solution)/shard_map/ppermute | solution.py:715
  10.4 3.9 %collective-permute-start.5 = (bf16[11,8,128]{2,1,0:T(8,128)(2,1)S(1)}, bf16[11,8,128]{2,1,0:T(8,128)(2,1)S(1)}, u32[]{:S(2)}, u32[]{:S(2)}) collective-permute-start(bf16[11,8,128]{2,1,0:T(8,128)(2,1)S(1)} %get-tuple-element.33), channel_id=1, source_target_pairs={{0,16},{1,17},{2,18},{3,19},{4,20},{5,21},{6,22},{7,23},{8,24},{9,... | collective-permute-start | bytes 67592 | tf_op jit(solution)/shard_map/ppermute | solution.py:756
  14.4 5.5 %collective-permute-start.6 = (bf16[52,8,128]{2,1,0:T(8,128)(2,1)S(1)}, bf16[52,8,128]{2,1,0:T(8,128)(2,1)S(1)}, u32[]{:S(2)}, u32[]{:S(2)}) collective-permute-start(bf16[52,8,128]{2,1,0:T(8,128)(2,1)S(1)} %get-tuple-element.36), channel_id=1, source_target_pairs={{0,16},{1,5},{2,18},{3,7},{4,8},{5,1},{6,10},{7,3},{8,4},{9,13},{1... | collective-permute-start | bytes 319496 | tf_op jit(solution)/shard_map/ppermute | solution.py:756
  16.1 4.7 %collective-permute-start.7 = (bf16[52,8,128]{2,1,0:T(8,128)(2,1)S(1)}, bf16[52,8,128]{2,1,0:T(8,128)(2,1)S(1)}, u32[]{:S(2)}, u32[]{:S(2)}) collective-permute-start(bf16[52,8,128]{2,1,0:T(8,128)(2,1)S(1)} %get-tuple-element.41), channel_id=1, source_target_pairs={{0,4},{1,17},{2,6},{3,19},{4,0},{5,9},{6,2},{7,11},{8,12},{9,5},{1... | collective-permute-start | bytes 319496 | tf_op jit(solution)/shard_map/ppermute | solution.py:756

commit v12 on v11

--- a/solution.py
+++ b/solution.py
@@ -190,24 +190,30 @@
 
 def start_kernel(
     cz, store, adjoint, lam, mu, buoy, source, wavelet, receiver, traces, plan, peer, slot,
-    near_out, far_out, own, peer_out, slot_out, cells, samples, spots, wave, steps, sems,
+    near_out, far_out, own, codes, cells, samples, spots, wave, steps, peers, slots, sems,
 ):
     cy, lanes = own.shape[2], own.shape[3]
     rows = cz * cy
     tiles = store.shape[0]
-    small = copies(sems, (plan, steps), (wavelet, wave), (source, spots), (receiver, cells), (traces, samples))
+    small = copies(
+        sems, (plan, steps), (wavelet, wave), (source, spots), (receiver, cells), (traces, samples),
+        (peer, peers), (slot, slots),
+    )
     large = copies(
-        sems.at[pl.ds(len(small), 7)],
+        sems.at[pl.ds(len(small), 5)],
         (adjoint, own.at[pl.ds(0, 9)]),
         (buoy, own.at[BUOY - ADJ]),
         (lam, own.at[LAM - ADJ]),
         (mu, own.at[MU - ADJ]),
         (store, near_out.at[pl.ds(0, tiles)]),
-        (peer, peer_out),
-        (slot, slot_out),
     )
     for copy in small:
         copy.wait()
+    lane = lax.broadcasted_iota(jnp.int32, (cy, lanes), 1)
+    code = jnp.zeros((cy, lanes), jnp.int32)
+    for z, hops, row in pieces(cz, peers, slots):
+        code = jnp.where(lane == z, row * 4 + hops, code)
+    codes[...] = code
     listed = cells[...]
     count = listed.shape[1]
     row_hot = (lax.broadcasted_iota(jnp.int32, (rows, count), 0) == listed // lanes).astype(jnp.float32)
@@ -275,19 +281,26 @@
 def pieces(cz, peers, slots):
     me, count = lax.axis_index("gz"), lax.axis_size("gz")
     below, above = jnp.maximum(me - 1, 0), jnp.minimum(me + 1, count - 1)
-    has_below, has_above = has_neighbours("gz")
     for z in range(cz + 2 * HALO):
         if z < HALO:
-            brick, piece, keep = below, cz - HALO + z, has_below
+            brick, piece = below, cz - HALO + z
         elif z < HALO + cz:
-            brick, piece, keep = me, z - HALO, None
+            brick, piece = me, z - HALO
         else:
-            brick, piece, keep = above, z - HALO - cz, has_above
-        yield z, peers[brick, piece] ^ me, slots[brick, piece] * 9, keep
-
-
-def frame_kernel(cz, mine, core, chip, peer, slot, own, ring_f, ring, peers, slots, sems):
-    moves = copies(sems, (peer, peers), (slot, slots))
+            brick, piece = above, z - HALO - cz
+        yield z, peers[brick, piece] ^ me, slots[brick, piece] * 9
+
+
+def coded(cz, codes):
+    has_below, has_above = has_neighbours("gz")
+    listed = codes[0:1, :]
+    for z in range(cz + 2 * HALO):
+        code = listed[0, z]
+        keep = has_below if z < HALO else None if z < HALO + cz else has_above
+        yield z, code & 3, code >> 2, keep
+
+
+def frame_kernel(cz, mine, core, chip, codes, own, ring_f, ring):
     cy, lanes = own.shape[2], own.shape[3]
     layers = cz + 2 * HALO
     zero = jnp.zeros((cy, lanes), jnp.float32)
@@ -299,9 +312,7 @@
             if (f, z) not in filled:
                 ring[f, z] = zero
         ring[f, layers] = strip_part(zero, lambda z: own[f, z - HALO], range(HALO, HALO + cz))
-    for move in moves:
-        move.wait()
-    for z, hops, row, keep in pieces(cz, peers, slots):
+    for z, hops, row, keep in coded(cz, codes):
         hops = jnp.full((cy, lanes), hops, jnp.int32)
         for f in range(9):
             a, b, c = (ref[row + f].astype(jnp.float32) for ref in (mine, core, chip))
@@ -310,14 +321,12 @@
 
 
 def column_kernel(
-    cz, core, both_a, both_b, far, peer, slot, ring_f_in, ring_w_in,
-    ring_f, ring, x_a, x_b, peers, slots, sems,
+    cz, core, both_a, both_b, far, codes, ring_f_in, ring_w_in, ring_f, ring, x_a, x_b
 ):
     cy, lanes = core.shape[1], core.shape[2]
     layers = cz + 2 * HALO
     half = both_a.shape[0]
     tiles = half + both_b.shape[0]
-    moves = copies(sems, (peer, peers), (slot, slots))
     near, _ = face_counts(cz)
     even = even_mask("gz", (cy, lanes))
     has_below, has_above = has_neighbours("gz")
@@ -342,9 +351,7 @@
         tile = strip_whole(strip_part(ring[f, layers], lambda z: there[z], sorted(there)))
         ring[f, layers] = tile
         strip.append(tile)
-    for move in moves:
-        move.wait()
-    for z, hops, row, keep in pieces(cz, peers, slots):
+    for z, hops, row, keep in coded(cz, codes):
         last = jnp.full((cy, lanes), hops, jnp.int32) == 3
         late = jnp.full((cy, lanes), row, jnp.int32) >= half
         row_a, row_b = jnp.minimum(row, half - 9), jnp.maximum(row - half, 0)
@@ -688,18 +695,20 @@
 
     wide_x = lax.axis_size("gx") > 2
     chip = lax.ppermute(store, "gz", [(i, i ^ 2) for i in range(holders)])
-    to_core, to_far, own, peer, slot = kernel_call(
+    to_core, to_far, own, codes = kernel_call(
         functools.partial(start_kernel, cz),
         (store, adjoint_state, lame_lambda, lame_mu, buoyancy, source, wavelet, receiver, traces, plan, peer, slot),
         [hbm()] * 12,
         (shape(tiles + face, cy, cx, dtype=bf16), shape(max(face, half) + PAD, cy, cx, dtype=bf16), shape(15, cz, cy, cx),
-         shape(*peer.shape, dtype=jnp.int32), shape(*slot.shape, dtype=jnp.int32)),
+         shape(cy, cx, dtype=jnp.int32)),
         [
             pltpu.VMEM(receiver.shape, jnp.int32),
             pltpu.VMEM(traces.shape, f32),
             pltpu.SMEM(source.shape, jnp.int32),
             pltpu.SMEM(wavelet.shape, f32),
             pltpu.SMEM(plan.shape, jnp.int32),
+            pltpu.SMEM(peer.shape, jnp.int32),
+            pltpu.SMEM(slot.shape, jnp.int32),
             pltpu.SemaphoreType.DMA((12,)),
         ],
     )
@@ -714,26 +723,20 @@
     )
     both = [lax.ppermute(part, "gz", [(i, i ^ 1) for i in range(holders)]) for part in (chip[:half], chip[half:])]
 
-    table_scratch = [
-        pltpu.SMEM(peer.shape, jnp.int32),
-        pltpu.SMEM(slot.shape, jnp.int32),
-        pltpu.SemaphoreType.DMA((2,)),
-    ]
     ring_f, ring_w = kernel_call(
         functools.partial(frame_kernel, cz),
-        (to_core, core, chip, peer, slot, own),
-        [vmem()] * 6,
+        (to_core, core, chip, codes, own),
+        [vmem()] * 5,
         (shape(ADJ, layers + 1, cy, cx), shape(FIELDS - ADJ, layers + 1, cy, cx)),
-        table_scratch,
     )
     x_send = shape(x_tiles(), cy, cx, dtype=bf16)
     ring_f, ring_w, x_a, x_b = kernel_call(
         functools.partial(column_kernel, cz),
-        (core, *both, far_face, peer, slot, ring_f, ring_w),
-        [vmem()] * 8,
+        (core, *both, far_face, codes, ring_f, ring_w),
+        [vmem()] * 7,
         (shape(*ring_f.shape), shape(*ring_w.shape), x_send, x_send if wide_x else None),
-        table_scratch,
-        {6: 0, 7: 1},
+        (),
+        {5: 0, 6: 1},
     )
     axes = ("gx", "gy", "gz")
     gx = lax.axis_size("gx")

time: 22.8 us -> 22.3 us (0.978)
  Pallas kernels: 6.55 us -> 5.58 us
  waiting for transfers between devices: 5.22 us -> 5.86 us
    pallas_call x8, Pallas kernels: 6.55 us -> 5.58 us  [kernel_call(): pl.pallas_call(run, out_shape=tuple((o for o in out_shape if o is not Non...]
    ppermute x1, waiting for transfers between devices: 0.07 us -> 0.76 us  [on_device(): lax.ppermute(to_far, ('gy', 'gz'), [(a[0] * holders + a[1], b[0] * holder...]
  transfers between devices with their start and end apart: 8 -> 8, of which waited for: 5 -> 5; matrix products, arithmetic and copies ran while one was open for 0% -> 0% of each run, Pallas kernels for 16% -> 14%
where the time goes in v12:
time: 22.3 us; the launch traced here: 22.2 us
  starting transfers between devices  10 us (45%)
  waiting for transfers between devices  5.86 us (26%)
  Pallas kernels  5.58 us (25%)
  between operations  0.69 us (3%)
    pallas_call x8, Pallas kernels, kernel_call(): pl.pallas_call(run, out_shape=tuple((o for o in out_shape if o is not Non...  5.58 us
    ppermute x3, starting transfers between devices, swap(): return lax.ppermute(value, axes, pairs)  4.8 us
    ppermute x3, waiting for transfers between devices, swap(): return lax.ppermute(value, axes, pairs)  3.91 us
    ppermute x1, starting transfers between devices, on_device(): chip = lax.ppermute(store, 'gz', [(i, i ^ 2) for i in range(holders)])  3 us
    ppermute x1, starting transfers between devices, on_device(): lax.ppermute(to_far, ('gy', 'gz'), [(a[0] * holders + a[1], b[0] * holder...  1.64 us
    ppermute x1, waiting for transfers between devices, on_device(): chip = lax.ppermute(store, 'gz', [(i, i ^ 2) for i in range(holders)])  1.18 us
    ppermute x1, waiting for transfers between devices, on_device(): lax.ppermute(to_far, ('gy', 'gz'), [(a[0] * holders + a[1], b[0] * holder...  0.76 us
    ppermute x2, starting transfers between devices, on_device(): lax.ppermute(part, 'gz', [(i, i ^ 1) for i in range(holders)])  0.57 us
  transfers between devices with their start and end apart: 8, of which 5 were waited for; matrix products, arithmetic and copies ran while one was open for 0% of the time, Pallas kernels for 14%

profile of v12, /device:TPU:0, one launch (start us, length us, event | category | flops | bytes accessed | tf_op | source)
XLA Modules:
  0.0 22.2 jit_solution(1685080539447251743)
XLA Ops:
  0.6 3.0 %collective-permute-start.1 = (bf16[72,8,128]{2,1,0:T(8,128)(2,1)}, bf16[72,8,128]{2,1,0:T(8,128)(2,1)S(1)}, u32[]{:S(2)}, u32[]{:S(2)}) collective-permute-start(bf16[72,8,128]{2,1,0:T(8,128)(2,1)} %bitcast.6), channel_id=1, source_target_pairs={{0,2},{1,3},{2,0},{3,1},{4,6},{5,7},{6,4},{7,5},{8,10},{9,11},{10,... | collective-permute-start | bytes 442376 | tf_op jit(solution)/shard_map/ppermute | solution.py:697
  3.6 1.4 %shard_map.139 = (bf16[107,8,128]{2,1,0:T(8,128)(2,1)S(1)}, bf16[37,8,128]{2,1,0:T(8,128)(2,1)S(1)}, f32[15,8,8,128]{3,2,1,0:T(8,128)S(1)}, s32[8,128]{1,0:T(8,128)S(1)}) custom-call(bf16[72,8,128]{2,1,0:T(8,128)(2,1)} %bitcast.7, f32[9,8,8,128]{3,2,1,0:T(8,128)} %refs_1_.1, f32[8,8,128]{2,1,0:T(8,128)} %refs_2_.1, f32[8,8,128]{2,1,0:T(8,128)} %refs_3_.1, ...), custom_call_target="tpu_custom_call" | custom-call | tf_op jit(solution)/shard_map/pallas_call | solution.py:652
  5.0 1.6 %collective-permute-start.4 = (bf16[37,8,128]{2,1,0:T(8,128)(2,1)S(1)}, bf16[37,8,128]{2,1,0:T(8,128)(2,1)S(1)}, u32[]{:S(2)}, u32[]{:S(2)}) collective-permute-start(bf16[37,8,128]{2,1,0:T(8,128)(2,1)S(1)} %get-tuple-element.24), channel_id=1, source_target_pairs={{0,4},{1,2},{2,1},{3,7},{4,0},{5,6},{6,5},{7,3},{8,12},{9,10},{10,... | collective-permute-start | bytes 227336 | tf_op jit(solution)/shard_map/ppermute | solution.py:721
  6.7 0.0 collective-permute-start
  6.7 1.2 %collective-permute-done.1.refs_2_ = bf16[72,8,128]{2,1,0:T(8,128)(2,1)S(1)} collective-permute-done((bf16[72,8,128]{2,1,0:T(8,128)(2,1)}, bf16[72,8,128]{2,1,0:T(8,128)(2,1)S(1)}, u32[]{:S(2)}, u32[]{:S(2)}) %collective-permute-start.1) | collective-permute-done | bytes 147488 | tf_op jit(solution)/shard_map/ppermute | solution.py:697
  7.9 0.1 collective-permute-start.3
  8.0 0.5 %collective-permute-start.2 = (bf16[36,8,128]{2,1,0:T(8,128)(2,1)S(1)}, bf16[36,8,128]{2,1,0:T(8,128)(2,1)S(1)}, u32[]{:S(2)}, u32[]{:S(2)}) collective-permute-start(bf16[36,8,128]{2,1,0:T(8,128)(2,1)S(1)} %get-tuple-element.44), channel_id=1, source_target_pairs={{0,1},{1,0},{2,3},{3,2},{4,5},{5,4},{6,7},{7,6},{8,9},{9,8},{10,11... | collective-permute-start | bytes 221192 | tf_op jit(solution)/shard_map/ppermute | solution.py:724
  8.5 0.0 collective-permute-done.refs_1_.refs_0_
  8.5 0.3 %shard_map.140 = (f32[9,13,8,128]{3,2,1,0:T(8,128)S(1)}, f32[14,13,8,128]{3,2,1,0:T(8,128)S(1)}) custom-call(bf16[107,8,128]{2,1,0:T(8,128)(2,1)S(1)} %get-tuple-element.23.refs_0_, bf16[107,8,128]{2,1,0:T(8,128)(2,1)S(1)} %collective-permute-done.refs_1_.refs_0_, bf16[72,8,128]{2,1,0:T(8,128)(2,1)S(1)} %collective-permute-done.1.refs_2_, ...), custom_call_target="tpu_custom_call" | custom-call | tf_op jit(solution)/shard_map/pallas_call | solution.py:652
  8.7 0.8 %collective-permute-done.4.refs_3_ = bf16[37,8,128]{2,1,0:T(8,128)(2,1)S(1)} collective-permute-done((bf16[37,8,128]{2,1,0:T(8,128)(2,1)S(1)}, bf16[37,8,128]{2,1,0:T(8,128)(2,1)S(1)}, u32[]{:S(2)}, u32[]{:S(2)}) %collective-permute-start.4) | collective-permute-done | bytes 75808 | tf_op jit(solution)/shard_map/ppermute | solution.py:721
  9.5 0.0 collective-permute-done.3.refs_2_
  9.5 0.0 collective-permute-done.2.refs_1_
  9.5 0.6 %shard_map.141 = (f32[9,13,8,128]{3,2,1,0:T(8,128)S(1)}, f32[14,13,8,128]{3,2,1,0:T(8,128)S(1)}, bf16[11,8,128]{2,1,0:T(8,128)(2,1)S(1)}) custom-call(bf16[107,8,128]{2,1,0:T(8,128)(2,1)S(1)} %collective-permute-done.refs_1_.refs_0_, bf16[36,8,128]{2,1,0:T(8,128)(2,1)S(1)} %collective-permute-done.2.refs_1_, ...), custom_call_target="tpu_custom_call", output_to_operand_aliasing={{0}: (5, {}), {1}: (6, {})} | custom-call | tf_op jit(solution)/shard_map/pallas_call | solution.py:652
  10.1 1.6 %collective-permute-start.5 = (bf16[11,8,128]{2,1,0:T(8,128)(2,1)S(1)}, bf16[11,8,128]{2,1,0:T(8,128)(2,1)S(1)}, u32[]{:S(2)}, u32[]{:S(2)}) collective-permute-start(bf16[11,8,128]{2,1,0:T(8,128)(2,1)S(1)} %get-tuple-element.31), channel_id=1, source_target_pairs={{0,16},{1,17},{2,18},{3,19},{4,20},{5,21},{6,22},{7,23},{8,24},{9,... | collective-permute-start | bytes 67592 | tf_op jit(solution)/shard_map/ppermute | solution.py:759
  11.6 0.3 %shard_map.142 = (bf16[52,8,128]{2,1,0:T(8,128)(2,1)S(1)}, bf16[52,8,128]{2,1,0:T(8,128)(2,1)S(1)}) custom-call(f32[9,13,8,128]{3,2,1,0:T(8,128)S(1)} %get-tuple-element.29.refs_0_, f32[14,13,8,128]{3,2,1,0:T(8,128)S(1)} %get-tuple-element.30.refs_1_), custom_call_target="tpu_custom_call" | custom-call | tf_op jit(solution)/shard_map/pallas_call | solution.py:652
  11.9 2.0 %collective-permute-done.5.refs_2_ = bf16[11,8,128]{2,1,0:T(8,128)(2,1)S(1)} collective-permute-done((bf16[11,8,128]{2,1,0:T(8,128)(2,1)S(1)}, bf16[11,8,128]{2,1,0:T(8,128)(2,1)S(1)}, u32[]{:S(2)}, u32[]{:S(2)}) %collective-permute-start.5) | collective-permute-done | bytes 22560 | tf_op jit(solution)/shard_map/ppermute | solution.py:759
  13.9 0.1 shard_map.143
  14.1 1.6 %collective-permute-start.6 = (bf16[52,8,128]{2,1,0:T(8,128)(2,1)S(1)}, bf16[52,8,128]{2,1,0:T(8,128)(2,1)S(1)}, u32[]{:S(2)}, u32[]{:S(2)}) collective-permute-start(bf16[52,8,128]{2,1,0:T(8,128)(2,1)S(1)} %get-tuple-element.34), channel_id=1, source_target_pairs={{0,16},{1,5},{2,18},{3,7},{4,8},{5,1},{6,10},{7,3},{8,4},{9,13},{1... | collective-permute-start | bytes 319496 | tf_op jit(solution)/shard_map/ppermute | solution.py:759
  15.7 1.6 %collective-permute-start.7 = (bf16[52,8,128]{2,1,0:T(8,128)(2,1)S(1)}, bf16[52,8,128]{2,1,0:T(8,128)(2,1)S(1)}, u32[]{:S(2)}, u32[]{:S(2)}) collective-permute-start(bf16[52,8,128]{2,1,0:T(8,128)(2,1)S(1)} %get-tuple-element.39), channel_id=1, source_target_pairs={{0,4},{1,17},{2,6},{3,19},{4,0},{5,9},{6,2},{7,11},{8,12},{9,5},{1... | collective-permute-start | bytes 319496 | tf_op jit(solution)/shard_map/ppermute | solution.py:759
  17.3 1.0 %shard_map.144 = (f32[24,13,8,128]{3,2,1,0:T(8,128)S(1)}, f32[8,3,13,8,128]{4,3,2,1,0:T(8,128)S(1)}, f32[11,8,8,128]{3,2,1,0:T(8,128)S(1)}) custom-call(f32[9,13,8,128]{3,2,1,0:T(8,128)S(1)} %get-tuple-element.29.refs_0_, f32[14,13,8,128]{3,2,1,0:T(8,128)S(1)} %get-tuple-element.30.refs_1_, f32[23,8,128]{2,1,0:T(8,128)S(1)} %get-tuple-element.35.refs_2_, ...), custom_call_target="tpu_custom_call" | custom-call | tf_op jit(solution)/shard_map/pallas_call | solution.py:652
  18.3 1.1 %collective-permute-done.6.refs_0_ = bf16[52,8,128]{2,1,0:T(8,128)(2,1)S(1)} collective-permute-done((bf16[52,8,128]{2,1,0:T(8,128)(2,1)S(1)}, bf16[52,8,128]{2,1,0:T(8,128)(2,1)S(1)}, u32[]{:S(2)}, u32[]{:S(2)}) %collective-permute-start.6) | collective-permute-done | bytes 106528 | tf_op jit(solution)/shard_map/ppermute | solution.py:759
  19.5 0.1 shard_map.145.refs_0_
  19.6 0.8 %collective-permute-done.7.refs_3_ = bf16[52,8,128]{2,1,0:T(8,128)(2,1)S(1)} collective-permute-done((bf16[52,8,128]{2,1,0:T(8,128)(2,1)S(1)}, bf16[52,8,128]{2,1,0:T(8,128)(2,1)S(1)}, u32[]{:S(2)}, u32[]{:S(2)}) %collective-permute-start.7) | collective-permute-done | bytes 106528 | tf_op jit(solution)/shard_map/ppermute | solution.py:759
  20.4 1.8 %shard_map.146 = (f32[9,8,8,128]{3,2,1,0:T(8,128)}, f32[8,8,128]{2,1,0:T(8,128)}, f32[8,8,128]{2,1,0:T(8,128)}, f32[24,13,8,128]{3,2,1,0:T(8,128)S(1)}) custom-call(f32[24,13,8,128]{3,2,1,0:T(8,128)S(1)} %shard_map.145.refs_0_, f32[8,3,13,8,128]{4,3,2,1,0:T(8,128)S(1)} %get-tuple-element.37.refs_1_, ...), custom_call_target="tpu_custom_call", output_to_operand_aliasing={{3}: (0, {})} | custom-call | tf_op jit(solution)/shard_map/pallas_call | solution.py:652
  (1 shorter events, 0.0 us)
Async XLA Ops:
  0.6 7.2 %collective-permute-start.1 = (bf16[72,8,128]{2,1,0:T(8,128)(2,1)}, bf16[72,8,128]{2,1,0:T(8,128)(2,1)S(1)}, u32[]{:S(2)}, u32[]{:S(2)}) collective-permute-start(bf16[72,8,128]{2,1,0:T(8,128)(2,1)} %bitcast.6), channel_id=1, source_target_pairs={{0,2},{1,3},{2,0},{3,1},{4,6},{5,7},{6,4},{7,5},{8,10},{9,11},{10,... | collective-permute-start | bytes 442376 | tf_op jit(solution)/shard_map/ppermute | solution.py:697
  5.0 4.4 %collective-permute-start.4 = (bf16[37,8,128]{2,1,0:T(8,128)(2,1)S(1)}, bf16[37,8,128]{2,1,0:T(8,128)(2,1)S(1)}, u32[]{:S(2)}, u32[]{:S(2)}) collective-permute-start(bf16[37,8,128]{2,1,0:T(8,128)(2,1)S(1)} %get-tuple-element.24), channel_id=1, source_target_pairs={{0,4},{1,2},{2,1},{3,7},{4,0},{5,6},{6,5},{7,3},{8,12},{9,10},{10,... | collective-permute-start | bytes 227336 | tf_op jit(solution)/shard_map/ppermute | solution.py:721
  6.7 1.8 %collective-permute-start = (bf16[107,8,128]{2,1,0:T(8,128)(2,1)S(1)}, bf16[107,8,128]{2,1,0:T(8,128)(2,1)S(1)}, u32[]{:S(2)}, u32[]{:S(2)}) collective-permute-start(bf16[107,8,128]{2,1,0:T(8,128)(2,1)S(1)} %get-tuple-element.23.refs_0_), channel_id=1, source_target_pairs={{0,1},{1,0},{2,3},{3,2},{4,5},{5,4},{6,7},{7,6},{8,9},{9,8},{10,11... | collective-permute-start | bytes 657416 | tf_op jit(solution)/shard_map/ppermute | solution.py:715
  7.9 1.6 %collective-permute-start.3 = (bf16[36,8,128]{2,1,0:T(8,128)(2,1)S(1)}, bf16[36,8,128]{2,1,0:T(8,128)(2,1)S(1)}, u32[]{:S(2)}, u32[]{:S(2)}) collective-permute-start(bf16[36,8,128]{2,1,0:T(8,128)(2,1)S(1)} %get-tuple-element.43), channel_id=1, source_target_pairs={{0,1},{1,0},{2,3},{3,2},{4,5},{5,4},{6,7},{7,6},{8,9},{9,8},{10,11... | collective-permute-start | bytes 221192 | tf_op jit(solution)/shard_map/ppermute | solution.py:724
  8.0 1.5 %collective-permute-start.2 = (bf16[36,8,128]{2,1,0:T(8,128)(2,1)S(1)}, bf16[36,8,128]{2,1,0:T(8,128)(2,1)S(1)}, u32[]{:S(2)}, u32[]{:S(2)}) collective-permute-start(bf16[36,8,128]{2,1,0:T(8,128)(2,1)S(1)} %get-tuple-element.44), channel_id=1, source_target_pairs={{0,1},{1,0},{2,3},{3,2},{4,5},{5,4},{6,7},{7,6},{8,9},{9,8},{10,11... | collective-permute-start | bytes 221192 | tf_op jit(solution)/shard_map/ppermute | solution.py:724
  10.1 3.9 %collective-permute-start.5 = (bf16[11,8,128]{2,1,0:T(8,128)(2,1)S(1)}, bf16[11,8,128]{2,1,0:T(8,128)(2,1)S(1)}, u32[]{:S(2)}, u32[]{:S(2)}) collective-permute-start(bf16[11,8,128]{2,1,0:T(8,128)(2,1)S(1)} %get-tuple-element.31), channel_id=1, source_target_pairs={{0,16},{1,17},{2,18},{3,19},{4,20},{5,21},{6,22},{7,23},{8,24},{9,... | collective-permute-start | bytes 67592 | tf_op jit(solution)/shard_map/ppermute | solution.py:759
  14.1 5.4 %collective-permute-start.6 = (bf16[52,8,128]{2,1,0:T(8,128)(2,1)S(1)}, bf16[52,8,128]{2,1,0:T(8,128)(2,1)S(1)}, u32[]{:S(2)}, u32[]{:S(2)}) collective-permute-start(bf16[52,8,128]{2,1,0:T(8,128)(2,1)S(1)} %get-tuple-element.34), channel_id=1, source_target_pairs={{0,16},{1,5},{2,18},{3,7},{4,8},{5,1},{6,10},{7,3},{8,4},{9,13},{1... | collective-permute-start | bytes 319496 | tf_op jit(solution)/shard_map/ppermute | solution.py:759
  15.7 4.7 %collective-permute-start.7 = (bf16[52,8,128]{2,1,0:T(8,128)(2,1)S(1)}, bf16[52,8,128]{2,1,0:T(8,128)(2,1)S(1)}, u32[]{:S(2)}, u32[]{:S(2)}) collective-permute-start(bf16[52,8,128]{2,1,0:T(8,128)(2,1)S(1)} %get-tuple-element.39), channel_id=1, source_target_pairs={{0,4},{1,17},{2,6},{3,19},{4,0},{5,9},{6,2},{7,11},{8,12},{9,5},{1... | collective-permute-start | bytes 319496 | tf_op jit(solution)/shard_map/ppermute | solution.py:759

commit v13 on v12

--- a/solution.py
+++ b/solution.py
@@ -368,7 +368,7 @@
         if out is None:
             continue
         place = 0
-        for fields, narrow in ((range(ADJ), True), (range(ADJ, FIELDS), False)):
+        for fields in (range(ADJ), range(ADJ, FIELDS)):
             quads = [fields[i : i + 4] for i in range(0, len(fields), 4)]
             for i, quad in enumerate(quads):
                 tile = zero
@@ -379,13 +379,13 @@
                     tile = jnp.where(position // 2 == g, value, tile)
                 high, low = split(tile)
                 out[place + i] = high
-                if not narrow:
-                    out[place + len(quads) + i] = low
-            place += len(quads) if narrow else 2 * len(quads)
+                if quad[-1] >= INJ:
+                    out[x_tiles() - 1] = low
+            place += len(quads)
 
 
 def x_tiles():
-    return -(-ADJ // 4) + 2 * -(-(FIELDS - ADJ) // 4)
+    return -(-ADJ // 4) + -(-(FIELDS - ADJ) // 4) + 1
 
 
 def strip_rows_kernel(cz, ring_f, ring_w, x_a, x_b, y_a_in, y_b_in, strips, y_a, y_b, packed):
@@ -396,24 +396,24 @@
     has_left, has_right = has_neighbours("gx")
     zero = jnp.zeros((cy, lanes), jnp.float32)
     place = 0
-    for fields, narrow in ((range(ADJ), True), (range(ADJ, FIELDS), False)):
+    for fields in (range(ADJ), range(ADJ, FIELDS)):
         quads = [fields[i : i + 4] for i in range(0, len(fields), 4)]
         for i, quad in enumerate(quads):
             got = []
             for ref in (x_a, x_b):
                 if ref is None:
                     got.append(zero)
-                elif narrow:
+                elif quad[-1] < INJ:
                     got.append(ref[place + i].astype(jnp.float32))
                 else:
-                    got.append(joined(ref[place + i], ref[place + len(quads) + i]))
+                    got.append(joined(ref[place + i], ref[x_tiles() - 1]))
             right = jnp.where(even_x, got[0], got[1]) * has_right
             left = jnp.where(even_x, got[1], got[0]) * has_left
             for g, f in enumerate(quad):
                 strip = ring_f[f, layers] if f < ADJ else ring_w[f - ADJ, layers]
                 tile = jnp.where(pair == 1, pltpu.roll(right, (2 - 2 * g) % lanes, 1), strip)
                 strips[f] = jnp.where(pair == 2, pltpu.roll(left, (4 - 2 * g) % lanes, 1), tile)
-        place += len(quads) if narrow else 2 * len(quads)
+        place += len(quads)
     sides = []
     for side, up in enumerate((True, False)):
         scatter_rows(packed.at[side], y_rows(cz, cy, up)[2], lambda f, z, y: strips[f, y : y + 1, :])
@@ -714,13 +714,13 @@
     )
     core = lax.ppermute(to_core, "gz", [(i, i ^ 1) for i in range(holders)])
     gy = lax.axis_size("gy")
-    across = {
-        (i, c): (i, 3 - c) if c in (1, 2) else (i ^ 1, c)
-        for i in range(gy) for c in range(holders)
-    }
-    far_face = lax.ppermute(
-        to_far, ("gy", "gz"), [(a[0] * holders + a[1], b[0] * holders + b[1]) for a, b in across.items()]
-    )
+    axes = ("gx", "gy", "gz")
+    gx = lax.axis_size("gx")
+    across = [
+        ((i * gy + j) * holders + c, (i * gy + j) * holders + 3 - c if c in (1, 2) else ((i ^ 1) * gy + j) * holders + c)
+        for i in range(gx) for j in range(gy) for c in range(holders)
+    ]
+    far_face = lax.ppermute(to_far, axes, across)
     both = [lax.ppermute(part, "gz", [(i, i ^ 1) for i in range(holders)]) for part in (chip[:half], chip[half:])]
 
     ring_f, ring_w = kernel_call(
@@ -738,9 +738,6 @@
         (),
         {5: 0, 6: 1},
     )
-    axes = ("gx", "gy", "gz")
-    gx = lax.axis_size("gx")
-
     def partner(i, j, c, x_turn, y_turn):
         if x_turn is not None:
             i = dict(swap_pairs(gx, x_turn))[i]

time: 22.3 us -> 22.3 us (level)
  no operation moved by 1% of the time
where the time goes in v13:
time: 22.3 us; the launch traced here: 22.1 us
  starting transfers between devices  9.96 us (45%)
  waiting for transfers between devices  5.86 us (26%)
  Pallas kernels  5.58 us (25%)
  between operations  0.69 us (3%)
    pallas_call x8, Pallas kernels, kernel_call(): pl.pallas_call(run, out_shape=tuple((o for o in out_shape if o is not Non...  5.58 us
    ppermute x3, starting transfers between devices, swap(): return lax.ppermute(value, axes, pairs)  4.8 us
    ppermute x3, waiting for transfers between devices, swap(): return lax.ppermute(value, axes, pairs)  3.85 us
    ppermute x1, starting transfers between devices, on_device(): chip = lax.ppermute(store, 'gz', [(i, i ^ 2) for i in range(holders)])  3 us
    ppermute x1, starting transfers between devices, on_device(): far_face = lax.ppermute(to_far, axes, across)  1.58 us
    ppermute x1, waiting for transfers between devices, on_device(): chip = lax.ppermute(store, 'gz', [(i, i ^ 2) for i in range(holders)])  1.24 us
    ppermute x1, waiting for transfers between devices, on_device(): far_face = lax.ppermute(to_far, axes, across)  0.76 us
    ppermute x2, starting transfers between devices, on_device(): lax.ppermute(part, 'gz', [(i, i ^ 1) for i in range(holders)])  0.57 us
  transfers between devices with their start and end apart: 8, of which 5 were waited for; matrix products, arithmetic and copies ran while one was open for 0% of the time, Pallas kernels for 14%

profile of v13, /device:TPU:0, one launch (start us, length us, event | category | flops | bytes accessed | tf_op | source)
XLA Modules:
  0.0 22.1 jit_solution(6491736670485724686)
XLA Ops:
  0.6 3.0 %collective-permute-start.1 = (bf16[72,8,128]{2,1,0:T(8,128)(2,1)}, bf16[72,8,128]{2,1,0:T(8,128)(2,1)S(1)}, u32[]{:S(2)}, u32[]{:S(2)}) collective-permute-start(bf16[72,8,128]{2,1,0:T(8,128)(2,1)} %bitcast.6), channel_id=1, source_target_pairs={{0,2},{1,3},{2,0},{3,1},{4,6},{5,7},{6,4},{7,5},{8,10},{9,11},{10,... | collective-permute-start | bytes 442376 | tf_op jit(solution)/shard_map/ppermute | solution.py:697
  3.6 1.4 %shard_map.139 = (bf16[107,8,128]{2,1,0:T(8,128)(2,1)S(1)}, bf16[37,8,128]{2,1,0:T(8,128)(2,1)S(1)}, f32[15,8,8,128]{3,2,1,0:T(8,128)S(1)}, s32[8,128]{1,0:T(8,128)S(1)}) custom-call(bf16[72,8,128]{2,1,0:T(8,128)(2,1)} %bitcast.7, f32[9,8,8,128]{3,2,1,0:T(8,128)} %refs_1_.1, f32[8,8,128]{2,1,0:T(8,128)} %refs_2_.1, f32[8,8,128]{2,1,0:T(8,128)} %refs_3_.1, ...), custom_call_target="tpu_custom_call" | custom-call | tf_op jit(solution)/shard_map/pallas_call | solution.py:652
  5.0 1.6 %collective-permute-start.4 = (bf16[37,8,128]{2,1,0:T(8,128)(2,1)S(1)}, bf16[37,8,128]{2,1,0:T(8,128)(2,1)S(1)}, u32[]{:S(2)}, u32[]{:S(2)}) collective-permute-start(bf16[37,8,128]{2,1,0:T(8,128)(2,1)S(1)} %get-tuple-element.24), channel_id=1, source_target_pairs={{0,16},{1,2},{2,1},{3,19},{4,20},{5,6},{6,5},{7,23},{8,24},{9,10},... | collective-permute-start | bytes 227336 | tf_op jit(solution)/shard_map/ppermute | solution.py:723
  6.6 0.0 collective-permute-start
  6.6 1.2 %collective-permute-done.1.refs_2_ = bf16[72,8,128]{2,1,0:T(8,128)(2,1)S(1)} collective-permute-done((bf16[72,8,128]{2,1,0:T(8,128)(2,1)}, bf16[72,8,128]{2,1,0:T(8,128)(2,1)S(1)}, u32[]{:S(2)}, u32[]{:S(2)}) %collective-permute-start.1) | collective-permute-done | bytes 147488 | tf_op jit(solution)/shard_map/ppermute | solution.py:697
  7.9 0.1 collective-permute-start.3
  8.0 0.5 %collective-permute-start.2 = (bf16[36,8,128]{2,1,0:T(8,128)(2,1)S(1)}, bf16[36,8,128]{2,1,0:T(8,128)(2,1)S(1)}, u32[]{:S(2)}, u32[]{:S(2)}) collective-permute-start(bf16[36,8,128]{2,1,0:T(8,128)(2,1)S(1)} %get-tuple-element.44), channel_id=1, source_target_pairs={{0,1},{1,0},{2,3},{3,2},{4,5},{5,4},{6,7},{7,6},{8,9},{9,8},{10,11... | collective-permute-start | bytes 221192 | tf_op jit(solution)/shard_map/ppermute | solution.py:724
  8.5 0.0 collective-permute-done.refs_1_.refs_0_
  8.5 0.3 %shard_map.140 = (f32[9,13,8,128]{3,2,1,0:T(8,128)S(1)}, f32[14,13,8,128]{3,2,1,0:T(8,128)S(1)}) custom-call(bf16[107,8,128]{2,1,0:T(8,128)(2,1)S(1)} %get-tuple-element.23.refs_0_, bf16[107,8,128]{2,1,0:T(8,128)(2,1)S(1)} %collective-permute-done.refs_1_.refs_0_, bf16[72,8,128]{2,1,0:T(8,128)(2,1)S(1)} %collective-permute-done.1.refs_2_, ...), custom_call_target="tpu_custom_call" | custom-call | tf_op jit(solution)/shard_map/pallas_call | solution.py:652
  8.7 0.8 %collective-permute-done.4.refs_3_ = bf16[37,8,128]{2,1,0:T(8,128)(2,1)S(1)} collective-permute-done((bf16[37,8,128]{2,1,0:T(8,128)(2,1)S(1)}, bf16[37,8,128]{2,1,0:T(8,128)(2,1)S(1)}, u32[]{:S(2)}, u32[]{:S(2)}) %collective-permute-start.4) | collective-permute-done | bytes 75808 | tf_op jit(solution)/shard_map/ppermute | solution.py:723
  9.5 0.0 collective-permute-done.3.refs_2_
  9.5 0.0 collective-permute-done.2.refs_1_
  9.5 0.6 %shard_map.141 = (f32[9,13,8,128]{3,2,1,0:T(8,128)S(1)}, f32[14,13,8,128]{3,2,1,0:T(8,128)S(1)}, bf16[8,8,128]{2,1,0:T(8,128)(2,1)S(1)}) custom-call(bf16[107,8,128]{2,1,0:T(8,128)(2,1)S(1)} %collective-permute-done.refs_1_.refs_0_, bf16[36,8,128]{2,1,0:T(8,128)(2,1)S(1)} %collective-permute-done.2.refs_1_, ...), custom_call_target="tpu_custom_call", output_to_operand_aliasing={{0}: (5, {}), {1}: (6, {})} | custom-call | tf_op jit(solution)/shard_map/pallas_call | solution.py:652
  10.1 1.6 %collective-permute-start.5 = (bf16[8,8,128]{2,1,0:T(8,128)(2,1)S(1)}, bf16[8,8,128]{2,1,0:T(8,128)(2,1)S(1)}, u32[]{:S(2)}, u32[]{:S(2)}) collective-permute-start(bf16[8,8,128]{2,1,0:T(8,128)(2,1)S(1)} %get-tuple-element.31), channel_id=1, source_target_pairs={{0,16},{1,17},{2,18},{3,19},{4,20},{5,21},{6,22},{7,23},{8,24},{9,... | collective-permute-start | bytes 49160 | tf_op jit(solution)/shard_map/ppermute | solution.py:756
  11.7 0.3 %shard_map.142 = (bf16[52,8,128]{2,1,0:T(8,128)(2,1)S(1)}, bf16[52,8,128]{2,1,0:T(8,128)(2,1)S(1)}) custom-call(f32[9,13,8,128]{3,2,1,0:T(8,128)S(1)} %get-tuple-element.29.refs_0_, f32[14,13,8,128]{3,2,1,0:T(8,128)S(1)} %get-tuple-element.30.refs_1_), custom_call_target="tpu_custom_call" | custom-call | tf_op jit(solution)/shard_map/pallas_call | solution.py:652
  11.9 1.9 %collective-permute-done.5.refs_2_ = bf16[8,8,128]{2,1,0:T(8,128)(2,1)S(1)} collective-permute-done((bf16[8,8,128]{2,1,0:T(8,128)(2,1)S(1)}, bf16[8,8,128]{2,1,0:T(8,128)(2,1)S(1)}, u32[]{:S(2)}, u32[]{:S(2)}) %collective-permute-start.5) | collective-permute-done | bytes 16416 | tf_op jit(solution)/shard_map/ppermute | solution.py:756
  13.9 0.1 shard_map.143
  14.0 1.6 %collective-permute-start.6 = (bf16[52,8,128]{2,1,0:T(8,128)(2,1)S(1)}, bf16[52,8,128]{2,1,0:T(8,128)(2,1)S(1)}, u32[]{:S(2)}, u32[]{:S(2)}) collective-permute-start(bf16[52,8,128]{2,1,0:T(8,128)(2,1)S(1)} %get-tuple-element.34), channel_id=1, source_target_pairs={{0,16},{1,5},{2,18},{3,7},{4,8},{5,1},{6,10},{7,3},{8,4},{9,13},{1... | collective-permute-start | bytes 319496 | tf_op jit(solution)/shard_map/ppermute | solution.py:756
  15.6 1.6 %collective-permute-start.7 = (bf16[52,8,128]{2,1,0:T(8,128)(2,1)S(1)}, bf16[52,8,128]{2,1,0:T(8,128)(2,1)S(1)}, u32[]{:S(2)}, u32[]{:S(2)}) collective-permute-start(bf16[52,8,128]{2,1,0:T(8,128)(2,1)S(1)} %get-tuple-element.39), channel_id=1, source_target_pairs={{0,4},{1,17},{2,6},{3,19},{4,0},{5,9},{6,2},{7,11},{8,12},{9,5},{1... | collective-permute-start | bytes 319496 | tf_op jit(solution)/shard_map/ppermute | solution.py:756
  17.2 1.0 %shard_map.144 = (f32[24,13,8,128]{3,2,1,0:T(8,128)S(1)}, f32[8,3,13,8,128]{4,3,2,1,0:T(8,128)S(1)}, f32[11,8,8,128]{3,2,1,0:T(8,128)S(1)}) custom-call(f32[9,13,8,128]{3,2,1,0:T(8,128)S(1)} %get-tuple-element.29.refs_0_, f32[14,13,8,128]{3,2,1,0:T(8,128)S(1)} %get-tuple-element.30.refs_1_, f32[23,8,128]{2,1,0:T(8,128)S(1)} %get-tuple-element.35.refs_2_, ...), custom_call_target="tpu_custom_call" | custom-call | tf_op jit(solution)/shard_map/pallas_call | solution.py:652
  18.3 1.1 %collective-permute-done.6.refs_0_ = bf16[52,8,128]{2,1,0:T(8,128)(2,1)S(1)} collective-permute-done((bf16[52,8,128]{2,1,0:T(8,128)(2,1)S(1)}, bf16[52,8,128]{2,1,0:T(8,128)(2,1)S(1)}, u32[]{:S(2)}, u32[]{:S(2)}) %collective-permute-start.6) | collective-permute-done | bytes 106528 | tf_op jit(solution)/shard_map/ppermute | solution.py:756
  19.4 0.1 shard_map.145.refs_0_
  19.5 0.8 %collective-permute-done.7.refs_3_ = bf16[52,8,128]{2,1,0:T(8,128)(2,1)S(1)} collective-permute-done((bf16[52,8,128]{2,1,0:T(8,128)(2,1)S(1)}, bf16[52,8,128]{2,1,0:T(8,128)(2,1)S(1)}, u32[]{:S(2)}, u32[]{:S(2)}) %collective-permute-start.7) | collective-permute-done | bytes 106528 | tf_op jit(solution)/shard_map/ppermute | solution.py:756
  20.3 1.8 %shard_map.146 = (f32[9,8,8,128]{3,2,1,0:T(8,128)}, f32[8,8,128]{2,1,0:T(8,128)}, f32[8,8,128]{2,1,0:T(8,128)}, f32[24,13,8,128]{3,2,1,0:T(8,128)S(1)}) custom-call(f32[24,13,8,128]{3,2,1,0:T(8,128)S(1)} %shard_map.145.refs_0_, f32[8,3,13,8,128]{4,3,2,1,0:T(8,128)S(1)} %get-tuple-element.37.refs_1_, ...), custom_call_target="tpu_custom_call", output_to_operand_aliasing={{3}: (0, {})} | custom-call | tf_op jit(solution)/shard_map/pallas_call | solution.py:652
  (1 shorter events, 0.0 us)
Async XLA Ops:
  0.6 7.2 %collective-permute-start.1 = (bf16[72,8,128]{2,1,0:T(8,128)(2,1)}, bf16[72,8,128]{2,1,0:T(8,128)(2,1)S(1)}, u32[]{:S(2)}, u32[]{:S(2)}) collective-permute-start(bf16[72,8,128]{2,1,0:T(8,128)(2,1)} %bitcast.6), channel_id=1, source_target_pairs={{0,2},{1,3},{2,0},{3,1},{4,6},{5,7},{6,4},{7,5},{8,10},{9,11},{10,... | collective-permute-start | bytes 442376 | tf_op jit(solution)/shard_map/ppermute | solution.py:697
  5.0 4.4 %collective-permute-start.4 = (bf16[37,8,128]{2,1,0:T(8,128)(2,1)S(1)}, bf16[37,8,128]{2,1,0:T(8,128)(2,1)S(1)}, u32[]{:S(2)}, u32[]{:S(2)}) collective-permute-start(bf16[37,8,128]{2,1,0:T(8,128)(2,1)S(1)} %get-tuple-element.24), channel_id=1, source_target_pairs={{0,16},{1,2},{2,1},{3,19},{4,20},{5,6},{6,5},{7,23},{8,24},{9,10},... | collective-permute-start | bytes 227336 | tf_op jit(solution)/shard_map/ppermute | solution.py:723
  6.6 1.8 %collective-permute-start = (bf16[107,8,128]{2,1,0:T(8,128)(2,1)S(1)}, bf16[107,8,128]{2,1,0:T(8,128)(2,1)S(1)}, u32[]{:S(2)}, u32[]{:S(2)}) collective-permute-start(bf16[107,8,128]{2,1,0:T(8,128)(2,1)S(1)} %get-tuple-element.23.refs_0_), channel_id=1, source_target_pairs={{0,1},{1,0},{2,3},{3,2},{4,5},{5,4},{6,7},{7,6},{8,9},{9,8},{10,11... | collective-permute-start | bytes 657416 | tf_op jit(solution)/shard_map/ppermute | solution.py:715
  7.9 1.6 %collective-permute-start.3 = (bf16[36,8,128]{2,1,0:T(8,128)(2,1)S(1)}, bf16[36,8,128]{2,1,0:T(8,128)(2,1)S(1)}, u32[]{:S(2)}, u32[]{:S(2)}) collective-permute-start(bf16[36,8,128]{2,1,0:T(8,128)(2,1)S(1)} %get-tuple-element.43), channel_id=1, source_target_pairs={{0,1},{1,0},{2,3},{3,2},{4,5},{5,4},{6,7},{7,6},{8,9},{9,8},{10,11... | collective-permute-start | bytes 221192 | tf_op jit(solution)/shard_map/ppermute | solution.py:724
  8.0 1.5 %collective-permute-start.2 = (bf16[36,8,128]{2,1,0:T(8,128)(2,1)S(1)}, bf16[36,8,128]{2,1,0:T(8,128)(2,1)S(1)}, u32[]{:S(2)}, u32[]{:S(2)}) collective-permute-start(bf16[36,8,128]{2,1,0:T(8,128)(2,1)S(1)} %get-tuple-element.44), channel_id=1, source_target_pairs={{0,1},{1,0},{2,3},{3,2},{4,5},{5,4},{6,7},{7,6},{8,9},{9,8},{10,11... | collective-permute-start | bytes 221192 | tf_op jit(solution)/shard_map/ppermute | solution.py:724
  10.1 3.8 %collective-permute-start.5 = (bf16[8,8,128]{2,1,0:T(8,128)(2,1)S(1)}, bf16[8,8,128]{2,1,0:T(8,128)(2,1)S(1)}, u32[]{:S(2)}, u32[]{:S(2)}) collective-permute-start(bf16[8,8,128]{2,1,0:T(8,128)(2,1)S(1)} %get-tuple-element.31), channel_id=1, source_target_pairs={{0,16},{1,17},{2,18},{3,19},{4,20},{5,21},{6,22},{7,23},{8,24},{9,... | collective-permute-start | bytes 49160 | tf_op jit(solution)/shard_map/ppermute | solution.py:756
  14.0 5.4 %collective-permute-start.6 = (bf16[52,8,128]{2,1,0:T(8,128)(2,1)S(1)}, bf16[52,8,128]{2,1,0:T(8,128)(2,1)S(1)}, u32[]{:S(2)}, u32[]{:S(2)}) collective-permute-start(bf16[52,8,128]{2,1,0:T(8,128)(2,1)S(1)} %get-tuple-element.34), channel_id=1, source_target_pairs={{0,16},{1,5},{2,18},{3,7},{4,8},{5,1},{6,10},{7,3},{8,4},{9,13},{1... | collective-permute-start | bytes 319496 | tf_op jit(solution)/shard_map/ppermute | solution.py:756
  15.6 4.7 %collective-permute-start.7 = (bf16[52,8,128]{2,1,0:T(8,128)(2,1)S(1)}, bf16[52,8,128]{2,1,0:T(8,128)(2,1)S(1)}, u32[]{:S(2)}, u32[]{:S(2)}) collective-permute-start(bf16[52,8,128]{2,1,0:T(8,128)(2,1)S(1)} %get-tuple-element.39), channel_id=1, source_target_pairs={{0,4},{1,17},{2,6},{3,19},{4,0},{5,9},{6,2},{7,11},{8,12},{9,5},{1... | collective-permute-start | bytes 319496 | tf_op jit(solution)/shard_map/ppermute | solution.py:756

commit v14 on v12

--- a/solution.py
+++ b/solution.py
@@ -216,19 +216,17 @@
     codes[...] = code
     listed = cells[...]
     count = listed.shape[1]
-    row_hot = (lax.broadcasted_iota(jnp.int32, (rows, count), 0) == listed // lanes).astype(jnp.float32)
+    row_hot = (lax.broadcasted_iota(jnp.int32, (rows, count), 0) == listed // lanes).astype(jnp.bfloat16)
     lane_hit = lax.broadcasted_iota(jnp.int32, (lanes, count), 0) == listed % lanes
-    injected = []
-    for step in (1, 0):
-        sample = samples[pl.ds(steps[step], 1), :]
-        field = lax.dot_general(
-            row_hot,
-            jnp.where(lane_hit, sample, 0.0),
-            (((1,), (1,)), ((), ())),
-            precision=lax.Precision.HIGHEST,
-            preferred_element_type=jnp.float32,
+    rest = jnp.concatenate([jnp.where(lane_hit, samples[pl.ds(steps[step], 1), :], 0.0) for step in (1, 0)], axis=0)
+    both = jnp.zeros((rows, 2 * lanes), jnp.float32)
+    for _ in range(3):
+        part = rest.astype(jnp.bfloat16)
+        rest = rest - part.astype(jnp.float32)
+        both = both + lax.dot_general(
+            row_hot, part, (((1,), (1,)), ((), ())), preferred_element_type=jnp.float32
         )
-        injected.append(field.reshape(cz, cy, lanes))
+    injected = [both[:, :lanes].reshape(cz, cy, lanes), both[:, lanes:].reshape(cz, cy, lanes)]
     own[INJ - ADJ] = injected[1]
     flat = lax.broadcasted_iota(jnp.int32, (rows, lanes), 0) * lanes + lax.broadcasted_iota(jnp.int32, (rows, lanes), 1)
     for step in range(2):
@@ -435,12 +433,23 @@
     first_lane, last_lane = lane == 0, lane == lanes - 1
     inner = range(HALO, HALO + cz)
 
+    seen = {}
+
+    def once(key, z, load):
+        if (key, z) not in seen:
+            seen[key, z] = load()
+        return seen[key, z]
+
+    def forget(step):
+        for key in [key for key in seen if step or key[1] != edge]:
+            del seen[key]
+
     def start(field):
-        return lambda z: base(field, z)
+        return lambda z: once(field, z, lambda: base(field, z))
 
     def kept(name, field):
         index = STAGE[name] + field
-        return lambda z: stage[index, z]
+        return lambda z: once(("stage", index), z, lambda: stage[index, z])
 
     def x_next(of, z):
         value = pltpu.roll(of(z), lanes - 1, 1)
@@ -503,9 +512,11 @@
         return out
 
     def spread(ranges):
+        forget(True)
         for z in range(layers + 1):
             want = {f for f, (a, b) in ranges.items() if z == edge or a <= z < b}
             if want:
+                forget(False)
                 yield z, want
 
     def velocity_step(k, name, v, s, sign, ranges):
@@ -538,7 +549,9 @@
     fv = velocity_step(1, "fv", fv, fs, 1, {VX: (1, n), VY: (1, n), VZ: (0, n - 1)})
     fs = stress_step(2, "fs", fv, fs, 1, {SXX: (1, n - 1), SXY: (1, n - 1), SXZ: (1, n - 1)}, behind=SRC)
     fv = velocity_step(3, "fw", fv, fs, 1, {VX: (2, n - 1), VY: (2, n - 1), VZ: (1, n - 2)})
+    forget(True)
     for z in inner:
+        forget(False)
         rates = stress_rates(4, fv, z, set(STRESS))
         now = [of(z) for of in fs]
         later = [now[s - SXX] + rates[s] + (base(FIELDS, z) if s in NORMAL else 0.0) for s in STRESS]
@@ -549,10 +562,13 @@
         put(10, z - HALO, mu_late + mu_early)
     av = velocity_step(5, "av", av, a_s, -1, {VX: (1, n - 1), VY: (1, n - 1), VZ: (1, n - 1)})
     a_s = stress_step(6, "at", av, a_s, -1, {SXX: (2, n - 1), SXY: (1, n - 1), SXZ: (1, n - 2)}, ahead=INJ)
+    forget(True)
     for s, of in zip(STRESS, a_s):
         for z in inner:
             put(s, z - HALO, of(z))
+    forget(True)
     for z in inner:
+        forget(False)
         rates = velocity_rates(7, a_s, z, {VX, VY, VZ})
         for f in (VX, VY, VZ):
             put(f, z - HALO, av[f](z) - rates[f])

time: 22.3 us -> 22.3 us (level)
  transfers between devices with their start and end apart: 8 -> 8, of which waited for: 5 -> 5; matrix products, arithmetic and copies ran while one was open for 0% -> 0% of each run, Pallas kernels for 14% -> 13%
where the time goes in v14:
time: 22.3 us; the launch traced here: 22.1 us
  starting transfers between devices  10.2 us (46%)
  waiting for transfers between devices  5.81 us (26%)
  Pallas kernels  5.46 us (24%)
  between operations  0.69 us (3%)
    pallas_call x8, Pallas kernels, kernel_call(): pl.pallas_call(run, out_shape=tuple((o for o in out_shape if o is not Non...  5.46 us
    ppermute x3, starting transfers between devices, swap(): return lax.ppermute(value, axes, pairs)  4.94 us
    ppermute x3, waiting for transfers between devices, swap(): return lax.ppermute(value, axes, pairs)  3.83 us
    ppermute x1, starting transfers between devices, on_device(): chip = lax.ppermute(store, 'gz', [(i, i ^ 2) for i in range(holders)])  3 us
    ppermute x1, starting transfers between devices, on_device(): lax.ppermute(to_far, ('gy', 'gz'), [(a[0] * holders + a[1], b[0] * holder...  1.64 us
    ppermute x1, waiting for transfers between devices, on_device(): chip = lax.ppermute(store, 'gz', [(i, i ^ 2) for i in range(holders)])  1.32 us
    ppermute x1, waiting for transfers between devices, on_device(): lax.ppermute(to_far, ('gy', 'gz'), [(a[0] * holders + a[1], b[0] * holder...  0.62 us
    ppermute x2, starting transfers between devices, on_device(): lax.ppermute(part, 'gz', [(i, i ^ 1) for i in range(holders)])  0.57 us
  transfers between devices with their start and end apart: 8, of which 5 were waited for; matrix products, arithmetic and copies ran while one was open for 0% of the time, Pallas kernels for 13%

profile of v14, /device:TPU:0, one launch (start us, length us, event | category | flops | bytes accessed | tf_op | source)
XLA Modules:
  0.0 22.1 jit_solution(15903901385659426970)
XLA Ops:
  0.6 3.0 %collective-permute-start.1 = (bf16[72,8,128]{2,1,0:T(8,128)(2,1)}, bf16[72,8,128]{2,1,0:T(8,128)(2,1)S(1)}, u32[]{:S(2)}, u32[]{:S(2)}) collective-permute-start(bf16[72,8,128]{2,1,0:T(8,128)(2,1)} %bitcast.6), channel_id=1, source_target_pairs={{0,2},{1,3},{2,0},{3,1},{4,6},{5,7},{6,4},{7,5},{8,10},{9,11},{10,... | collective-permute-start | bytes 442376 | tf_op jit(solution)/shard_map/ppermute | solution.py:713
  3.6 1.3 %shard_map.139 = (bf16[107,8,128]{2,1,0:T(8,128)(2,1)S(1)}, bf16[37,8,128]{2,1,0:T(8,128)(2,1)S(1)}, f32[15,8,8,128]{3,2,1,0:T(8,128)S(1)}, s32[8,128]{1,0:T(8,128)S(1)}) custom-call(bf16[72,8,128]{2,1,0:T(8,128)(2,1)} %bitcast.7, f32[9,8,8,128]{3,2,1,0:T(8,128)} %refs_1_.1, f32[8,8,128]{2,1,0:T(8,128)} %refs_2_.1, f32[8,8,128]{2,1,0:T(8,128)} %refs_3_.1, ...), custom_call_target="tpu_custom_call" | custom-call | tf_op jit(solution)/shard_map/pallas_call | solution.py:668
  4.9 1.6 %collective-permute-start.4 = (bf16[37,8,128]{2,1,0:T(8,128)(2,1)S(1)}, bf16[37,8,128]{2,1,0:T(8,128)(2,1)S(1)}, u32[]{:S(2)}, u32[]{:S(2)}) collective-permute-start(bf16[37,8,128]{2,1,0:T(8,128)(2,1)S(1)} %get-tuple-element.24), channel_id=1, source_target_pairs={{0,4},{1,2},{2,1},{3,7},{4,0},{5,6},{6,5},{7,3},{8,12},{9,10},{10,... | collective-permute-start | bytes 227336 | tf_op jit(solution)/shard_map/ppermute | solution.py:737
  6.5 0.0 collective-permute-start
  6.5 1.3 %collective-permute-done.1.refs_2_ = bf16[72,8,128]{2,1,0:T(8,128)(2,1)S(1)} collective-permute-done((bf16[72,8,128]{2,1,0:T(8,128)(2,1)}, bf16[72,8,128]{2,1,0:T(8,128)(2,1)S(1)}, u32[]{:S(2)}, u32[]{:S(2)}) %collective-permute-start.1) | collective-permute-done | bytes 147488 | tf_op jit(solution)/shard_map/ppermute | solution.py:713
  7.9 0.1 collective-permute-start.3
  8.0 0.5 %collective-permute-start.2 = (bf16[36,8,128]{2,1,0:T(8,128)(2,1)S(1)}, bf16[36,8,128]{2,1,0:T(8,128)(2,1)S(1)}, u32[]{:S(2)}, u32[]{:S(2)}) collective-permute-start(bf16[36,8,128]{2,1,0:T(8,128)(2,1)S(1)} %get-tuple-element.44), channel_id=1, source_target_pairs={{0,1},{1,0},{2,3},{3,2},{4,5},{5,4},{6,7},{7,6},{8,9},{9,8},{10,11... | collective-permute-start | bytes 221192 | tf_op jit(solution)/shard_map/ppermute | solution.py:740
  8.5 0.0 collective-permute-done.refs_1_.refs_0_
  8.5 0.3 %shard_map.140 = (f32[9,13,8,128]{3,2,1,0:T(8,128)S(1)}, f32[14,13,8,128]{3,2,1,0:T(8,128)S(1)}) custom-call(bf16[107,8,128]{2,1,0:T(8,128)(2,1)S(1)} %get-tuple-element.23.refs_0_, bf16[107,8,128]{2,1,0:T(8,128)(2,1)S(1)} %collective-permute-done.refs_1_.refs_0_, bf16[72,8,128]{2,1,0:T(8,128)(2,1)S(1)} %collective-permute-done.1.refs_2_, ...), custom_call_target="tpu_custom_call" | custom-call | tf_op jit(solution)/shard_map/pallas_call | solution.py:668
  8.7 0.6 %collective-permute-done.4.refs_3_ = bf16[37,8,128]{2,1,0:T(8,128)(2,1)S(1)} collective-permute-done((bf16[37,8,128]{2,1,0:T(8,128)(2,1)S(1)}, bf16[37,8,128]{2,1,0:T(8,128)(2,1)S(1)}, u32[]{:S(2)}, u32[]{:S(2)}) %collective-permute-start.4) | collective-permute-done | bytes 75808 | tf_op jit(solution)/shard_map/ppermute | solution.py:737
  9.3 0.0 collective-permute-done.3.refs_2_
  9.3 0.0 collective-permute-done.2.refs_1_
  9.4 0.6 %shard_map.141 = (f32[9,13,8,128]{3,2,1,0:T(8,128)S(1)}, f32[14,13,8,128]{3,2,1,0:T(8,128)S(1)}, bf16[11,8,128]{2,1,0:T(8,128)(2,1)S(1)}) custom-call(bf16[107,8,128]{2,1,0:T(8,128)(2,1)S(1)} %collective-permute-done.refs_1_.refs_0_, bf16[36,8,128]{2,1,0:T(8,128)(2,1)S(1)} %collective-permute-done.2.refs_1_, ...), custom_call_target="tpu_custom_call", output_to_operand_aliasing={{0}: (5, {}), {1}: (6, {})} | custom-call | tf_op jit(solution)/shard_map/pallas_call | solution.py:668
  9.9 1.7 %collective-permute-start.5 = (bf16[11,8,128]{2,1,0:T(8,128)(2,1)S(1)}, bf16[11,8,128]{2,1,0:T(8,128)(2,1)S(1)}, u32[]{:S(2)}, u32[]{:S(2)}) collective-permute-start(bf16[11,8,128]{2,1,0:T(8,128)(2,1)S(1)} %get-tuple-element.31), channel_id=1, source_target_pairs={{0,16},{1,17},{2,18},{3,19},{4,20},{5,21},{6,22},{7,23},{8,24},{9,... | collective-permute-start | bytes 67592 | tf_op jit(solution)/shard_map/ppermute | solution.py:775
  11.6 0.3 %shard_map.142 = (bf16[52,8,128]{2,1,0:T(8,128)(2,1)S(1)}, bf16[52,8,128]{2,1,0:T(8,128)(2,1)S(1)}) custom-call(f32[9,13,8,128]{3,2,1,0:T(8,128)S(1)} %get-tuple-element.29.refs_0_, f32[14,13,8,128]{3,2,1,0:T(8,128)S(1)} %get-tuple-element.30.refs_1_), custom_call_target="tpu_custom_call" | custom-call | tf_op jit(solution)/shard_map/pallas_call | solution.py:668
  11.9 1.9 %collective-permute-done.5.refs_2_ = bf16[11,8,128]{2,1,0:T(8,128)(2,1)S(1)} collective-permute-done((bf16[11,8,128]{2,1,0:T(8,128)(2,1)S(1)}, bf16[11,8,128]{2,1,0:T(8,128)(2,1)S(1)}, u32[]{:S(2)}, u32[]{:S(2)}) %collective-permute-start.5) | collective-permute-done | bytes 22560 | tf_op jit(solution)/shard_map/ppermute | solution.py:775
  13.8 0.1 shard_map.143
  14.0 1.7 %collective-permute-start.6 = (bf16[52,8,128]{2,1,0:T(8,128)(2,1)S(1)}, bf16[52,8,128]{2,1,0:T(8,128)(2,1)S(1)}, u32[]{:S(2)}, u32[]{:S(2)}) collective-permute-start(bf16[52,8,128]{2,1,0:T(8,128)(2,1)S(1)} %get-tuple-element.34), channel_id=1, source_target_pairs={{0,16},{1,5},{2,18},{3,7},{4,8},{5,1},{6,10},{7,3},{8,4},{9,13},{1... | collective-permute-start | bytes 319496 | tf_op jit(solution)/shard_map/ppermute | solution.py:775
  15.6 1.6 %collective-permute-start.7 = (bf16[52,8,128]{2,1,0:T(8,128)(2,1)S(1)}, bf16[52,8,128]{2,1,0:T(8,128)(2,1)S(1)}, u32[]{:S(2)}, u32[]{:S(2)}) collective-permute-start(bf16[52,8,128]{2,1,0:T(8,128)(2,1)S(1)} %get-tuple-element.39), channel_id=1, source_target_pairs={{0,4},{1,17},{2,6},{3,19},{4,0},{5,9},{6,2},{7,11},{8,12},{9,5},{1... | collective-permute-start | bytes 319496 | tf_op jit(solution)/shard_map/ppermute | solution.py:775
  17.2 1.0 %shard_map.144 = (f32[24,13,8,128]{3,2,1,0:T(8,128)S(1)}, f32[8,3,13,8,128]{4,3,2,1,0:T(8,128)S(1)}, f32[11,8,8,128]{3,2,1,0:T(8,128)S(1)}) custom-call(f32[9,13,8,128]{3,2,1,0:T(8,128)S(1)} %get-tuple-element.29.refs_0_, f32[14,13,8,128]{3,2,1,0:T(8,128)S(1)} %get-tuple-element.30.refs_1_, f32[23,8,128]{2,1,0:T(8,128)S(1)} %get-tuple-element.35.refs_2_, ...), custom_call_target="tpu_custom_call" | custom-call | tf_op jit(solution)/shard_map/pallas_call | solution.py:668
  18.3 1.2 %collective-permute-done.6.refs_0_ = bf16[52,8,128]{2,1,0:T(8,128)(2,1)S(1)} collective-permute-done((bf16[52,8,128]{2,1,0:T(8,128)(2,1)S(1)}, bf16[52,8,128]{2,1,0:T(8,128)(2,1)S(1)}, u32[]{:S(2)}, u32[]{:S(2)}) %collective-permute-start.6) | collective-permute-done | bytes 106528 | tf_op jit(solution)/shard_map/ppermute | solution.py:775
  19.5 0.1 shard_map.145.refs_0_
  19.6 0.7 %collective-permute-done.7.refs_3_ = bf16[52,8,128]{2,1,0:T(8,128)(2,1)S(1)} collective-permute-done((bf16[52,8,128]{2,1,0:T(8,128)(2,1)S(1)}, bf16[52,8,128]{2,1,0:T(8,128)(2,1)S(1)}, u32[]{:S(2)}, u32[]{:S(2)}) %collective-permute-start.7) | collective-permute-done | bytes 106528 | tf_op jit(solution)/shard_map/ppermute | solution.py:775
  20.3 1.8 %shard_map.146 = (f32[9,8,8,128]{3,2,1,0:T(8,128)}, f32[8,8,128]{2,1,0:T(8,128)}, f32[8,8,128]{2,1,0:T(8,128)}, f32[24,13,8,128]{3,2,1,0:T(8,128)S(1)}) custom-call(f32[24,13,8,128]{3,2,1,0:T(8,128)S(1)} %shard_map.145.refs_0_, f32[8,3,13,8,128]{4,3,2,1,0:T(8,128)S(1)} %get-tuple-element.37.refs_1_, ...), custom_call_target="tpu_custom_call", output_to_operand_aliasing={{3}: (0, {})} | custom-call | tf_op jit(solution)/shard_map/pallas_call | solution.py:668
  (1 shorter events, 0.0 us)
Async XLA Ops:
  0.6 7.2 %collective-permute-start.1 = (bf16[72,8,128]{2,1,0:T(8,128)(2,1)}, bf16[72,8,128]{2,1,0:T(8,128)(2,1)S(1)}, u32[]{:S(2)}, u32[]{:S(2)}) collective-permute-start(bf16[72,8,128]{2,1,0:T(8,128)(2,1)} %bitcast.6), channel_id=1, source_target_pairs={{0,2},{1,3},{2,0},{3,1},{4,6},{5,7},{6,4},{7,5},{8,10},{9,11},{10,... | collective-permute-start | bytes 442376 | tf_op jit(solution)/shard_map/ppermute | solution.py:713
  4.9 4.4 %collective-permute-start.4 = (bf16[37,8,128]{2,1,0:T(8,128)(2,1)S(1)}, bf16[37,8,128]{2,1,0:T(8,128)(2,1)S(1)}, u32[]{:S(2)}, u32[]{:S(2)}) collective-permute-start(bf16[37,8,128]{2,1,0:T(8,128)(2,1)S(1)} %get-tuple-element.24), channel_id=1, source_target_pairs={{0,4},{1,2},{2,1},{3,7},{4,0},{5,6},{6,5},{7,3},{8,12},{9,10},{10,... | collective-permute-start | bytes 227336 | tf_op jit(solution)/shard_map/ppermute | solution.py:737
  6.5 1.9 %collective-permute-start = (bf16[107,8,128]{2,1,0:T(8,128)(2,1)S(1)}, bf16[107,8,128]{2,1,0:T(8,128)(2,1)S(1)}, u32[]{:S(2)}, u32[]{:S(2)}) collective-permute-start(bf16[107,8,128]{2,1,0:T(8,128)(2,1)S(1)} %get-tuple-element.23.refs_0_), channel_id=1, source_target_pairs={{0,1},{1,0},{2,3},{3,2},{4,5},{5,4},{6,7},{7,6},{8,9},{9,8},{10,11... | collective-permute-start | bytes 657416 | tf_op jit(solution)/shard_map/ppermute | solution.py:731
  7.9 1.5 %collective-permute-start.3 = (bf16[36,8,128]{2,1,0:T(8,128)(2,1)S(1)}, bf16[36,8,128]{2,1,0:T(8,128)(2,1)S(1)}, u32[]{:S(2)}, u32[]{:S(2)}) collective-permute-start(bf16[36,8,128]{2,1,0:T(8,128)(2,1)S(1)} %get-tuple-element.43), channel_id=1, source_target_pairs={{0,1},{1,0},{2,3},{3,2},{4,5},{5,4},{6,7},{7,6},{8,9},{9,8},{10,11... | collective-permute-start | bytes 221192 | tf_op jit(solution)/shard_map/ppermute | solution.py:740
  8.0 1.4 %collective-permute-start.2 = (bf16[36,8,128]{2,1,0:T(8,128)(2,1)S(1)}, bf16[36,8,128]{2,1,0:T(8,128)(2,1)S(1)}, u32[]{:S(2)}, u32[]{:S(2)}) collective-permute-start(bf16[36,8,128]{2,1,0:T(8,128)(2,1)S(1)} %get-tuple-element.44), channel_id=1, source_target_pairs={{0,1},{1,0},{2,3},{3,2},{4,5},{5,4},{6,7},{7,6},{8,9},{9,8},{10,11... | collective-permute-start | bytes 221192 | tf_op jit(solution)/shard_map/ppermute | solution.py:740
  9.9 3.9 %collective-permute-start.5 = (bf16[11,8,128]{2,1,0:T(8,128)(2,1)S(1)}, bf16[11,8,128]{2,1,0:T(8,128)(2,1)S(1)}, u32[]{:S(2)}, u32[]{:S(2)}) collective-permute-start(bf16[11,8,128]{2,1,0:T(8,128)(2,1)S(1)} %get-tuple-element.31), channel_id=1, source_target_pairs={{0,16},{1,17},{2,18},{3,19},{4,20},{5,21},{6,22},{7,23},{8,24},{9,... | collective-permute-start | bytes 67592 | tf_op jit(solution)/shard_map/ppermute | solution.py:775
  14.0 5.5 %collective-permute-start.6 = (bf16[52,8,128]{2,1,0:T(8,128)(2,1)S(1)}, bf16[52,8,128]{2,1,0:T(8,128)(2,1)S(1)}, u32[]{:S(2)}, u32[]{:S(2)}) collective-permute-start(bf16[52,8,128]{2,1,0:T(8,128)(2,1)S(1)} %get-tuple-element.34), channel_id=1, source_target_pairs={{0,16},{1,5},{2,18},{3,7},{4,8},{5,1},{6,10},{7,3},{8,4},{9,13},{1... | collective-permute-start | bytes 319496 | tf_op jit(solution)/shard_map/ppermute | solution.py:775
  15.6 4.7 %collective-permute-start.7 = (bf16[52,8,128]{2,1,0:T(8,128)(2,1)S(1)}, bf16[52,8,128]{2,1,0:T(8,128)(2,1)S(1)}, u32[]{:S(2)}, u32[]{:S(2)}) collective-permute-start(bf16[52,8,128]{2,1,0:T(8,128)(2,1)S(1)} %get-tuple-element.39), channel_id=1, source_target_pairs={{0,4},{1,17},{2,6},{3,19},{4,0},{5,9},{6,2},{7,11},{8,12},{9,5},{1... | collective-permute-start | bytes 319496 | tf_op jit(solution)/shard_map/ppermute | solution.py:775

commit v15 on v13

--- a/solution.py
+++ b/solution.py
@@ -216,19 +216,17 @@
     codes[...] = code
     listed = cells[...]
     count = listed.shape[1]
-    row_hot = (lax.broadcasted_iota(jnp.int32, (rows, count), 0) == listed // lanes).astype(jnp.float32)
+    row_hot = (lax.broadcasted_iota(jnp.int32, (rows, count), 0) == listed // lanes).astype(jnp.bfloat16)
     lane_hit = lax.broadcasted_iota(jnp.int32, (lanes, count), 0) == listed % lanes
-    injected = []
-    for step in (1, 0):
-        sample = samples[pl.ds(steps[step], 1), :]
-        field = lax.dot_general(
-            row_hot,
-            jnp.where(lane_hit, sample, 0.0),
-            (((1,), (1,)), ((), ())),
-            precision=lax.Precision.HIGHEST,
-            preferred_element_type=jnp.float32,
+    rest = jnp.concatenate([jnp.where(lane_hit, samples[pl.ds(steps[step], 1), :], 0.0) for step in (1, 0)], axis=0)
+    both = jnp.zeros((rows, 2 * lanes), jnp.float32)
+    for _ in range(3):
+        part = rest.astype(jnp.bfloat16)
+        rest = rest - part.astype(jnp.float32)
+        both = both + lax.dot_general(
+            row_hot, part, (((1,), (1,)), ((), ())), preferred_element_type=jnp.float32
         )
-        injected.append(field.reshape(cz, cy, lanes))
+    injected = [both[:, :lanes].reshape(cz, cy, lanes), both[:, lanes:].reshape(cz, cy, lanes)]
     own[INJ - ADJ] = injected[1]
     flat = lax.broadcasted_iota(jnp.int32, (rows, lanes), 0) * lanes + lax.broadcasted_iota(jnp.int32, (rows, lanes), 1)
     for step in range(2):

time: 22.3 us -> 22.2 us (level)
  transfers between devices with their start and end apart: 8 -> 8, of which waited for: 5 -> 5; matrix products, arithmetic and copies ran while one was open for 0% -> 0% of each run, Pallas kernels for 14% -> 13%
where the time goes in v15:
time: 22.2 us; the launch traced here: 22.1 us
  starting transfers between devices  10.1 us (45%)
  waiting for transfers between devices  5.81 us (26%)
  Pallas kernels  5.44 us (25%)
  between operations  0.7 us (3%)
    pallas_call x8, Pallas kernels, kernel_call(): pl.pallas_call(run, out_shape=tuple((o for o in out_shape if o is not Non...  5.44 us
    ppermute x3, starting transfers between devices, swap(): return lax.ppermute(value, axes, pairs)  4.95 us
    ppermute x3, waiting for transfers between devices, swap(): return lax.ppermute(value, axes, pairs)  3.77 us
    ppermute x1, starting transfers between devices, on_device(): chip = lax.ppermute(store, 'gz', [(i, i ^ 2) for i in range(holders)])  3 us
    ppermute x1, starting transfers between devices, on_device(): far_face = lax.ppermute(to_far, axes, across)  1.58 us
    ppermute x1, waiting for transfers between devices, on_device(): chip = lax.ppermute(store, 'gz', [(i, i ^ 2) for i in range(holders)])  1.38 us
    ppermute x1, waiting for transfers between devices, on_device(): far_face = lax.ppermute(to_far, axes, across)  0.62 us
    ppermute x2, starting transfers between devices, on_device(): lax.ppermute(part, 'gz', [(i, i ^ 1) for i in range(holders)])  0.57 us
  transfers between devices with their start and end apart: 8, of which 5 were waited for; matrix products, arithmetic and copies ran while one was open for 0% of the time, Pallas kernels for 13%

profile of v15, /device:TPU:0, one launch (start us, length us, event | category | flops | bytes accessed | tf_op | source)
XLA Modules:
  0.0 22.1 jit_solution(6545222138413938196)
XLA Ops:
  0.6 3.0 %collective-permute-start.1 = (bf16[72,8,128]{2,1,0:T(8,128)(2,1)}, bf16[72,8,128]{2,1,0:T(8,128)(2,1)S(1)}, u32[]{:S(2)}, u32[]{:S(2)}) collective-permute-start(bf16[72,8,128]{2,1,0:T(8,128)(2,1)} %bitcast.6), channel_id=1, source_target_pairs={{0,2},{1,3},{2,0},{3,1},{4,6},{5,7},{6,4},{7,5},{8,10},{9,11},{10,... | collective-permute-start | bytes 442376 | tf_op jit(solution)/shard_map/ppermute | solution.py:695
  3.6 1.3 %shard_map.139 = (bf16[107,8,128]{2,1,0:T(8,128)(2,1)S(1)}, bf16[37,8,128]{2,1,0:T(8,128)(2,1)S(1)}, f32[15,8,8,128]{3,2,1,0:T(8,128)S(1)}, s32[8,128]{1,0:T(8,128)S(1)}) custom-call(bf16[72,8,128]{2,1,0:T(8,128)(2,1)} %bitcast.7, f32[9,8,8,128]{3,2,1,0:T(8,128)} %refs_1_.1, f32[8,8,128]{2,1,0:T(8,128)} %refs_2_.1, f32[8,8,128]{2,1,0:T(8,128)} %refs_3_.1, ...), custom_call_target="tpu_custom_call" | custom-call | tf_op jit(solution)/shard_map/pallas_call | solution.py:650
  4.9 1.6 %collective-permute-start.4 = (bf16[37,8,128]{2,1,0:T(8,128)(2,1)S(1)}, bf16[37,8,128]{2,1,0:T(8,128)(2,1)S(1)}, u32[]{:S(2)}, u32[]{:S(2)}) collective-permute-start(bf16[37,8,128]{2,1,0:T(8,128)(2,1)S(1)} %get-tuple-element.24), channel_id=1, source_target_pairs={{0,16},{1,2},{2,1},{3,19},{4,20},{5,6},{6,5},{7,23},{8,24},{9,10},... | collective-permute-start | bytes 227336 | tf_op jit(solution)/shard_map/ppermute | solution.py:721
  6.5 0.0 collective-permute-start
  6.5 1.4 %collective-permute-done.1.refs_2_ = bf16[72,8,128]{2,1,0:T(8,128)(2,1)S(1)} collective-permute-done((bf16[72,8,128]{2,1,0:T(8,128)(2,1)}, bf16[72,8,128]{2,1,0:T(8,128)(2,1)S(1)}, u32[]{:S(2)}, u32[]{:S(2)}) %collective-permute-start.1) | collective-permute-done | bytes 147488 | tf_op jit(solution)/shard_map/ppermute | solution.py:695
  7.9 0.1 collective-permute-start.3
  8.0 0.5 %collective-permute-start.2 = (bf16[36,8,128]{2,1,0:T(8,128)(2,1)S(1)}, bf16[36,8,128]{2,1,0:T(8,128)(2,1)S(1)}, u32[]{:S(2)}, u32[]{:S(2)}) collective-permute-start(bf16[36,8,128]{2,1,0:T(8,128)(2,1)S(1)} %get-tuple-element.44), channel_id=1, source_target_pairs={{0,1},{1,0},{2,3},{3,2},{4,5},{5,4},{6,7},{7,6},{8,9},{9,8},{10,11... | collective-permute-start | bytes 221192 | tf_op jit(solution)/shard_map/ppermute | solution.py:722
  8.5 0.0 collective-permute-done.refs_1_.refs_0_
  8.5 0.3 %shard_map.140 = (f32[9,13,8,128]{3,2,1,0:T(8,128)S(1)}, f32[14,13,8,128]{3,2,1,0:T(8,128)S(1)}) custom-call(bf16[107,8,128]{2,1,0:T(8,128)(2,1)S(1)} %get-tuple-element.23.refs_0_, bf16[107,8,128]{2,1,0:T(8,128)(2,1)S(1)} %collective-permute-done.refs_1_.refs_0_, bf16[72,8,128]{2,1,0:T(8,128)(2,1)S(1)} %collective-permute-done.1.refs_2_, ...), custom_call_target="tpu_custom_call" | custom-call | tf_op jit(solution)/shard_map/pallas_call | solution.py:650
  8.7 0.6 %collective-permute-done.4.refs_3_ = bf16[37,8,128]{2,1,0:T(8,128)(2,1)S(1)} collective-permute-done((bf16[37,8,128]{2,1,0:T(8,128)(2,1)S(1)}, bf16[37,8,128]{2,1,0:T(8,128)(2,1)S(1)}, u32[]{:S(2)}, u32[]{:S(2)}) %collective-permute-start.4) | collective-permute-done | bytes 75808 | tf_op jit(solution)/shard_map/ppermute | solution.py:721
  9.3 0.0 collective-permute-done.3.refs_2_
  9.3 0.0 collective-permute-done.2.refs_1_
  9.4 0.6 %shard_map.141 = (f32[9,13,8,128]{3,2,1,0:T(8,128)S(1)}, f32[14,13,8,128]{3,2,1,0:T(8,128)S(1)}, bf16[8,8,128]{2,1,0:T(8,128)(2,1)S(1)}) custom-call(bf16[107,8,128]{2,1,0:T(8,128)(2,1)S(1)} %collective-permute-done.refs_1_.refs_0_, bf16[36,8,128]{2,1,0:T(8,128)(2,1)S(1)} %collective-permute-done.2.refs_1_, ...), custom_call_target="tpu_custom_call", output_to_operand_aliasing={{0}: (5, {}), {1}: (6, {})} | custom-call | tf_op jit(solution)/shard_map/pallas_call | solution.py:650
  9.9 1.7 %collective-permute-start.5 = (bf16[8,8,128]{2,1,0:T(8,128)(2,1)S(1)}, bf16[8,8,128]{2,1,0:T(8,128)(2,1)S(1)}, u32[]{:S(2)}, u32[]{:S(2)}) collective-permute-start(bf16[8,8,128]{2,1,0:T(8,128)(2,1)S(1)} %get-tuple-element.31), channel_id=1, source_target_pairs={{0,16},{1,17},{2,18},{3,19},{4,20},{5,21},{6,22},{7,23},{8,24},{9,... | collective-permute-start | bytes 49160 | tf_op jit(solution)/shard_map/ppermute | solution.py:754
  11.6 0.3 %shard_map.142 = (bf16[52,8,128]{2,1,0:T(8,128)(2,1)S(1)}, bf16[52,8,128]{2,1,0:T(8,128)(2,1)S(1)}) custom-call(f32[9,13,8,128]{3,2,1,0:T(8,128)S(1)} %get-tuple-element.29.refs_0_, f32[14,13,8,128]{3,2,1,0:T(8,128)S(1)} %get-tuple-element.30.refs_1_), custom_call_target="tpu_custom_call" | custom-call | tf_op jit(solution)/shard_map/pallas_call | solution.py:650
  11.9 1.9 %collective-permute-done.5.refs_2_ = bf16[8,8,128]{2,1,0:T(8,128)(2,1)S(1)} collective-permute-done((bf16[8,8,128]{2,1,0:T(8,128)(2,1)S(1)}, bf16[8,8,128]{2,1,0:T(8,128)(2,1)S(1)}, u32[]{:S(2)}, u32[]{:S(2)}) %collective-permute-start.5) | collective-permute-done | bytes 16416 | tf_op jit(solution)/shard_map/ppermute | solution.py:754
  13.8 0.1 shard_map.143
  13.9 1.7 %collective-permute-start.6 = (bf16[52,8,128]{2,1,0:T(8,128)(2,1)S(1)}, bf16[52,8,128]{2,1,0:T(8,128)(2,1)S(1)}, u32[]{:S(2)}, u32[]{:S(2)}) collective-permute-start(bf16[52,8,128]{2,1,0:T(8,128)(2,1)S(1)} %get-tuple-element.34), channel_id=1, source_target_pairs={{0,16},{1,5},{2,18},{3,7},{4,8},{5,1},{6,10},{7,3},{8,4},{9,13},{1... | collective-permute-start | bytes 319496 | tf_op jit(solution)/shard_map/ppermute | solution.py:754
  15.5 1.6 %collective-permute-start.7 = (bf16[52,8,128]{2,1,0:T(8,128)(2,1)S(1)}, bf16[52,8,128]{2,1,0:T(8,128)(2,1)S(1)}, u32[]{:S(2)}, u32[]{:S(2)}) collective-permute-start(bf16[52,8,128]{2,1,0:T(8,128)(2,1)S(1)} %get-tuple-element.39), channel_id=1, source_target_pairs={{0,4},{1,17},{2,6},{3,19},{4,0},{5,9},{6,2},{7,11},{8,12},{9,5},{1... | collective-permute-start | bytes 319496 | tf_op jit(solution)/shard_map/ppermute | solution.py:754
  17.2 1.0 %shard_map.144 = (f32[24,13,8,128]{3,2,1,0:T(8,128)S(1)}, f32[8,3,13,8,128]{4,3,2,1,0:T(8,128)S(1)}, f32[11,8,8,128]{3,2,1,0:T(8,128)S(1)}) custom-call(f32[9,13,8,128]{3,2,1,0:T(8,128)S(1)} %get-tuple-element.29.refs_0_, f32[14,13,8,128]{3,2,1,0:T(8,128)S(1)} %get-tuple-element.30.refs_1_, f32[23,8,128]{2,1,0:T(8,128)S(1)} %get-tuple-element.35.refs_2_, ...), custom_call_target="tpu_custom_call" | custom-call | tf_op jit(solution)/shard_map/pallas_call | solution.py:650
  18.2 1.2 %collective-permute-done.6.refs_0_ = bf16[52,8,128]{2,1,0:T(8,128)(2,1)S(1)} collective-permute-done((bf16[52,8,128]{2,1,0:T(8,128)(2,1)S(1)}, bf16[52,8,128]{2,1,0:T(8,128)(2,1)S(1)}, u32[]{:S(2)}, u32[]{:S(2)}) %collective-permute-start.6) | collective-permute-done | bytes 106528 | tf_op jit(solution)/shard_map/ppermute | solution.py:754
  19.4 0.1 shard_map.145.refs_0_
  19.5 0.7 %collective-permute-done.7.refs_3_ = bf16[52,8,128]{2,1,0:T(8,128)(2,1)S(1)} collective-permute-done((bf16[52,8,128]{2,1,0:T(8,128)(2,1)S(1)}, bf16[52,8,128]{2,1,0:T(8,128)(2,1)S(1)}, u32[]{:S(2)}, u32[]{:S(2)}) %collective-permute-start.7) | collective-permute-done | bytes 106528 | tf_op jit(solution)/shard_map/ppermute | solution.py:754
  20.2 1.8 %shard_map.146 = (f32[9,8,8,128]{3,2,1,0:T(8,128)}, f32[8,8,128]{2,1,0:T(8,128)}, f32[8,8,128]{2,1,0:T(8,128)}, f32[24,13,8,128]{3,2,1,0:T(8,128)S(1)}) custom-call(f32[24,13,8,128]{3,2,1,0:T(8,128)S(1)} %shard_map.145.refs_0_, f32[8,3,13,8,128]{4,3,2,1,0:T(8,128)S(1)} %get-tuple-element.37.refs_1_, ...), custom_call_target="tpu_custom_call", output_to_operand_aliasing={{3}: (0, {})} | custom-call | tf_op jit(solution)/shard_map/pallas_call | solution.py:650
  (1 shorter events, 0.0 us)
Async XLA Ops:
  0.6 7.2 %collective-permute-start.1 = (bf16[72,8,128]{2,1,0:T(8,128)(2,1)}, bf16[72,8,128]{2,1,0:T(8,128)(2,1)S(1)}, u32[]{:S(2)}, u32[]{:S(2)}) collective-permute-start(bf16[72,8,128]{2,1,0:T(8,128)(2,1)} %bitcast.6), channel_id=1, source_target_pairs={{0,2},{1,3},{2,0},{3,1},{4,6},{5,7},{6,4},{7,5},{8,10},{9,11},{10,... | collective-permute-start | bytes 442376 | tf_op jit(solution)/shard_map/ppermute | solution.py:695
  4.9 4.4 %collective-permute-start.4 = (bf16[37,8,128]{2,1,0:T(8,128)(2,1)S(1)}, bf16[37,8,128]{2,1,0:T(8,128)(2,1)S(1)}, u32[]{:S(2)}, u32[]{:S(2)}) collective-permute-start(bf16[37,8,128]{2,1,0:T(8,128)(2,1)S(1)} %get-tuple-element.24), channel_id=1, source_target_pairs={{0,16},{1,2},{2,1},{3,19},{4,20},{5,6},{6,5},{7,23},{8,24},{9,10},... | collective-permute-start | bytes 227336 | tf_op jit(solution)/shard_map/ppermute | solution.py:721
  6.5 2.0 %collective-permute-start = (bf16[107,8,128]{2,1,0:T(8,128)(2,1)S(1)}, bf16[107,8,128]{2,1,0:T(8,128)(2,1)S(1)}, u32[]{:S(2)}, u32[]{:S(2)}) collective-permute-start(bf16[107,8,128]{2,1,0:T(8,128)(2,1)S(1)} %get-tuple-element.23.refs_0_), channel_id=1, source_target_pairs={{0,1},{1,0},{2,3},{3,2},{4,5},{5,4},{6,7},{7,6},{8,9},{9,8},{10,11... | collective-permute-start | bytes 657416 | tf_op jit(solution)/shard_map/ppermute | solution.py:713
  7.9 1.5 %collective-permute-start.3 = (bf16[36,8,128]{2,1,0:T(8,128)(2,1)S(1)}, bf16[36,8,128]{2,1,0:T(8,128)(2,1)S(1)}, u32[]{:S(2)}, u32[]{:S(2)}) collective-permute-start(bf16[36,8,128]{2,1,0:T(8,128)(2,1)S(1)} %get-tuple-element.43), channel_id=1, source_target_pairs={{0,1},{1,0},{2,3},{3,2},{4,5},{5,4},{6,7},{7,6},{8,9},{9,8},{10,11... | collective-permute-start | bytes 221192 | tf_op jit(solution)/shard_map/ppermute | solution.py:722
  8.0 1.4 %collective-permute-start.2 = (bf16[36,8,128]{2,1,0:T(8,128)(2,1)S(1)}, bf16[36,8,128]{2,1,0:T(8,128)(2,1)S(1)}, u32[]{:S(2)}, u32[]{:S(2)}) collective-permute-start(bf16[36,8,128]{2,1,0:T(8,128)(2,1)S(1)} %get-tuple-element.44), channel_id=1, source_target_pairs={{0,1},{1,0},{2,3},{3,2},{4,5},{5,4},{6,7},{7,6},{8,9},{9,8},{10,11... | collective-permute-start | bytes 221192 | tf_op jit(solution)/shard_map/ppermute | solution.py:722
  9.9 3.8 %collective-permute-start.5 = (bf16[8,8,128]{2,1,0:T(8,128)(2,1)S(1)}, bf16[8,8,128]{2,1,0:T(8,128)(2,1)S(1)}, u32[]{:S(2)}, u32[]{:S(2)}) collective-permute-start(bf16[8,8,128]{2,1,0:T(8,128)(2,1)S(1)} %get-tuple-element.31), channel_id=1, source_target_pairs={{0,16},{1,17},{2,18},{3,19},{4,20},{5,21},{6,22},{7,23},{8,24},{9,... | collective-permute-start | bytes 49160 | tf_op jit(solution)/shard_map/ppermute | solution.py:754
  13.9 5.5 %collective-permute-start.6 = (bf16[52,8,128]{2,1,0:T(8,128)(2,1)S(1)}, bf16[52,8,128]{2,1,0:T(8,128)(2,1)S(1)}, u32[]{:S(2)}, u32[]{:S(2)}) collective-permute-start(bf16[52,8,128]{2,1,0:T(8,128)(2,1)S(1)} %get-tuple-element.34), channel_id=1, source_target_pairs={{0,16},{1,5},{2,18},{3,7},{4,8},{5,1},{6,10},{7,3},{8,4},{9,13},{1... | collective-permute-start | bytes 319496 | tf_op jit(solution)/shard_map/ppermute | solution.py:754
  15.5 4.7 %collective-permute-start.7 = (bf16[52,8,128]{2,1,0:T(8,128)(2,1)S(1)}, bf16[52,8,128]{2,1,0:T(8,128)(2,1)S(1)}, u32[]{:S(2)}, u32[]{:S(2)}) collective-permute-start(bf16[52,8,128]{2,1,0:T(8,128)(2,1)S(1)} %get-tuple-element.39), channel_id=1, source_target_pairs={{0,4},{1,17},{2,6},{3,19},{4,0},{5,9},{6,2},{7,11},{8,12},{9,5},{1... | collective-permute-start | bytes 319496 | tf_op jit(solution)/shard_map/ppermute | solution.py:754

commit v16 on v12

--- a/solution.py
+++ b/solution.py
@@ -130,12 +130,12 @@
         packed[r // 8, r % 8 : r % 8 + 1, :] = row_of(f, z, y)
 
 
-def pack_tiles(sides, sends, first, count):
+def pack_tiles(sides, sends, firsts, count):
     even = even_mask(("gy", "gz"), sends[0].shape[1:])
     for t in range(count):
         up, down = (side[min(t, len(side) - 1)] for side in sides)
-        sends[0][first + t] = jnp.where(even, down, up).astype(jnp.bfloat16)
-        sends[1][first + t] = jnp.where(even, up, down).astype(jnp.bfloat16)
+        sends[0][firsts[0] + t] = jnp.where(even, down, up).astype(jnp.bfloat16)
+        sends[1][firsts[1] + t] = jnp.where(even, up, down).astype(jnp.bfloat16)
 
 
 def layer_rows_kernel(cz, ring_f, ring_w, send_a, send_b, packed):
@@ -153,24 +153,26 @@
         scatter_rows(packed.at[side, pl.ds(n, w)], wide, row_of)
         rest = [split(packed[side, n + t])[1].astype(jnp.float32) for t in range(w)]
         sides.append([packed[side, t] for t in range(n + w)] + rest)
-    pack_tiles(sides, (send_a, send_b), strip_tiles, tiles)
-
-
-def unpack_rows(cz, cy, first, message, packed, edges):
+    pack_tiles(sides, (send_a, send_b), (0, strip_tiles), tiles)
+    for t in range(tiles, send_a.shape[0]):
+        send_a[t] = jnp.zeros(send_a.shape[1:], send_a.dtype)
+
+
+def unpack_rows(cz, cy, first, strips, message, packed, edges):
     has_lower, has_upper = has_neighbours("gy")
-    strip_tiles, _ = row_tiles(cz, cy)
+    skipped = 0 if first else row_tiles(cz, cy)[0]
     parity = lax.rem(lax.axis_index("gy") + lax.axis_index("gz"), 2)
 
     def side(up, keep):
         narrow, wide, strip = y_rows(cz, cy, up)
         n, w, c = row_counts(cz, cy, up)
         for t in range(n + w):
-            value = message[strip_tiles + t].astype(jnp.float32)
+            value = message[skipped + t].astype(jnp.float32)
             if t >= n:
-                value = value + message[strip_tiles + w + t].astype(jnp.float32)
+                value = value + message[skipped + w + t].astype(jnp.float32)
             packed[t] = value * keep
         for t in range(c):
-            packed[n + w + t] = message[t].astype(jnp.float32) * keep
+            packed[n + w + t] = strips[t].astype(jnp.float32) * keep
         for base, listed in ((0, narrow), (n, wide), (n + w, strip)):
             for r, (f, z, _, y) in enumerate(listed):
                 edges[f, z, y : y + 1, :] = packed[base + r // 8, r % 8 : r % 8 + 1, :]
@@ -184,8 +186,8 @@
         side(False, has_upper)
 
 
-def first_rows_kernel(cz, message, edges_in, edges, packed):
-    unpack_rows(cz, edges.shape[2], True, message, packed, edges)
+def first_rows_kernel(cz, strips, message, edges_in, edges, packed):
+    unpack_rows(cz, edges.shape[2], True, strips, message, packed, edges)
 
 
 def start_kernel(
@@ -388,7 +390,7 @@
     return -(-ADJ // 4) + 2 * -(-(FIELDS - ADJ) // 4)
 
 
-def strip_rows_kernel(cz, ring_f, ring_w, x_a, x_b, y_a_in, y_b_in, strips, y_a, y_b, packed):
+def strip_rows_kernel(cz, ring_f, ring_w, x_a, x_b, y_b_in, strips, y_s, y_b, packed):
     cy, lanes = strips.shape[1], strips.shape[2]
     layers = cz + 2 * HALO
     pair = lax.broadcasted_iota(jnp.int32, (cy, lanes), 1) % 8 // 2
@@ -418,7 +420,7 @@
     for side, up in enumerate((True, False)):
         scatter_rows(packed.at[side], y_rows(cz, cy, up)[2], lambda f, z, y: strips[f, y : y + 1, :])
         sides.append([packed[side, t] for t in range(row_counts(cz, cy, up)[2])])
-    pack_tiles(sides, (y_a, y_b), 0, packed.shape[1])
+    pack_tiles(sides, (y_s, y_b), (0, 0), packed.shape[1])
 
 
 STAGE = {"fv": 0, "fs": 3, "fw": 9, "as": 12, "av": 18, "at": 21}
@@ -595,7 +597,7 @@
 ):
     cy, lanes = middle.shape[2], middle.shape[3]
 
-    unpack_rows(cz, cy, False, message, packed, edges)
+    unpack_rows(cz, cy, False, message, message, packed, edges)
     row = lax.broadcasted_iota(jnp.int32, (cy, lanes), 0)
 
     def after(k, j, z, tile):
@@ -765,16 +767,16 @@
         functools.partial(layer_rows_kernel, cz),
         (ring_f, ring_w),
         [vmem()] * 2,
-        (y_send, y_send),
+        (shape(strip_tiles + tiles + PAD, cy, cx, dtype=bf16), y_send),
         [pltpu.VMEM((2, scratch_tiles, 8, cx), f32)],
     )
-    strips, y_a, y_b = kernel_call(
+    strips, y_s, y_b = kernel_call(
         functools.partial(strip_rows_kernel, cz),
-        (ring_f, ring_w, swap(x_a, 0, None), swap(x_b, 1, None), y_a, y_b),
-        [vmem()] * 6,
-        (shape(FIELDS, cy, cx), y_send, y_send),
+        (ring_f, ring_w, swap(x_a, 0, None), swap(x_b, 1, None), y_b),
+        [vmem()] * 5,
+        (shape(FIELDS, cy, cx), shape(strip_tiles, cy, cx, dtype=bf16), y_send),
         [pltpu.VMEM((2, strip_tiles, 8, cx), f32)],
-        {4 if wide_x else 3: 1, 5 if wide_x else 4: 2},
+        {4 if wide_x else 3: 2},
     )
     edges, sides, middle = kernel_call(
         functools.partial(middle_kernel, cz),
@@ -790,11 +792,11 @@
     row_scratch = pltpu.VMEM((scratch_tiles, 8, cx), f32)
     (edges,) = kernel_call(
         functools.partial(first_rows_kernel, cz),
-        (swap(y_a, None, 0), edges),
-        [vmem()] * 2,
+        (swap(y_s, None, 0), swap(y_a, None, 0), edges),
+        [vmem()] * 3,
         (shape(*edges.shape),),
         [row_scratch],
-        {1: 0},
+        {2: 0},
     )
     result = kernel_call(
         functools.partial(edge_kernel, cz),

time: 22.3 us -> 21.5 us (0.964)
  waiting for transfers between devices: 5.86 us -> 4.47 us
  starting transfers between devices: 10 us -> 10.5 us
    ppermute x3 -> x4, waiting for transfers between devices: 3.91 us -> 2.52 us  [swap(): return lax.ppermute(value, axes, pairs)]
    ppermute x3 -> x4, starting transfers between devices: 4.8 us -> 5.32 us  [swap(): return lax.ppermute(value, axes, pairs)]
  transfers between devices with their start and end apart: 8 -> 9, of which waited for: 5 -> 4; matrix products, arithmetic and copies ran while one was open for 0% -> 0% of each run, Pallas kernels for 14% -> 15%
where the time goes in v16:
time: 21.5 us; the launch traced here: 21.3 us
  starting transfers between devices  10.5 us (49%)
  Pallas kernels  5.61 us (26%)
  waiting for transfers between devices  4.47 us (21%)
  between operations  0.7 us (3%)
    pallas_call x8, Pallas kernels, kernel_call(): pl.pallas_call(run, out_shape=tuple((o for o in out_shape if o is not Non...  5.61 us
    ppermute x4, starting transfers between devices, swap(): return lax.ppermute(value, axes, pairs)  5.32 us
    ppermute x1, starting transfers between devices, on_device(): chip = lax.ppermute(store, 'gz', [(i, i ^ 2) for i in range(holders)])  3 us
    ppermute x4, waiting for transfers between devices, swap(): return lax.ppermute(value, axes, pairs)  2.52 us
    ppermute x1, starting transfers between devices, on_device(): lax.ppermute(to_far, ('gy', 'gz'), [(a[0] * holders + a[1], b[0] * holder...  1.64 us
    ppermute x1, waiting for transfers between devices, on_device(): chip = lax.ppermute(store, 'gz', [(i, i ^ 2) for i in range(holders)])  1.18 us
    ppermute x1, waiting for transfers between devices, on_device(): lax.ppermute(to_far, ('gy', 'gz'), [(a[0] * holders + a[1], b[0] * holder...  0.76 us
    ppermute x2, starting transfers between devices, on_device(): lax.ppermute(part, 'gz', [(i, i ^ 1) for i in range(holders)])  0.57 us
  transfers between devices with their start and end apart: 9, of which 4 were waited for; matrix products, arithmetic and copies ran while one was open for 0% of the time, Pallas kernels for 15%

profile of v16, /device:TPU:0, one launch (start us, length us, event | category | flops | bytes accessed | tf_op | source)
XLA Modules:
  0.0 21.3 jit_solution(2656155330884026756)
XLA Ops:
  0.6 3.0 %collective-permute-start.1 = (bf16[72,8,128]{2,1,0:T(8,128)(2,1)}, bf16[72,8,128]{2,1,0:T(8,128)(2,1)S(1)}, u32[]{:S(2)}, u32[]{:S(2)}) collective-permute-start(bf16[72,8,128]{2,1,0:T(8,128)(2,1)} %bitcast.6), channel_id=1, source_target_pairs={{0,2},{1,3},{2,0},{3,1},{4,6},{5,7},{6,4},{7,5},{8,10},{9,11},{10,... | collective-permute-start | bytes 442376 | tf_op jit(solution)/shard_map/ppermute | solution.py:699
  3.6 1.4 %shard_map.139 = (bf16[107,8,128]{2,1,0:T(8,128)(2,1)S(1)}, bf16[37,8,128]{2,1,0:T(8,128)(2,1)S(1)}, f32[15,8,8,128]{3,2,1,0:T(8,128)S(1)}, s32[8,128]{1,0:T(8,128)S(1)}) custom-call(bf16[72,8,128]{2,1,0:T(8,128)(2,1)} %bitcast.7, f32[9,8,8,128]{3,2,1,0:T(8,128)} %refs_1_.1, f32[8,8,128]{2,1,0:T(8,128)} %refs_2_.1, f32[8,8,128]{2,1,0:T(8,128)} %refs_3_.1, ...), custom_call_target="tpu_custom_call" | custom-call | tf_op jit(solution)/shard_map/pallas_call | solution.py:654
  5.0 1.6 %collective-permute-start.4 = (bf16[37,8,128]{2,1,0:T(8,128)(2,1)S(1)}, bf16[37,8,128]{2,1,0:T(8,128)(2,1)S(1)}, u32[]{:S(2)}, u32[]{:S(2)}) collective-permute-start(bf16[37,8,128]{2,1,0:T(8,128)(2,1)S(1)} %get-tuple-element.24), channel_id=1, source_target_pairs={{0,4},{1,2},{2,1},{3,7},{4,0},{5,6},{6,5},{7,3},{8,12},{9,10},{10,... | collective-permute-start | bytes 227336 | tf_op jit(solution)/shard_map/ppermute | solution.py:723
  6.7 0.0 collective-permute-start
  6.7 1.2 %collective-permute-done.1.refs_2_ = bf16[72,8,128]{2,1,0:T(8,128)(2,1)S(1)} collective-permute-done((bf16[72,8,128]{2,1,0:T(8,128)(2,1)}, bf16[72,8,128]{2,1,0:T(8,128)(2,1)S(1)}, u32[]{:S(2)}, u32[]{:S(2)}) %collective-permute-start.1) | collective-permute-done | bytes 147488 | tf_op jit(solution)/shard_map/ppermute | solution.py:699
  7.9 0.1 collective-permute-start.3
  8.0 0.5 %collective-permute-start.2 = (bf16[36,8,128]{2,1,0:T(8,128)(2,1)S(1)}, bf16[36,8,128]{2,1,0:T(8,128)(2,1)S(1)}, u32[]{:S(2)}, u32[]{:S(2)}) collective-permute-start(bf16[36,8,128]{2,1,0:T(8,128)(2,1)S(1)} %get-tuple-element.44), channel_id=1, source_target_pairs={{0,1},{1,0},{2,3},{3,2},{4,5},{5,4},{6,7},{7,6},{8,9},{9,8},{10,11... | collective-permute-start | bytes 221192 | tf_op jit(solution)/shard_map/ppermute | solution.py:726
  8.5 0.0 collective-permute-done.refs_1_.refs_0_
  8.5 0.3 %shard_map.140 = (f32[9,13,8,128]{3,2,1,0:T(8,128)S(1)}, f32[14,13,8,128]{3,2,1,0:T(8,128)S(1)}) custom-call(bf16[107,8,128]{2,1,0:T(8,128)(2,1)S(1)} %get-tuple-element.23.refs_0_, bf16[107,8,128]{2,1,0:T(8,128)(2,1)S(1)} %collective-permute-done.refs_1_.refs_0_, bf16[72,8,128]{2,1,0:T(8,128)(2,1)S(1)} %collective-permute-done.1.refs_2_, ...), custom_call_target="tpu_custom_call" | custom-call | tf_op jit(solution)/shard_map/pallas_call | solution.py:654
  8.7 0.8 %collective-permute-done.4.refs_3_ = bf16[37,8,128]{2,1,0:T(8,128)(2,1)S(1)} collective-permute-done((bf16[37,8,128]{2,1,0:T(8,128)(2,1)S(1)}, bf16[37,8,128]{2,1,0:T(8,128)(2,1)S(1)}, u32[]{:S(2)}, u32[]{:S(2)}) %collective-permute-start.4) | collective-permute-done | bytes 75808 | tf_op jit(solution)/shard_map/ppermute | solution.py:723
  9.5 0.0 collective-permute-done.3.refs_2_
  9.5 0.0 collective-permute-done.2.refs_1_
  9.5 0.6 %shard_map.141 = (f32[9,13,8,128]{3,2,1,0:T(8,128)S(1)}, f32[14,13,8,128]{3,2,1,0:T(8,128)S(1)}, bf16[11,8,128]{2,1,0:T(8,128)(2,1)S(1)}) custom-call(bf16[107,8,128]{2,1,0:T(8,128)(2,1)S(1)} %collective-permute-done.refs_1_.refs_0_, bf16[36,8,128]{2,1,0:T(8,128)(2,1)S(1)} %collective-permute-done.2.refs_1_, ...), custom_call_target="tpu_custom_call", output_to_operand_aliasing={{0}: (5, {}), {1}: (6, {})} | custom-call | tf_op jit(solution)/shard_map/pallas_call | solution.py:654
  10.1 1.6 %collective-permute-start.5 = (bf16[11,8,128]{2,1,0:T(8,128)(2,1)S(1)}, bf16[11,8,128]{2,1,0:T(8,128)(2,1)S(1)}, u32[]{:S(2)}, u32[]{:S(2)}) collective-permute-start(bf16[11,8,128]{2,1,0:T(8,128)(2,1)S(1)} %get-tuple-element.31), channel_id=1, source_target_pairs={{0,16},{1,17},{2,18},{3,19},{4,20},{5,21},{6,22},{7,23},{8,24},{9,... | collective-permute-start | bytes 67592 | tf_op jit(solution)/shard_map/ppermute | solution.py:761
  11.7 0.3 %shard_map.142 = (bf16[53,8,128]{2,1,0:T(8,128)(2,1)S(1)}, bf16[52,8,128]{2,1,0:T(8,128)(2,1)S(1)}) custom-call(f32[9,13,8,128]{3,2,1,0:T(8,128)S(1)} %get-tuple-element.29.refs_0_, f32[14,13,8,128]{3,2,1,0:T(8,128)S(1)} %get-tuple-element.30.refs_1_), custom_call_target="tpu_custom_call" | custom-call | tf_op jit(solution)/shard_map/pallas_call | solution.py:654
  11.9 0.6 %collective-permute-start.7 = (bf16[53,8,128]{2,1,0:T(8,128)(2,1)S(1)}, bf16[53,8,128]{2,1,0:T(8,128)(2,1)S(1)}, u32[]{:S(2)}, u32[]{:S(2)}) collective-permute-start(bf16[53,8,128]{2,1,0:T(8,128)(2,1)S(1)} %get-tuple-element.34), channel_id=1, source_target_pairs={{0,16},{1,5},{2,18},{3,7},{4,8},{5,1},{6,10},{7,3},{8,4},{9,13},{1... | collective-permute-start | bytes 325640 | tf_op jit(solution)/shard_map/ppermute | solution.py:761
  12.5 1.4 %collective-permute-done.5.refs_2_ = bf16[11,8,128]{2,1,0:T(8,128)(2,1)S(1)} collective-permute-done((bf16[11,8,128]{2,1,0:T(8,128)(2,1)S(1)}, bf16[11,8,128]{2,1,0:T(8,128)(2,1)S(1)}, u32[]{:S(2)}, u32[]{:S(2)}) %collective-permute-start.5) | collective-permute-done | bytes 22560 | tf_op jit(solution)/shard_map/ppermute | solution.py:761
  13.9 0.1 shard_map.143
  14.1 1.6 %collective-permute-start.8 = (bf16[52,8,128]{2,1,0:T(8,128)(2,1)S(1)}, bf16[52,8,128]{2,1,0:T(8,128)(2,1)S(1)}, u32[]{:S(2)}, u32[]{:S(2)}) collective-permute-start(bf16[52,8,128]{2,1,0:T(8,128)(2,1)S(1)} %get-tuple-element.39), channel_id=1, source_target_pairs={{0,4},{1,17},{2,6},{3,19},{4,0},{5,9},{6,2},{7,11},{8,12},{9,5},{1... | collective-permute-start | bytes 319496 | tf_op jit(solution)/shard_map/ppermute | solution.py:761
  15.7 1.5 %collective-permute-start.6 = (bf16[3,8,128]{2,1,0:T(8,128)(2,1)S(1)}, bf16[3,8,128]{2,1,0:T(8,128)(2,1)S(1)}, u32[]{:S(2)}, u32[]{:S(2)}) collective-permute-start(bf16[3,8,128]{2,1,0:T(8,128)(2,1)S(1)} %get-tuple-element.33), channel_id=1, source_target_pairs={{0,16},{1,5},{2,18},{3,7},{4,8},{5,1},{6,10},{7,3},{8,4},{9,13},{1... | collective-permute-start | bytes 18440 | tf_op jit(solution)/shard_map/ppermute | solution.py:761
  17.2 1.0 %shard_map.144 = (f32[24,13,8,128]{3,2,1,0:T(8,128)S(1)}, f32[8,3,13,8,128]{4,3,2,1,0:T(8,128)S(1)}, f32[11,8,8,128]{3,2,1,0:T(8,128)S(1)}) custom-call(f32[9,13,8,128]{3,2,1,0:T(8,128)S(1)} %get-tuple-element.29.refs_0_, f32[14,13,8,128]{3,2,1,0:T(8,128)S(1)} %get-tuple-element.30.refs_1_, f32[23,8,128]{2,1,0:T(8,128)S(1)} %get-tuple-element.35.refs_2_, ...), custom_call_target="tpu_custom_call" | custom-call | tf_op jit(solution)/shard_map/pallas_call | solution.py:654
  18.3 1.1 %collective-permute-done.6.refs_0_ = bf16[3,8,128]{2,1,0:T(8,128)(2,1)S(1)} collective-permute-done((bf16[3,8,128]{2,1,0:T(8,128)(2,1)S(1)}, bf16[3,8,128]{2,1,0:T(8,128)(2,1)S(1)}, u32[]{:S(2)}, u32[]{:S(2)}) %collective-permute-start.6) | collective-permute-done | bytes 6176 | tf_op jit(solution)/shard_map/ppermute | solution.py:761
  19.3 0.1 shard_map.145.refs_0_
  19.5 1.8 %shard_map.146 = (f32[9,8,8,128]{3,2,1,0:T(8,128)}, f32[8,8,128]{2,1,0:T(8,128)}, f32[8,8,128]{2,1,0:T(8,128)}, f32[24,13,8,128]{3,2,1,0:T(8,128)S(1)}) custom-call(f32[24,13,8,128]{3,2,1,0:T(8,128)S(1)} %shard_map.145.refs_0_, f32[8,3,13,8,128]{4,3,2,1,0:T(8,128)S(1)} %get-tuple-element.37.refs_1_, ...), custom_call_target="tpu_custom_call", output_to_operand_aliasing={{3}: (0, {})} | custom-call | tf_op jit(solution)/shard_map/pallas_call | solution.py:654
  (3 shorter events, 0.0 us)
Async XLA Ops:
  0.6 7.2 %collective-permute-start.1 = (bf16[72,8,128]{2,1,0:T(8,128)(2,1)}, bf16[72,8,128]{2,1,0:T(8,128)(2,1)S(1)}, u32[]{:S(2)}, u32[]{:S(2)}) collective-permute-start(bf16[72,8,128]{2,1,0:T(8,128)(2,1)} %bitcast.6), channel_id=1, source_target_pairs={{0,2},{1,3},{2,0},{3,1},{4,6},{5,7},{6,4},{7,5},{8,10},{9,11},{10,... | collective-permute-start | bytes 442376 | tf_op jit(solution)/shard_map/ppermute | solution.py:699
  5.0 4.4 %collective-permute-start.4 = (bf16[37,8,128]{2,1,0:T(8,128)(2,1)S(1)}, bf16[37,8,128]{2,1,0:T(8,128)(2,1)S(1)}, u32[]{:S(2)}, u32[]{:S(2)}) collective-permute-start(bf16[37,8,128]{2,1,0:T(8,128)(2,1)S(1)} %get-tuple-element.24), channel_id=1, source_target_pairs={{0,4},{1,2},{2,1},{3,7},{4,0},{5,6},{6,5},{7,3},{8,12},{9,10},{10,... | collective-permute-start | bytes 227336 | tf_op jit(solution)/shard_map/ppermute | solution.py:723
  6.7 1.8 %collective-permute-start = (bf16[107,8,128]{2,1,0:T(8,128)(2,1)S(1)}, bf16[107,8,128]{2,1,0:T(8,128)(2,1)S(1)}, u32[]{:S(2)}, u32[]{:S(2)}) collective-permute-start(bf16[107,8,128]{2,1,0:T(8,128)(2,1)S(1)} %get-tuple-element.23.refs_0_), channel_id=1, source_target_pairs={{0,1},{1,0},{2,3},{3,2},{4,5},{5,4},{6,7},{7,6},{8,9},{9,8},{10,11... | collective-permute-start | bytes 657416 | tf_op jit(solution)/shard_map/ppermute | solution.py:717
  7.9 1.6 %collective-permute-start.3 = (bf16[36,8,128]{2,1,0:T(8,128)(2,1)S(1)}, bf16[36,8,128]{2,1,0:T(8,128)(2,1)S(1)}, u32[]{:S(2)}, u32[]{:S(2)}) collective-permute-start(bf16[36,8,128]{2,1,0:T(8,128)(2,1)S(1)} %get-tuple-element.43), channel_id=1, source_target_pairs={{0,1},{1,0},{2,3},{3,2},{4,5},{5,4},{6,7},{7,6},{8,9},{9,8},{10,11... | collective-permute-start | bytes 221192 | tf_op jit(solution)/shard_map/ppermute | solution.py:726
  8.0 1.5 %collective-permute-start.2 = (bf16[36,8,128]{2,1,0:T(8,128)(2,1)S(1)}, bf16[36,8,128]{2,1,0:T(8,128)(2,1)S(1)}, u32[]{:S(2)}, u32[]{:S(2)}) collective-permute-start(bf16[36,8,128]{2,1,0:T(8,128)(2,1)S(1)} %get-tuple-element.44), channel_id=1, source_target_pairs={{0,1},{1,0},{2,3},{3,2},{4,5},{5,4},{6,7},{7,6},{8,9},{9,8},{10,11... | collective-permute-start | bytes 221192 | tf_op jit(solution)/shard_map/ppermute | solution.py:726
  10.1 3.9 %collective-permute-start.5 = (bf16[11,8,128]{2,1,0:T(8,128)(2,1)S(1)}, bf16[11,8,128]{2,1,0:T(8,128)(2,1)S(1)}, u32[]{:S(2)}, u32[]{:S(2)}) collective-permute-start(bf16[11,8,128]{2,1,0:T(8,128)(2,1)S(1)} %get-tuple-element.31), channel_id=1, source_target_pairs={{0,16},{1,17},{2,18},{3,19},{4,20},{5,21},{6,22},{7,23},{8,24},{9,... | collective-permute-start | bytes 67592 | tf_op jit(solution)/shard_map/ppermute | solution.py:761
  11.9 7.4 %collective-permute-start.7 = (bf16[53,8,128]{2,1,0:T(8,128)(2,1)S(1)}, bf16[53,8,128]{2,1,0:T(8,128)(2,1)S(1)}, u32[]{:S(2)}, u32[]{:S(2)}) collective-permute-start(bf16[53,8,128]{2,1,0:T(8,128)(2,1)S(1)} %get-tuple-element.34), channel_id=1, source_target_pairs={{0,16},{1,5},{2,18},{3,7},{4,8},{5,1},{6,10},{7,3},{8,4},{9,13},{1... | collective-permute-start | bytes 325640 | tf_op jit(solution)/shard_map/ppermute | solution.py:761
  14.1 5.4 %collective-permute-start.8 = (bf16[52,8,128]{2,1,0:T(8,128)(2,1)S(1)}, bf16[52,8,128]{2,1,0:T(8,128)(2,1)S(1)}, u32[]{:S(2)}, u32[]{:S(2)}) collective-permute-start(bf16[52,8,128]{2,1,0:T(8,128)(2,1)S(1)} %get-tuple-element.39), channel_id=1, source_target_pairs={{0,4},{1,17},{2,6},{3,19},{4,0},{5,9},{6,2},{7,11},{8,12},{9,5},{1... | collective-permute-start | bytes 319496 | tf_op jit(solution)/shard_map/ppermute | solution.py:761
  15.7 3.6 %collective-permute-start.6 = (bf16[3,8,128]{2,1,0:T(8,128)(2,1)S(1)}, bf16[3,8,128]{2,1,0:T(8,128)(2,1)S(1)}, u32[]{:S(2)}, u32[]{:S(2)}) collective-permute-start(bf16[3,8,128]{2,1,0:T(8,128)(2,1)S(1)} %get-tuple-element.33), channel_id=1, source_target_pairs={{0,16},{1,5},{2,18},{3,7},{4,8},{5,1},{6,10},{7,3},{8,4},{9,13},{1... | collective-permute-start | bytes 18440 | tf_op jit(solution)/shard_map/ppermute | solution.py:761
